TPU v7x, 512 devices: a whole 4x8x8 slice. The times are simulated.
512 devices in a mesh: dp: 8 (over y_hi, core), sp: 64 (over z, y_lo, x).
Axes of the slice: x: 4, y: 8 (y_hi: 4, y_lo: 2; y = y_hi * 2 + y_lo), z: 8, core: 2. Of those that a mesh axis runs over, the one named last changes fastest.
Arguments:
- query: bfloat16 [8, 256, 64, 576], P('dp', 'sp'), may hold values from -320 to 320
- latent: bfloat16 [8, 4096, 576], P('dp', 'sp'), may hold values from -6 to 6
- dout: bfloat16 [8, 256, 64, 512], P('dp', 'sp'), may hold values from -6 to 6
- hidden: bfloat16 [8, 4096, 7168], P('dp', 'sp'), may hold values from -0.119628906 to 0.119628906
Outputs:
- dquery: bfloat16 [8, 256, 64, 576], P('dp', 'sp')
- dlatent: float32 [8, 4096, 576], P('dp', 'sp')
- dweight: float32 [7168, 64], P(('dp', 'sp'))
All inputs are finite; a program needn't handle non-finite values.
Results may differ from a plain program's by a relative error of at most 0.039.
Values may be sent and summed in bfloat16 or wider, within the bound.
No kernel may reach another device: no remote copies, remote signals or barrier semaphores. Data moves between devices by JAX's collectives and lax.ppermute only.
A program may use at most 128 MiB of HBM per device.

v0:
```python
import jax
import jax.numpy as jnp
from jax import lax
from jax.sharding import PartitionSpec as P

softmax_scale = 0.07216878364870323


def attend(query_rows, dout_rows, positions, keys):
    lat_width = dout_rows.shape[1]
    rope_width = keys.shape[1] - lat_width
    scores = (
        lax.dot_general(
            query_rows, keys, (((1,), (1,)), ((), ())), preferred_element_type=jnp.float32
        )
        * softmax_scale
    )
    key_pos = jnp.arange(keys.shape[0], dtype=jnp.int32)
    scores = jnp.where(key_pos[None, :] <= positions[:, None], scores, -jnp.inf)
    top = jnp.max(scores, axis=1, keepdims=True)
    expd = jnp.exp(scores - top)
    probs = expd / jnp.sum(expd, axis=1, keepdims=True)
    probs_low = probs.astype(jnp.bfloat16)
    value = keys[:, :lat_width]
    out = jnp.dot(probs_low, value, preferred_element_type=jnp.float32)
    delta = jnp.sum(dout_rows.astype(jnp.float32) * out, axis=1, keepdims=True)
    dprobs = lax.dot_general(
        dout_rows, value, (((1,), (1,)), ((), ())), preferred_element_type=jnp.float32
    )
    dscores_low = (probs * (dprobs - delta)).astype(jnp.bfloat16)
    dq_rows = (
        jnp.dot(dscores_low, keys, preferred_element_type=jnp.float32) * softmax_scale
    ).astype(jnp.bfloat16)
    from_scores = (
        lax.dot_general(
            dscores_low, query_rows, (((0,), (0,)), ((), ())), preferred_element_type=jnp.float32
        )
        * softmax_scale
    )
    from_values = lax.dot_general(
        probs_low, dout_rows, (((0,), (0,)), ((), ())), preferred_element_type=jnp.float32
    )
    return (dq_rows, from_scores + jnp.pad(from_values, ((0, 0), (0, rope_width))))


def body(query, latent, dout, hidden):
    n_seq = lax.axis_size("sp")
    n_data = lax.axis_size("dp")
    q_dev = query.shape[1]
    heads = query.shape[2]
    width = query.shape[3]
    lat_width = dout.shape[3]
    k_dev = latent.shape[1]
    k_total = k_dev * n_seq
    q_total = q_dev * n_seq
    keys = lax.all_gather(latent[0], "sp", axis=0, tiled=True)
    q_heads, d_heads = (
        lax.all_to_all(query, "sp", split_axis=2, concat_axis=1, tiled=True),
        lax.all_to_all(dout, "sp", split_axis=2, concat_axis=1, tiled=True),
    )
    local = heads // n_seq
    query_rows = q_heads.reshape(q_total * local, width)
    dout_rows = d_heads.reshape(q_total * local, lat_width)
    grid = jnp.arange(q_total, dtype=jnp.int32)[:, None]
    positions = (grid + (k_total - q_total)).reshape(-1)
    dq_rows, partial_value = attend(query_rows, dout_rows, positions, keys)
    dquery = lax.all_to_all(
        dq_rows.reshape(1, q_total, local, width), "sp", split_axis=1, concat_axis=2, tiled=True
    )
    received = lax.all_to_all(
        partial_value.reshape(n_seq, k_dev, width).astype(jnp.bfloat16),
        "sp",
        split_axis=0,
        concat_axis=0,
        tiled=True,
    ).astype(jnp.float32)
    mine = jnp.sum(received, axis=0)
    rope_all = lax.all_gather(mine[:, lat_width:].astype(jnp.bfloat16), "sp", axis=0, tiled=True)
    model = hidden.shape[2]
    block = model // (n_data * n_seq)
    columns = lax.all_to_all(
        hidden.reshape(1, k_dev, n_data, n_seq, block),
        "sp",
        split_axis=3,
        concat_axis=1,
        tiled=True,
    )
    columns = columns.reshape(k_total, n_data * block)
    terms = lax.dot_general(
        columns, rope_all, (((0,), (0,)), ((), ())), preferred_element_type=jnp.float32
    )
    rope_width = width - lat_width
    dweight = lax.psum_scatter(
        terms.reshape(n_data, block, rope_width), "dp", scatter_dimension=0, tiled=True
    ).reshape(block, rope_width)
    return (dquery, mine[None], dweight)


def solution(mesh):
    in_specs = (
        P("dp", "sp", None, None),
        P("dp", "sp", None),
        P("dp", "sp", None, None),
        P("dp", "sp", None),
    )
    out_specs = (P("dp", "sp", None, None), P("dp", "sp", None), P(("dp", "sp"), None))
    return jax.shard_map(body, mesh=mesh, in_specs=in_specs, out_specs=out_specs, check_vma=False)
```

profile of v0, /device:TPU:6, one launch (start us, length us, event | category | flops | bytes accessed | tf_op | source)
XLA Modules:
  0.0 671.0 jit_solution(14946203204328737894)
XLA Ops:
  7.9 1.9 copy.19
  9.8 14.8 %all-to-all-start.1 = ((bf16[1,4,64,512]{3,1,0,2:T(4,128)(2,1)}), bf16[1,4,64,512]{3,1,0,2:T(4,128)(2,1)S(1)}, u32[]{:S(2)}, u32[]{:S(2)}) async-start(bf16[1,4,64,512]{3,1,0,2:T(4,128)(2,1)} %copy.19), calls=%async_computation.1 | async-start | bytes 524288 | tf_op jit(solution)/shard_map/all_to_all | solution.py:59
  24.6 2.0 copy.18
  26.5 9.4 %all-to-all-done.1 = bf16[1,4,64,512]{3,1,0,2:T(4,128)(2,1)S(1)} async-done(((bf16[1,4,64,512]{3,1,0,2:T(4,128)(2,1)}), bf16[1,4,64,512]{3,1,0,2:T(4,128)(2,1)S(1)}, u32[]{:S(2)}, u32[]{:S(2)}) %all-to-all-start.1) | async-done | bytes 262176 | tf_op jit(solution)/shard_map/all_to_all | solution.py:59
  35.9 6.8 %all-to-all-start = ((bf16[1,4,64,576]{3,1,0,2:T(4,128)(2,1)}), bf16[1,4,64,576]{3,1,0,2:T(4,128)(2,1)S(1)}, u32[]{:S(2)}, u32[]{:S(2)}) async-start(bf16[1,4,64,576]{3,1,0,2:T(4,128)(2,1)} %copy.18), calls=%async_computation | async-start | bytes 655360 | tf_op jit(solution)/shard_map/all_to_all | solution.py:58
  42.7 2.6 copy.22
  45.3 2.7 reshape.43
  48.0 3.4 copy.29
  51.4 4.2 reshape.51
  55.7 1.3 all-to-all-done
  57.0 9.9 %all-to-all-start.4 = ((bf16[64,2,3584]{2,1,0:T(2,128)(2,1)}), bf16[64,2,3584]{2,1,0:T(2,128)(2,1)S(1)}, u32[]{:S(2)}, u32[]{:S(2)}) async-start(bf16[64,2,3584]{2,1,0:T(2,128)(2,1)} %reshape.51), calls=%async_computation.4 | async-start | bytes 1835008 | tf_op jit(solution)/shard_map/all_to_all | solution.py:81
  67.1 254.0 %all-gather.3.cloned.1.call-done = bf16[1,4096,576]{2,1,0:T(8,128)(2,1)} async-done(((bf16[1,64,576]{2,1,0:T(8,128)(2,1)}), bf16[1,4096,576]{2,1,0:T(8,128)(2,1)}) %all-gather.3.cloned.1.call-update) | async-done | bytes 4718608 | tf_op jit(solution)/shard_map/all_gather | solution.py:56
  321.1 4.7 fusion.23
  326.6 1.4 fusion.13
  328.0 1.7 fusion.2
  329.7 1.3 copy-done.3
  331.0 2.1 fusion.12
  334.3 2.7 reduce.2
  337.0 1.1 reshape.49
  338.1 12.4 %all-to-all-start.2 = ((bf16[64,2,1152]{2,1,0:T(2,128)(2,1)}), bf16[64,2,1152]{2,1,0:T(2,128)(2,1)S(1)}, u32[]{:S(2)}, u32[]{:S(2)}) async-start(bf16[64,2,1152]{2,1,0:T(2,128)(2,1)} %reshape.49), calls=%async_computation.2 | async-start | bytes 589824 | tf_op jit(solution)/shard_map/all_to_all | solution.py:67
  350.5 3.8 fusion.16
  354.3 3.8 add_convert_fusion
  358.1 7.6 %copy.21 = bf16[4096,576]{1,0:T(8,128)(2,1)} copy(bf16[4096,576]{0,1:T(8,128)(2,1)} %add_convert_fusion) | data formatting | bytes 9437184 | tf_op jit(solution)/shard_map/convert_element_type | solution.py:71
  365.7 18.1 %all-to-all-done.2 = bf16[64,2,1152]{2,1,0:T(2,128)(2,1)S(1)} async-done(((bf16[64,2,1152]{2,1,0:T(2,128)(2,1)}), bf16[64,2,1152]{2,1,0:T(2,128)(2,1)S(1)}, u32[]{:S(2)}, u32[]{:S(2)}) %all-to-all-start.2) | async-done | bytes 294944 | tf_op jit(solution)/shard_map/all_to_all | solution.py:67
  383.9 10.3 %all-to-all-start.3 = ((bf16[64,64,576]{2,1,0:T(8,128)(2,1)}), bf16[64,64,576]{2,1,0:T(8,128)(2,1)}, u32[]{:S(2)}, u32[]{:S(2)}) async-start(bf16[64,64,576]{2,1,0:T(8,128)(2,1)} %bitcast.53), calls=%async_computation.3 | async-start | bytes 10485760 | tf_op jit(solution)/shard_map/all_to_all | solution.py:70
  394.3 1.1 reshape.52
  396.0 1.5 reshape.44
  398.0 66.4 %all-to-all-done.3 = bf16[64,64,576]{2,1,0:T(8,128)(2,1)} async-done(((bf16[64,64,576]{2,1,0:T(8,128)(2,1)}), bf16[64,64,576]{2,1,0:T(8,128)(2,1)}, u32[]{:S(2)}, u32[]{:S(2)}) %all-to-all-start.3) | async-done | bytes 4718624 | tf_op jit(solution)/shard_map/all_to_all | solution.py:70
  464.4 3.3 convert_reduce_fusion
  467.7 149.3 %all_gather.7 = bf16[4096,64]{1,0:T(8,128)(2,1)S(1)} all-gather(bf16[64,64]{1,0:T(8,128)(2,1)S(1)} %slice.20), channel_id=1, replica_groups=mesh['dp'=8,'sp'=64] {'sp'}, dimensions={0}, use_global_device_ids=true | all-gather | bytes 532480 | tf_op jit(solution)/shard_map/all_gather | solution.py:78
  618.2 1.8 bitcast_reduce_fusion
  620.9 43.3 %reduce-scatter.2.cloned.1.call-done = f32[1,14,64]{2,1,0:T(8,128)} async-done(((f32[8,14,64]{2,1,0:T(8,128)}), f32[1,14,64]{2,1,0:T(8,128)}) %reduce-scatter.2.cloned.1.call-update) | async-done | bytes 3600 | tf_op jit(solution)/shard_map/reduce_scatter | solution.py:93
  (29 shorter events, 6.0 us)
Async XLA Ops:
  7.2 314.0 %all-gather.3.cloned.1.call-start = ((), (), s32[]{:S(2)}) async-start(), calls=%async_computation.7 | async-start | bytes 5324800 | tf_op jit(solution)/shard_map/all_gather | solution.py:56
  9.8 26.1 %all-to-all-start.1 = ((bf16[1,4,64,512]{3,1,0,2:T(4,128)(2,1)}), bf16[1,4,64,512]{3,1,0,2:T(4,128)(2,1)S(1)}, u32[]{:S(2)}, u32[]{:S(2)}) async-start(bf16[1,4,64,512]{3,1,0,2:T(4,128)(2,1)} %copy.19), calls=%async_computation.1 | async-start | bytes 524288 | tf_op jit(solution)/shard_map/all_to_all | solution.py:59
  35.9 21.1 %all-to-all-start = ((bf16[1,4,64,576]{3,1,0,2:T(4,128)(2,1)}), bf16[1,4,64,576]{3,1,0,2:T(4,128)(2,1)S(1)}, u32[]{:S(2)}, u32[]{:S(2)}) async-start(bf16[1,4,64,576]{3,1,0,2:T(4,128)(2,1)} %copy.18), calls=%async_computation | async-start | bytes 655360 | tf_op jit(solution)/shard_map/all_to_all | solution.py:58
  57.0 281.1 %all-to-all-start.4 = ((bf16[64,2,3584]{2,1,0:T(2,128)(2,1)}), bf16[64,2,3584]{2,1,0:T(2,128)(2,1)S(1)}, u32[]{:S(2)}, u32[]{:S(2)}) async-start(bf16[64,2,3584]{2,1,0:T(2,128)(2,1)} %reshape.51), calls=%async_computation.4 | async-start | bytes 1835008 | tf_op jit(solution)/shard_map/all_to_all | solution.py:81
  321.1 5.5 copy-start.2
  325.9 2.1 copy-start
  329.7 1.3 copy-start.3
  338.1 45.8 %all-to-all-start.2 = ((bf16[64,2,1152]{2,1,0:T(2,128)(2,1)}), bf16[64,2,1152]{2,1,0:T(2,128)(2,1)S(1)}, u32[]{:S(2)}, u32[]{:S(2)}) async-start(bf16[64,2,1152]{2,1,0:T(2,128)(2,1)} %reshape.49), calls=%async_computation.2 | async-start | bytes 589824 | tf_op jit(solution)/shard_map/all_to_all | solution.py:67
  350.5 3.8 copy-start.4
  383.9 80.6 %all-to-all-start.3 = ((bf16[64,64,576]{2,1,0:T(8,128)(2,1)}), bf16[64,64,576]{2,1,0:T(8,128)(2,1)}, u32[]{:S(2)}, u32[]{:S(2)}) async-start(bf16[64,64,576]{2,1,0:T(8,128)(2,1)} %bitcast.53), calls=%async_computation.3 | async-start | bytes 10485760 | tf_op jit(solution)/shard_map/all_to_all | solution.py:70
  394.2 270.0 %reduce-scatter.2.cloned.1.call-start = ((), (), s32[]{:S(2)}) async-start(), calls=%async_computation.6 | async-start | bytes 73728 | tf_op jit(solution)/shard_map/reduce_scatter | solution.py:93
  467.7 196.5 %copy-start.1 = (f32[64,576]{1,0:T(8,128)}, f32[64,576]{1,0:T(8,128)S(1)}, u32[]{:S(2)}) copy-start(f32[64,576]{1,0:T(8,128)S(1)} %convert_reduce_fusion) | copy-start | bytes 442372
Sparse Core Ops, SparseCore 0:
  10.1 310.9 all-gather.2
  618.3 45.7 reduce-scatter.1
where the time goes:
time: 672 us; the launch traced here: 671 us
  waiting for transfers between devices  393 us (58%)
  blocking collectives  149 us (22%)
  starting transfers between devices  54.3 us (8%)
  local copies, waits for them, and re-layouts  35.3 us (5%)
  matrix products  17.9 us (3%)
  between operations  14.3 us (2%)
    all_gather x1, waiting for transfers between devices, body(): keys = lax.all_gather(latent[0], 'sp', axis=0, tiled=True)  254 us
    all_gather x1, blocking collectives, body(): lax.all_gather(mine[:, lat_width:].astype(jnp.bfloat16), 'sp', axis=0, ti...  149 us
    all_to_all x1, waiting for transfers between devices, body(): lax.all_to_all(partial_value.reshape(n_seq, k_dev, width).astype(jnp.bflo...  66.4 us
    reduce_scatter x1, waiting for transfers between devices, body(): lax.psum_scatter(terms.reshape(n_data, block, rope_width), 'dp', scatter_...  43.3 us
    all_to_all x1, waiting for transfers between devices, body(): lax.all_to_all(dq_rows.reshape(1, q_total, local, width), 'sp', split_axi...  18.1 us
    unnamed x19, local copies, waits for them, and re-layouts  16 us
    all_to_all x1, starting transfers between devices, body(): lax.all_to_all(dout, 'sp', split_axis=2, concat_axis=1, tiled=True)  14.8 us
  transfers between devices with their start and end apart: 7, of which 6 were waited for; matrix products, arithmetic and copies ran while one was open for 8% of the time, Pallas kernels for 0%

commit v1 on v0

v1 whole, which is shorter than its diff:
```python
import jax
import jax.numpy as jnp
from jax import lax
from jax.sharding import Mesh, PartitionSpec as P

softmax_scale = 0.07216878364870323
f32, bf16 = jnp.float32, jnp.bfloat16


def fetch(value, offset, n):
    return lax.ppermute(value, "x", [(s, (s - offset) % n) for s in range(n)])


def spread(value, axes, n):
    return lax.all_to_all(
        jnp.broadcast_to(value[None], (n,) + value.shape), axes, 0, 0, tiled=True
    )


def body(query, latent, dout, hidden):
    nd, nz, ny, nx = (lax.axis_size(a) for a in ("dp", "z", "y", "x"))
    grp = nz * ny
    tok, heads, width = query.shape[1:]
    lat_width = dout.shape[3]
    rope_width = width - lat_width
    k_dev, model = hidden.shape[1:]
    rows = tok * heads
    k_total = k_dev * grp * nx
    q_total = tok * grp * nx
    z, y, x = (lax.axis_index(a) for a in ("z", "y", "x"))
    q0 = query.reshape(rows, width)
    o0 = dout.reshape(rows, lat_width)
    keys = spread(latent[0], ("z", "y"), grp).reshape(grp * k_dev, width)
    q = jnp.concatenate([q0] + [fetch(q0, k, nx) for k in range(1, nx)])
    o = jnp.concatenate([o0] + [fetch(o0, k, nx) for k in range(1, nx)])
    value = keys[:, :lat_width]
    block = model // (nd * grp * nx)
    cols = hidden[0].reshape(k_dev, nd, grp, nx * block).transpose(2, 0, 1, 3)
    cols = cols.reshape(grp, k_dev, nd * nx * block)
    cols = lax.all_to_all(cols, ("z", "y"), 0, 0, tiled=True).reshape(grp * k_dev, -1)

    n_rows, n_keys = nx * rows, grp * k_dev
    r = jnp.arange(n_rows, dtype=jnp.int32)
    owner = lax.rem(x + r // rows, nx)
    q_pos = ((z * ny + y) * nx + owner) * tok + (r % rows) // heads
    j = jnp.arange(n_keys, dtype=jnp.int32)
    k_pos = ((j // k_dev) * nx + x) * k_dev + j % k_dev
    s = lax.dot_general(q, keys, (((1,), (1,)), ((), ())), preferred_element_type=f32)
    s = s * softmax_scale
    s = jnp.where(k_pos[None, :] <= q_pos[:, None] + (k_total - q_total), s, -jnp.inf)
    m = jnp.max(s, axis=1)
    e = jnp.exp(s - m[:, None])
    l = jnp.sum(e, axis=1)
    dp = lax.dot_general(o, value, (((1,), (1,)), ((), ())), preferred_element_type=f32)
    d = jnp.sum(e * dp, axis=1)
    mine = jnp.stack([m, l, d]).reshape(3, nx, rows)
    stats = [mine]
    for k in range(1, nx):
        stats.append(jnp.roll(fetch(mine, k, nx), k, axis=1))
    stats = jnp.stack(stats).reshape(nx, 3, n_rows)
    top = jnp.max(stats[:, 0], axis=0)
    w = jnp.exp(stats[:, 0] - top)
    total = jnp.sum(stats[:, 1] * w, axis=0)
    delta = jnp.sum(stats[:, 2] * w, axis=0) / total
    f = jnp.exp(m - top) / total
    p = e * f[:, None]
    p_low = p.astype(bf16)
    ds = (p * (dp - delta[:, None])).astype(bf16)

    def down(a, b):
        return lax.dot_general(a, b, (((0,), (0,)), ((), ())), preferred_element_type=f32)

    rope = (down(ds, q[:, lat_width:]) * softmax_scale).astype(bf16)
    rope = lax.all_to_all(rope.reshape(grp, k_dev, rope_width), ("z", "y"), 0, 0, tiled=True)
    rope = jnp.sum(rope.astype(f32), axis=0)
    rope_all = spread(rope.astype(bf16), ("z", "y"), grp).reshape(n_keys, rope_width)
    terms = down(cols, rope_all).reshape(nd, nx, block, rope_width)
    terms = lax.all_to_all(terms.reshape(nd * nx, block, rope_width), ("dp", "x"), 0, 0, tiled=True)
    dweight = jnp.sum(terms, axis=0)

    lat = (down(ds, q[:, :lat_width]) * softmax_scale + down(p_low, o)).astype(bf16)
    lat = lax.all_to_all(lat.reshape(grp, k_dev, lat_width), ("z", "y"), 0, 0, tiled=True)
    lat = jnp.sum(lat.astype(f32), axis=0)
    dlatent = jnp.concatenate([lat, rope], axis=1)[None]

    dq = jnp.dot(ds, keys, preferred_element_type=f32) * softmax_scale
    total_q = dq[:rows]
    parts = [fetch(dq[k * rows : (k + 1) * rows].astype(bf16), nx - k, nx) for k in range(1, nx)]
    for part in parts:
        total_q = total_q + part.astype(f32)
    dquery = total_q.astype(bf16).reshape(1, tok, heads, width)
    return dquery, dlatent, dweight


def solution(mesh):
    fine = Mesh(mesh.devices.reshape(8, 8, 2, 4), ("dp", "z", "y", "x"))
    sp = ("z", "y", "x")
    in_specs = (
        P("dp", sp, None, None),
        P("dp", sp, None),
        P("dp", sp, None, None),
        P("dp", sp, None),
    )
    out_specs = (P("dp", sp, None, None), P("dp", sp, None), P(("dp",) + sp, None))
    return jax.shard_map(body, mesh=fine, in_specs=in_specs, out_specs=out_specs, check_vma=False)
```

time: 672 us -> 197 us (0.29)
  waiting for transfers between devices: 393 us -> 50 us
  blocking collectives: 149 us -> 14.4 us
  starting transfers between devices: 54.3 us -> 73.7 us
  local copies, waits for them, and re-layouts: 35.3 us -> 22.1 us
  between operations: 14.3 us -> 1.12 us
    all_gather x1 -> x0, waiting for transfers between devices: 254 us -> none  [body(): keys = lax.all_gather(latent[0], 'sp', axis=0, tiled=True)]
    all_gather x1 -> x0, blocking collectives: 149 us -> none  [body(): lax.all_gather(mine[:, lat_width:].astype(jnp.bfloat16), 'sp', axis=0, ti...]
    all_to_all x5, waiting for transfers between devices: 95.2 us -> 34.8 us  [the longest x1 20.3 us: body(): lax.all_to_all(cols, ('z', 'y'), 0, 0, tiled=True).reshape(grp * k_dev, -1)]
    reduce_scatter x1 -> x0, waiting for transfers between devices: 43.3 us -> none  [body(): lax.psum_scatter(terms.reshape(n_data, block, rope_width), 'dp', scatter_...]
    ppermute x0 -> x12, starting transfers between devices: none -> 37.9 us  [fetch(): return lax.ppermute(value, 'x', [(s, (s - offset) % n) for s in range(n)])]
    all_to_all x5, starting transfers between devices: 54.3 us -> 35.7 us  [the longest x2 14.9 us: spread(): lax.all_to_all(jnp.broadcast_to(value[None], (n,) + value.shape), axes, 0...]
    ppermute x0 -> x12, waiting for transfers between devices: none -> 15.2 us  [fetch(): return lax.ppermute(value, 'x', [(s, (s - offset) % n) for s in range(n)])]
    all_to_all x0 -> x1, blocking collectives: none -> 14.4 us  [body(): lax.all_to_all(rope.reshape(grp, k_dev, rope_width), ('z', 'y'), 0, 0, ti...]
  transfers between devices with their start and end apart: 7 -> 17, of which waited for: 6 -> 9; matrix products, arithmetic and copies ran while one was open for 8% -> 19% of each run, Pallas kernels for 0% -> 0%
where the time goes in v1:
time: 197 us; the launch traced here: 194 us
  starting transfers between devices  73.7 us (37%)
  waiting for transfers between devices  50 us (25%)
  matrix products  22.9 us (12%)
  local copies, waits for them, and re-layouts  22.1 us (11%)
  blocking collectives  14.4 us (7%)
  other arithmetic  9.39 us (5%)
    ppermute x12, starting transfers between devices, fetch(): return lax.ppermute(value, 'x', [(s, (s - offset) % n) for s in range(n)])  37.9 us
    all_to_all x1, waiting for transfers between devices, body(): lax.all_to_all(cols, ('z', 'y'), 0, 0, tiled=True).reshape(grp * k_dev, -1)  20.3 us
    ppermute x12, waiting for transfers between devices, fetch(): return lax.ppermute(value, 'x', [(s, (s - offset) % n) for s in range(n)])  15.2 us
    all_to_all x2, starting transfers between devices, spread(): lax.all_to_all(jnp.broadcast_to(value[None], (n,) + value.shape), axes, 0...  14.9 us
    all_to_all x1, blocking collectives, body(): lax.all_to_all(rope.reshape(grp, k_dev, rope_width), ('z', 'y'), 0, 0, ti...  14.4 us
    dot_general x4, matrix products, down(): lax.dot_general(a, b, (((0,), (0,)), ((), ())), preferred_element_type=f32)  10 us
    all_to_all x2, waiting for transfers between devices, spread(): lax.all_to_all(jnp.broadcast_to(value[None], (n,) + value.shape), axes, 0...  9.92 us
    all_to_all x1, starting transfers between devices, body(): lax.all_to_all(terms.reshape(nd * nx, block, rope_width), ('dp', 'x'), 0,...  9.06 us
  transfers between devices with their start and end apart: 17, of which 9 were waited for; matrix products, arithmetic and copies ran while one was open for 19% of the time, Pallas kernels for 0%

profile of v1, /device:TPU:6, one launch (start us, length us, event | category | flops | bytes accessed | tf_op | source)
XLA Modules:
  0.0 193.7 jit_solution(14198320169701560317)
XLA Ops:
  0.7 2.2 %broadcast_in_dim.13 = bf16[16,64,576]{2,1,0:T(8,128)(2,1)} broadcast(bf16[64,576]{1,0:T(8,128)(2,1)} %bitcast.70), dimensions={1,2} | broadcast | bytes 1253376 | tf_op jit(solution)/shard_map/broadcast_in_dim | solution.py:16
  2.8 11.4 %all-to-all-start = ((bf16[16,64,576]{2,1,0:T(8,128)(2,1)}), bf16[16,64,576]{2,1,0:T(8,128)(2,1)S(1)}, u32[]{:S(2)}, u32[]{:S(2)}) async-start(bf16[16,64,576]{2,1,0:T(8,128)(2,1)} %broadcast_in_dim.13), calls=%async_computation | async-start | bytes 2621440 | tf_op jit(solution)/shard_map/all_to_all | solution.py:15
  14.3 2.7 %collective-permute-start = (bf16[256,576]{1,0:T(8,128)(2,1)S(1)}, bf16[256,576]{1,0:T(8,128)(2,1)S(1)}, u32[]{:S(2)}, u32[]{:S(2)}) collective-permute-start(bf16[256,576]{1,0:T(8,128)(2,1)S(1)} %bitcast.58), channel_id=1, source_target_pairs={{0,3},{1,0},{2,1},{3,2},{4,7},{5,4},{6,5},{7,6},{8,11},{9,8},{10,9... | collective-permute-start | bytes 884744 | tf_op jit(solution)/shard_map/ppermute | solution.py:11
  17.0 3.0 %collective-permute-start.1 = (bf16[256,576]{1,0:T(8,128)(2,1)S(1)}, bf16[256,576]{1,0:T(8,128)(2,1)S(1)}, u32[]{:S(2)}, u32[]{:S(2)}) collective-permute-start(bf16[256,576]{1,0:T(8,128)(2,1)S(1)} %bitcast.59), channel_id=1, source_target_pairs={{0,2},{1,3},{2,0},{3,1},{4,6},{5,7},{6,4},{7,5},{8,10},{9,11},{10,... | collective-permute-start | bytes 884744 | tf_op jit(solution)/shard_map/ppermute | solution.py:11
  20.1 4.0 %collective-permute-start.2 = (bf16[256,576]{1,0:T(8,128)(2,1)S(1)}, bf16[256,576]{1,0:T(8,128)(2,1)S(1)}, u32[]{:S(2)}, u32[]{:S(2)}) collective-permute-start(bf16[256,576]{1,0:T(8,128)(2,1)S(1)} %bitcast.60), channel_id=1, source_target_pairs={{0,1},{1,2},{2,3},{3,0},{4,5},{5,6},{6,7},{7,4},{8,9},{9,10},{10,1... | collective-permute-start | bytes 884744 | tf_op jit(solution)/shard_map/ppermute | solution.py:11
  26.1 4.2 %collective-permute-start.4 = (bf16[256,512]{1,0:T(8,128)(2,1)S(1)}, bf16[256,512]{1,0:T(8,128)(2,1)S(1)}, u32[]{:S(2)}, u32[]{:S(2)}) collective-permute-start(bf16[256,512]{1,0:T(8,128)(2,1)S(1)} %bitcast.77), channel_id=1, source_target_pairs={{0,2},{1,3},{2,0},{3,1},{4,6},{5,7},{6,4},{7,5},{8,10},{9,11},{10,... | collective-permute-start | bytes 786440 | tf_op jit(solution)/shard_map/ppermute | solution.py:11
  30.3 4.4 %collective-permute-done = bf16[256,576]{1,0:T(8,128)(2,1)S(1)} collective-permute-done((bf16[256,576]{1,0:T(8,128)(2,1)S(1)}, bf16[256,576]{1,0:T(8,128)(2,1)S(1)}, u32[]{:S(2)}, u32[]{:S(2)}) %collective-permute-start) | collective-permute-done | bytes 294944 | tf_op jit(solution)/shard_map/ppermute | solution.py:11
  37.9 9.9 %all-to-all-done = bf16[16,64,576]{2,1,0:T(8,128)(2,1)S(1)} async-done(((bf16[16,64,576]{2,1,0:T(8,128)(2,1)}), bf16[16,64,576]{2,1,0:T(8,128)(2,1)S(1)}, u32[]{:S(2)}, u32[]{:S(2)}) %all-to-all-start) | async-done | bytes 1179680 | tf_op jit(solution)/shard_map/all_to_all | solution.py:15
  47.8 3.8 %fusion = (f32[1024]{0:T(1024)S(1)}, f32[1024,1024]{0,1:T(8,128)}) fusion(s32[1024]{0:T(1024)S(1)} %get-tuple-element.29, s32[1024]{0:T(1024)S(1)} %get-tuple-element.28, bf16[1024,576]{1,0:T(8,128)(2,1)S(1)} %bitcast.64, bf16[256,576]{1,0:T(8,128)(2,1)S(1)} %collective-permute-done.2, bf16[256,576]{1,0:T(8,128)(2,1)S(1)} %collective-permute-done.1, ...), kind=kOutput, calls=%fused_computation.5 | convolution fusion | flops 1216871424 | bytes 6565888 | tf_op jit(solution)/shard_map/dot_general | solution.py:48
  51.6 5.0 %multiply_reduce_fusion = (f32[1024]{0:T(1024)S(1)}, f32[1024]{0:T(1024)S(1)}, f32[1024,1024]{0,1:T(8,128)}) fusion(f32[1024]{0:T(1024)S(1)} %get-tuple-element.23, f32[1024,1024]{0,1:T(8,128)} %get-tuple-element.24, s32[1024]{0:T(1024)S(1)} %get-tuple-element.29, s32[1024]{0:T(1024)S(1)} %get-tuple-element.28, bf16[1024,576]{1,0:T(8,128)(2,1)S(1)} %bitcast.65, ...), kind=kOutput, calls=%fused_computation.1 | convolution fusion | flops 1085274112 | bytes 10506240 | tf_op jit(solution)/shard_map/dot_general | solution.py:54
  56.6 2.7 %collective-permute-start.6 = (f32[3,4,256]{2,1,0:T(4,128)S(1)}, f32[3,4,256]{2,1,0:T(4,128)S(1)}, u32[]{:S(2)}, u32[]{:S(2)}) collective-permute-start(f32[3,4,256]{2,1,0:T(4,128)S(1)} %constant_dynamic-update-slice_fusion), channel_id=1, source_target_pairs={{0,3},{1,0},{2,1},{3,2},{4,7},{5,4},{6,5},{7,6},{8,11},{9,8},{10,9... | collective-permute-start | bytes 36872 | tf_op jit(solution)/shard_map/ppermute | solution.py:11
  59.4 3.0 %collective-permute-start.7 = (f32[3,4,256]{2,1,0:T(4,128)S(1)}, f32[3,4,256]{2,1,0:T(4,128)S(1)}, u32[]{:S(2)}, u32[]{:S(2)}) collective-permute-start(f32[3,4,256]{2,1,0:T(4,128)S(1)} %constant_dynamic-update-slice_fusion), channel_id=1, source_target_pairs={{0,2},{1,3},{2,0},{3,1},{4,6},{5,7},{6,4},{7,5},{8,10},{9,11},{10,... | collective-permute-start | bytes 36872 | tf_op jit(solution)/shard_map/ppermute | solution.py:11
  62.4 4.0 %collective-permute-start.8 = (f32[3,4,256]{2,1,0:T(4,128)S(1)}, f32[3,4,256]{2,1,0:T(4,128)S(1)}, u32[]{:S(2)}, u32[]{:S(2)}) collective-permute-start(f32[3,4,256]{2,1,0:T(4,128)S(1)} %constant_dynamic-update-slice_fusion), channel_id=1, source_target_pairs={{0,1},{1,2},{2,3},{3,0},{4,5},{5,6},{6,7},{7,4},{8,9},{9,10},{10,1... | collective-permute-start | bytes 36872 | tf_op jit(solution)/shard_map/ppermute | solution.py:11
  68.3 4.3 %multiply_convert_fusion = bf16[1024,1024]{0,1:T(8,128)(2,1)S(1)} fusion(f32[1024,1024]{0,1:T(8,128)} %get-tuple-element.25, f32[1024]{0:T(1024)S(1)} %get-tuple-element.22, f32[1024]{0:T(1024)S(1)} %get-tuple-element.21, f32[1024]{0:T(1024)S(1)} %get-tuple-element.23, f32[1024,1024]{0,1:T(8,128)} %get-tuple-element.24, s32[1024]{0:T(1024)S(1)} %get-tuple-element.29, ...), kind=kLoop, calls=%fused_computation | loop fusion | flops 8388608 | bytes 10506240 | tf_op jit(solution)/shard_map/convert_element_type | solution.py:68
  75.5 14.4 %all_to_all.30 = bf16[16,2,2048]{2,1,0:T(2,128)(2,1)S(1)} all-to-all(bf16[16,2,2048]{2,1,0:T(2,128)(2,1)S(1)} %reshape.156), channel_id=1, replica_groups=mesh['dp'=8,'z'=8,'y'=2,'x'=4] {'z','y'}, dimensions={0} | all-to-all | bytes 262144 | tf_op jit(solution)/shard_map/all_to_all | solution.py:74
  91.2 3.5 %all-to-all-start.3 = ((bf16[16,2,2048]{2,1,0:T(2,128)(2,1)}), bf16[16,2,2048]{2,1,0:T(2,128)(2,1)S(1)}, u32[]{:S(2)}, u32[]{:S(2)}) async-start(bf16[16,2,2048]{2,1,0:T(2,128)(2,1)} %reshape.158), calls=%async_computation.3 | async-start | bytes 262144 | tf_op jit(solution)/shard_map/all_to_all | solution.py:15
  94.7 6.2 %reshape_squeeze.3 = bf16[64,8,16,56]{3,2,1,0:T(8,128)(2,1)} reshape(bf16[1,64,7168]{2,1,0:T(8,128)(2,1)} %param.7) | data formatting | bytes 1835008 | tf_op jit(solution)/shard_map/reshape;squeeze | solution.py:38
  100.9 3.5 %copy.24 = bf16[16,64,8,56]{3,2,1,0:T(8,128)(2,1)} copy(bf16[16,64,8,56]{3,0,2,1:T(8,128)(2,1)} %bitcast.57) | data formatting | bytes 1835008 | tf_op jit(solution)/shard_map/transpose | solution.py:38
  104.4 4.1 %reshape.154 = bf16[16,64,448]{2,1,0:T(8,128)(2,1)} reshape(bf16[16,64,8,56]{3,2,1,0:T(8,128)(2,1)} %copy.24) | data formatting | bytes 1835008 | tf_op jit(solution)/shard_map/reshape | solution.py:39
  109.1 8.1 %all-to-all-start.4 = ((bf16[16,64,448]{2,1,0:T(8,128)(2,1)}), bf16[16,64,448]{2,1,0:T(8,128)(2,1)S(1)}, u32[]{:S(2)}, u32[]{:S(2)}) async-start(bf16[16,64,448]{2,1,0:T(8,128)(2,1)} %reshape.154), calls=%async_computation.4 | async-start | bytes 2097152 | tf_op jit(solution)/shard_map/all_to_all | solution.py:40
  118.5 2.6 %fusion.4 = f32[1024,512]{1,0:T(8,128)} fusion(bf16[1024,1024]{0,1:T(8,128)(2,1)S(1)} %multiply_convert_fusion, bf16[1024,576]{1,0:T(8,128)(2,1)S(1)} %pad_maximum_fusion), kind=kOutput, calls=%fused_computation.15 | convolution fusion | flops 1073741824 | bytes 5242880 | tf_op jit(solution)/shard_map/dot_general | solution.py:71
  121.3 20.3 %all-to-all-done.4 = bf16[16,64,448]{2,1,0:T(8,128)(2,1)S(1)} async-done(((bf16[16,64,448]{2,1,0:T(8,128)(2,1)}), bf16[16,64,448]{2,1,0:T(8,128)(2,1)S(1)}, u32[]{:S(2)}, u32[]{:S(2)}) %all-to-all-start.4) | async-done | bytes 917536 | tf_op jit(solution)/shard_map/all_to_all | solution.py:40
  142.9 9.1 %all-to-all-start.5 = ((f32[32,1,896]{2,1,0:T(1,128)}), f32[32,1,896]{2,1,0:T(1,128)S(1)}, u32[]{:S(2)}, u32[]{:S(2)}) async-start(f32[32,1,896]{2,1,0:T(1,128)} %reshape.160), calls=%async_computation.5 | async-start | bytes 229376 | tf_op jit(solution)/shard_map/all_to_all | solution.py:78
  152.0 5.7 %add_convert_fusion = bf16[1024,512]{1,0:T(8,128)(2,1)} fusion(f32[1024,512]{1,0:T(8,128)} %fusion.4, f32[1024]{0:T(1024)S(1)} %get-tuple-element.21, bf16[256,512]{1,0:T(8,128)(2,1)} %collective-permute-done.5, bf16[256,512]{1,0:T(8,128)(2,1)} %copy-done.11, bf16[256,512]{1,0:T(8,128)(2,1)} %copy-done.10, bf16[256,512]{1,0:T(8,128)(2,1)} %bitcast.75, ...), kind=kOutput, calls=%fused_computation.8 | convolution fusion | flops 1085800448 | bytes 8404992 | tf_op jit(solution)/shard_map/dot_general | solution.py:71
  157.7 3.8 %all-to-all-done.5 = f32[32,1,896]{2,1,0:T(1,128)S(1)} async-done(((f32[32,1,896]{2,1,0:T(1,128)}), f32[32,1,896]{2,1,0:T(1,128)S(1)}, u32[]{:S(2)}, u32[]{:S(2)}) %all-to-all-start.5) | async-done | bytes 114720 | tf_op jit(solution)/shard_map/all_to_all | solution.py:78
  161.4 3.7 %all-to-all-start.1 = ((bf16[16,64,512]{2,1,0:T(8,128)(2,1)}), bf16[16,64,512]{2,1,0:T(8,128)(2,1)S(1)}, u32[]{:S(2)}, u32[]{:S(2)}) async-start(bf16[16,64,512]{2,1,0:T(8,128)(2,1)} %bitcast.67), calls=%async_computation.1 | async-start | bytes 2097152 | tf_op jit(solution)/shard_map/all_to_all | solution.py:82
  165.1 4.2 %fusion.57 = (bf16[1024,576]{0,1:T(8,128)(2,1)S(1)}, f32[1024,576]{0,1:T(8,128)}) fusion(bf16[1024,1024]{0,1:T(8,128)(2,1)S(1)} %multiply_convert_fusion, bf16[1024,576]{1,0:T(8,128)(2,1)} %bitcast.66), kind=kOutput, calls=%fused_computation.103 | convolution fusion | flops 1209139200 | bytes 6815744 | tf_op jit(solution)/shard_map/dot_general | solution.py:86
  169.4 3.3 %collective-permute-start.10 = (bf16[256,576]{0,1:T(8,128)(2,1)S(1)}, bf16[256,576]{0,1:T(8,128)(2,1)S(1)}, u32[]{:S(2)}, u32[]{:S(2)}) collective-permute-start(bf16[256,576]{0,1:T(8,128)(2,1)S(1)} %get-tuple-element.14), channel_id=1, source_target_pairs={{0,2},{1,3},{2,0},{3,1},{4,6},{5,7},{6,4},{7,5},{8,10},{9,11},{10,... | collective-permute-start | bytes 884744 | tf_op jit(solution)/shard_map/ppermute | solution.py:11
  172.7 3.4 %collective-permute-start.11 = (bf16[256,576]{0,1:T(8,128)(2,1)S(1)}, bf16[256,576]{0,1:T(8,128)(2,1)S(1)}, u32[]{:S(2)}, u32[]{:S(2)}) collective-permute-start(bf16[256,576]{0,1:T(8,128)(2,1)S(1)} %get-tuple-element.13), channel_id=1, source_target_pairs={{0,3},{1,0},{2,1},{3,2},{4,7},{5,4},{6,5},{7,6},{8,11},{9,8},{10,9... | collective-permute-start | bytes 884744 | tf_op jit(solution)/shard_map/ppermute | solution.py:11
  176.0 3.7 %collective-permute-start.9 = (bf16[256,576]{0,1:T(8,128)(2,1)S(1)}, bf16[256,576]{0,1:T(8,128)(2,1)S(1)}, u32[]{:S(2)}, u32[]{:S(2)}) collective-permute-start(bf16[256,576]{0,1:T(8,128)(2,1)S(1)} %get-tuple-element.12), channel_id=1, source_target_pairs={{0,1},{1,2},{2,3},{3,0},{4,5},{5,6},{6,7},{7,4},{8,9},{9,10},{10,1... | collective-permute-start | bytes 884744 | tf_op jit(solution)/shard_map/ppermute | solution.py:11
  179.8 2.9 %collective-permute-done.10 = bf16[256,576]{0,1:T(8,128)(2,1)S(1)} collective-permute-done((bf16[256,576]{0,1:T(8,128)(2,1)S(1)}, bf16[256,576]{0,1:T(8,128)(2,1)S(1)}, u32[]{:S(2)}, u32[]{:S(2)}) %collective-permute-start.10) | collective-permute-done | bytes 294944 | tf_op jit(solution)/shard_map/ppermute | solution.py:11
  182.7 5.1 %collective-permute-done.11 = bf16[256,576]{0,1:T(8,128)(2,1)S(1)} collective-permute-done((bf16[256,576]{0,1:T(8,128)(2,1)S(1)}, bf16[256,576]{0,1:T(8,128)(2,1)S(1)}, u32[]{:S(2)}, u32[]{:S(2)}) %collective-permute-start.11) | collective-permute-done | bytes 294944 | tf_op jit(solution)/shard_map/ppermute | solution.py:11
  (82 shorter events, 20.6 us)
Async XLA Ops:
  0.6 13.6 %copy-start = (bf16[1,4,64,576]{3,2,1,0:T(8,128)(2,1)S(1)}, bf16[1,4,64,576]{3,2,1,0:T(8,128)(2,1)}, u32[]{:S(2)}) copy-start(bf16[1,4,64,576]{3,2,1,0:T(8,128)(2,1)} %param.4) | copy-start | bytes 884740
  0.6 23.4 %copy-start.9 = (bf16[1,4,64,512]{3,2,1,0:T(8,128)(2,1)S(1)}, bf16[1,4,64,512]{3,2,1,0:T(8,128)(2,1)}, u32[]{:S(2)}) copy-start(bf16[1,4,64,512]{3,2,1,0:T(8,128)(2,1)} %param.6) | copy-start | bytes 786436
  2.8 45.0 %all-to-all-start = ((bf16[16,64,576]{2,1,0:T(8,128)(2,1)}), bf16[16,64,576]{2,1,0:T(8,128)(2,1)S(1)}, u32[]{:S(2)}, u32[]{:S(2)}) async-start(bf16[16,64,576]{2,1,0:T(8,128)(2,1)} %broadcast_in_dim.13), calls=%async_computation | async-start | bytes 2621440 | tf_op jit(solution)/shard_map/all_to_all | solution.py:15
  14.3 20.4 %collective-permute-start = (bf16[256,576]{1,0:T(8,128)(2,1)S(1)}, bf16[256,576]{1,0:T(8,128)(2,1)S(1)}, u32[]{:S(2)}, u32[]{:S(2)}) collective-permute-start(bf16[256,576]{1,0:T(8,128)(2,1)S(1)} %bitcast.58), channel_id=1, source_target_pairs={{0,3},{1,0},{2,1},{3,2},{4,7},{5,4},{6,5},{7,6},{8,11},{9,8},{10,9... | collective-permute-start | bytes 884744 | tf_op jit(solution)/shard_map/ppermute | solution.py:11
  17.0 19.6 %collective-permute-start.1 = (bf16[256,576]{1,0:T(8,128)(2,1)S(1)}, bf16[256,576]{1,0:T(8,128)(2,1)S(1)}, u32[]{:S(2)}, u32[]{:S(2)}) collective-permute-start(bf16[256,576]{1,0:T(8,128)(2,1)S(1)} %bitcast.59), channel_id=1, source_target_pairs={{0,2},{1,3},{2,0},{3,1},{4,6},{5,7},{6,4},{7,5},{8,10},{9,11},{10,... | collective-permute-start | bytes 884744 | tf_op jit(solution)/shard_map/ppermute | solution.py:11
  20.1 17.8 %collective-permute-start.2 = (bf16[256,576]{1,0:T(8,128)(2,1)S(1)}, bf16[256,576]{1,0:T(8,128)(2,1)S(1)}, u32[]{:S(2)}, u32[]{:S(2)}) collective-permute-start(bf16[256,576]{1,0:T(8,128)(2,1)S(1)} %bitcast.60), channel_id=1, source_target_pairs={{0,1},{1,2},{2,3},{3,0},{4,5},{5,6},{6,7},{7,4},{8,9},{9,10},{10,1... | collective-permute-start | bytes 884744 | tf_op jit(solution)/shard_map/ppermute | solution.py:11
  24.1 27.5 %collective-permute-start.3 = (bf16[256,512]{1,0:T(8,128)(2,1)S(1)}, bf16[256,512]{1,0:T(8,128)(2,1)S(1)}, u32[]{:S(2)}, u32[]{:S(2)}) collective-permute-start(bf16[256,512]{1,0:T(8,128)(2,1)S(1)} %bitcast.76), channel_id=1, source_target_pairs={{0,3},{1,0},{2,1},{3,2},{4,7},{5,4},{6,5},{7,6},{8,11},{9,8},{10,9... | collective-permute-start | bytes 786440 | tf_op jit(solution)/shard_map/ppermute | solution.py:11
  26.1 25.5 %collective-permute-start.4 = (bf16[256,512]{1,0:T(8,128)(2,1)S(1)}, bf16[256,512]{1,0:T(8,128)(2,1)S(1)}, u32[]{:S(2)}, u32[]{:S(2)}) collective-permute-start(bf16[256,512]{1,0:T(8,128)(2,1)S(1)} %bitcast.77), channel_id=1, source_target_pairs={{0,2},{1,3},{2,0},{3,1},{4,6},{5,7},{6,4},{7,5},{8,10},{9,11},{10,... | collective-permute-start | bytes 786440 | tf_op jit(solution)/shard_map/ppermute | solution.py:11
  34.7 37.9 %copy-start.1 = (bf16[256,576]{1,0:T(8,128)(2,1)}, bf16[256,576]{1,0:T(8,128)(2,1)S(1)}, u32[]{:S(2)}) copy-start(bf16[256,576]{1,0:T(8,128)(2,1)S(1)} %collective-permute-done) | copy-start | bytes 884740
  34.7 16.9 %collective-permute-start.5 = (bf16[256,512]{1,0:T(8,128)(2,1)S(1)}, bf16[256,512]{1,0:T(8,128)(2,1)}, u32[]{:S(2)}, u32[]{:S(2)}) collective-permute-start(bf16[256,512]{1,0:T(8,128)(2,1)S(1)} %bitcast.78), channel_id=1, source_target_pairs={{0,1},{1,2},{2,3},{3,0},{4,5},{5,6},{6,7},{7,4},{8,9},{9,10},{10,1... | collective-permute-start | bytes 786440 | tf_op jit(solution)/shard_map/ppermute | solution.py:11
  36.6 36.0 %copy-start.2 = (bf16[256,576]{1,0:T(8,128)(2,1)}, bf16[256,576]{1,0:T(8,128)(2,1)S(1)}, u32[]{:S(2)}) copy-start(bf16[256,576]{1,0:T(8,128)(2,1)S(1)} %collective-permute-done.1) | copy-start | bytes 884740
  37.9 34.8 %copy-start.3 = (bf16[256,576]{1,0:T(8,128)(2,1)}, bf16[256,576]{1,0:T(8,128)(2,1)S(1)}, u32[]{:S(2)}) copy-start(bf16[256,576]{1,0:T(8,128)(2,1)S(1)} %collective-permute-done.2) | copy-start | bytes 884740
  47.8 3.8 %copy-start.4 = (bf16[16,64,576]{2,1,0:T(8,128)(2,1)}, bf16[16,64,576]{2,1,0:T(8,128)(2,1)S(1)}, u32[]{:S(2)}) copy-start(bf16[16,64,576]{2,1,0:T(8,128)(2,1)S(1)} %all-to-all-done) | copy-start | bytes 3538948
  51.6 5.0 %copy-start.10 = (bf16[256,512]{1,0:T(8,128)(2,1)}, bf16[256,512]{1,0:T(8,128)(2,1)S(1)}, u32[]{:S(2)}) copy-start(bf16[256,512]{1,0:T(8,128)(2,1)S(1)} %collective-permute-done.3) | copy-start | bytes 786436
  51.6 5.0 %copy-start.11 = (bf16[256,512]{1,0:T(8,128)(2,1)}, bf16[256,512]{1,0:T(8,128)(2,1)S(1)}, u32[]{:S(2)}) copy-start(bf16[256,512]{1,0:T(8,128)(2,1)S(1)} %collective-permute-done.4) | copy-start | bytes 786436
  56.6 9.8 %collective-permute-start.6 = (f32[3,4,256]{2,1,0:T(4,128)S(1)}, f32[3,4,256]{2,1,0:T(4,128)S(1)}, u32[]{:S(2)}, u32[]{:S(2)}) collective-permute-start(f32[3,4,256]{2,1,0:T(4,128)S(1)} %constant_dynamic-update-slice_fusion), channel_id=1, source_target_pairs={{0,3},{1,0},{2,1},{3,2},{4,7},{5,4},{6,5},{7,6},{8,11},{9,8},{10,9... | collective-permute-start | bytes 36872 | tf_op jit(solution)/shard_map/ppermute | solution.py:11
  59.4 7.1 %collective-permute-start.7 = (f32[3,4,256]{2,1,0:T(4,128)S(1)}, f32[3,4,256]{2,1,0:T(4,128)S(1)}, u32[]{:S(2)}, u32[]{:S(2)}) collective-permute-start(f32[3,4,256]{2,1,0:T(4,128)S(1)} %constant_dynamic-update-slice_fusion), channel_id=1, source_target_pairs={{0,2},{1,3},{2,0},{3,1},{4,6},{5,7},{6,4},{7,5},{8,10},{9,11},{10,... | collective-permute-start | bytes 36872 | tf_op jit(solution)/shard_map/ppermute | solution.py:11
  62.4 5.7 %collective-permute-start.8 = (f32[3,4,256]{2,1,0:T(4,128)S(1)}, f32[3,4,256]{2,1,0:T(4,128)S(1)}, u32[]{:S(2)}, u32[]{:S(2)}) collective-permute-start(f32[3,4,256]{2,1,0:T(4,128)S(1)} %constant_dynamic-update-slice_fusion), channel_id=1, source_target_pairs={{0,1},{1,2},{2,3},{3,0},{4,5},{5,6},{6,7},{7,4},{8,9},{9,10},{10,1... | collective-permute-start | bytes 36872 | tf_op jit(solution)/shard_map/ppermute | solution.py:11
  90.2 14.1 %copy-start.7 = (f32[64,64]{0,1:T(8,128)}, f32[64,64]{0,1:T(8,128)S(1)}, u32[]{:S(2)}) copy-start(f32[64,64]{0,1:T(8,128)S(1)} %convert_reduce_fusion.1) | copy-start | bytes 49156
  91.2 17.3 %all-to-all-start.3 = ((bf16[16,2,2048]{2,1,0:T(2,128)(2,1)}), bf16[16,2,2048]{2,1,0:T(2,128)(2,1)S(1)}, u32[]{:S(2)}, u32[]{:S(2)}) async-start(bf16[16,2,2048]{2,1,0:T(2,128)(2,1)} %reshape.158), calls=%async_computation.3 | async-start | bytes 262144 | tf_op jit(solution)/shard_map/all_to_all | solution.py:15
  108.5 0.7 copy-start.5
  109.1 32.5 %all-to-all-start.4 = ((bf16[16,64,448]{2,1,0:T(8,128)(2,1)}), bf16[16,64,448]{2,1,0:T(8,128)(2,1)S(1)}, u32[]{:S(2)}, u32[]{:S(2)}) async-start(bf16[16,64,448]{2,1,0:T(8,128)(2,1)} %reshape.154), calls=%async_computation.4 | async-start | bytes 2097152 | tf_op jit(solution)/shard_map/all_to_all | solution.py:40
  118.5 2.6 %copy-start.6 = (bf16[16,2,2048]{2,1,0:T(2,128)(2,1)S(1)}, bf16[16,2,2048]{2,1,0:T(2,128)(2,1)}, u32[]{:S(2)}) copy-start(bf16[16,2,2048]{2,1,0:T(2,128)(2,1)} %copy-done.5) | copy-start | bytes 393220
  142.9 18.5 %all-to-all-start.5 = ((f32[32,1,896]{2,1,0:T(1,128)}), f32[32,1,896]{2,1,0:T(1,128)S(1)}, u32[]{:S(2)}, u32[]{:S(2)}) async-start(f32[32,1,896]{2,1,0:T(1,128)} %reshape.160), calls=%async_computation.5 | async-start | bytes 229376 | tf_op jit(solution)/shard_map/all_to_all | solution.py:78
  161.4 31.4 %all-to-all-start.1 = ((bf16[16,64,512]{2,1,0:T(8,128)(2,1)}), bf16[16,64,512]{2,1,0:T(8,128)(2,1)S(1)}, u32[]{:S(2)}, u32[]{:S(2)}) async-start(bf16[16,64,512]{2,1,0:T(8,128)(2,1)} %bitcast.67), calls=%async_computation.1 | async-start | bytes 2097152 | tf_op jit(solution)/shard_map/all_to_all | solution.py:82
  165.1 14.6 %copy-start.8 = (f32[64,64]{0,1:T(8,128)S(1)}, f32[64,64]{0,1:T(8,128)}, u32[]{:S(2)}) copy-start(f32[64,64]{0,1:T(8,128)} %copy-done.7) | copy-start | bytes 49156
  169.4 13.3 %collective-permute-start.10 = (bf16[256,576]{0,1:T(8,128)(2,1)S(1)}, bf16[256,576]{0,1:T(8,128)(2,1)S(1)}, u32[]{:S(2)}, u32[]{:S(2)}) collective-permute-start(bf16[256,576]{0,1:T(8,128)(2,1)S(1)} %get-tuple-element.14), channel_id=1, source_target_pairs={{0,2},{1,3},{2,0},{3,1},{4,6},{5,7},{6,4},{7,5},{8,10},{9,11},{10,... | collective-permute-start | bytes 884744 | tf_op jit(solution)/shard_map/ppermute | solution.py:11
  172.7 15.1 %collective-permute-start.11 = (bf16[256,576]{0,1:T(8,128)(2,1)S(1)}, bf16[256,576]{0,1:T(8,128)(2,1)S(1)}, u32[]{:S(2)}, u32[]{:S(2)}) collective-permute-start(bf16[256,576]{0,1:T(8,128)(2,1)S(1)} %get-tuple-element.13), channel_id=1, source_target_pairs={{0,3},{1,0},{2,1},{3,2},{4,7},{5,4},{6,5},{7,6},{8,11},{9,8},{10,9... | collective-permute-start | bytes 884744 | tf_op jit(solution)/shard_map/ppermute | solution.py:11
  176.0 11.7 %collective-permute-start.9 = (bf16[256,576]{0,1:T(8,128)(2,1)S(1)}, bf16[256,576]{0,1:T(8,128)(2,1)S(1)}, u32[]{:S(2)}, u32[]{:S(2)}) collective-permute-start(bf16[256,576]{0,1:T(8,128)(2,1)S(1)} %get-tuple-element.12), channel_id=1, source_target_pairs={{0,1},{1,2},{2,3},{3,0},{4,5},{5,6},{6,7},{7,4},{8,9},{9,10},{10,1... | collective-permute-start | bytes 884744 | tf_op jit(solution)/shard_map/ppermute | solution.py:11

commit v2 on v1

v2 whole, which is shorter than its diff:
```python
import functools

import jax
import jax.numpy as jnp
from jax import lax
from jax.experimental import pallas as pl
from jax.experimental.pallas import tpu as pltpu
from jax.sharding import Mesh, PartitionSpec as P

softmax_scale = 0.07216878364870323
f32, bf16 = jnp.float32, jnp.bfloat16
TILE = 256
SLOT = 16


def nt(a, b):
    return lax.dot_general(a, b, (((1,), (1,)), ((), ())), preferred_element_type=f32)


def nn(a, b):
    return lax.dot_general(a, b, (((1,), (0,)), ((), ())), preferred_element_type=f32)


def tn(a, b):
    return lax.dot_general(a, b, (((0,), (0,)), ((), ())), preferred_element_type=f32)


def call(kernel, outs, n_in, smem=(), unused=(), flops=0, moved=0, limit=48):
    vmem = pl.BlockSpec(memory_space=pltpu.VMEM)
    specs = [
        pl.BlockSpec(memory_space=pltpu.SMEM)
        if i in smem
        else (pl.BlockSpec(memory_space=pl.ANY) if i in unused else vmem)
        for i in range(n_in)
    ]
    return pl.pallas_call(
        kernel,
        out_shape=[jax.ShapeDtypeStruct(s, d) for s, d in outs],
        in_specs=specs,
        out_specs=[vmem] * len(outs),
        compiler_params=pltpu.CompilerParams(vmem_limit_bytes=limit * 2**20),
        cost_estimate=pl.CostEstimate(flops=flops, bytes_accessed=moved, transcendentals=0),
    )


def pack_kernel(dout, query, out):
    lat = dout.shape[1]
    width = query.shape[1]
    out[:, :lat] = dout[...]
    out[:, lat : lat + width] = query[...]
    out[:, lat + width :] = jnp.zeros((out.shape[0], out.shape[1] - lat - width), out.dtype)


def row_blocks(refs):
    own, right, first, second, left = refs
    return [
        lambda c: own[:, c],
        lambda c: right[:, c],
        lambda c: jnp.concatenate([first[:, c], second[:, c]]),
        lambda c: left[:, c],
    ]


def columns_kernel(block, n_z, n_grp, hid, after, after2, after3, out):
    k_dev, model = hid.shape
    n_data = model // (n_z * n_grp * block)
    span = n_z * n_grp * block
    wide = n_z * SLOT
    c = lax.broadcasted_iota(jnp.int32, (span, n_grp * wide), 0)
    o = lax.broadcasted_iota(jnp.int32, (span, n_grp * wide), 1)
    g, zz, k = o // wide, (o % wide) // SLOT, o % SLOT
    pick = jnp.where((c == (zz * n_grp + g) * block + k) & (k < block), 1.0, 0.0).astype(bf16)
    stacked = jnp.concatenate([hid[:, d * span : (d + 1) * span] for d in range(n_data)])
    moved = nn(stacked, pick).astype(bf16)
    for d in range(n_data):
        for g in range(n_grp):
            out[g, :, d * wide : (d + 1) * wide] = moved[
                d * k_dev : (d + 1) * k_dev, g * wide : (g + 1) * wide
            ]


def key_tile(near, far, i, per):
    ref, first = (near, i * per) if i * per < near.shape[0] else (far, i * per - near.shape[0])
    k = ref[first : first + per]
    return k.reshape(k.shape[0] * k.shape[1], k.shape[2])


def scores_kernel(lat, heads, pos, near, far, *refs):
    blocks, (e_ref, dp_ref, st_ref) = row_blocks(refs[1:-3]), refs[-3:]
    z, y, x = pos[0], pos[1], pos[2]
    n_z, k_dev, _ = near.shape
    n_x = len(blocks)
    rows = refs[1].shape[0]
    n_keys = 2 * n_z * k_dev
    tiles = n_keys // TILE
    per = TILE // k_dev
    tok = rows // heads
    first_query = n_z * 2 * n_x * (k_dev - tok)
    for b, t in enumerate(blocks):
        q, o = t(slice(lat, lat + near.shape[2])), t(slice(0, lat))
        cols = slice(b * rows, (b + 1) * rows)
        lane = lax.broadcasted_iota(jnp.int32, (k_dev, rows), 1)
        q_pos = ((z * 2 + y) * n_x + lax.rem(x + b, n_x)) * tok + lane // heads + first_query
        top = None
        for i in range(tiles):
            s = nt(key_tile(near, far, i, per), q) * softmax_scale
            half, zz = divmod((i + 1) * per - 1, n_z)
            if zz == n_z - 1:
                side = y if half == 0 else 1 - y
                k_pos = ((zz * 2 + side) * n_x + x) * k_dev + lax.broadcasted_iota(
                    jnp.int32, (k_dev, rows), 0
                )
                last = jnp.where(k_pos <= q_pos, s[TILE - k_dev :], -jnp.inf)
                s = jnp.concatenate([s[: TILE - k_dev], last])
            e_ref[i * TILE : (i + 1) * TILE, cols] = s
            m = jnp.max(s, axis=0, keepdims=True)
            top = m if top is None else jnp.maximum(top, m)
        total = jnp.zeros_like(top)
        delta = jnp.zeros_like(top)
        for i in range(tiles):
            part = slice(i * TILE, (i + 1) * TILE)
            dp = nt(key_tile(near, far, i, per)[:, :lat], o)
            e = jnp.exp(e_ref[part, cols] - top)
            e_ref[part, cols] = e
            dp_ref[part, cols] = dp
            total += jnp.sum(e, axis=0, keepdims=True)
            delta += jnp.sum(e * dp, axis=0, keepdims=True)
        st_ref[4 * b : 4 * b + 4] = jnp.concatenate([top, total, delta, jnp.zeros_like(top)])


def copies_kernel(st, after, out):
    out[...] = jnp.broadcast_to(st[...][None], out.shape)


def dscores_kernel(lat, pos, stats, st, e_ref, dp_ref, *refs):
    blocks, (p_ref, ds_ref, rope_ref) = row_blocks(refs[:-3]), refs[-3:]
    y, x = pos[1], pos[2]
    n_x = len(blocks)
    rows = refs[0].shape[0]
    tiles = e_ref.shape[0] // TILE
    grp, half_keys, _ = rope_ref.shape
    k_dev = 2 * half_keys
    for b in range(n_x):
        cols = slice(b * rows, (b + 1) * rows)
        theirs = []
        for s in range(n_x):
            at = lax.rem(x + b + n_x - s, n_x)
            v = stats[s, 0:4]
            for j in range(1, n_x):
                v = jnp.where(at == j, stats[s, 4 * j : 4 * j + 4], v)
            theirs.append(v)
        top = functools.reduce(jnp.maximum, [v[0:1] for v in theirs])
        w = [jnp.exp(v[0:1] - top) for v in theirs]
        total = sum(v[1:2] * u for v, u in zip(theirs, w))
        delta = sum(v[2:3] * u for v, u in zip(theirs, w)) / total
        f = jnp.exp(st[4 * b : 4 * b + 1] - top) / total
        for i in range(tiles):
            part = slice(i * TILE, (i + 1) * TILE)
            p = e_ref[part, cols] * f
            p_ref[part, cols] = p.astype(bf16)
            ds_ref[part, cols] = (p * (dp_ref[part, cols] - delta)).astype(bf16)
    n_z = grp // 2
    for i in range(tiles):
        part = slice(i * TILE, (i + 1) * TILE)
        r = None
        for b, t in enumerate(blocks):
            q = t(slice(2 * lat, 2 * lat + rope_ref.shape[2] // 2))
            v = nn(ds_ref[part, b * rows : (b + 1) * rows], q)
            r = v if r is None else r + v
        r = (r * softmax_scale).astype(bf16)
        for j in range(TILE // k_dev):
            half, zz = divmod(i * (TILE // k_dev) + j, n_z)
            side = y if half == 0 else 1 - y
            k = r[j * k_dev : (j + 1) * k_dev]
            rope_ref[2 * zz + side] = jnp.concatenate([k[:half_keys], k[half_keys:]], axis=1)


def grads_kernel(lat, p_ref, ds_ref, near, far, *refs):
    blocks, (mine, other), dq_refs = row_blocks(refs[:5]), refs[5:7], refs[7:]
    n_z, k_dev, _ = near.shape
    rows = refs[0].shape[0]
    tiles = p_ref.shape[0] // TILE
    per = TILE // k_dev
    for i in range(tiles):
        part = slice(i * TILE, (i + 1) * TILE)
        v = None
        for b, t in enumerate(blocks):
            a = nn(ds_ref[part, b * rows : (b + 1) * rows], t(slice(lat, 2 * lat)))
            v = a if v is None else v + a
        v = v * softmax_scale
        for b, t in enumerate(blocks):
            v += nn(p_ref[part, b * rows : (b + 1) * rows], t(slice(0, lat)))
        out, first = (mine, i * per) if i * per < n_z else (other, i * per - n_z)
        out[first : first + per] = v.astype(bf16).reshape(per, k_dev, lat)
    for b, out in enumerate(dq_refs):
        v = None
        for i in range(tiles):
            a = tn(
                ds_ref[i * TILE : (i + 1) * TILE, b * rows : (b + 1) * rows],
                key_tile(near, far, i, per),
            )
            v = a if v is None else v + a
        out[...] = (v * softmax_scale).astype(out.dtype)


def rope_kernel(parts, all_ref, rope_ref):
    half = parts.shape[1]
    v = jnp.sum(parts[...].astype(f32), axis=0)
    rope_ref[...] = jnp.concatenate([v[:, : v.shape[1] // 2], v[:, v.shape[1] // 2 :]])
    all_ref[...] = jnp.broadcast_to(v.astype(bf16)[None], all_ref.shape)


def weight_kernel(cols, rope, out):
    n, k_dev, wide = cols.shape
    e = rope.shape[2] // 2
    r = jnp.concatenate([rope[:, :, :e], rope[:, :, e:]], axis=1).reshape(n * k_dev, e)
    v = tn(cols[...].reshape(n * k_dev, wide), r).reshape(wide // SLOT, SLOT, e)
    out[...] = jnp.concatenate([v[:, : SLOT // 2], v[:, SLOT // 2 :]], axis=2)


def weight_sum_kernel(parts, out):
    v = jnp.sum(parts[...], axis=0)
    e = v.shape[1] // 2
    out[...] = jnp.concatenate([v[:, :e], v[:, e:]])[: out.shape[0]]


def latent_sum_kernel(parts, rope, out):
    lat = parts.shape[2]
    out[:, :lat] = jnp.sum(parts[...].astype(f32), axis=0)
    out[:, lat:] = rope[...]


def fetch(value, offset, n):
    return lax.ppermute(value, "x", [(s, (s - offset) % n) for s in range(n)])


def trade(value, axes):
    return lax.all_to_all(value, axes, 0, 0, tiled=True)


def body(query, latent, dout, hidden):
    nd, nz, ny, nx = (lax.axis_size(a) for a in ("dp", "z", "y", "x"))
    tok, heads, width = query.shape[1:]
    lat = dout.shape[3]
    rope = width - lat
    k_dev, model = hidden.shape[1:]
    rows = tok * heads
    n_rows, n_keys = nx * rows, nz * ny * k_dev
    block = model // (nd * nz * ny * nx)
    pos = jnp.stack([lax.axis_index(a) for a in ("z", "y", "x")]).astype(jnp.int32)

    near = trade(jnp.broadcast_to(latent, (nz, k_dev, width)), "z")
    (own,) = call(pack_kernel, [((rows, -(-(lat + width) // 128) * 128), bf16)], 2, moved=4 * rows * width)(
        dout.reshape(rows, lat), query.reshape(rows, width)
    )
    right, left = fetch(own, 1, nx), fetch(own, nx - 1, nx)
    first, second = fetch(right[: rows // 2], 1, nx), fetch(left[rows // 2 :], nx - 1, nx)
    blocks = [own, right, first, second, left]
    far = lax.ppermute(near, "y", [(0, 1), (1, 0)])

    wide = nd * nz * SLOT
    (cols,) = call(
        functools.partial(columns_kernel, block, nz, ny * nx),
        [((ny * nx, k_dev, wide), bf16)], 4, unused=(1, 2, 3),
        flops=2 * k_dev * nd * (model // nd) * 1024, moved=2 * k_dev * model * 2,
    )(hidden[0], near, right, left)
    sorted_cols = cols
    cols = trade(cols, ("y", "x"))

    pairs = n_rows * n_keys
    e, dp, st = call(
        functools.partial(scores_kernel, lat, heads),
        [((n_keys, n_rows), f32)] * 2 + [((4 * nx, rows), f32)], 5 + nx, smem=(0,),
        unused=(3,),
        flops=2 * pairs * (width + lat), moved=8 * pairs,
    )(pos, near, far, sorted_cols, *blocks)
    (stats,) = call(copies_kernel, [((nx,) + st.shape, f32)], 2, unused=(1,))(st, cols)
    stats = trade(stats, "x")
    p, ds, rope_part = call(
        functools.partial(dscores_kernel, lat),
        [((n_keys, n_rows), bf16)] * 2 + [((nz * ny, k_dev // 2, 2 * rope), bf16)],
        6 + nx, smem=(0,),
        flops=2 * pairs * rope, moved=12 * pairs,
    )(pos, stats, st, e, dp, *blocks)
    rope_part = trade(rope_part, ("z", "y"))

    mine, other, *dq = call(
        functools.partial(grads_kernel, lat),
        [((nz, k_dev, lat), bf16)] * 2 + [((rows, width), f32)] + [((rows, width), bf16)] * (nx - 1),
        5 + nx, flops=2 * pairs * (width + 2 * lat), moved=4 * pairs,
    )(p, ds, near, far, *blocks)
    other = lax.ppermute(other, "y", [(0, 1), (1, 0)])
    dq = [dq[0]] + [fetch(dq[k], nx - k, nx) for k in range(1, nx)]

    rope_all, rope_sum = call(
        rope_kernel, [((ny * nx, k_dev // 2, 2 * rope), bf16), ((k_dev, rope), f32)], 1
    )(rope_part)
    rope_all = trade(rope_all, ("y", "x"))
    (terms,) = call(
        weight_kernel, [((nd * nz, SLOT // 2, 2 * rope), f32)], 2,
        flops=2 * ny * nx * k_dev * wide * rope, moved=2 * ny * nx * k_dev * wide,
    )(cols, rope_all)
    terms = trade(terms, ("dp", "z"))
    (dweight,) = call(weight_sum_kernel, [((block, rope), f32)], 1)(terms)

    half = (mine.astype(f32) + other.astype(f32)).astype(bf16)
    half = trade(half, "z")
    (dlatent,) = call(latent_sum_kernel, [((k_dev, width), f32)], 2)(half, rope_sum)

    total = dq[0]
    for part in dq[1:]:
        total = total + part.astype(f32)
    return total.astype(bf16).reshape(query.shape), dlatent[None], dweight


def solution(mesh):
    fine = Mesh(mesh.devices.reshape(8, 8, 2, 4), ("dp", "z", "y", "x"))
    sp = ("z", "y", "x")
    in_specs = (
        P("dp", sp, None, None),
        P("dp", sp, None),
        P("dp", sp, None, None),
        P("dp", sp, None),
    )
    out_specs = (P("dp", sp, None, None), P("dp", sp, None), P(("dp",) + sp, None))
    return jax.shard_map(body, mesh=fine, in_specs=in_specs, out_specs=out_specs, check_vma=False)
```

time: 197 us -> 184 us (0.934)
  Pallas kernels: 0 us -> 27 us
  matrix products: 22.9 us -> 0 us
  local copies, waits for them, and re-layouts: 22.1 us -> 12.2 us
  starting transfers between devices: 73.7 us -> 66.2 us
  other arithmetic: 9.39 us -> 2.93 us
  waiting for transfers between devices: 50 us -> 55.6 us
  blocking collectives: 14.4 us -> 16.9 us
    pallas_call x0 -> x10, Pallas kernels: none -> 27 us  [the longest x1 8.19 us: body(): call(functools.partial(scores_kernel, lat, heads), [((n_keys, n_rows), f3...]
    dot_general x7 -> x0, matrix products: 22.9 us -> none  [the longest x4 10 us: down(): lax.dot_general(a, b, (((0,), (0,)), ((), ())), preferred_element_type=f32)]
    all_to_all x5, waiting for transfers between devices: 34.8 us -> 12.8 us  [trade(): return lax.all_to_all(value, axes, 0, 0, tiled=True)]
    ppermute x12 -> x7, waiting for transfers between devices: 15.2 us -> 35.1 us  [fetch(): return lax.ppermute(value, 'x', [(s, (s - offset) % n) for s in range(n)])]
    ppermute x12 -> x7, starting transfers between devices: 37.9 us -> 20.8 us  [fetch(): return lax.ppermute(value, 'x', [(s, (s - offset) % n) for s in range(n)])]
    ppermute x0 -> x2, waiting for transfers between devices: none -> 7.78 us  [the longest x1 7.77 us: body(): far = lax.ppermute(near, 'y', [(0, 1), (1, 0)])]
    ppermute x0 -> x2, starting transfers between devices: none -> 7.26 us  [the longest x1 3.89 us: body(): other = lax.ppermute(other, 'y', [(0, 1), (1, 0)])]
    another operation x9 -> x0, local copies, waits for them, and re-layouts: 6.27 us -> none  [the longest x1 6.16 us: body(): cols = hidden[0].reshape(k_dev, nd, grp, nx * block).transpose(2, 0, 1, 3)]
  transfers between devices with their start and end apart: 17 -> 14, of which waited for: 9 -> 9; matrix products, arithmetic and copies ran while one was open for 19% -> 2% of each run, Pallas kernels for 0% -> 10%
where the time goes in v2:
time: 184 us; the launch traced here: 182 us
  starting transfers between devices  66.2 us (36%)
  waiting for transfers between devices  55.6 us (30%)
  Pallas kernels  27 us (15%)
  blocking collectives  16.9 us (9%)
  local copies, waits for them, and re-layouts  12.2 us (7%)
  other arithmetic  2.93 us (2%)
    all_to_all x5, starting transfers between devices, trade(): return lax.all_to_all(value, axes, 0, 0, tiled=True)  38.1 us
    ppermute x7, waiting for transfers between devices, fetch(): return lax.ppermute(value, 'x', [(s, (s - offset) % n) for s in range(n)])  35.1 us
    ppermute x7, starting transfers between devices, fetch(): return lax.ppermute(value, 'x', [(s, (s - offset) % n) for s in range(n)])  20.8 us
    all_to_all x2, blocking collectives, trade(): return lax.all_to_all(value, axes, 0, 0, tiled=True)  16.9 us
    all_to_all x5, waiting for transfers between devices, trade(): return lax.all_to_all(value, axes, 0, 0, tiled=True)  12.8 us
    unnamed x26, local copies, waits for them, and re-layouts  8.93 us
    pallas_call x1, Pallas kernels, body(): call(functools.partial(scores_kernel, lat, heads), [((n_keys, n_rows), f3...  8.19 us
    ppermute x1, waiting for transfers between devices, body(): far = lax.ppermute(near, 'y', [(0, 1), (1, 0)])  7.77 us
  transfers between devices with their start and end apart: 14, of which 9 were waited for; matrix products, arithmetic and copies ran while one was open for 2% of the time, Pallas kernels for 10%

profile of v2, /device:TPU:6, one launch (start us, length us, event | category | flops | bytes accessed | tf_op | source)
XLA Modules:
  0.0 181.7 jit_solution(1442748192979057451)
XLA Ops:
  0.6 1.8 broadcast_in_dim.11
  2.4 10.3 %all-to-all-start = ((bf16[8,64,576]{2,1,0:T(8,128)(2,1)}), bf16[8,64,576]{2,1,0:T(8,128)(2,1)S(1)}, u32[]{:S(2)}, u32[]{:S(2)}) async-start(bf16[8,64,576]{2,1,0:T(8,128)(2,1)} %broadcast_in_dim.11), calls=%async_computation | async-start | bytes 1310720 | tf_op jit(solution)/shard_map/all_to_all | solution.py:238
  14.7 2.4 %collective-permute-start.2 = (bf16[256,1152]{1,0:T(8,128)(2,1)S(1)}, bf16[256,1152]{1,0:T(8,128)(2,1)S(1)}, u32[]{:S(2)}, u32[]{:S(2)}) collective-permute-start(bf16[256,1152]{1,0:T(8,128)(2,1)S(1)} %shard_map.67.refs_1_.refs_0_), channel_id=1, source_target_pairs={{0,1},{1,2},{2,3},{3,0},{4,5},{5,6},{6,7},{7,4},{8,9},{9,10},{10,1... | collective-permute-start | bytes 1769480 | tf_op jit(solution)/shard_map/ppermute | solution.py:234
  17.1 3.5 %collective-permute-start.1 = (bf16[256,1152]{1,0:T(8,128)(2,1)S(1)}, bf16[256,1152]{1,0:T(8,128)(2,1)S(1)}, u32[]{:S(2)}, u32[]{:S(2)}) collective-permute-start(bf16[256,1152]{1,0:T(8,128)(2,1)S(1)} %shard_map.67.refs_1_.refs_0_), channel_id=1, source_target_pairs={{0,3},{1,0},{2,1},{3,2},{4,7},{5,4},{6,5},{7,6},{8,11},{9,8},{10,9... | collective-permute-start | bytes 1769480 | tf_op jit(solution)/shard_map/ppermute | solution.py:234
  20.6 10.8 %collective-permute-done.2.after3.refs_5_.refs_4_ = bf16[256,1152]{1,0:T(8,128)(2,1)S(1)} collective-permute-done((bf16[256,1152]{1,0:T(8,128)(2,1)S(1)}, bf16[256,1152]{1,0:T(8,128)(2,1)S(1)}, u32[]{:S(2)}, u32[]{:S(2)}) %collective-permute-start.2) | collective-permute-done | bytes 589856 | tf_op jit(solution)/shard_map/ppermute | solution.py:234
  31.4 3.3 %collective-permute-done.1.after2.refs_2_.refs_1_ = bf16[256,1152]{1,0:T(8,128)(2,1)S(1)} collective-permute-done((bf16[256,1152]{1,0:T(8,128)(2,1)S(1)}, bf16[256,1152]{1,0:T(8,128)(2,1)S(1)}, u32[]{:S(2)}, u32[]{:S(2)}) %collective-permute-start.1) | collective-permute-done | bytes 589856 | tf_op jit(solution)/shard_map/ppermute | solution.py:234
  35.9 2.3 %shard_map.68.refs_0_ = bf16[8,64,1024]{2,1,0:T(8,128)(2,1)} custom-call(bf16[64,7168]{1,0:T(8,128)(2,1)S(1)} %bitcast.9, bf16[8,64,576]{2,1,0:T(8,128)(2,1)S(1)} %all-to-all-done.after.near, bf16[256,1152]{1,0:T(8,128)(2,1)S(1)} %collective-permute-done.1.after2.refs_2_.refs_1_, bf16[256,1152]{1,0:T(8,128)(2,1)S(1)} %collective-permute-done.2.after3.refs_5_.refs_4_), custom_call_target="tpu_custom_call" | custom-call | flops 939524096 | bytes 1835008 | tf_op jit(solution)/shard_map/pallas_call | solution.py:262
  38.2 5.5 %all-to-all-start.1 = ((bf16[8,64,1024]{2,1,0:T(8,128)(2,1)}), bf16[8,64,1024]{2,1,0:T(8,128)(2,1)S(1)}, u32[]{:S(2)}, u32[]{:S(2)}) async-start(bf16[8,64,1024]{2,1,0:T(8,128)(2,1)} %shard_map.68.refs_0_), calls=%async_computation.1 | async-start | bytes 2097152 | tf_op jit(solution)/shard_map/all_to_all | solution.py:238
  43.8 3.4 %collective-permute-start = (bf16[8,64,576]{2,1,0:T(8,128)(2,1)S(1)}, bf16[8,64,576]{2,1,0:T(8,128)(2,1)}, u32[]{:S(2)}, u32[]{:S(2)}) collective-permute-start(bf16[8,64,576]{2,1,0:T(8,128)(2,1)S(1)} %all-to-all-done.after.near), channel_id=1, source_target_pairs={{0,4},{4,0},{1,5},{5,1},{2,6},{6,2},{3,7},{7,3},{8,12},{12,8},{9,1... | collective-permute-start | bytes 1769480 | tf_op jit(solution)/shard_map/ppermute | solution.py:259
  47.9 2.5 %collective-permute-start.4 = (bf16[128,1152]{1,0:T(8,128)(2,1)}, bf16[128,1152]{1,0:T(8,128)(2,1)}, u32[]{:S(2)}, u32[]{:S(2)}) collective-permute-start(bf16[128,1152]{1,0:T(8,128)(2,1)} %slice.9), channel_id=1, source_target_pairs={{0,1},{1,2},{2,3},{3,0},{4,5},{5,6},{6,7},{7,4},{8,9},{9,10},{10,1... | collective-permute-start | bytes 884744 | tf_op jit(solution)/shard_map/ppermute | solution.py:234
  51.1 3.4 %collective-permute-start.3 = (bf16[128,1152]{1,0:T(8,128)(2,1)}, bf16[128,1152]{1,0:T(8,128)(2,1)}, u32[]{:S(2)}, u32[]{:S(2)}) collective-permute-start(bf16[128,1152]{1,0:T(8,128)(2,1)} %slice.8), channel_id=1, source_target_pairs={{0,3},{1,0},{2,1},{3,2},{4,7},{5,4},{6,5},{7,6},{8,11},{9,8},{10,9... | collective-permute-start | bytes 884744 | tf_op jit(solution)/shard_map/ppermute | solution.py:234
  54.5 6.9 %collective-permute-done.4.refs_4_.refs_3_ = bf16[128,1152]{1,0:T(8,128)(2,1)} collective-permute-done((bf16[128,1152]{1,0:T(8,128)(2,1)}, bf16[128,1152]{1,0:T(8,128)(2,1)}, u32[]{:S(2)}, u32[]{:S(2)}) %collective-permute-start.4) | collective-permute-done | bytes 294944 | tf_op jit(solution)/shard_map/ppermute | solution.py:234
  62.0 7.8 %collective-permute-done.far = bf16[8,64,576]{2,1,0:T(8,128)(2,1)} collective-permute-done((bf16[8,64,576]{2,1,0:T(8,128)(2,1)S(1)}, bf16[8,64,576]{2,1,0:T(8,128)(2,1)}, u32[]{:S(2)}, u32[]{:S(2)}) %collective-permute-start) | collective-permute-done | bytes 589856 | tf_op jit(solution)/shard_map/ppermute | solution.py:259
  69.7 8.2 %shard_map.69 = (f32[1024,1024]{1,0:T(8,128)}, f32[1024,1024]{1,0:T(8,128)}, f32[16,256]{1,0:T(8,128)S(1)}) custom-call(s32[3]{0:T(128)S(1)} %pad_add_fusion.pos, bf16[8,64,576]{2,1,0:T(8,128)(2,1)S(1)} %all-to-all-done.after.near, bf16[8,64,576]{2,1,0:T(8,128)(2,1)} %collective-permute-done.far, bf16[8,64,1024]{2,1,0:T(8,128)(2,1)} %shard_map.68.refs_0_, ...), custom_call_target="tpu_custom_call" | custom-call | flops 2281701376 | bytes 8388608 | tf_op jit(solution)/shard_map/pallas_call | solution.py:271
  77.9 8.2 %all_to_all.35.stats = f32[4,16,256]{2,1,0:T(8,128)S(1)} all-to-all(f32[4,16,256]{2,1,0:T(8,128)S(1)} %shard_map.70), channel_id=1, replica_groups=mesh['dp'=8,'z'=8,'y'=2,'x'=4] {'x'}, dimensions={0} | all-to-all | bytes 131072 | tf_op jit(solution)/shard_map/all_to_all | solution.py:238
  86.1 5.8 %shard_map.71 = (bf16[1024,1024]{1,0:T(8,128)(2,1)S(1)}, bf16[1024,1024]{1,0:T(8,128)(2,1)}, bf16[16,32,128]{2,1,0:T(8,128)(2,1)S(1)}) custom-call(s32[3]{0:T(128)S(1)} %pad_add_fusion.pos, f32[4,16,256]{2,1,0:T(8,128)S(1)} %all_to_all.35.stats, f32[16,256]{1,0:T(8,128)S(1)} %get-tuple-element.17.st, f32[1024,1024]{1,0:T(8,128)} %get-tuple-element.18.e_ref, ...), custom_call_target="tpu_custom_call" | custom-call | flops 134217728 | bytes 12582912 | tf_op jit(solution)/shard_map/pallas_call | solution.py:279
  92.6 1.3 copy-done.7
  94.0 6.6 %all-to-all-start.4 = ((bf16[16,32,128]{2,1,0:T(8,128)(2,1)}), bf16[16,32,128]{2,1,0:T(8,128)(2,1)}, u32[]{:S(2)}, u32[]{:S(2)}) async-start(bf16[16,32,128]{2,1,0:T(8,128)(2,1)} %copy-done.6), calls=%async_computation.4 | async-start | bytes 262144 | tf_op jit(solution)/shard_map/all_to_all | solution.py:238
  100.5 6.9 %shard_map.72 = (bf16[8,64,512]{2,1,0:T(8,128)(2,1)S(1)}, bf16[8,64,512]{2,1,0:T(8,128)(2,1)}, f32[256,576]{1,0:T(8,128)S(1)}, bf16[256,576]{1,0:T(8,128)(2,1)S(...) custom-call(bf16[1024,1024]{1,0:T(8,128)(2,1)} %copy-done.7, ...), custom_call_target="tpu_custom_call" | custom-call | flops 3355443200 | bytes 4194304 | tf_op jit(solution)/shard_map/pallas_call | solution.py:287
  111.2 3.9 %collective-permute-start.8 = (bf16[8,64,512]{2,1,0:T(8,128)(2,1)}, bf16[8,64,512]{2,1,0:T(8,128)(2,1)S(1)}, u32[]{:S(2)}, u32[]{:S(2)}) collective-permute-start(bf16[8,64,512]{2,1,0:T(8,128)(2,1)} %get-tuple-element.27), channel_id=1, source_target_pairs={{0,4},{4,0},{1,5},{5,1},{2,6},{6,2},{3,7},{7,3},{8,12},{12,8},{9,1... | collective-permute-start | bytes 1572872 | tf_op jit(solution)/shard_map/ppermute | solution.py:292
  116.1 8.7 %all_to_all.36.rope = bf16[8,32,128]{2,1,0:T(8,128)(2,1)S(1)} all-to-all(bf16[8,32,128]{2,1,0:T(8,128)(2,1)S(1)} %get-tuple-element.30), channel_id=1, replica_groups=mesh['dp'=8,'z'=8,'y'=2,'x'=4] {'y','x'}, dimensions={0} | all-to-all | bytes 131072 | tf_op jit(solution)/shard_map/all_to_all | solution.py:238
  124.9 1.3 shard_map.75
  126.1 12.0 %all-to-all-start.6 = ((f32[64,8,128]{2,1,0:T(8,128)}), f32[64,8,128]{2,1,0:T(8,128)S(1)}, u32[]{:S(2)}, u32[]{:S(2)}) async-start(f32[64,8,128]{2,1,0:T(8,128)} %shard_map.75), calls=%async_computation.6 | async-start | bytes 524288 | tf_op jit(solution)/shard_map/all_to_all | solution.py:238
  138.2 2.0 %add_convert_fusion = bf16[8,64,512]{2,1,0:T(8,128)(2,1)} fusion(bf16[8,64,512]{2,1,0:T(8,128)(2,1)S(1)} %collective-permute-done.8, bf16[8,64,512]{2,1,0:T(8,128)(2,1)} %copy-done.3), kind=kLoop, calls=%fused_computation | loop fusion | flops 1048576 | bytes 1572864 | tf_op jit(solution)/shard_map/convert_element_type | solution.py:306
  140.2 12.7 %all-to-all-done.6.parts = f32[64,8,128]{2,1,0:T(8,128)S(1)} async-done(((f32[64,8,128]{2,1,0:T(8,128)}), f32[64,8,128]{2,1,0:T(8,128)S(1)}, u32[]{:S(2)}, u32[]{:S(2)}) %all-to-all-start.6) | async-done | bytes 262176 | tf_op jit(solution)/shard_map/all_to_all | solution.py:238
  152.9 3.7 %all-to-all-start.3 = ((bf16[8,64,512]{2,1,0:T(8,128)(2,1)}), bf16[8,64,512]{2,1,0:T(8,128)(2,1)S(1)}, u32[]{:S(2)}, u32[]{:S(2)}) async-start(bf16[8,64,512]{2,1,0:T(8,128)(2,1)} %add_convert_fusion), calls=%async_computation.3 | async-start | bytes 1048576 | tf_op jit(solution)/shard_map/all_to_all | solution.py:238
  156.6 3.8 %collective-permute-start.5 = (bf16[256,576]{1,0:T(8,128)(2,1)}, bf16[256,576]{1,0:T(8,128)(2,1)S(1)}, u32[]{:S(2)}, u32[]{:S(2)}) collective-permute-start(bf16[256,576]{1,0:T(8,128)(2,1)} %copy-done.12), channel_id=1, source_target_pairs={{0,1},{1,2},{2,3},{3,0},{4,5},{5,6},{6,7},{7,4},{8,9},{9,10},{10,1... | collective-permute-start | bytes 884744 | tf_op jit(solution)/shard_map/ppermute | solution.py:234
  160.4 3.0 %collective-permute-start.6 = (bf16[256,576]{1,0:T(8,128)(2,1)S(1)}, bf16[256,576]{1,0:T(8,128)(2,1)S(1)}, u32[]{:S(2)}, u32[]{:S(2)}) collective-permute-start(bf16[256,576]{1,0:T(8,128)(2,1)S(1)} %copy-done.11), channel_id=1, source_target_pairs={{0,2},{1,3},{2,0},{3,1},{4,6},{5,7},{6,4},{7,5},{8,10},{9,11},{10,... | collective-permute-start | bytes 884744 | tf_op jit(solution)/shard_map/ppermute | solution.py:234
  163.4 2.4 %collective-permute-start.7 = (bf16[256,576]{1,0:T(8,128)(2,1)S(1)}, bf16[256,576]{1,0:T(8,128)(2,1)S(1)}, u32[]{:S(2)}, u32[]{:S(2)}) collective-permute-start(bf16[256,576]{1,0:T(8,128)(2,1)S(1)} %copy-done.9), channel_id=1, source_target_pairs={{0,3},{1,0},{2,1},{3,2},{4,7},{5,4},{6,5},{7,6},{8,11},{9,8},{10,9... | collective-permute-start | bytes 884744 | tf_op jit(solution)/shard_map/ppermute | solution.py:234
  165.9 3.5 %collective-permute-done.5 = bf16[256,576]{1,0:T(8,128)(2,1)S(1)} collective-permute-done((bf16[256,576]{1,0:T(8,128)(2,1)}, bf16[256,576]{1,0:T(8,128)(2,1)S(1)}, u32[]{:S(2)}, u32[]{:S(2)}) %collective-permute-start.5) | collective-permute-done | bytes 294944 | tf_op jit(solution)/shard_map/ppermute | solution.py:234
  169.4 5.1 %collective-permute-done.6 = bf16[256,576]{1,0:T(8,128)(2,1)S(1)} collective-permute-done((bf16[256,576]{1,0:T(8,128)(2,1)S(1)}, bf16[256,576]{1,0:T(8,128)(2,1)S(1)}, u32[]{:S(2)}, u32[]{:S(2)}) %collective-permute-start.6) | collective-permute-done | bytes 294944 | tf_op jit(solution)/shard_map/ppermute | solution.py:234
  174.5 4.8 %collective-permute-done.7 = bf16[256,576]{1,0:T(8,128)(2,1)S(1)} collective-permute-done((bf16[256,576]{1,0:T(8,128)(2,1)S(1)}, bf16[256,576]{1,0:T(8,128)(2,1)S(1)}, u32[]{:S(2)}, u32[]{:S(2)}) %collective-permute-start.7) | collective-permute-done | bytes 294944 | tf_op jit(solution)/shard_map/ppermute | solution.py:234
  (40 shorter events, 13.1 us)
Async XLA Ops:
  2.4 32.3 %all-to-all-start = ((bf16[8,64,576]{2,1,0:T(8,128)(2,1)}), bf16[8,64,576]{2,1,0:T(8,128)(2,1)S(1)}, u32[]{:S(2)}, u32[]{:S(2)}) async-start(bf16[8,64,576]{2,1,0:T(8,128)(2,1)} %broadcast_in_dim.11), calls=%async_computation | async-start | bytes 1310720 | tf_op jit(solution)/shard_map/all_to_all | solution.py:238
  12.7 1.0 copy-start.4
  13.7 0.9 copy-start.5
  14.7 16.7 %collective-permute-start.2 = (bf16[256,1152]{1,0:T(8,128)(2,1)S(1)}, bf16[256,1152]{1,0:T(8,128)(2,1)S(1)}, u32[]{:S(2)}, u32[]{:S(2)}) collective-permute-start(bf16[256,1152]{1,0:T(8,128)(2,1)S(1)} %shard_map.67.refs_1_.refs_0_), channel_id=1, source_target_pairs={{0,1},{1,2},{2,3},{3,0},{4,5},{5,6},{6,7},{7,4},{8,9},{9,10},{10,1... | collective-permute-start | bytes 1769480 | tf_op jit(solution)/shard_map/ppermute | solution.py:234
  17.1 17.6 %collective-permute-start.1 = (bf16[256,1152]{1,0:T(8,128)(2,1)S(1)}, bf16[256,1152]{1,0:T(8,128)(2,1)S(1)}, u32[]{:S(2)}, u32[]{:S(2)}) collective-permute-start(bf16[256,1152]{1,0:T(8,128)(2,1)S(1)} %shard_map.67.refs_1_.refs_0_), channel_id=1, source_target_pairs={{0,3},{1,0},{2,1},{3,2},{4,7},{5,4},{6,5},{7,6},{8,11},{9,8},{10,9... | collective-permute-start | bytes 1769480 | tf_op jit(solution)/shard_map/ppermute | solution.py:234
  34.7 1.2 copy-start
  38.2 39.7 %all-to-all-start.1 = ((bf16[8,64,1024]{2,1,0:T(8,128)(2,1)}), bf16[8,64,1024]{2,1,0:T(8,128)(2,1)S(1)}, u32[]{:S(2)}, u32[]{:S(2)}) async-start(bf16[8,64,1024]{2,1,0:T(8,128)(2,1)} %shard_map.68.refs_0_), calls=%async_computation.1 | async-start | bytes 2097152 | tf_op jit(solution)/shard_map/all_to_all | solution.py:238
  43.8 26.0 %collective-permute-start = (bf16[8,64,576]{2,1,0:T(8,128)(2,1)S(1)}, bf16[8,64,576]{2,1,0:T(8,128)(2,1)}, u32[]{:S(2)}, u32[]{:S(2)}) collective-permute-start(bf16[8,64,576]{2,1,0:T(8,128)(2,1)S(1)} %all-to-all-done.after.near), channel_id=1, source_target_pairs={{0,4},{4,0},{1,5},{5,1},{2,6},{6,2},{3,7},{7,3},{8,12},{12,8},{9,1... | collective-permute-start | bytes 1769480 | tf_op jit(solution)/shard_map/ppermute | solution.py:259
  47.9 13.6 %collective-permute-start.4 = (bf16[128,1152]{1,0:T(8,128)(2,1)}, bf16[128,1152]{1,0:T(8,128)(2,1)}, u32[]{:S(2)}, u32[]{:S(2)}) collective-permute-start(bf16[128,1152]{1,0:T(8,128)(2,1)} %slice.9), channel_id=1, source_target_pairs={{0,1},{1,2},{2,3},{3,0},{4,5},{5,6},{6,7},{7,4},{8,9},{9,10},{10,1... | collective-permute-start | bytes 884744 | tf_op jit(solution)/shard_map/ppermute | solution.py:234
  51.1 10.9 %collective-permute-start.3 = (bf16[128,1152]{1,0:T(8,128)(2,1)}, bf16[128,1152]{1,0:T(8,128)(2,1)}, u32[]{:S(2)}, u32[]{:S(2)}) collective-permute-start(bf16[128,1152]{1,0:T(8,128)(2,1)} %slice.8), channel_id=1, source_target_pairs={{0,3},{1,0},{2,1},{3,2},{4,7},{5,4},{6,5},{7,6},{8,11},{9,8},{10,9... | collective-permute-start | bytes 884744 | tf_op jit(solution)/shard_map/ppermute | solution.py:234
  92.0 0.7 copy-start.6
  92.6 1.3 copy-start.7
  94.0 21.2 %all-to-all-start.4 = ((bf16[16,32,128]{2,1,0:T(8,128)(2,1)}), bf16[16,32,128]{2,1,0:T(8,128)(2,1)}, u32[]{:S(2)}, u32[]{:S(2)}) async-start(bf16[16,32,128]{2,1,0:T(8,128)(2,1)} %copy-done.6), calls=%async_computation.4 | async-start | bytes 262144 | tf_op jit(solution)/shard_map/all_to_all | solution.py:238
  107.4 0.8 copy-start.1
  108.2 0.8 copy-start.3
  109.1 0.7 copy-start.8
  109.8 0.7 copy-start.10
  110.5 0.7 copy-start.12
  111.2 49.2 %copy-start.11 = (bf16[256,576]{1,0:T(8,128)(2,1)S(1)}, bf16[256,576]{1,0:T(8,128)(2,1)}, u32[]{:S(2)}) copy-start(bf16[256,576]{1,0:T(8,128)(2,1)} %copy-done.10) | copy-start | bytes 884740
  111.2 52.2 %copy-start.9 = (bf16[256,576]{1,0:T(8,128)(2,1)S(1)}, bf16[256,576]{1,0:T(8,128)(2,1)}, u32[]{:S(2)}) copy-start(bf16[256,576]{1,0:T(8,128)(2,1)} %copy-done.8) | copy-start | bytes 884740
  111.2 68.1 %copy-start.2 = (f32[256,576]{1,0:T(8,128)S(1)}, f32[256,576]{1,0:T(8,128)}, u32[]{:S(2)}) copy-start(f32[256,576]{1,0:T(8,128)} %copy-done.1) | copy-start | bytes 1769476
  111.2 26.9 %collective-permute-start.8 = (bf16[8,64,512]{2,1,0:T(8,128)(2,1)}, bf16[8,64,512]{2,1,0:T(8,128)(2,1)S(1)}, u32[]{:S(2)}, u32[]{:S(2)}) collective-permute-start(bf16[8,64,512]{2,1,0:T(8,128)(2,1)} %get-tuple-element.27), channel_id=1, source_target_pairs={{0,4},{4,0},{1,5},{5,1},{2,6},{6,2},{3,7},{7,3},{8,12},{12,8},{9,1... | collective-permute-start | bytes 1572872 | tf_op jit(solution)/shard_map/ppermute | solution.py:292
  126.1 26.8 %all-to-all-start.6 = ((f32[64,8,128]{2,1,0:T(8,128)}), f32[64,8,128]{2,1,0:T(8,128)S(1)}, u32[]{:S(2)}, u32[]{:S(2)}) async-start(f32[64,8,128]{2,1,0:T(8,128)} %shard_map.75), calls=%async_computation.6 | async-start | bytes 524288 | tf_op jit(solution)/shard_map/all_to_all | solution.py:238
  152.9 28.0 %all-to-all-start.3 = ((bf16[8,64,512]{2,1,0:T(8,128)(2,1)}), bf16[8,64,512]{2,1,0:T(8,128)(2,1)S(1)}, u32[]{:S(2)}, u32[]{:S(2)}) async-start(bf16[8,64,512]{2,1,0:T(8,128)(2,1)} %add_convert_fusion), calls=%async_computation.3 | async-start | bytes 1048576 | tf_op jit(solution)/shard_map/all_to_all | solution.py:238
  156.6 12.7 %collective-permute-start.5 = (bf16[256,576]{1,0:T(8,128)(2,1)}, bf16[256,576]{1,0:T(8,128)(2,1)S(1)}, u32[]{:S(2)}, u32[]{:S(2)}) collective-permute-start(bf16[256,576]{1,0:T(8,128)(2,1)} %copy-done.12), channel_id=1, source_target_pairs={{0,1},{1,2},{2,3},{3,0},{4,5},{5,6},{6,7},{7,4},{8,9},{9,10},{10,1... | collective-permute-start | bytes 884744 | tf_op jit(solution)/shard_map/ppermute | solution.py:234
  160.4 14.1 %collective-permute-start.6 = (bf16[256,576]{1,0:T(8,128)(2,1)S(1)}, bf16[256,576]{1,0:T(8,128)(2,1)S(1)}, u32[]{:S(2)}, u32[]{:S(2)}) collective-permute-start(bf16[256,576]{1,0:T(8,128)(2,1)S(1)} %copy-done.11), channel_id=1, source_target_pairs={{0,2},{1,3},{2,0},{3,1},{4,6},{5,7},{6,4},{7,5},{8,10},{9,11},{10,... | collective-permute-start | bytes 884744 | tf_op jit(solution)/shard_map/ppermute | solution.py:234
  163.4 15.9 %collective-permute-start.7 = (bf16[256,576]{1,0:T(8,128)(2,1)S(1)}, bf16[256,576]{1,0:T(8,128)(2,1)S(1)}, u32[]{:S(2)}, u32[]{:S(2)}) collective-permute-start(bf16[256,576]{1,0:T(8,128)(2,1)S(1)} %copy-done.9), channel_id=1, source_target_pairs={{0,3},{1,0},{2,1},{3,2},{4,7},{5,4},{6,5},{7,6},{8,11},{9,8},{10,9... | collective-permute-start | bytes 884744 | tf_op jit(solution)/shard_map/ppermute | solution.py:234

commit v3 on v2

--- a/solution.py
+++ b/solution.py
@@ -61,7 +61,7 @@
     ]
 
 
-def columns_kernel(block, n_z, n_grp, hid, after, after2, after3, out):
+def columns_kernel(block, n_z, n_grp, n_core, hid, out):
     k_dev, model = hid.shape
     n_data = model // (n_z * n_grp * block)
     span = n_z * n_grp * block
@@ -73,8 +73,9 @@
     stacked = jnp.concatenate([hid[:, d * span : (d + 1) * span] for d in range(n_data)])
     moved = nn(stacked, pick).astype(bf16)
     for d in range(n_data):
+        first = d // n_core * wide
         for g in range(n_grp):
-            out[g, :, d * wide : (d + 1) * wide] = moved[
+            out[d % n_core * n_grp + g, :, first : first + wide] = moved[
                 d * k_dev : (d + 1) * k_dev, g * wide : (g + 1) * wide
             ]
 
@@ -85,12 +86,12 @@
     return k.reshape(k.shape[0] * k.shape[1], k.shape[2])
 
 
-def scores_kernel(lat, heads, pos, near, far, *refs):
-    blocks, (e_ref, dp_ref, st_ref) = row_blocks(refs[1:-3]), refs[-3:]
+def scores_kernel(lat, heads, pos, near, far, after, *refs):
+    blocks, (e_ref, dp_ref, st_ref) = row_blocks(refs[:-3]), refs[-3:]
     z, y, x = pos[0], pos[1], pos[2]
     n_z, k_dev, _ = near.shape
     n_x = len(blocks)
-    rows = refs[1].shape[0]
+    rows = refs[0].shape[0]
     n_keys = 2 * n_z * k_dev
     tiles = n_keys // TILE
     per = TILE // k_dev
@@ -126,10 +127,6 @@
             total += jnp.sum(e, axis=0, keepdims=True)
             delta += jnp.sum(e * dp, axis=0, keepdims=True)
         st_ref[4 * b : 4 * b + 4] = jnp.concatenate([top, total, delta, jnp.zeros_like(top)])
-
-
-def copies_kernel(st, after, out):
-    out[...] = jnp.broadcast_to(st[...][None], out.shape)
 
 
 def dscores_kernel(lat, pos, stats, st, e_ref, dp_ref, *refs):
@@ -175,13 +172,12 @@
             rope_ref[2 * zz + side] = jnp.concatenate([k[:half_keys], k[half_keys:]], axis=1)
 
 
-def grads_kernel(lat, p_ref, ds_ref, near, far, *refs):
-    blocks, (mine, other), dq_refs = row_blocks(refs[:5]), refs[5:7], refs[7:]
-    n_z, k_dev, _ = near.shape
+def latent_kernel(lat, p_ref, ds_ref, *refs):
+    blocks, outs = row_blocks(refs[:5]), refs[5:]
+    n_z, k_dev, _ = outs[0].shape
     rows = refs[0].shape[0]
-    tiles = p_ref.shape[0] // TILE
     per = TILE // k_dev
-    for i in range(tiles):
+    for i in range(p_ref.shape[0] // TILE):
         part = slice(i * TILE, (i + 1) * TILE)
         v = None
         for b, t in enumerate(blocks):
@@ -190,11 +186,16 @@
         v = v * softmax_scale
         for b, t in enumerate(blocks):
             v += nn(p_ref[part, b * rows : (b + 1) * rows], t(slice(0, lat)))
-        out, first = (mine, i * per) if i * per < n_z else (other, i * per - n_z)
+        out, first = outs[i * per // n_z], i * per % n_z
         out[first : first + per] = v.astype(bf16).reshape(per, k_dev, lat)
-    for b, out in enumerate(dq_refs):
+
+
+def query_kernel(ds_ref, near, far, after, *outs):
+    rows = outs[0].shape[0]
+    per = TILE // near.shape[1]
+    for b, out in enumerate(outs):
         v = None
-        for i in range(tiles):
+        for i in range(ds_ref.shape[0] // TILE):
             a = tn(
                 ds_ref[i * TILE : (i + 1) * TILE, b * rows : (b + 1) * rows],
                 key_tile(near, far, i, per),
@@ -203,18 +204,20 @@
         out[...] = (v * softmax_scale).astype(out.dtype)
 
 
-def rope_kernel(parts, all_ref, rope_ref):
-    half = parts.shape[1]
+def weight_kernel(parts, cols, after, rope_ref, out):
     v = jnp.sum(parts[...].astype(f32), axis=0)
-    rope_ref[...] = jnp.concatenate([v[:, : v.shape[1] // 2], v[:, v.shape[1] // 2 :]])
-    all_ref[...] = jnp.broadcast_to(v.astype(bf16)[None], all_ref.shape)
-
-
-def weight_kernel(cols, rope, out):
-    n, k_dev, wide = cols.shape
-    e = rope.shape[2] // 2
-    r = jnp.concatenate([rope[:, :, :e], rope[:, :, e:]], axis=1).reshape(n * k_dev, e)
-    v = tn(cols[...].reshape(n * k_dev, wide), r).reshape(wide // SLOT, SLOT, e)
+    e = v.shape[1] // 2
+    rope = jnp.concatenate([v[:, :e], v[:, e:]])
+    rope_ref[...] = rope
+    low = rope.astype(bf16)
+    for i in range(cols.shape[0]):
+        out[i] = tn(low, cols[i]).astype(bf16)
+
+
+def weight_half_kernel(parts, out):
+    v = jnp.sum(parts[...].astype(f32), axis=0)
+    v = jnp.swapaxes(v, 0, 1)
+    v = v.reshape(v.shape[0] // SLOT, SLOT, v.shape[1])
     out[...] = jnp.concatenate([v[:, : SLOT // 2], v[:, SLOT // 2 :]], axis=2)
 
 
@@ -225,8 +228,8 @@
 
 
 def latent_sum_kernel(parts, rope, out):
-    lat = parts.shape[2]
-    out[:, :lat] = jnp.sum(parts[...].astype(f32), axis=0)
+    lat = parts.shape[1]
+    out[:, :lat] = parts[...].astype(f32)
     out[:, lat:] = rope[...]
 
 
@@ -239,14 +242,16 @@
 
 
 def body(query, latent, dout, hidden):
-    nd, nz, ny, nx = (lax.axis_size(a) for a in ("dp", "z", "y", "x"))
+    nw, nc, nz, ny, nx = (lax.axis_size(a) for a in ("w", "c", "z", "y", "x"))
     tok, heads, width = query.shape[1:]
     lat = dout.shape[3]
     rope = width - lat
     k_dev, model = hidden.shape[1:]
     rows = tok * heads
     n_rows, n_keys = nx * rows, nz * ny * k_dev
-    block = model // (nd * nz * ny * nx)
+    pairs = n_rows * n_keys
+    block = model // (nw * nc * nz * ny * nx)
+    swap = [(0, 1), (1, 0)]
     pos = jnp.stack([lax.axis_index(a) for a in ("z", "y", "x")]).astype(jnp.int32)
 
     near = trade(jnp.broadcast_to(latent, (nz, k_dev, width)), "z")
@@ -256,56 +261,48 @@
     right, left = fetch(own, 1, nx), fetch(own, nx - 1, nx)
     first, second = fetch(right[: rows // 2], 1, nx), fetch(left[rows // 2 :], nx - 1, nx)
     blocks = [own, right, first, second, left]
-    far = lax.ppermute(near, "y", [(0, 1), (1, 0)])
-
-    wide = nd * nz * SLOT
+    far = lax.ppermute(near, "y", swap)
+
+    wide = nw * nz * SLOT
     (cols,) = call(
-        functools.partial(columns_kernel, block, nz, ny * nx),
-        [((ny * nx, k_dev, wide), bf16)], 4, unused=(1, 2, 3),
-        flops=2 * k_dev * nd * (model // nd) * 1024, moved=2 * k_dev * model * 2,
-    )(hidden[0], near, right, left)
-    sorted_cols = cols
-    cols = trade(cols, ("y", "x"))
-
-    pairs = n_rows * n_keys
+        functools.partial(columns_kernel, block, nz, ny * nx, nc), [((nc * ny * nx, k_dev, wide), bf16)], 1,
+        flops=2 * k_dev * model * 1024, moved=4 * k_dev * model, limit=20,
+    )(hidden[0])
     e, dp, st = call(
         functools.partial(scores_kernel, lat, heads),
-        [((n_keys, n_rows), f32)] * 2 + [((4 * nx, rows), f32)], 5 + nx, smem=(0,),
+        [((n_keys, n_rows), f32)] * 2 + [((4 * nx, rows), f32)], 9, smem=(0,),
         unused=(3,),
-        flops=2 * pairs * (width + lat), moved=8 * pairs,
-    )(pos, near, far, sorted_cols, *blocks)
-    (stats,) = call(copies_kernel, [((nx,) + st.shape, f32)], 2, unused=(1,))(st, cols)
-    stats = trade(stats, "x")
+        flops=2 * pairs * (width + lat), moved=8 * pairs, limit=20,
+    )(pos, near, far, cols, *blocks)
+    stats = trade(jnp.broadcast_to(st[None], (nx,) + st.shape), "x")
     p, ds, rope_part = call(
         functools.partial(dscores_kernel, lat),
-        [((n_keys, n_rows), bf16)] * 2 + [((nz * ny, k_dev // 2, 2 * rope), bf16)],
-        6 + nx, smem=(0,),
-        flops=2 * pairs * rope, moved=12 * pairs,
+        [((n_keys, n_rows), bf16)] * 2 + [((nz * ny, k_dev // 2, 2 * rope), bf16)], 10, smem=(0,),
+        flops=2 * pairs * rope, moved=12 * pairs, limit=20,
     )(pos, stats, st, e, dp, *blocks)
     rope_part = trade(rope_part, ("z", "y"))
-
-    mine, other, *dq = call(
-        functools.partial(grads_kernel, lat),
-        [((nz, k_dev, lat), bf16)] * 2 + [((rows, width), f32)] + [((rows, width), bf16)] * (nx - 1),
-        5 + nx, flops=2 * pairs * (width + 2 * lat), moved=4 * pairs,
-    )(p, ds, near, far, *blocks)
-    other = lax.ppermute(other, "y", [(0, 1), (1, 0)])
+    mine, other = call(
+        functools.partial(latent_kernel, lat), [((nz, k_dev, lat), bf16)] * 2, 7,
+        flops=4 * pairs * lat, moved=4 * pairs, limit=20,
+    )(p, ds, *blocks)
+    other = lax.ppermute(other, "y", swap)
+    rope_sum, terms = call(
+        weight_kernel, [((k_dev, rope), f32), ((nc * ny * nx, rope, wide), bf16)], 3, unused=(2,),
+        flops=2 * k_dev * nc * ny * nx * wide * rope, moved=4 * k_dev * model, limit=20,
+    )(rope_part, cols, mine)
+    after = terms
+    terms = trade(terms, ("c", "y", "x"))
+    dq = call(
+        query_kernel, [((rows, width), f32)] + [((rows, width), bf16)] * (nx - 1), 4, unused=(3,),
+        flops=2 * pairs * width, moved=4 * pairs, limit=20,
+    )(ds, near, far, after)
     dq = [dq[0]] + [fetch(dq[k], nx - k, nx) for k in range(1, nx)]
-
-    rope_all, rope_sum = call(
-        rope_kernel, [((ny * nx, k_dev // 2, 2 * rope), bf16), ((k_dev, rope), f32)], 1
-    )(rope_part)
-    rope_all = trade(rope_all, ("y", "x"))
-    (terms,) = call(
-        weight_kernel, [((nd * nz, SLOT // 2, 2 * rope), f32)], 2,
-        flops=2 * ny * nx * k_dev * wide * rope, moved=2 * ny * nx * k_dev * wide,
-    )(cols, rope_all)
-    terms = trade(terms, ("dp", "z"))
-    (dweight,) = call(weight_sum_kernel, [((block, rope), f32)], 1)(terms)
-
     half = (mine.astype(f32) + other.astype(f32)).astype(bf16)
-    half = trade(half, "z")
-    (dlatent,) = call(latent_sum_kernel, [((k_dev, width), f32)], 2)(half, rope_sum)
+    half = lax.psum_scatter(half.reshape(nz * k_dev, lat), "z", scatter_dimension=0, tiled=True)
+    (terms,) = call(weight_half_kernel, [((nw * nz, SLOT // 2, 2 * rope), f32)], 1, limit=20)(terms)
+    terms = trade(terms, ("w", "z"))
+    (dweight,) = call(weight_sum_kernel, [((block, rope), f32)], 1, limit=20)(terms)
+    (dlatent,) = call(latent_sum_kernel, [((k_dev, width), f32)], 2, limit=20)(half, rope_sum)
 
     total = dq[0]
     for part in dq[1:]:
@@ -314,13 +311,14 @@
 
 
 def solution(mesh):
-    fine = Mesh(mesh.devices.reshape(8, 8, 2, 4), ("dp", "z", "y", "x"))
-    sp = ("z", "y", "x")
-    in_specs = (
-        P("dp", sp, None, None),
-        P("dp", sp, None),
-        P("dp", sp, None, None),
-        P("dp", sp, None),
+    fine = Mesh(mesh.devices.reshape(4, 2, 8, 2, 4), ("w", "c", "z", "y", "x"))
+    dp, sp = ("w", "c"), ("z", "y", "x")
+    tokens = P(dp, sp, None, None)
+    keys = P(dp, sp, None)
+    return jax.shard_map(
+        body,
+        mesh=fine,
+        in_specs=(tokens, keys, tokens, keys),
+        out_specs=(tokens, keys, P(dp + sp, None)),
+        check_vma=False,
     )
-    out_specs = (P("dp", sp, None, None), P("dp", sp, None), P(("dp",) + sp, None))
-    return jax.shard_map(body, mesh=fine, in_specs=in_specs, out_specs=out_specs, check_vma=False)

time: 184 us -> 174 us (0.946)
  between operations: 0.79 us -> 14.3 us
  Pallas kernels: 27 us -> 17.4 us
  blocking collectives: 16.9 us -> 7.86 us
  starting transfers between devices: 66.2 us -> 57.3 us
  local copies, waits for them, and re-layouts: 12.2 us -> 17.6 us
    ppermute x7, waiting for transfers between devices: 35.1 us -> 7.34 us  [fetch(): return lax.ppermute(value, 'x', [(s, (s - offset) % n) for s in range(n)])]
    ppermute x2, waiting for transfers between devices: 7.78 us -> 21.7 us  [the longest x1 21.7 us: body(): other = lax.ppermute(other, 'y', swap)]
    reduce_scatter x0 -> x1, waiting for transfers between devices: none -> 11.9 us  [body(): lax.psum_scatter(half.reshape(nz * k_dev, lat), 'z', scatter_dimension=0,...]
    all_to_all x2 -> x1, blocking collectives: 16.9 us -> 7.86 us  [trade(): return lax.all_to_all(value, axes, 0, 0, tiled=True)]
    all_to_all x5 -> x4, starting transfers between devices: 38.1 us -> 30 us  [trade(): return lax.all_to_all(value, axes, 0, 0, tiled=True)]
    unnamed x26 -> x28, local copies, waits for them, and re-layouts: 8.93 us -> 14.3 us
    pallas_call x1, Pallas kernels: 8.19 us -> 4.54 us  [body(): call(functools.partial(scores_kernel, lat, heads), [((n_keys, n_rows), f3...]
    pallas_call x1, Pallas kernels: 5.81 us -> 2.42 us  [body(): call(functools.partial(dscores_kernel, lat), [((n_keys, n_rows), bf16)] *...]
  transfers between devices with their start and end apart: 14 -> 14, of which waited for: 9 -> 7; matrix products, arithmetic and copies ran while one was open for 2% -> 3% of each run, Pallas kernels for 10% -> 5%
where the time goes in v3:
time: 174 us; the launch traced here: 172 us
  starting transfers between devices  57.3 us (33%)
  waiting for transfers between devices  55.2 us (32%)
  local copies, waits for them, and re-layouts  17.6 us (10%)
  Pallas kernels  17.4 us (10%)
  between operations  14.3 us (8%)
  blocking collectives  7.86 us (5%)
  other arithmetic  2.85 us (2%)
    all_to_all x4, starting transfers between devices, trade(): return lax.all_to_all(value, axes, 0, 0, tiled=True)  30 us
    ppermute x1, waiting for transfers between devices, body(): other = lax.ppermute(other, 'y', swap)  21.7 us
    ppermute x7, starting transfers between devices, fetch(): return lax.ppermute(value, 'x', [(s, (s - offset) % n) for s in range(n)])  20.3 us
    unnamed x28, local copies, waits for them, and re-layouts  14.3 us
    all_to_all x4, waiting for transfers between devices, trade(): return lax.all_to_all(value, axes, 0, 0, tiled=True)  14.2 us
    reduce_scatter x1, waiting for transfers between devices, body(): lax.psum_scatter(half.reshape(nz * k_dev, lat), 'z', scatter_dimension=0,...  11.9 us
    all_to_all x1, blocking collectives, trade(): return lax.all_to_all(value, axes, 0, 0, tiled=True)  7.86 us
    ppermute x7, waiting for transfers between devices, fetch(): return lax.ppermute(value, 'x', [(s, (s - offset) % n) for s in range(n)])  7.34 us
  transfers between devices with their start and end apart: 14, of which 7 were waited for; matrix products, arithmetic and copies ran while one was open for 3% of the time, Pallas kernels for 5%

profile of v3, /device:TPU:6, one launch (start us, length us, event | category | flops | bytes accessed | tf_op | source)
XLA Modules:
  0.0 172.5 jit_solution(12388866451868746678)
XLA Ops:
  7.2 1.8 %broadcast_in_dim.17 = bf16[8,64,576]{2,1,0:T(8,128)(2,1)} broadcast(bf16[64,576]{1,0:T(8,128)(2,1)} %bitcast.16), dimensions={1,2} | broadcast | bytes 663552 | tf_op jit(solution)/shard_map/broadcast_in_dim | solution.py:257
  9.0 10.3 %all-to-all-start = ((bf16[8,64,576]{2,1,0:T(8,128)(2,1)}), bf16[8,64,576]{2,1,0:T(8,128)(2,1)S(1)}, u32[]{:S(2)}, u32[]{:S(2)}) async-start(bf16[8,64,576]{2,1,0:T(8,128)(2,1)} %broadcast_in_dim.17), calls=%async_computation | async-start | bytes 1310720 | tf_op jit(solution)/shard_map/all_to_all | solution.py:241
  21.3 2.4 %collective-permute-start.3 = (bf16[256,1152]{1,0:T(8,128)(2,1)S(1)}, bf16[256,1152]{1,0:T(8,128)(2,1)S(1)}, u32[]{:S(2)}, u32[]{:S(2)}) collective-permute-start(bf16[256,1152]{1,0:T(8,128)(2,1)S(1)} %shard_map.68.refs_0_), channel_id=1, source_target_pairs={{0,1},{1,2},{2,3},{3,0},{4,5},{5,6},{6,7},{7,4},{8,9},{9,10},{10,1... | collective-permute-start | bytes 1769480 | tf_op jit(solution)/shard_map/ppermute | solution.py:237
  23.6 3.5 %collective-permute-start.1 = (bf16[256,1152]{1,0:T(8,128)(2,1)S(1)}, bf16[256,1152]{1,0:T(8,128)(2,1)S(1)}, u32[]{:S(2)}, u32[]{:S(2)}) collective-permute-start(bf16[256,1152]{1,0:T(8,128)(2,1)S(1)} %shard_map.68.refs_0_), channel_id=1, source_target_pairs={{0,3},{1,0},{2,1},{3,2},{4,7},{5,4},{6,5},{7,6},{8,11},{9,8},{10,9... | collective-permute-start | bytes 1769480 | tf_op jit(solution)/shard_map/ppermute | solution.py:237
  27.1 12.5 %all-to-all-done.near = bf16[8,64,576]{2,1,0:T(8,128)(2,1)S(1)} async-done(((bf16[8,64,576]{2,1,0:T(8,128)(2,1)}), bf16[8,64,576]{2,1,0:T(8,128)(2,1)S(1)}, u32[]{:S(2)}, u32[]{:S(2)}) %all-to-all-start) | async-done | bytes 589856 | tf_op jit(solution)/shard_map/all_to_all | solution.py:241
  39.6 3.5 %collective-permute-start = (bf16[8,64,576]{2,1,0:T(8,128)(2,1)S(1)}, bf16[8,64,576]{2,1,0:T(8,128)(2,1)}, u32[]{:S(2)}, u32[]{:S(2)}) collective-permute-start(bf16[8,64,576]{2,1,0:T(8,128)(2,1)S(1)} %all-to-all-done.near), channel_id=1, source_target_pairs={{0,4},{4,0},{1,5},{5,1},{2,6},{6,2},{3,7},{7,3},{8,12},{12,8},{9,1... | collective-permute-start | bytes 1769480 | tf_op jit(solution)/shard_map/ppermute | solution.py:264
  43.8 2.4 %collective-permute-start.4 = (bf16[128,1152]{1,0:T(8,128)(2,1)}, bf16[128,1152]{1,0:T(8,128)(2,1)S(1)}, u32[]{:S(2)}, u32[]{:S(2)}) collective-permute-start(bf16[128,1152]{1,0:T(8,128)(2,1)} %slice.9), channel_id=1, source_target_pairs={{0,1},{1,2},{2,3},{3,0},{4,5},{5,6},{6,7},{7,4},{8,9},{9,10},{10,1... | collective-permute-start | bytes 884744 | tf_op jit(solution)/shard_map/ppermute | solution.py:237
  46.9 3.4 %collective-permute-start.2 = (bf16[128,1152]{1,0:T(8,128)(2,1)}, bf16[128,1152]{1,0:T(8,128)(2,1)S(1)}, u32[]{:S(2)}, u32[]{:S(2)}) collective-permute-start(bf16[128,1152]{1,0:T(8,128)(2,1)} %slice.8), channel_id=1, source_target_pairs={{0,3},{1,0},{2,1},{3,2},{4,7},{5,4},{6,5},{7,6},{8,11},{9,8},{10,9... | collective-permute-start | bytes 884744 | tf_op jit(solution)/shard_map/ppermute | solution.py:237
  53.0 1.6 collective-permute-done.4.refs_3_
  54.6 4.1 %collective-permute-done.2.refs_2_ = bf16[128,1152]{1,0:T(8,128)(2,1)S(1)} collective-permute-done((bf16[128,1152]{1,0:T(8,128)(2,1)}, bf16[128,1152]{1,0:T(8,128)(2,1)S(1)}, u32[]{:S(2)}, u32[]{:S(2)}) %collective-permute-start.2) | collective-permute-done | bytes 294944 | tf_op jit(solution)/shard_map/ppermute | solution.py:237
  58.6 4.5 %shard_map.69 = (f32[1024,1024]{1,0:T(8,128)S(1)}, f32[1024,1024]{1,0:T(8,128)S(1)}, f32[16,256]{1,0:T(8,128)S(1)}) custom-call(s32[3]{0:T(128)S(1)} %pad_add_fusion.pos, bf16[8,64,576]{2,1,0:T(8,128)(2,1)S(1)} %all-to-all-done.near, bf16[8,64,576]{2,1,0:T(8,128)(2,1)} %collective-permute-done.far, bf16[16,64,512]{2,1,0:T(8,128)(2,1)S(1)} %shard_map.67.after.cols, ...), custom_call_target="tpu_custom_call" | custom-call | flops 2281701376 | bytes 8388608 | tf_op jit(solution)/shard_map/pallas_call | solution.py:271
  63.2 7.9 %all_to_all.25.stats = f32[4,16,256]{2,1,0:T(8,128)S(1)} all-to-all(f32[4,16,256]{2,1,0:T(8,128)S(1)} %broadcast_in_dim.18), channel_id=1, replica_groups=mesh['w'=4,'c'=2,'z'=8,'y'=2,'x'=4] {'x'}, dimensions={0} | all-to-all | bytes 131072 | tf_op jit(solution)/shard_map/all_to_all | solution.py:241
  71.1 2.4 %shard_map.70 = (bf16[1024,1024]{1,0:T(8,128)(2,1)S(1)}, bf16[1024,1024]{1,0:T(8,128)(2,1)S(1)}, bf16[16,32,128]{2,1,0:T(8,128)(2,1)}) custom-call(s32[3]{0:T(128)S(1)} %pad_add_fusion.pos, f32[4,16,256]{2,1,0:T(8,128)S(1)} %all_to_all.25.stats, f32[16,256]{1,0:T(8,128)S(1)} %get-tuple-element.17.st, f32[1024,1024]{1,0:T(8,128)S(1)} %get-tuple-element.18.e_ref, ...), custom_call_target="tpu_custom_call" | custom-call | flops 134217728 | bytes 12582912 | tf_op jit(solution)/shard_map/pallas_call | solution.py:278
  73.5 1.3 copy-done.7
  76.2 3.5 %all-to-all-start.2 = ((bf16[16,32,128]{2,1,0:T(8,128)(2,1)}), bf16[16,32,128]{2,1,0:T(8,128)(2,1)S(1)}, u32[]{:S(2)}, u32[]{:S(2)}) async-start(bf16[16,32,128]{2,1,0:T(8,128)(2,1)} %get-tuple-element.21), calls=%async_computation.2 | async-start | bytes 262144 | tf_op jit(solution)/shard_map/all_to_all | solution.py:241
  80.6 1.6 copy-done.8
  82.2 1.6 copy-done.11
  83.8 2.3 %shard_map.71 = (bf16[8,64,512]{2,1,0:T(8,128)(2,1)S(1)}, bf16[8,64,512]{2,1,0:T(8,128)(2,1)S(1)}) custom-call(bf16[1024,1024]{1,0:T(8,128)(2,1)S(1)} %copy-done.11, bf16[1024,1024]{1,0:T(8,128)(2,1)S(1)} %copy-done.8, bf16[256,1152]{1,0:T(8,128)(2,1)S(1)} %shard_map.68.refs_0_, bf16[256,1152]{1,0:T(8,128)(2,1)S(1)} %collective-permute-done.1.refs_1_, ...), custom_call_target="tpu_custom_call" | custom-call | flops 2147483648 | bytes 4194304 | tf_op jit(solution)/shard_map/pallas_call | solution.py:284
  87.0 1.8 %all-to-all-done.2.parts = bf16[16,32,128]{2,1,0:T(8,128)(2,1)S(1)} async-done(((bf16[16,32,128]{2,1,0:T(8,128)(2,1)}), bf16[16,32,128]{2,1,0:T(8,128)(2,1)S(1)}, u32[]{:S(2)}, u32[]{:S(2)}) %all-to-all-start.2) | async-done | bytes 131104 | tf_op jit(solution)/shard_map/all_to_all | solution.py:241
  89.9 1.5 shard_map.72
  91.5 5.5 %all-to-all-start.3 = ((bf16[16,64,512]{2,1,0:T(8,128)(2,1)}), bf16[16,64,512]{2,1,0:T(8,128)(2,1)S(1)}, u32[]{:S(2)}, u32[]{:S(2)}) async-start(bf16[16,64,512]{2,1,0:T(8,128)(2,1)} %get-tuple-element.24.after), calls=%async_computation.4 | async-start | bytes 2097152 | tf_op jit(solution)/shard_map/all_to_all | solution.py:241
  97.0 3.4 %collective-permute-start.8 = (bf16[8,64,512]{2,1,0:T(8,128)(2,1)}, bf16[8,64,512]{2,1,0:T(8,128)(2,1)S(1)}, u32[]{:S(2)}, u32[]{:S(2)}) collective-permute-start(bf16[8,64,512]{2,1,0:T(8,128)(2,1)} %copy-done.13), channel_id=1, source_target_pairs={{0,4},{4,0},{1,5},{5,1},{2,6},{6,2},{3,7},{7,3},{8,12},{12,8},{9,1... | collective-permute-start | bytes 1572872 | tf_op jit(solution)/shard_map/ppermute | solution.py:288
  100.4 21.7 %collective-permute-done.8 = bf16[8,64,512]{2,1,0:T(8,128)(2,1)S(1)} collective-permute-done((bf16[8,64,512]{2,1,0:T(8,128)(2,1)}, bf16[8,64,512]{2,1,0:T(8,128)(2,1)S(1)}, u32[]{:S(2)}, u32[]{:S(2)}) %collective-permute-start.8) | collective-permute-done | bytes 524320 | tf_op jit(solution)/shard_map/ppermute | solution.py:288
  123.1 1.6 copy-done.9
  124.7 2.9 %shard_map.73 = (f32[256,576]{1,0:T(8,128)S(1)}, bf16[256,576]{1,0:T(8,128)(2,1)S(1)}, bf16[256,576]{1,0:T(8,128)(2,1)S(1)}, bf16[256,576]{1,0:T(8,128)(2,1)S(1)}) custom-call(bf16[1024,1024]{1,0:T(8,128)(2,1)S(1)} %copy-done.9, bf16[8,64,576]{2,1,0:T(8,128)(2,1)S(1)} %all-to-all-done.near, bf16[8,64,576]{2,1,0:T(8,128)(2,1)} %collective-permute-done.far, ...), custom_call_target="tpu_custom_call" | custom-call | flops 1207959552 | bytes 4194304 | tf_op jit(solution)/shard_map/pallas_call | solution.py:295
  127.6 2.5 %collective-permute-start.5 = (bf16[256,576]{1,0:T(8,128)(2,1)S(1)}, bf16[256,576]{1,0:T(8,128)(2,1)S(1)}, u32[]{:S(2)}, u32[]{:S(2)}) collective-permute-start(bf16[256,576]{1,0:T(8,128)(2,1)S(1)} %get-tuple-element.26), channel_id=1, source_target_pairs={{0,1},{1,2},{2,3},{3,0},{4,5},{5,6},{6,7},{7,4},{8,9},{9,10},{10,1... | collective-permute-start | bytes 884744 | tf_op jit(solution)/shard_map/ppermute | solution.py:237
  130.1 4.2 %collective-permute-start.6 = (bf16[256,576]{1,0:T(8,128)(2,1)S(1)}, bf16[256,576]{1,0:T(8,128)(2,1)S(1)}, u32[]{:S(2)}, u32[]{:S(2)}) collective-permute-start(bf16[256,576]{1,0:T(8,128)(2,1)S(1)} %get-tuple-element.27), channel_id=1, source_target_pairs={{0,2},{1,3},{2,0},{3,1},{4,6},{5,7},{6,4},{7,5},{8,10},{9,11},{10,... | collective-permute-start | bytes 884744 | tf_op jit(solution)/shard_map/ppermute | solution.py:237
  134.4 1.9 %collective-permute-start.7 = (bf16[256,576]{1,0:T(8,128)(2,1)S(1)}, bf16[256,576]{1,0:T(8,128)(2,1)}, u32[]{:S(2)}, u32[]{:S(2)}) collective-permute-start(bf16[256,576]{1,0:T(8,128)(2,1)S(1)} %get-tuple-element.28), channel_id=1, source_target_pairs={{0,3},{1,0},{2,1},{3,2},{4,7},{5,4},{6,5},{7,6},{8,11},{9,8},{10,9... | collective-permute-start | bytes 884744 | tf_op jit(solution)/shard_map/ppermute | solution.py:237
  137.3 10.7 %all-to-all-start.4 = ((f32[32,8,128]{2,1,0:T(8,128)}), f32[32,8,128]{2,1,0:T(8,128)S(1)}, u32[]{:S(2)}, u32[]{:S(2)}) async-start(f32[32,8,128]{2,1,0:T(8,128)} %shard_map.75), calls=%async_computation.5 | async-start | bytes 262144 | tf_op jit(solution)/shard_map/all_to_all | solution.py:241
  148.0 1.7 collective-permute-done.7
  149.7 1.8 %add_convert_fusion.1 = bf16[256,576]{1,0:T(8,128)(2,1)} fusion(bf16[256,576]{1,0:T(8,128)(2,1)} %collective-permute-done.7, bf16[256,576]{1,0:T(8,128)(2,1)S(1)} %collective-permute-done.6, f32[256,576]{1,0:T(8,128)S(1)} %get-tuple-element.25, bf16[256,576]{1,0:T(8,128)(2,1)S(1)} %collective-permute-done.5), kind=kLoop, calls=%fused_computation.1 | loop fusion | flops 1032192 | bytes 1769472 | tf_op jit(solution)/shard_map/convert_element_type | solution.py:310
  151.5 11.9 %reduce-scatter.2.cloned.1.call-done.parts = bf16[64,512]{1,0:T(8,128)(2,1)} async-done(((bf16[512,512]{1,0:T(8,128)(2,1)}), bf16[64,512]{1,0:T(8,128)(2,1)}) %reduce-scatter.2.cloned.1.call-update) | async-done | bytes 65552 | tf_op jit(solution)/shard_map/reduce_scatter | solution.py:301
  (43 shorter events, 14.5 us)
Async XLA Ops:
  9.0 30.6 %all-to-all-start = ((bf16[8,64,576]{2,1,0:T(8,128)(2,1)}), bf16[8,64,576]{2,1,0:T(8,128)(2,1)S(1)}, u32[]{:S(2)}, u32[]{:S(2)}) async-start(bf16[8,64,576]{2,1,0:T(8,128)(2,1)} %broadcast_in_dim.17), calls=%async_computation | async-start | bytes 1310720 | tf_op jit(solution)/shard_map/all_to_all | solution.py:241
  19.3 1.0 copy-start.2
  20.2 0.9 copy-start.5
  21.3 21.8 %collective-permute-start.3 = (bf16[256,1152]{1,0:T(8,128)(2,1)S(1)}, bf16[256,1152]{1,0:T(8,128)(2,1)S(1)}, u32[]{:S(2)}, u32[]{:S(2)}) collective-permute-start(bf16[256,1152]{1,0:T(8,128)(2,1)S(1)} %shard_map.68.refs_0_), channel_id=1, source_target_pairs={{0,1},{1,2},{2,3},{3,0},{4,5},{5,6},{6,7},{7,4},{8,9},{9,10},{10,1... | collective-permute-start | bytes 1769480 | tf_op jit(solution)/shard_map/ppermute | solution.py:237
  23.6 22.6 %collective-permute-start.1 = (bf16[256,1152]{1,0:T(8,128)(2,1)S(1)}, bf16[256,1152]{1,0:T(8,128)(2,1)S(1)}, u32[]{:S(2)}, u32[]{:S(2)}) collective-permute-start(bf16[256,1152]{1,0:T(8,128)(2,1)S(1)} %shard_map.68.refs_0_), channel_id=1, source_target_pairs={{0,3},{1,0},{2,1},{3,2},{4,7},{5,4},{6,5},{7,6},{8,11},{9,8},{10,9... | collective-permute-start | bytes 1769480 | tf_op jit(solution)/shard_map/ppermute | solution.py:237
  39.6 19.0 %collective-permute-start = (bf16[8,64,576]{2,1,0:T(8,128)(2,1)S(1)}, bf16[8,64,576]{2,1,0:T(8,128)(2,1)}, u32[]{:S(2)}, u32[]{:S(2)}) collective-permute-start(bf16[8,64,576]{2,1,0:T(8,128)(2,1)S(1)} %all-to-all-done.near), channel_id=1, source_target_pairs={{0,4},{4,0},{1,5},{5,1},{2,6},{6,2},{3,7},{7,3},{8,12},{12,8},{9,1... | collective-permute-start | bytes 1769480 | tf_op jit(solution)/shard_map/ppermute | solution.py:264
  43.8 10.7 %collective-permute-start.4 = (bf16[128,1152]{1,0:T(8,128)(2,1)}, bf16[128,1152]{1,0:T(8,128)(2,1)S(1)}, u32[]{:S(2)}, u32[]{:S(2)}) collective-permute-start(bf16[128,1152]{1,0:T(8,128)(2,1)} %slice.9), channel_id=1, source_target_pairs={{0,1},{1,2},{2,3},{3,0},{4,5},{5,6},{6,7},{7,4},{8,9},{9,10},{10,1... | collective-permute-start | bytes 884744 | tf_op jit(solution)/shard_map/ppermute | solution.py:237
  46.9 11.7 %collective-permute-start.2 = (bf16[128,1152]{1,0:T(8,128)(2,1)}, bf16[128,1152]{1,0:T(8,128)(2,1)S(1)}, u32[]{:S(2)}, u32[]{:S(2)}) collective-permute-start(bf16[128,1152]{1,0:T(8,128)(2,1)} %slice.8), channel_id=1, source_target_pairs={{0,3},{1,0},{2,1},{3,2},{4,7},{5,4},{6,5},{7,6},{8,11},{9,8},{10,9... | collective-permute-start | bytes 884744 | tf_op jit(solution)/shard_map/ppermute | solution.py:237
  50.4 1.2 copy-start.12
  52.9 10.3 %copy-start = (bf16[16,64,512]{2,1,0:T(8,128)(2,1)}, bf16[16,64,512]{2,1,0:T(8,128)(2,1)S(1)}, u32[]{:S(2)}) copy-start(bf16[16,64,512]{2,1,0:T(8,128)(2,1)S(1)} %shard_map.67.after.cols) | copy-start | bytes 3145732
  58.6 12.4 %copy-start.3 = (bf16[128,1152]{1,0:T(8,128)(2,1)}, bf16[128,1152]{1,0:T(8,128)(2,1)S(1)}, u32[]{:S(2)}) copy-start(bf16[128,1152]{1,0:T(8,128)(2,1)S(1)} %collective-permute-done.2.refs_2_) | copy-start | bytes 884740
  73.5 1.3 copy-start.7
  74.8 1.3 copy-start.10
  76.2 12.6 %all-to-all-start.2 = ((bf16[16,32,128]{2,1,0:T(8,128)(2,1)}), bf16[16,32,128]{2,1,0:T(8,128)(2,1)S(1)}, u32[]{:S(2)}, u32[]{:S(2)}) async-start(bf16[16,32,128]{2,1,0:T(8,128)(2,1)} %get-tuple-element.21), calls=%async_computation.2 | async-start | bytes 262144 | tf_op jit(solution)/shard_map/all_to_all | solution.py:241
  79.7 1.0 copy-start.4
  80.6 1.6 copy-start.8
  82.2 1.6 copy-start.11
  86.2 0.8 copy-start.13
  88.7 1.2 copy-start.1
  91.5 44.9 %all-to-all-start.3 = ((bf16[16,64,512]{2,1,0:T(8,128)(2,1)}), bf16[16,64,512]{2,1,0:T(8,128)(2,1)S(1)}, u32[]{:S(2)}, u32[]{:S(2)}) async-start(bf16[16,64,512]{2,1,0:T(8,128)(2,1)} %get-tuple-element.24.after), calls=%async_computation.4 | async-start | bytes 2097152 | tf_op jit(solution)/shard_map/all_to_all | solution.py:241
  97.0 66.4 %reduce-scatter.2.cloned.1.call-start = ((), (), s32[]{:S(2)}) async-start(), calls=%async_computation.6 | async-start | bytes 589824 | tf_op jit(solution)/shard_map/reduce_scatter | solution.py:301
  97.0 25.1 %collective-permute-start.8 = (bf16[8,64,512]{2,1,0:T(8,128)(2,1)}, bf16[8,64,512]{2,1,0:T(8,128)(2,1)S(1)}, u32[]{:S(2)}, u32[]{:S(2)}) collective-permute-start(bf16[8,64,512]{2,1,0:T(8,128)(2,1)} %copy-done.13), channel_id=1, source_target_pairs={{0,4},{4,0},{1,5},{5,1},{2,6},{6,2},{3,7},{7,3},{8,12},{12,8},{9,1... | collective-permute-start | bytes 1572872 | tf_op jit(solution)/shard_map/ppermute | solution.py:288
  123.1 1.6 copy-start.9
  127.6 20.3 %collective-permute-start.5 = (bf16[256,576]{1,0:T(8,128)(2,1)S(1)}, bf16[256,576]{1,0:T(8,128)(2,1)S(1)}, u32[]{:S(2)}, u32[]{:S(2)}) collective-permute-start(bf16[256,576]{1,0:T(8,128)(2,1)S(1)} %get-tuple-element.26), channel_id=1, source_target_pairs={{0,1},{1,2},{2,3},{3,0},{4,5},{5,6},{6,7},{7,4},{8,9},{9,10},{10,1... | collective-permute-start | bytes 884744 | tf_op jit(solution)/shard_map/ppermute | solution.py:237
  130.1 17.9 %collective-permute-start.6 = (bf16[256,576]{1,0:T(8,128)(2,1)S(1)}, bf16[256,576]{1,0:T(8,128)(2,1)S(1)}, u32[]{:S(2)}, u32[]{:S(2)}) collective-permute-start(bf16[256,576]{1,0:T(8,128)(2,1)S(1)} %get-tuple-element.27), channel_id=1, source_target_pairs={{0,2},{1,3},{2,0},{3,1},{4,6},{5,7},{6,4},{7,5},{8,10},{9,11},{10,... | collective-permute-start | bytes 884744 | tf_op jit(solution)/shard_map/ppermute | solution.py:237
  134.4 15.3 %collective-permute-start.7 = (bf16[256,576]{1,0:T(8,128)(2,1)S(1)}, bf16[256,576]{1,0:T(8,128)(2,1)}, u32[]{:S(2)}, u32[]{:S(2)}) collective-permute-start(bf16[256,576]{1,0:T(8,128)(2,1)S(1)} %get-tuple-element.28), channel_id=1, source_target_pairs={{0,3},{1,0},{2,1},{3,2},{4,7},{5,4},{6,5},{7,6},{8,11},{9,8},{10,9... | collective-permute-start | bytes 884744 | tf_op jit(solution)/shard_map/ppermute | solution.py:237
  137.3 27.7 %all-to-all-start.4 = ((f32[32,8,128]{2,1,0:T(8,128)}), f32[32,8,128]{2,1,0:T(8,128)S(1)}, u32[]{:S(2)}, u32[]{:S(2)}) async-start(f32[32,8,128]{2,1,0:T(8,128)} %shard_map.75), calls=%async_computation.5 | async-start | bytes 262144 | tf_op jit(solution)/shard_map/all_to_all | solution.py:241
  163.4 0.8 copy-start.6
Sparse Core Ops, SparseCore 0:
  123.2 40.1 reduce-scatter.1

commit v4 on v3

--- a/solution.py
+++ b/solution.py
@@ -25,7 +25,7 @@
     return lax.dot_general(a, b, (((0,), (0,)), ((), ())), preferred_element_type=f32)
 
 
-def call(kernel, outs, n_in, smem=(), unused=(), flops=0, moved=0, limit=48):
+def call(kernel, outs, n_in, smem=(), unused=(), scratch=(), flops=0, moved=0, limit=20):
     vmem = pl.BlockSpec(memory_space=pltpu.VMEM)
     specs = [
         pl.BlockSpec(memory_space=pltpu.SMEM)
@@ -38,6 +38,7 @@
         out_shape=[jax.ShapeDtypeStruct(s, d) for s, d in outs],
         in_specs=specs,
         out_specs=[vmem] * len(outs),
+        scratch_shapes=scratch,
         compiler_params=pltpu.CompilerParams(vmem_limit_bytes=limit * 2**20),
         cost_estimate=pl.CostEstimate(flops=flops, bytes_accessed=moved, transcendentals=0),
     )
@@ -49,16 +50,6 @@
     out[:, :lat] = dout[...]
     out[:, lat : lat + width] = query[...]
     out[:, lat + width :] = jnp.zeros((out.shape[0], out.shape[1] - lat - width), out.dtype)
-
-
-def row_blocks(refs):
-    own, right, first, second, left = refs
-    return [
-        lambda c: own[:, c],
-        lambda c: right[:, c],
-        lambda c: jnp.concatenate([first[:, c], second[:, c]]),
-        lambda c: left[:, c],
-    ]
 
 
 def columns_kernel(block, n_z, n_grp, n_core, hid, out):
@@ -87,7 +78,7 @@
 
 
 def scores_kernel(lat, heads, pos, near, far, after, *refs):
-    blocks, (e_ref, dp_ref, st_ref) = row_blocks(refs[:-3]), refs[-3:]
+    blocks, (e_ref, dp_ref, st_ref) = refs[:-3], refs[-3:]
     z, y, x = pos[0], pos[1], pos[2]
     n_z, k_dev, _ = near.shape
     n_x = len(blocks)
@@ -98,7 +89,7 @@
     tok = rows // heads
     first_query = n_z * 2 * n_x * (k_dev - tok)
     for b, t in enumerate(blocks):
-        q, o = t(slice(lat, lat + near.shape[2])), t(slice(0, lat))
+        q, o = t[:, lat : lat + near.shape[2]], t[:, :lat]
         cols = slice(b * rows, (b + 1) * rows)
         lane = lax.broadcasted_iota(jnp.int32, (k_dev, rows), 1)
         q_pos = ((z * 2 + y) * n_x + lax.rem(x + b, n_x)) * tok + lane // heads + first_query
@@ -130,7 +121,7 @@
 
 
 def dscores_kernel(lat, pos, stats, st, e_ref, dp_ref, *refs):
-    blocks, (p_ref, ds_ref, rope_ref) = row_blocks(refs[:-3]), refs[-3:]
+    blocks, (ds_ref, rope_ref, mine, other, p_ref) = refs[:-5], refs[-5:]
     y, x = pos[1], pos[2]
     n_x = len(blocks)
     rows = refs[0].shape[0]
@@ -161,7 +152,7 @@
         part = slice(i * TILE, (i + 1) * TILE)
         r = None
         for b, t in enumerate(blocks):
-            q = t(slice(2 * lat, 2 * lat + rope_ref.shape[2] // 2))
+            q = t[:, 2 * lat : 2 * lat + rope_ref.shape[2] // 2]
             v = nn(ds_ref[part, b * rows : (b + 1) * rows], q)
             r = v if r is None else r + v
         r = (r * softmax_scale).astype(bf16)
@@ -170,23 +161,17 @@
             side = y if half == 0 else 1 - y
             k = r[j * k_dev : (j + 1) * k_dev]
             rope_ref[2 * zz + side] = jnp.concatenate([k[:half_keys], k[half_keys:]], axis=1)
-
-
-def latent_kernel(lat, p_ref, ds_ref, *refs):
-    blocks, outs = row_blocks(refs[:5]), refs[5:]
-    n_z, k_dev, _ = outs[0].shape
-    rows = refs[0].shape[0]
     per = TILE // k_dev
-    for i in range(p_ref.shape[0] // TILE):
+    for i in range(tiles):
         part = slice(i * TILE, (i + 1) * TILE)
         v = None
         for b, t in enumerate(blocks):
-            a = nn(ds_ref[part, b * rows : (b + 1) * rows], t(slice(lat, 2 * lat)))
+            a = nn(ds_ref[part, b * rows : (b + 1) * rows], t[:, lat : 2 * lat])
             v = a if v is None else v + a
         v = v * softmax_scale
         for b, t in enumerate(blocks):
-            v += nn(p_ref[part, b * rows : (b + 1) * rows], t(slice(0, lat)))
-        out, first = outs[i * per // n_z], i * per % n_z
+            v += nn(p_ref[part, b * rows : (b + 1) * rows], t[:, :lat])
+        out, first = (mine, other)[i * per // n_z], i * per % n_z
         out[first : first + per] = v.astype(bf16).reshape(per, k_dev, lat)
 
 
@@ -214,7 +199,7 @@
         out[i] = tn(low, cols[i]).astype(bf16)
 
 
-def weight_half_kernel(parts, out):
+def weight_half_kernel(parts, after, after2, out):
     v = jnp.sum(parts[...].astype(f32), axis=0)
     v = jnp.swapaxes(v, 0, 1)
     v = v.reshape(v.shape[0] // SLOT, SLOT, v.shape[1])
@@ -227,9 +212,18 @@
     out[...] = jnp.concatenate([v[:, :e], v[:, e:]])[: out.shape[0]]
 
 
-def latent_sum_kernel(parts, rope, out):
-    lat = parts.shape[1]
-    out[:, :lat] = parts[...].astype(f32)
+def halve_kernel(bit, pos, a, b, after, *refs):
+    keep, send = refs[-2:]
+    mine = (pos[0] >> bit) & 1
+    for i in range(keep.shape[0]):
+        at, away = 2 * i + mine, 2 * i + 1 - mine
+        keep[i] = a[at].astype(f32) + b[at].astype(f32)
+        send[i] = (a[away].astype(f32) + b[away].astype(f32)).astype(send.dtype)
+
+
+def latent_sum_kernel(a, b, rope, out):
+    lat = a.shape[2]
+    out[:, :lat] = a[0] + b[0].astype(f32)
     out[:, lat:] = rope[...]
 
 
@@ -258,9 +252,7 @@
     (own,) = call(pack_kernel, [((rows, -(-(lat + width) // 128) * 128), bf16)], 2, moved=4 * rows * width)(
         dout.reshape(rows, lat), query.reshape(rows, width)
     )
-    right, left = fetch(own, 1, nx), fetch(own, nx - 1, nx)
-    first, second = fetch(right[: rows // 2], 1, nx), fetch(left[rows // 2 :], nx - 1, nx)
-    blocks = [own, right, first, second, left]
+    blocks = [own] + [fetch(own, k, nx) for k in range(1, nx)]
     far = lax.ppermute(near, "y", swap)
 
     wide = nw * nz * SLOT
@@ -270,39 +262,47 @@
     )(hidden[0])
     e, dp, st = call(
         functools.partial(scores_kernel, lat, heads),
-        [((n_keys, n_rows), f32)] * 2 + [((4 * nx, rows), f32)], 9, smem=(0,),
+        [((n_keys, n_rows), f32)] * 2 + [((4 * nx, rows), f32)], 8, smem=(0,),
         unused=(3,),
         flops=2 * pairs * (width + lat), moved=8 * pairs, limit=20,
     )(pos, near, far, cols, *blocks)
     stats = trade(jnp.broadcast_to(st[None], (nx,) + st.shape), "x")
-    p, ds, rope_part = call(
+    ds, rope_part, mine, other = call(
         functools.partial(dscores_kernel, lat),
-        [((n_keys, n_rows), bf16)] * 2 + [((nz * ny, k_dev // 2, 2 * rope), bf16)], 10, smem=(0,),
-        flops=2 * pairs * rope, moved=12 * pairs, limit=20,
+        [((n_keys, n_rows), bf16), ((nz * ny, k_dev // 2, 2 * rope), bf16)] + [((nz, k_dev, lat), bf16)] * 2,
+        9, smem=(0,), scratch=[pltpu.VMEM((n_keys, n_rows), bf16)],
+        flops=2 * pairs * (rope + 2 * lat), moved=12 * pairs,
     )(pos, stats, st, e, dp, *blocks)
     rope_part = trade(rope_part, ("z", "y"))
-    mine, other = call(
-        functools.partial(latent_kernel, lat), [((nz, k_dev, lat), bf16)] * 2, 7,
-        flops=4 * pairs * lat, moved=4 * pairs, limit=20,
-    )(p, ds, *blocks)
     other = lax.ppermute(other, "y", swap)
     rope_sum, terms = call(
         weight_kernel, [((k_dev, rope), f32), ((nc * ny * nx, rope, wide), bf16)], 3, unused=(2,),
         flops=2 * k_dev * nc * ny * nx * wide * rope, moved=4 * k_dev * model, limit=20,
-    )(rope_part, cols, mine)
+    )(rope_part, cols, other)
     after = terms
     terms = trade(terms, ("c", "y", "x"))
     dq = call(
         query_kernel, [((rows, width), f32)] + [((rows, width), bf16)] * (nx - 1), 4, unused=(3,),
         flops=2 * pairs * width, moved=4 * pairs, limit=20,
     )(ds, near, far, after)
+    query_part = dq[1]
     dq = [dq[0]] + [fetch(dq[k], nx - k, nx) for k in range(1, nx)]
-    half = (mine.astype(f32) + other.astype(f32)).astype(bf16)
-    half = lax.psum_scatter(half.reshape(nz * k_dev, lat), "z", scatter_dimension=0, tiled=True)
-    (terms,) = call(weight_half_kernel, [((nw * nz, SLOT // 2, 2 * rope), f32)], 1, limit=20)(terms)
-    terms = trade(terms, ("w", "z"))
-    (dweight,) = call(weight_sum_kernel, [((block, rope), f32)], 1, limit=20)(terms)
-    (dlatent,) = call(latent_sum_kernel, [((k_dev, width), f32)], 2, limit=20)(half, rope_sum)
+    kept, came = mine, other
+    for bit in range(3):
+        if bit == 2:
+            (terms,) = call(
+                weight_half_kernel, [((nw * nz, SLOT // 2, 2 * rope), f32)], 3, unused=(1, 2)
+            )(terms, kept, query_part)
+            after = terms
+            terms = trade(terms, ("w", "z"))
+        n = nz >> (bit + 1)
+        kept, sent = call(
+            functools.partial(halve_kernel, bit), [((n, k_dev, lat), f32), ((n, k_dev, lat), bf16)], 4,
+            smem=(0,), unused=(3,), flops=8 * n * k_dev * lat, moved=12 * n * k_dev * lat, limit=20,
+        )(pos, kept, came, after)
+        came = lax.ppermute(sent, "z", [(i, i ^ (1 << bit)) for i in range(nz)])
+    (dweight,) = call(weight_sum_kernel, [((block, rope), f32)], 1)(terms)
+    (dlatent,) = call(latent_sum_kernel, [((k_dev, width), f32)], 3)(kept, came, rope_sum)
 
     total = dq[0]
     for part in dq[1:]:

time: 174 us -> 143 us (0.82)
  waiting for transfers between devices: 55.2 us -> 24.2 us
  between operations: 14.3 us -> 0.88 us
  blocking collectives: 7.86 us -> 21.2 us
  local copies, waits for them, and re-layouts: 17.6 us -> 8.85 us
  starting transfers between devices: 57.3 us -> 64.9 us
    ppermute x1, waiting for transfers between devices: 21.7 us -> 0.01 us  [body(): other = lax.ppermute(other, 'y', swap)]
    all_to_all x1 -> x2, blocking collectives: 7.86 us -> 21.2 us  [trade(): return lax.all_to_all(value, axes, 0, 0, tiled=True)]
    ppermute x0 -> x3, starting transfers between devices: none -> 13.3 us  [body(): came = lax.ppermute(sent, 'z', [(i, i ^ 1 << bit) for i in range(nz)])]
    reduce_scatter x1 -> x0, waiting for transfers between devices: 11.9 us -> none  [body(): lax.psum_scatter(half.reshape(nz * k_dev, lat), 'z', scatter_dimension=0,...]
    unnamed x28 -> x14, local copies, waits for them, and re-layouts: 14.3 us -> 7.06 us
    all_to_all x4 -> x3, waiting for transfers between devices: 14.2 us -> 9.67 us  [trade(): return lax.all_to_all(value, axes, 0, 0, tiled=True)]
    all_to_all x4 -> x3, starting transfers between devices: 30 us -> 25.7 us  [trade(): return lax.all_to_all(value, axes, 0, 0, tiled=True)]
    ppermute x1, waiting for transfers between devices: 0.01 us -> 4.03 us  [body(): far = lax.ppermute(near, 'y', swap)]
  transfers between devices with their start and end apart: 14 -> 14, of which waited for: 7 -> 4; matrix products, arithmetic and copies ran while one was open for 3% -> 1% of each run, Pallas kernels for 5% -> 6%
where the time goes in v4:
time: 143 us; the launch traced here: 141 us
  starting transfers between devices  64.9 us (45%)
  waiting for transfers between devices  24.2 us (17%)
  blocking collectives  21.2 us (15%)
  Pallas kernels  19 us (13%)
  local copies, waits for them, and re-layouts  8.85 us (6%)
  other arithmetic  1.92 us (1%)
    all_to_all x3, starting transfers between devices, trade(): return lax.all_to_all(value, axes, 0, 0, tiled=True)  25.7 us
    all_to_all x2, blocking collectives, trade(): return lax.all_to_all(value, axes, 0, 0, tiled=True)  21.2 us
    ppermute x6, starting transfers between devices, fetch(): return lax.ppermute(value, 'x', [(s, (s - offset) % n) for s in range(n)])  19 us
    ppermute x3, starting transfers between devices, body(): came = lax.ppermute(sent, 'z', [(i, i ^ 1 << bit) for i in range(nz)])  13.3 us
    all_to_all x3, waiting for transfers between devices, trade(): return lax.all_to_all(value, axes, 0, 0, tiled=True)  9.67 us
    ppermute x6, waiting for transfers between devices, fetch(): return lax.ppermute(value, 'x', [(s, (s - offset) % n) for s in range(n)])  8.6 us
    unnamed x14, local copies, waits for them, and re-layouts  7.06 us
    pallas_call x1, Pallas kernels, body(): call(functools.partial(scores_kernel, lat, heads), [((n_keys, n_rows), f3...  4.44 us
  transfers between devices with their start and end apart: 14, of which 4 were waited for; matrix products, arithmetic and copies ran while one was open for 1% of the time, Pallas kernels for 6%

profile of v4, /device:TPU:6, one launch (start us, length us, event | category | flops | bytes accessed | tf_op | source)
XLA Modules:
  0.0 140.9 jit_solution(1184312332554754517)
XLA Ops:
  0.6 1.8 %broadcast_in_dim.17 = bf16[8,64,576]{2,1,0:T(8,128)(2,1)} broadcast(bf16[64,576]{1,0:T(8,128)(2,1)} %bitcast.14), dimensions={1,2} | broadcast | bytes 663552 | tf_op jit(solution)/shard_map/broadcast_in_dim | solution.py:251
  2.4 10.3 %all-to-all-start = ((bf16[8,64,576]{2,1,0:T(8,128)(2,1)}), bf16[8,64,576]{2,1,0:T(8,128)(2,1)S(1)}, u32[]{:S(2)}, u32[]{:S(2)}) async-start(bf16[8,64,576]{2,1,0:T(8,128)(2,1)} %broadcast_in_dim.17), calls=%async_computation | async-start | bytes 1310720 | tf_op jit(solution)/shard_map/all_to_all | solution.py:235
  12.7 1.0 copy-done.2
  14.7 2.4 %collective-permute-start.3 = (bf16[256,1152]{1,0:T(8,128)(2,1)S(1)}, bf16[256,1152]{1,0:T(8,128)(2,1)S(1)}, u32[]{:S(2)}, u32[]{:S(2)}) collective-permute-start(bf16[256,1152]{1,0:T(8,128)(2,1)S(1)} %shard_map.68.refs_0_), channel_id=1, source_target_pairs={{0,1},{1,2},{2,3},{3,0},{4,5},{5,6},{6,7},{7,4},{8,9},{9,10},{10,1... | collective-permute-start | bytes 1769480 | tf_op jit(solution)/shard_map/ppermute | solution.py:231
  17.1 4.3 %collective-permute-start.2 = (bf16[256,1152]{1,0:T(8,128)(2,1)S(1)}, bf16[256,1152]{1,0:T(8,128)(2,1)S(1)}, u32[]{:S(2)}, u32[]{:S(2)}) collective-permute-start(bf16[256,1152]{1,0:T(8,128)(2,1)S(1)} %shard_map.68.refs_0_), channel_id=1, source_target_pairs={{0,2},{1,3},{2,0},{3,1},{4,6},{5,7},{6,4},{7,5},{8,10},{9,11},{10,... | collective-permute-start | bytes 1769480 | tf_op jit(solution)/shard_map/ppermute | solution.py:231
  21.4 1.9 %collective-permute-start.1 = (bf16[256,1152]{1,0:T(8,128)(2,1)S(1)}, bf16[256,1152]{1,0:T(8,128)(2,1)S(1)}, u32[]{:S(2)}, u32[]{:S(2)}) collective-permute-start(bf16[256,1152]{1,0:T(8,128)(2,1)S(1)} %shard_map.68.refs_0_), channel_id=1, source_target_pairs={{0,3},{1,0},{2,1},{3,2},{4,7},{5,4},{6,5},{7,6},{8,11},{9,8},{10,9... | collective-permute-start | bytes 1769480 | tf_op jit(solution)/shard_map/ppermute | solution.py:231
  23.4 9.7 %all-to-all-done.near = bf16[8,64,576]{2,1,0:T(8,128)(2,1)S(1)} async-done(((bf16[8,64,576]{2,1,0:T(8,128)(2,1)}), bf16[8,64,576]{2,1,0:T(8,128)(2,1)S(1)}, u32[]{:S(2)}, u32[]{:S(2)}) %all-to-all-start) | async-done | bytes 589856 | tf_op jit(solution)/shard_map/all_to_all | solution.py:235
  33.0 3.5 %collective-permute-start = (bf16[8,64,576]{2,1,0:T(8,128)(2,1)S(1)}, bf16[8,64,576]{2,1,0:T(8,128)(2,1)}, u32[]{:S(2)}, u32[]{:S(2)}) collective-permute-start(bf16[8,64,576]{2,1,0:T(8,128)(2,1)S(1)} %all-to-all-done.near), channel_id=1, source_target_pairs={{0,4},{4,0},{1,5},{5,1},{2,6},{6,2},{3,7},{7,3},{8,12},{12,8},{9,1... | collective-permute-start | bytes 1769480 | tf_op jit(solution)/shard_map/ppermute | solution.py:256
  36.5 1.2 copy-done.6
  37.7 1.3 shard_map.67.after.cols
  39.1 8.6 %collective-permute-done.1.refs_1_ = bf16[256,1152]{1,0:T(8,128)(2,1)S(1)} collective-permute-done((bf16[256,1152]{1,0:T(8,128)(2,1)S(1)}, bf16[256,1152]{1,0:T(8,128)(2,1)S(1)}, u32[]{:S(2)}, u32[]{:S(2)}) %collective-permute-start.1) | collective-permute-done | bytes 589856 | tf_op jit(solution)/shard_map/ppermute | solution.py:231
  47.7 4.0 %collective-permute-done.far = bf16[8,64,576]{2,1,0:T(8,128)(2,1)} collective-permute-done((bf16[8,64,576]{2,1,0:T(8,128)(2,1)S(1)}, bf16[8,64,576]{2,1,0:T(8,128)(2,1)}, u32[]{:S(2)}, u32[]{:S(2)}) %collective-permute-start) | collective-permute-done | bytes 589856 | tf_op jit(solution)/shard_map/ppermute | solution.py:256
  51.7 4.4 %shard_map.69 = (f32[1024,1024]{1,0:T(8,128)S(1)}, f32[1024,1024]{1,0:T(8,128)S(1)}, f32[16,256]{1,0:T(8,128)S(1)}) custom-call(s32[3]{0:T(128)S(1)} %pad_add_fusion.pos, bf16[8,64,576]{2,1,0:T(8,128)(2,1)S(1)} %all-to-all-done.near, bf16[8,64,576]{2,1,0:T(8,128)(2,1)} %collective-permute-done.far, bf16[16,64,512]{2,1,0:T(8,128)(2,1)S(1)} %shard_map.67.after.cols, ...), custom_call_target="tpu_custom_call" | custom-call | flops 2281701376 | bytes 8388608 | tf_op jit(solution)/shard_map/pallas_call | solution.py:263
  56.1 8.1 %all_to_all.25.stats = f32[4,16,256]{2,1,0:T(8,128)S(1)} all-to-all(f32[4,16,256]{2,1,0:T(8,128)S(1)} %broadcast_in_dim.18), channel_id=1, replica_groups=mesh['w'=4,'c'=2,'z'=8,'y'=2,'x'=4] {'x'}, dimensions={0} | all-to-all | bytes 131072 | tf_op jit(solution)/shard_map/all_to_all | solution.py:235
  64.3 3.9 %shard_map.70 = (bf16[1024,1024]{1,0:T(8,128)(2,1)S(1)}, bf16[16,32,128]{2,1,0:T(8,128)(2,1)S(1)}, bf16[8,64,512]{2,1,0:T(8,128)(2,1)S(1)}, bf16[8,64,512]{2,1,0:T(8,128)(2,1)S(1)}) custom-call(s32[3]{0:T(128)S(1)} %pad_add_fusion.pos, f32[4,16,256]{2,1,0:T(8,128)S(1)} %all_to_all.25.stats, f32[16,256]{1,0:T(8,128)S(1)} %get-tuple-element.22.st, ...), custom_call_target="tpu_custom_call" | custom-call | flops 2281701376 | bytes 12582912 | tf_op jit(solution)/shard_map/pallas_call | solution.py:270
  68.2 1.3 copy-done.4
  69.5 3.5 %collective-permute-start.4 = (bf16[8,64,512]{2,1,0:T(8,128)(2,1)S(1)}, bf16[8,64,512]{2,1,0:T(8,128)(2,1)S(1)}, u32[]{:S(2)}, u32[]{:S(2)}) collective-permute-start(bf16[8,64,512]{2,1,0:T(8,128)(2,1)S(1)} %get-tuple-element.27), channel_id=1, source_target_pairs={{0,4},{4,0},{1,5},{5,1},{2,6},{6,2},{3,7},{7,3},{8,12},{12,8},{9,1... | collective-permute-start | bytes 1572872 | tf_op jit(solution)/shard_map/ppermute | solution.py:277
  73.0 13.0 %all_to_all.26.parts = bf16[16,32,128]{2,1,0:T(8,128)(2,1)S(1)} all-to-all(bf16[16,32,128]{2,1,0:T(8,128)(2,1)S(1)} %get-tuple-element.26), channel_id=1, replica_groups=mesh['w'=4,'c'=2,'z'=8,'y'=2,'x'=4] {'z','y'}, dimensions={0} | all-to-all | bytes 262144 | tf_op jit(solution)/shard_map/all_to_all | solution.py:235
  86.0 1.5 %shard_map.71 = (f32[64,64]{1,0:T(8,128)S(1)}, bf16[16,64,512]{2,1,0:T(8,128)(2,1)}) custom-call(bf16[16,32,128]{2,1,0:T(8,128)(2,1)S(1)} %all_to_all.26.parts, bf16[16,64,512]{2,1,0:T(8,128)(2,1)S(1)} %shard_map.67.after.cols, bf16[8,64,512]{2,1,0:T(8,128)(2,1)S(1)} %collective-permute-done.4.after.b), custom_call_target="tpu_custom_call" | custom-call | flops 67108864 | bytes 1835008 | tf_op jit(solution)/shard_map/pallas_call | solution.py:278
  87.5 5.6 %all-to-all-start.3 = ((bf16[16,64,512]{2,1,0:T(8,128)(2,1)}), bf16[16,64,512]{2,1,0:T(8,128)(2,1)S(1)}, u32[]{:S(2)}, u32[]{:S(2)}) async-start(bf16[16,64,512]{2,1,0:T(8,128)(2,1)} %get-tuple-element.28.after), calls=%async_computation.3 | async-start | bytes 2097152 | tf_op jit(solution)/shard_map/all_to_all | solution.py:235
  93.2 1.0 copy-done.1
  94.9 2.4 %collective-permute-start.8 = (bf16[4,64,512]{2,1,0:T(8,128)(2,1)S(1)}, bf16[4,64,512]{2,1,0:T(8,128)(2,1)S(1)}, u32[]{:S(2)}, u32[]{:S(2)}) collective-permute-start(bf16[4,64,512]{2,1,0:T(8,128)(2,1)S(1)} %get-tuple-element.35), channel_id=1, source_target_pairs={{0,8},{8,0},{16,24},{24,16},{32,40},{40,32},{48,56},{56,48},{1,9},... | collective-permute-start | bytes 786440 | tf_op jit(solution)/shard_map/ppermute | solution.py:303
  97.3 1.6 %copy-done.5 = bf16[1024,1024]{1,0:T(8,128)(2,1)S(1)} copy-done((bf16[1024,1024]{1,0:T(8,128)(2,1)S(1)}, bf16[1024,1024]{1,0:T(8,128)(2,1)}, u32[]{:S(2)}) %copy-start.5) | copy-done | bytes 2097176
  98.9 3.6 %shard_map.72 = (f32[256,576]{1,0:T(8,128)S(1)}, bf16[256,576]{1,0:T(8,128)(2,1)S(1)}, bf16[256,576]{1,0:T(8,128)(2,1)}, bf16[256,576]{1,0:T(8,128)(2,1)}) custom-call(bf16[1024,1024]{1,0:T(8,128)(2,1)S(1)} %copy-done.5, bf16[8,64,576]{2,1,0:T(8,128)(2,1)S(1)} %all-to-all-done.near, bf16[8,64,576]{2,1,0:T(8,128)(2,1)} %collective-permute-done.far, ...), custom_call_target="tpu_custom_call" | custom-call | flops 1207959552 | bytes 4194304 | tf_op jit(solution)/shard_map/pallas_call | solution.py:284
  102.6 3.4 %collective-permute-start.6 = (bf16[256,576]{1,0:T(8,128)(2,1)}, bf16[256,576]{1,0:T(8,128)(2,1)S(1)}, u32[]{:S(2)}, u32[]{:S(2)}) collective-permute-start(bf16[256,576]{1,0:T(8,128)(2,1)} %get-tuple-element.31), channel_id=1, source_target_pairs={{0,2},{1,3},{2,0},{3,1},{4,6},{5,7},{6,4},{7,5},{8,10},{9,11},{10,... | collective-permute-start | bytes 884744 | tf_op jit(solution)/shard_map/ppermute | solution.py:231
  105.9 1.9 %collective-permute-start.7 = (bf16[256,576]{1,0:T(8,128)(2,1)}, bf16[256,576]{1,0:T(8,128)(2,1)S(1)}, u32[]{:S(2)}, u32[]{:S(2)}) collective-permute-start(bf16[256,576]{1,0:T(8,128)(2,1)} %get-tuple-element.32), channel_id=1, source_target_pairs={{0,3},{1,0},{2,1},{3,2},{4,7},{5,4},{6,5},{7,6},{8,11},{9,8},{10,9... | collective-permute-start | bytes 884744 | tf_op jit(solution)/shard_map/ppermute | solution.py:231
  107.8 5.1 %collective-permute-start.5 = (bf16[256,576]{1,0:T(8,128)(2,1)S(1)}, bf16[256,576]{1,0:T(8,128)(2,1)}, u32[]{:S(2)}, u32[]{:S(2)}) collective-permute-start(bf16[256,576]{1,0:T(8,128)(2,1)S(1)} %get-tuple-element.30.after2), channel_id=1, source_target_pairs={{0,1},{1,2},{2,3},{3,0},{4,5},{5,6},{6,7},{7,4},{8,9},{9,10},{10,1... | collective-permute-start | bytes 884744 | tf_op jit(solution)/shard_map/ppermute | solution.py:231
  113.6 3.2 %collective-permute-start.9 = (bf16[2,64,512]{2,1,0:T(8,128)(2,1)S(1)}, bf16[2,64,512]{2,1,0:T(8,128)(2,1)S(1)}, u32[]{:S(2)}, u32[]{:S(2)}) collective-permute-start(bf16[2,64,512]{2,1,0:T(8,128)(2,1)S(1)} %get-tuple-element.37), channel_id=1, source_target_pairs={{0,16},{8,24},{16,0},{24,8},{32,48},{40,56},{48,32},{56,40},{1,17}... | collective-permute-start | bytes 393224 | tf_op jit(solution)/shard_map/ppermute | solution.py:303
  117.8 9.7 %all-to-all-start.4 = ((f32[32,8,128]{2,1,0:T(8,128)}), f32[32,8,128]{2,1,0:T(8,128)S(1)}, u32[]{:S(2)}, u32[]{:S(2)}) async-start(f32[32,8,128]{2,1,0:T(8,128)} %shard_map.75.after), calls=%async_computation.4 | async-start | bytes 262144 | tf_op jit(solution)/shard_map/all_to_all | solution.py:235
  128.1 7.6 %collective-permute-start.10 = (bf16[1,64,512]{2,1,0:T(8,128)(2,1)S(1)}, bf16[1,64,512]{2,1,0:T(8,128)(2,1)S(1)}, u32[]{:S(2)}, u32[]{:S(2)}) collective-permute-start(bf16[1,64,512]{2,1,0:T(8,128)(2,1)S(1)} %get-tuple-element.39), channel_id=1, source_target_pairs={{0,32},{8,40},{16,48},{24,56},{32,0},{40,8},{48,16},{56,24},{1,33}... | collective-permute-start | bytes 196616 | tf_op jit(solution)/shard_map/ppermute | solution.py:303
  135.8 1.8 %add_convert_fusion = bf16[256,576]{1,0:T(8,128)(2,1)} fusion(bf16[256,576]{1,0:T(8,128)(2,1)S(1)} %collective-permute-done.7, bf16[256,576]{1,0:T(8,128)(2,1)S(1)} %collective-permute-done.6, f32[256,576]{1,0:T(8,128)S(1)} %get-tuple-element.29, bf16[256,576]{1,0:T(8,128)(2,1)} %collective-permute-done.5), kind=kLoop, calls=%fused_computation | loop fusion | flops 1032192 | bytes 1769472 | tf_op jit(solution)/shard_map/convert_element_type | solution.py:310
  137.6 1.9 %collective-permute-done.10.b = bf16[1,64,512]{2,1,0:T(8,128)(2,1)S(1)} collective-permute-done((bf16[1,64,512]{2,1,0:T(8,128)(2,1)S(1)}, bf16[1,64,512]{2,1,0:T(8,128)(2,1)S(1)}, u32[]{:S(2)}, u32[]{:S(2)}) %collective-permute-start.10) | collective-permute-done | bytes 65568 | tf_op jit(solution)/shard_map/ppermute | solution.py:303
  (28 shorter events, 5.3 us)
Async XLA Ops:
  2.4 30.6 %all-to-all-start = ((bf16[8,64,576]{2,1,0:T(8,128)(2,1)}), bf16[8,64,576]{2,1,0:T(8,128)(2,1)S(1)}, u32[]{:S(2)}, u32[]{:S(2)}) async-start(bf16[8,64,576]{2,1,0:T(8,128)(2,1)} %broadcast_in_dim.17), calls=%async_computation | async-start | bytes 1310720 | tf_op jit(solution)/shard_map/all_to_all | solution.py:235
  12.7 1.0 copy-start.2
  13.7 0.9 copy-start.3
  14.7 24.4 %collective-permute-start.3 = (bf16[256,1152]{1,0:T(8,128)(2,1)S(1)}, bf16[256,1152]{1,0:T(8,128)(2,1)S(1)}, u32[]{:S(2)}, u32[]{:S(2)}) collective-permute-start(bf16[256,1152]{1,0:T(8,128)(2,1)S(1)} %shard_map.68.refs_0_), channel_id=1, source_target_pairs={{0,1},{1,2},{2,3},{3,0},{4,5},{5,6},{6,7},{7,4},{8,9},{9,10},{10,1... | collective-permute-start | bytes 1769480 | tf_op jit(solution)/shard_map/ppermute | solution.py:231
  17.1 22.0 %collective-permute-start.2 = (bf16[256,1152]{1,0:T(8,128)(2,1)S(1)}, bf16[256,1152]{1,0:T(8,128)(2,1)S(1)}, u32[]{:S(2)}, u32[]{:S(2)}) collective-permute-start(bf16[256,1152]{1,0:T(8,128)(2,1)S(1)} %shard_map.68.refs_0_), channel_id=1, source_target_pairs={{0,2},{1,3},{2,0},{3,1},{4,6},{5,7},{6,4},{7,5},{8,10},{9,11},{10,... | collective-permute-start | bytes 1769480 | tf_op jit(solution)/shard_map/ppermute | solution.py:231
  21.4 26.2 %collective-permute-start.1 = (bf16[256,1152]{1,0:T(8,128)(2,1)S(1)}, bf16[256,1152]{1,0:T(8,128)(2,1)S(1)}, u32[]{:S(2)}, u32[]{:S(2)}) collective-permute-start(bf16[256,1152]{1,0:T(8,128)(2,1)S(1)} %shard_map.68.refs_0_), channel_id=1, source_target_pairs={{0,3},{1,0},{2,1},{3,2},{4,7},{5,4},{6,5},{7,6},{8,11},{9,8},{10,9... | collective-permute-start | bytes 1769480 | tf_op jit(solution)/shard_map/ppermute | solution.py:231
  33.0 18.6 %collective-permute-start = (bf16[8,64,576]{2,1,0:T(8,128)(2,1)S(1)}, bf16[8,64,576]{2,1,0:T(8,128)(2,1)}, u32[]{:S(2)}, u32[]{:S(2)}) collective-permute-start(bf16[8,64,576]{2,1,0:T(8,128)(2,1)S(1)} %all-to-all-done.near), channel_id=1, source_target_pairs={{0,4},{4,0},{1,5},{5,1},{2,6},{6,2},{3,7},{7,3},{8,12},{12,8},{9,1... | collective-permute-start | bytes 1769480 | tf_op jit(solution)/shard_map/ppermute | solution.py:256
  36.5 1.2 copy-start.6
  68.1 1.4 copy-start.4
  69.5 18.0 %copy-start = (bf16[8,64,512]{2,1,0:T(8,128)(2,1)}, bf16[8,64,512]{2,1,0:T(8,128)(2,1)S(1)}, u32[]{:S(2)}) copy-start(bf16[8,64,512]{2,1,0:T(8,128)(2,1)S(1)} %get-tuple-element.33.a) | copy-start | bytes 1572868
  69.5 16.5 %collective-permute-start.4 = (bf16[8,64,512]{2,1,0:T(8,128)(2,1)S(1)}, bf16[8,64,512]{2,1,0:T(8,128)(2,1)S(1)}, u32[]{:S(2)}, u32[]{:S(2)}) collective-permute-start(bf16[8,64,512]{2,1,0:T(8,128)(2,1)S(1)} %get-tuple-element.27), channel_id=1, source_target_pairs={{0,4},{4,0},{1,5},{5,1},{2,6},{6,2},{3,7},{7,3},{8,12},{12,8},{9,1... | collective-permute-start | bytes 1572872 | tf_op jit(solution)/shard_map/ppermute | solution.py:277
  87.5 29.3 %all-to-all-start.3 = ((bf16[16,64,512]{2,1,0:T(8,128)(2,1)}), bf16[16,64,512]{2,1,0:T(8,128)(2,1)S(1)}, u32[]{:S(2)}, u32[]{:S(2)}) async-start(bf16[16,64,512]{2,1,0:T(8,128)(2,1)} %get-tuple-element.28.after), calls=%async_computation.3 | async-start | bytes 2097152 | tf_op jit(solution)/shard_map/all_to_all | solution.py:235
  93.2 1.0 copy-start.1
  94.9 18.1 %collective-permute-start.8 = (bf16[4,64,512]{2,1,0:T(8,128)(2,1)S(1)}, bf16[4,64,512]{2,1,0:T(8,128)(2,1)S(1)}, u32[]{:S(2)}, u32[]{:S(2)}) collective-permute-start(bf16[4,64,512]{2,1,0:T(8,128)(2,1)S(1)} %get-tuple-element.35), channel_id=1, source_target_pairs={{0,8},{8,0},{16,24},{24,16},{32,40},{40,32},{48,56},{56,48},{1,9},... | collective-permute-start | bytes 786440 | tf_op jit(solution)/shard_map/ppermute | solution.py:303
  97.3 1.6 %copy-start.5 = (bf16[1024,1024]{1,0:T(8,128)(2,1)S(1)}, bf16[1024,1024]{1,0:T(8,128)(2,1)}, u32[]{:S(2)}) copy-start(bf16[1024,1024]{1,0:T(8,128)(2,1)} %copy-done.4) | copy-start | bytes 6291460
  102.6 33.2 %collective-permute-start.6 = (bf16[256,576]{1,0:T(8,128)(2,1)}, bf16[256,576]{1,0:T(8,128)(2,1)S(1)}, u32[]{:S(2)}, u32[]{:S(2)}) collective-permute-start(bf16[256,576]{1,0:T(8,128)(2,1)} %get-tuple-element.31), channel_id=1, source_target_pairs={{0,2},{1,3},{2,0},{3,1},{4,6},{5,7},{6,4},{7,5},{8,10},{9,11},{10,... | collective-permute-start | bytes 884744 | tf_op jit(solution)/shard_map/ppermute | solution.py:231
  105.9 29.8 %collective-permute-start.7 = (bf16[256,576]{1,0:T(8,128)(2,1)}, bf16[256,576]{1,0:T(8,128)(2,1)S(1)}, u32[]{:S(2)}, u32[]{:S(2)}) collective-permute-start(bf16[256,576]{1,0:T(8,128)(2,1)} %get-tuple-element.32), channel_id=1, source_target_pairs={{0,3},{1,0},{2,1},{3,2},{4,7},{5,4},{6,5},{7,6},{8,11},{9,8},{10,9... | collective-permute-start | bytes 884744 | tf_op jit(solution)/shard_map/ppermute | solution.py:231
  107.8 27.9 %collective-permute-start.5 = (bf16[256,576]{1,0:T(8,128)(2,1)S(1)}, bf16[256,576]{1,0:T(8,128)(2,1)}, u32[]{:S(2)}, u32[]{:S(2)}) collective-permute-start(bf16[256,576]{1,0:T(8,128)(2,1)S(1)} %get-tuple-element.30.after2), channel_id=1, source_target_pairs={{0,1},{1,2},{2,3},{3,0},{4,5},{5,6},{6,7},{7,4},{8,9},{9,10},{10,1... | collective-permute-start | bytes 884744 | tf_op jit(solution)/shard_map/ppermute | solution.py:231
  113.6 13.9 %collective-permute-start.9 = (bf16[2,64,512]{2,1,0:T(8,128)(2,1)S(1)}, bf16[2,64,512]{2,1,0:T(8,128)(2,1)S(1)}, u32[]{:S(2)}, u32[]{:S(2)}) collective-permute-start(bf16[2,64,512]{2,1,0:T(8,128)(2,1)S(1)} %get-tuple-element.37), channel_id=1, source_target_pairs={{0,16},{8,24},{16,0},{24,8},{32,48},{40,56},{48,32},{56,40},{1,17}... | collective-permute-start | bytes 393224 | tf_op jit(solution)/shard_map/ppermute | solution.py:303
  117.8 22.4 %all-to-all-start.4 = ((f32[32,8,128]{2,1,0:T(8,128)}), f32[32,8,128]{2,1,0:T(8,128)S(1)}, u32[]{:S(2)}, u32[]{:S(2)}) async-start(f32[32,8,128]{2,1,0:T(8,128)} %shard_map.75.after), calls=%async_computation.4 | async-start | bytes 262144 | tf_op jit(solution)/shard_map/all_to_all | solution.py:235
  128.1 11.4 %collective-permute-start.10 = (bf16[1,64,512]{2,1,0:T(8,128)(2,1)S(1)}, bf16[1,64,512]{2,1,0:T(8,128)(2,1)S(1)}, u32[]{:S(2)}, u32[]{:S(2)}) collective-permute-start(bf16[1,64,512]{2,1,0:T(8,128)(2,1)S(1)} %get-tuple-element.39), channel_id=1, source_target_pairs={{0,32},{8,40},{16,48},{24,56},{32,0},{40,8},{48,16},{56,24},{1,33}... | collective-permute-start | bytes 196616 | tf_op jit(solution)/shard_map/ppermute | solution.py:303

commit v5 on v4

--- a/solution.py
+++ b/solution.py
@@ -71,35 +71,32 @@
             ]
 
 
-def key_tile(near, far, i, per):
-    ref, first = (near, i * per) if i * per < near.shape[0] else (far, i * per - near.shape[0])
-    k = ref[first : first + per]
+def key_tile(keys, i, per):
+    k = keys[i * per : (i + 1) * per]
     return k.reshape(k.shape[0] * k.shape[1], k.shape[2])
 
 
-def scores_kernel(lat, heads, pos, near, far, after, *refs):
+def scores_kernel(lat, heads, pos, keys, after, *refs):
     blocks, (e_ref, dp_ref, st_ref) = refs[:-3], refs[-3:]
     z, y, x = pos[0], pos[1], pos[2]
-    n_z, k_dev, _ = near.shape
+    grp, k_dev, width = keys.shape
     n_x = len(blocks)
     rows = refs[0].shape[0]
-    n_keys = 2 * n_z * k_dev
+    n_keys = grp * k_dev
     tiles = n_keys // TILE
     per = TILE // k_dev
     tok = rows // heads
-    first_query = n_z * 2 * n_x * (k_dev - tok)
+    first_query = grp * n_x * (k_dev - tok)
     for b, t in enumerate(blocks):
-        q, o = t[:, lat : lat + near.shape[2]], t[:, :lat]
+        q, o = t[:, lat : lat + width], t[:, :lat]
         cols = slice(b * rows, (b + 1) * rows)
         lane = lax.broadcasted_iota(jnp.int32, (k_dev, rows), 1)
         q_pos = ((z * 2 + y) * n_x + lax.rem(x + b, n_x)) * tok + lane // heads + first_query
         top = None
         for i in range(tiles):
-            s = nt(key_tile(near, far, i, per), q) * softmax_scale
-            half, zz = divmod((i + 1) * per - 1, n_z)
-            if zz == n_z - 1:
-                side = y if half == 0 else 1 - y
-                k_pos = ((zz * 2 + side) * n_x + x) * k_dev + lax.broadcasted_iota(
+            s = nt(key_tile(keys, i, per), q) * softmax_scale
+            if i == tiles - 1:
+                k_pos = ((grp - 1) * n_x + x) * k_dev + lax.broadcasted_iota(
                     jnp.int32, (k_dev, rows), 0
                 )
                 last = jnp.where(k_pos <= q_pos, s[TILE - k_dev :], -jnp.inf)
@@ -111,7 +108,7 @@
         delta = jnp.zeros_like(top)
         for i in range(tiles):
             part = slice(i * TILE, (i + 1) * TILE)
-            dp = nt(key_tile(near, far, i, per)[:, :lat], o)
+            dp = nt(key_tile(keys, i, per)[:, :lat], o)
             e = jnp.exp(e_ref[part, cols] - top)
             e_ref[part, cols] = e
             dp_ref[part, cols] = dp
@@ -147,7 +144,6 @@
             p = e_ref[part, cols] * f
             p_ref[part, cols] = p.astype(bf16)
             ds_ref[part, cols] = (p * (dp_ref[part, cols] - delta)).astype(bf16)
-    n_z = grp // 2
     for i in range(tiles):
         part = slice(i * TILE, (i + 1) * TILE)
         r = None
@@ -157,10 +153,8 @@
             r = v if r is None else r + v
         r = (r * softmax_scale).astype(bf16)
         for j in range(TILE // k_dev):
-            half, zz = divmod(i * (TILE // k_dev) + j, n_z)
-            side = y if half == 0 else 1 - y
             k = r[j * k_dev : (j + 1) * k_dev]
-            rope_ref[2 * zz + side] = jnp.concatenate([k[:half_keys], k[half_keys:]], axis=1)
+            rope_ref[i * (TILE // k_dev) + j] = jnp.concatenate([k[:half_keys], k[half_keys:]], axis=1)
     per = TILE // k_dev
     for i in range(tiles):
         part = slice(i * TILE, (i + 1) * TILE)
@@ -171,25 +165,27 @@
         v = v * softmax_scale
         for b, t in enumerate(blocks):
             v += nn(p_ref[part, b * rows : (b + 1) * rows], t[:, :lat])
-        out, first = (mine, other)[i * per // n_z], i * per % n_z
-        out[first : first + per] = v.astype(bf16).reshape(per, k_dev, lat)
-
-
-def query_kernel(ds_ref, near, far, after, *outs):
+        v = v.astype(bf16).reshape(per // 2, 2, k_dev, lat)
+        first = i * per // 2
+        for out, side in ((mine, y), (other, 1 - y)):
+            out[first : first + per // 2] = jnp.where(side == 0, v[:, 0], v[:, 1])
+
+
+def query_kernel(ds_ref, keys, *outs):
     rows = outs[0].shape[0]
-    per = TILE // near.shape[1]
+    per = TILE // keys.shape[1]
     for b, out in enumerate(outs):
         v = None
         for i in range(ds_ref.shape[0] // TILE):
             a = tn(
                 ds_ref[i * TILE : (i + 1) * TILE, b * rows : (b + 1) * rows],
-                key_tile(near, far, i, per),
+                key_tile(keys, i, per),
             )
             v = a if v is None else v + a
         out[...] = (v * softmax_scale).astype(out.dtype)
 
 
-def weight_kernel(parts, cols, after, rope_ref, out):
+def weight_kernel(parts, cols, after, after2, rope_ref, out):
     v = jnp.sum(parts[...].astype(f32), axis=0)
     e = v.shape[1] // 2
     rope = jnp.concatenate([v[:, :e], v[:, e:]])
@@ -199,7 +195,7 @@
         out[i] = tn(low, cols[i]).astype(bf16)
 
 
-def weight_half_kernel(parts, after, after2, out):
+def weight_half_kernel(parts, after, out):
     v = jnp.sum(parts[...].astype(f32), axis=0)
     v = jnp.swapaxes(v, 0, 1)
     v = v.reshape(v.shape[0] // SLOT, SLOT, v.shape[1])
@@ -248,12 +244,11 @@
     swap = [(0, 1), (1, 0)]
     pos = jnp.stack([lax.axis_index(a) for a in ("z", "y", "x")]).astype(jnp.int32)
 
-    near = trade(jnp.broadcast_to(latent, (nz, k_dev, width)), "z")
+    keys = trade(jnp.broadcast_to(latent, (nz * ny, k_dev, width)), ("z", "y"))
     (own,) = call(pack_kernel, [((rows, -(-(lat + width) // 128) * 128), bf16)], 2, moved=4 * rows * width)(
         dout.reshape(rows, lat), query.reshape(rows, width)
     )
     blocks = [own] + [fetch(own, k, nx) for k in range(1, nx)]
-    far = lax.ppermute(near, "y", swap)
 
     wide = nw * nz * SLOT
     (cols,) = call(
@@ -262,10 +257,10 @@
     )(hidden[0])
     e, dp, st = call(
         functools.partial(scores_kernel, lat, heads),
-        [((n_keys, n_rows), f32)] * 2 + [((4 * nx, rows), f32)], 8, smem=(0,),
-        unused=(3,),
+        [((n_keys, n_rows), f32)] * 2 + [((4 * nx, rows), f32)], 7, smem=(0,),
+        unused=(2,),
         flops=2 * pairs * (width + lat), moved=8 * pairs, limit=20,
-    )(pos, near, far, cols, *blocks)
+    )(pos, keys, cols, *blocks)
     stats = trade(jnp.broadcast_to(st[None], (nx,) + st.shape), "x")
     ds, rope_part, mine, other = call(
         functools.partial(dscores_kernel, lat),
@@ -275,24 +270,23 @@
     )(pos, stats, st, e, dp, *blocks)
     rope_part = trade(rope_part, ("z", "y"))
     other = lax.ppermute(other, "y", swap)
+    dq = call(
+        query_kernel, [((rows, width), f32)] + [((rows, width), bf16)] * (nx - 1), 2,
+        flops=2 * pairs * width, moved=4 * pairs,
+    )(ds, keys)
     rope_sum, terms = call(
-        weight_kernel, [((k_dev, rope), f32), ((nc * ny * nx, rope, wide), bf16)], 3, unused=(2,),
+        weight_kernel, [((k_dev, rope), f32), ((nc * ny * nx, rope, wide), bf16)], 4, unused=(2, 3),
         flops=2 * k_dev * nc * ny * nx * wide * rope, moved=4 * k_dev * model, limit=20,
-    )(rope_part, cols, other)
+    )(rope_part, cols, other, dq[1])
     after = terms
     terms = trade(terms, ("c", "y", "x"))
-    dq = call(
-        query_kernel, [((rows, width), f32)] + [((rows, width), bf16)] * (nx - 1), 4, unused=(3,),
-        flops=2 * pairs * width, moved=4 * pairs, limit=20,
-    )(ds, near, far, after)
-    query_part = dq[1]
     dq = [dq[0]] + [fetch(dq[k], nx - k, nx) for k in range(1, nx)]
     kept, came = mine, other
     for bit in range(3):
         if bit == 2:
             (terms,) = call(
-                weight_half_kernel, [((nw * nz, SLOT // 2, 2 * rope), f32)], 3, unused=(1, 2)
-            )(terms, kept, query_part)
+                weight_half_kernel, [((nw * nz, SLOT // 2, 2 * rope), f32)], 2, unused=(1,)
+            )(terms, kept)
             after = terms
             terms = trade(terms, ("w", "z"))
         n = nz >> (bit + 1)

time: 143 us -> 139 us (0.972)
  blocking collectives: 21.2 us -> 8.13 us
  waiting for transfers between devices: 24.2 us -> 29 us
  starting transfers between devices: 64.9 us -> 68.2 us
    all_to_all x2 -> x1, blocking collectives: 21.2 us -> 8.13 us  [trade(): return lax.all_to_all(value, axes, 0, 0, tiled=True)]
    ppermute x6, waiting for transfers between devices: 8.6 us -> 20.9 us  [fetch(): return lax.ppermute(value, 'x', [(s, (s - offset) % n) for s in range(n)])]
    all_to_all x3 -> x4, starting transfers between devices: 25.7 us -> 32.9 us  [trade(): return lax.all_to_all(value, axes, 0, 0, tiled=True)]
    ppermute x1 -> x0, waiting for transfers between devices: 4.03 us -> none  [body(): far = lax.ppermute(near, 'y', swap)]
    ppermute x1 -> x0, starting transfers between devices: 3.47 us -> none  [body(): far = lax.ppermute(near, 'y', swap)]
    all_to_all x3 -> x4, waiting for transfers between devices: 9.67 us -> 6.24 us  [trade(): return lax.all_to_all(value, axes, 0, 0, tiled=True)]
    unnamed x14 -> x22, local copies, waits for them, and re-layouts: 7.06 us -> 7.12 us
  transfers between devices with their start and end apart: 14 -> 14, of which waited for: 4 -> 6; matrix products, arithmetic and copies ran while one was open for 1% -> 1% of each run, Pallas kernels for 6% -> 5%
where the time goes in v5:
time: 139 us; the launch traced here: 138 us
  starting transfers between devices  68.2 us (49%)
  waiting for transfers between devices  29 us (21%)
  Pallas kernels  20.1 us (14%)
  local copies, waits for them, and re-layouts  9.3 us (7%)
  blocking collectives  8.13 us (6%)
  other arithmetic  1.92 us (1%)
    all_to_all x4, starting transfers between devices, trade(): return lax.all_to_all(value, axes, 0, 0, tiled=True)  32.9 us
    ppermute x6, waiting for transfers between devices, fetch(): return lax.ppermute(value, 'x', [(s, (s - offset) % n) for s in range(n)])  20.9 us
    ppermute x6, starting transfers between devices, fetch(): return lax.ppermute(value, 'x', [(s, (s - offset) % n) for s in range(n)])  19.1 us
    ppermute x3, starting transfers between devices, body(): came = lax.ppermute(sent, 'z', [(i, i ^ 1 << bit) for i in range(nz)])  12.9 us
    all_to_all x1, blocking collectives, trade(): return lax.all_to_all(value, axes, 0, 0, tiled=True)  8.13 us
    unnamed x22, local copies, waits for them, and re-layouts  7.12 us
    all_to_all x4, waiting for transfers between devices, trade(): return lax.all_to_all(value, axes, 0, 0, tiled=True)  6.24 us
    pallas_call x1, Pallas kernels, body(): call(functools.partial(dscores_kernel, lat), [((n_keys, n_rows), bf16), (...  5.22 us
  transfers between devices with their start and end apart: 14, of which 6 were waited for; matrix products, arithmetic and copies ran while one was open for 1% of the time, Pallas kernels for 5%

profile of v5, /device:TPU:6, one launch (start us, length us, event | category | flops | bytes accessed | tf_op | source)
XLA Modules:
  0.0 137.5 jit_solution(16113576558488630270)
XLA Ops:
  0.7 2.2 %broadcast_in_dim.17 = bf16[16,64,576]{2,1,0:T(8,128)(2,1)} broadcast(bf16[64,576]{1,0:T(8,128)(2,1)} %bitcast.14), dimensions={1,2} | broadcast | bytes 1253376 | tf_op jit(solution)/shard_map/broadcast_in_dim | solution.py:247
  2.8 11.4 %all-to-all-start = ((bf16[16,64,576]{2,1,0:T(8,128)(2,1)}), bf16[16,64,576]{2,1,0:T(8,128)(2,1)S(1)}, u32[]{:S(2)}, u32[]{:S(2)}) async-start(bf16[16,64,576]{2,1,0:T(8,128)(2,1)} %broadcast_in_dim.17), calls=%async_computation | async-start | bytes 2621440 | tf_op jit(solution)/shard_map/all_to_all | solution.py:231
  14.3 2.4 %collective-permute-start.2 = (bf16[256,1152]{1,0:T(8,128)(2,1)S(1)}, bf16[256,1152]{1,0:T(8,128)(2,1)S(1)}, u32[]{:S(2)}, u32[]{:S(2)}) collective-permute-start(bf16[256,1152]{1,0:T(8,128)(2,1)S(1)} %shard_map.68.refs_0_), channel_id=1, source_target_pairs={{0,1},{1,2},{2,3},{3,0},{4,5},{5,6},{6,7},{7,4},{8,9},{9,10},{10,1... | collective-permute-start | bytes 1769480 | tf_op jit(solution)/shard_map/ppermute | solution.py:227
  16.7 4.3 %collective-permute-start.1 = (bf16[256,1152]{1,0:T(8,128)(2,1)S(1)}, bf16[256,1152]{1,0:T(8,128)(2,1)S(1)}, u32[]{:S(2)}, u32[]{:S(2)}) collective-permute-start(bf16[256,1152]{1,0:T(8,128)(2,1)S(1)} %shard_map.68.refs_0_), channel_id=1, source_target_pairs={{0,2},{1,3},{2,0},{3,1},{4,6},{5,7},{6,4},{7,5},{8,10},{9,11},{10,... | collective-permute-start | bytes 1769480 | tf_op jit(solution)/shard_map/ppermute | solution.py:227
  21.1 1.9 %collective-permute-start = (bf16[256,1152]{1,0:T(8,128)(2,1)S(1)}, bf16[256,1152]{1,0:T(8,128)(2,1)}, u32[]{:S(2)}, u32[]{:S(2)}) collective-permute-start(bf16[256,1152]{1,0:T(8,128)(2,1)S(1)} %shard_map.68.refs_0_), channel_id=1, source_target_pairs={{0,3},{1,0},{2,1},{3,2},{4,7},{5,4},{6,5},{7,6},{8,11},{9,8},{10,9... | collective-permute-start | bytes 1769480 | tf_op jit(solution)/shard_map/ppermute | solution.py:227
  23.0 1.2 copy-done.10
  24.2 1.3 shard_map.67.after.cols
  25.5 1.0 copy-done
  26.5 6.0 %collective-permute-done.2.refs_3_ = bf16[256,1152]{1,0:T(8,128)(2,1)S(1)} collective-permute-done((bf16[256,1152]{1,0:T(8,128)(2,1)S(1)}, bf16[256,1152]{1,0:T(8,128)(2,1)S(1)}, u32[]{:S(2)}, u32[]{:S(2)}) %collective-permute-start.2) | collective-permute-done | bytes 589856 | tf_op jit(solution)/shard_map/ppermute | solution.py:227
  32.5 4.0 %collective-permute-done.1.refs_2_ = bf16[256,1152]{1,0:T(8,128)(2,1)S(1)} collective-permute-done((bf16[256,1152]{1,0:T(8,128)(2,1)S(1)}, bf16[256,1152]{1,0:T(8,128)(2,1)S(1)}, u32[]{:S(2)}, u32[]{:S(2)}) %collective-permute-start.1) | collective-permute-done | bytes 589856 | tf_op jit(solution)/shard_map/ppermute | solution.py:227
  36.5 10.9 %collective-permute-done.refs_1_ = bf16[256,1152]{1,0:T(8,128)(2,1)} collective-permute-done((bf16[256,1152]{1,0:T(8,128)(2,1)S(1)}, bf16[256,1152]{1,0:T(8,128)(2,1)}, u32[]{:S(2)}, u32[]{:S(2)}) %collective-permute-start) | collective-permute-done | bytes 589856 | tf_op jit(solution)/shard_map/ppermute | solution.py:227
  47.8 1.2 copy-done.1
  49.0 4.4 %shard_map.69 = (f32[1024,1024]{1,0:T(8,128)S(1)}, f32[1024,1024]{1,0:T(8,128)S(1)}, f32[16,256]{1,0:T(8,128)S(1)}) custom-call(s32[3]{0:T(128)S(1)} %pad_add_fusion.pos, bf16[16,64,576]{2,1,0:T(8,128)(2,1)S(1)} %all-to-all-done.keys, bf16[16,64,512]{2,1,0:T(8,128)(2,1)S(1)} %copy-done.1, bf16[256,1152]{1,0:T(8,128)(2,1)S(1)} %shard_map.68.refs_0_, ...), custom_call_target="tpu_custom_call" | custom-call | flops 2281701376 | bytes 8388608 | tf_op jit(solution)/shard_map/pallas_call | solution.py:258
  53.5 8.1 %all_to_all.25.stats = f32[4,16,256]{2,1,0:T(8,128)S(1)} all-to-all(f32[4,16,256]{2,1,0:T(8,128)S(1)} %broadcast_in_dim.18), channel_id=1, replica_groups=mesh['w'=4,'c'=2,'z'=8,'y'=2,'x'=4] {'x'}, dimensions={0} | all-to-all | bytes 131072 | tf_op jit(solution)/shard_map/all_to_all | solution.py:231
  61.6 5.2 %shard_map.70 = (bf16[1024,1024]{1,0:T(8,128)(2,1)S(1)}, bf16[16,32,128]{2,1,0:T(8,128)(2,1)S(1)}, bf16[8,64,512]{2,1,0:T(8,128)(2,1)S(1)}, bf16[8,64,512]{2,1,0:T(8,128)(2,1)}) custom-call(s32[3]{0:T(128)S(1)} %pad_add_fusion.pos, f32[4,16,256]{2,1,0:T(8,128)S(1)} %all_to_all.25.stats, f32[16,256]{1,0:T(8,128)S(1)} %get-tuple-element.22.st, ...), custom_call_target="tpu_custom_call" | custom-call | flops 2281701376 | bytes 12582912 | tf_op jit(solution)/shard_map/pallas_call | solution.py:265
  67.6 1.3 copy-done.8
  68.9 3.3 %collective-permute-start.6 = (bf16[8,64,512]{2,1,0:T(8,128)(2,1)}, bf16[8,64,512]{2,1,0:T(8,128)(2,1)S(1)}, u32[]{:S(2)}, u32[]{:S(2)}) collective-permute-start(bf16[8,64,512]{2,1,0:T(8,128)(2,1)} %get-tuple-element.31), channel_id=1, source_target_pairs={{0,4},{4,0},{1,5},{5,1},{2,6},{6,2},{3,7},{7,3},{8,12},{12,8},{9,1... | collective-permute-start | bytes 1572872 | tf_op jit(solution)/shard_map/ppermute | solution.py:272
  72.2 6.8 %all-to-all-start.2 = ((bf16[16,32,128]{2,1,0:T(8,128)(2,1)}), bf16[16,32,128]{2,1,0:T(8,128)(2,1)}, u32[]{:S(2)}, u32[]{:S(2)}) async-start(bf16[16,32,128]{2,1,0:T(8,128)(2,1)} %copy-done.7), calls=%async_computation.2 | async-start | bytes 262144 | tf_op jit(solution)/shard_map/all_to_all | solution.py:231
  79.1 1.6 %copy-done.9 = bf16[1024,1024]{1,0:T(8,128)(2,1)S(1)} copy-done((bf16[1024,1024]{1,0:T(8,128)(2,1)S(1)}, bf16[1024,1024]{1,0:T(8,128)(2,1)}, u32[]{:S(2)}) %copy-start.9) | copy-done | bytes 2097176
  80.7 2.6 %shard_map.71 = (f32[256,576]{1,0:T(8,128)S(1)}, bf16[256,576]{1,0:T(8,128)(2,1)}, bf16[256,576]{1,0:T(8,128)(2,1)}, bf16[256,576]{1,0:T(8,128)(2,1)}) custom-call(bf16[1024,1024]{1,0:T(8,128)(2,1)S(1)} %copy-done.9, bf16[16,64,576]{2,1,0:T(8,128)(2,1)S(1)} %all-to-all-done.keys), custom_call_target="tpu_custom_call" | custom-call | flops 1207959552 | bytes 4194304 | tf_op jit(solution)/shard_map/pallas_call | solution.py:273
  83.3 5.8 %all-to-all-done.2.parts = bf16[16,32,128]{2,1,0:T(8,128)(2,1)} async-done(((bf16[16,32,128]{2,1,0:T(8,128)(2,1)}), bf16[16,32,128]{2,1,0:T(8,128)(2,1)}, u32[]{:S(2)}, u32[]{:S(2)}) %all-to-all-start.2) | async-done | bytes 131104 | tf_op jit(solution)/shard_map/all_to_all | solution.py:231
  89.1 2.4 %shard_map.72 = (f32[64,64]{1,0:T(8,128)S(1)}, bf16[16,64,512]{2,1,0:T(8,128)(2,1)}) custom-call(bf16[16,32,128]{2,1,0:T(8,128)(2,1)} %all-to-all-done.2.parts, bf16[16,64,512]{2,1,0:T(8,128)(2,1)S(1)} %copy-done.2, bf16[8,64,512]{2,1,0:T(8,128)(2,1)S(1)} %collective-permute-done.6.after.b, bf16[256,576]{1,0:T(8,128)(2,1)} %get-tuple-element.27.after2), custom_call_target="tpu_custom_call" | custom-call | flops 67108864 | bytes 1835008 | tf_op jit(solution)/shard_map/pallas_call | solution.py:277
  91.5 5.7 %all-to-all-start.3 = ((bf16[16,64,512]{2,1,0:T(8,128)(2,1)}), bf16[16,64,512]{2,1,0:T(8,128)(2,1)S(1)}, u32[]{:S(2)}, u32[]{:S(2)}) async-start(bf16[16,64,512]{2,1,0:T(8,128)(2,1)} %get-tuple-element.33.after), calls=%async_computation.3 | async-start | bytes 2097152 | tf_op jit(solution)/shard_map/all_to_all | solution.py:231
  97.9 2.5 %collective-permute-start.7 = (bf16[4,64,512]{2,1,0:T(8,128)(2,1)S(1)}, bf16[4,64,512]{2,1,0:T(8,128)(2,1)S(1)}, u32[]{:S(2)}, u32[]{:S(2)}) collective-permute-start(bf16[4,64,512]{2,1,0:T(8,128)(2,1)S(1)} %get-tuple-element.35), channel_id=1, source_target_pairs={{0,8},{8,0},{16,24},{24,16},{32,40},{40,32},{48,56},{56,48},{1,9},... | collective-permute-start | bytes 786440 | tf_op jit(solution)/shard_map/ppermute | solution.py:297
  100.4 3.4 %collective-permute-start.4 = (bf16[256,576]{1,0:T(8,128)(2,1)}, bf16[256,576]{1,0:T(8,128)(2,1)S(1)}, u32[]{:S(2)}, u32[]{:S(2)}) collective-permute-start(bf16[256,576]{1,0:T(8,128)(2,1)} %get-tuple-element.28), channel_id=1, source_target_pairs={{0,2},{1,3},{2,0},{3,1},{4,6},{5,7},{6,4},{7,5},{8,10},{9,11},{10,... | collective-permute-start | bytes 884744 | tf_op jit(solution)/shard_map/ppermute | solution.py:227
  103.8 1.9 %collective-permute-start.5 = (bf16[256,576]{1,0:T(8,128)(2,1)}, bf16[256,576]{1,0:T(8,128)(2,1)S(1)}, u32[]{:S(2)}, u32[]{:S(2)}) collective-permute-start(bf16[256,576]{1,0:T(8,128)(2,1)} %get-tuple-element.29), channel_id=1, source_target_pairs={{0,3},{1,0},{2,1},{3,2},{4,7},{5,4},{6,5},{7,6},{8,11},{9,8},{10,9... | collective-permute-start | bytes 884744 | tf_op jit(solution)/shard_map/ppermute | solution.py:227
  105.7 5.1 %collective-permute-start.3 = (bf16[256,576]{1,0:T(8,128)(2,1)}, bf16[256,576]{1,0:T(8,128)(2,1)}, u32[]{:S(2)}, u32[]{:S(2)}) collective-permute-start(bf16[256,576]{1,0:T(8,128)(2,1)} %get-tuple-element.27.after2), channel_id=1, source_target_pairs={{0,1},{1,2},{2,3},{3,0},{4,5},{5,6},{6,7},{7,4},{8,9},{9,10},{10,1... | collective-permute-start | bytes 884744 | tf_op jit(solution)/shard_map/ppermute | solution.py:227
  111.5 2.8 %collective-permute-start.8 = (bf16[2,64,512]{2,1,0:T(8,128)(2,1)S(1)}, bf16[2,64,512]{2,1,0:T(8,128)(2,1)S(1)}, u32[]{:S(2)}, u32[]{:S(2)}) collective-permute-start(bf16[2,64,512]{2,1,0:T(8,128)(2,1)S(1)} %get-tuple-element.37), channel_id=1, source_target_pairs={{0,16},{8,24},{16,0},{24,8},{32,48},{40,56},{48,32},{56,40},{1,17}... | collective-permute-start | bytes 393224 | tf_op jit(solution)/shard_map/ppermute | solution.py:297
  115.3 8.9 %all-to-all-start.4 = ((f32[32,8,128]{2,1,0:T(8,128)}), f32[32,8,128]{2,1,0:T(8,128)S(1)}, u32[]{:S(2)}, u32[]{:S(2)}) async-start(f32[32,8,128]{2,1,0:T(8,128)} %shard_map.75.after), calls=%async_computation.4 | async-start | bytes 262144 | tf_op jit(solution)/shard_map/all_to_all | solution.py:231
  124.8 7.6 %collective-permute-start.9 = (bf16[1,64,512]{2,1,0:T(8,128)(2,1)S(1)}, bf16[1,64,512]{2,1,0:T(8,128)(2,1)S(1)}, u32[]{:S(2)}, u32[]{:S(2)}) collective-permute-start(bf16[1,64,512]{2,1,0:T(8,128)(2,1)S(1)} %get-tuple-element.39), channel_id=1, source_target_pairs={{0,32},{8,40},{16,48},{24,56},{32,0},{40,8},{48,16},{56,24},{1,33}... | collective-permute-start | bytes 196616 | tf_op jit(solution)/shard_map/ppermute | solution.py:297
  132.4 1.8 %add_convert_fusion = bf16[256,576]{1,0:T(8,128)(2,1)} fusion(bf16[256,576]{1,0:T(8,128)(2,1)S(1)} %collective-permute-done.5, bf16[256,576]{1,0:T(8,128)(2,1)S(1)} %collective-permute-done.4, f32[256,576]{1,0:T(8,128)S(1)} %get-tuple-element.26, bf16[256,576]{1,0:T(8,128)(2,1)} %collective-permute-done.3), kind=kLoop, calls=%fused_computation | loop fusion | flops 1032192 | bytes 1769472 | tf_op jit(solution)/shard_map/convert_element_type | solution.py:304
  134.3 1.9 %collective-permute-done.9.b = bf16[1,64,512]{2,1,0:T(8,128)(2,1)S(1)} collective-permute-done((bf16[1,64,512]{2,1,0:T(8,128)(2,1)S(1)}, bf16[1,64,512]{2,1,0:T(8,128)(2,1)S(1)}, u32[]{:S(2)}, u32[]{:S(2)}) %collective-permute-start.9) | collective-permute-done | bytes 65568 | tf_op jit(solution)/shard_map/ppermute | solution.py:297
  (35 shorter events, 5.5 us)
Async XLA Ops:
  0.6 13.6 %copy-start.6 = (bf16[1,4,64,512]{3,2,1,0:T(8,128)(2,1)S(1)}, bf16[1,4,64,512]{3,2,1,0:T(8,128)(2,1)}, u32[]{:S(2)}) copy-start(bf16[1,4,64,512]{3,2,1,0:T(8,128)(2,1)} %param.6) | copy-start | bytes 786436
  0.6 13.6 %copy-start.5 = (bf16[1,4,64,576]{3,2,1,0:T(8,128)(2,1)S(1)}, bf16[1,4,64,576]{3,2,1,0:T(8,128)(2,1)}, u32[]{:S(2)}) copy-start(bf16[1,4,64,576]{3,2,1,0:T(8,128)(2,1)} %param.4) | copy-start | bytes 884740
  2.8 45.0 %all-to-all-start = ((bf16[16,64,576]{2,1,0:T(8,128)(2,1)}), bf16[16,64,576]{2,1,0:T(8,128)(2,1)S(1)}, u32[]{:S(2)}, u32[]{:S(2)}) async-start(bf16[16,64,576]{2,1,0:T(8,128)(2,1)} %broadcast_in_dim.17), calls=%async_computation | async-start | bytes 2621440 | tf_op jit(solution)/shard_map/all_to_all | solution.py:231
  14.3 18.1 %collective-permute-start.2 = (bf16[256,1152]{1,0:T(8,128)(2,1)S(1)}, bf16[256,1152]{1,0:T(8,128)(2,1)S(1)}, u32[]{:S(2)}, u32[]{:S(2)}) collective-permute-start(bf16[256,1152]{1,0:T(8,128)(2,1)S(1)} %shard_map.68.refs_0_), channel_id=1, source_target_pairs={{0,1},{1,2},{2,3},{3,0},{4,5},{5,6},{6,7},{7,4},{8,9},{9,10},{10,1... | collective-permute-start | bytes 1769480 | tf_op jit(solution)/shard_map/ppermute | solution.py:227
  16.7 19.7 %collective-permute-start.1 = (bf16[256,1152]{1,0:T(8,128)(2,1)S(1)}, bf16[256,1152]{1,0:T(8,128)(2,1)S(1)}, u32[]{:S(2)}, u32[]{:S(2)}) collective-permute-start(bf16[256,1152]{1,0:T(8,128)(2,1)S(1)} %shard_map.68.refs_0_), channel_id=1, source_target_pairs={{0,2},{1,3},{2,0},{3,1},{4,6},{5,7},{6,4},{7,5},{8,10},{9,11},{10,... | collective-permute-start | bytes 1769480 | tf_op jit(solution)/shard_map/ppermute | solution.py:227
  21.1 26.3 %collective-permute-start = (bf16[256,1152]{1,0:T(8,128)(2,1)S(1)}, bf16[256,1152]{1,0:T(8,128)(2,1)}, u32[]{:S(2)}, u32[]{:S(2)}) collective-permute-start(bf16[256,1152]{1,0:T(8,128)(2,1)S(1)} %shard_map.68.refs_0_), channel_id=1, source_target_pairs={{0,3},{1,0},{2,1},{3,2},{4,7},{5,4},{6,5},{7,6},{8,11},{9,8},{10,9... | collective-permute-start | bytes 1769480 | tf_op jit(solution)/shard_map/ppermute | solution.py:227
  23.0 1.2 copy-start.10
  25.5 1.0 copy-start
  47.8 1.2 copy-start.1
  66.8 0.8 copy-start.3
  67.6 1.3 copy-start.8
  68.9 3.3 %copy-start.7 = (bf16[16,32,128]{2,1,0:T(8,128)(2,1)}, bf16[16,32,128]{2,1,0:T(8,128)(2,1)S(1)}, u32[]{:S(2)}) copy-start(bf16[16,32,128]{2,1,0:T(8,128)(2,1)S(1)} %get-tuple-element.32) | copy-start | bytes 393220
  68.9 20.1 %collective-permute-start.6 = (bf16[8,64,512]{2,1,0:T(8,128)(2,1)}, bf16[8,64,512]{2,1,0:T(8,128)(2,1)S(1)}, u32[]{:S(2)}, u32[]{:S(2)}) collective-permute-start(bf16[8,64,512]{2,1,0:T(8,128)(2,1)} %get-tuple-element.31), channel_id=1, source_target_pairs={{0,4},{4,0},{1,5},{5,1},{2,6},{6,2},{3,7},{7,3},{8,12},{12,8},{9,1... | collective-permute-start | bytes 1572872 | tf_op jit(solution)/shard_map/ppermute | solution.py:272
  72.2 16.9 %all-to-all-start.2 = ((bf16[16,32,128]{2,1,0:T(8,128)(2,1)}), bf16[16,32,128]{2,1,0:T(8,128)(2,1)}, u32[]{:S(2)}, u32[]{:S(2)}) async-start(bf16[16,32,128]{2,1,0:T(8,128)(2,1)} %copy-done.7), calls=%async_computation.2 | async-start | bytes 262144 | tf_op jit(solution)/shard_map/all_to_all | solution.py:231
  79.1 1.6 %copy-start.9 = (bf16[1024,1024]{1,0:T(8,128)(2,1)S(1)}, bf16[1024,1024]{1,0:T(8,128)(2,1)}, u32[]{:S(2)}) copy-start(bf16[1024,1024]{1,0:T(8,128)(2,1)} %copy-done.8) | copy-start | bytes 6291460
  80.7 8.4 %copy-start.2 = (bf16[16,64,512]{2,1,0:T(8,128)(2,1)S(1)}, bf16[16,64,512]{2,1,0:T(8,128)(2,1)}, u32[]{:S(2)}) copy-start(bf16[16,64,512]{2,1,0:T(8,128)(2,1)} %copy-done) | copy-start | bytes 3145732
  83.2 14.0 %copy-start.4 = (bf16[8,64,512]{2,1,0:T(8,128)(2,1)S(1)}, bf16[8,64,512]{2,1,0:T(8,128)(2,1)}, u32[]{:S(2)}) copy-start(bf16[8,64,512]{2,1,0:T(8,128)(2,1)} %copy-done.3) | copy-start | bytes 1572868
  91.5 22.8 %all-to-all-start.3 = ((bf16[16,64,512]{2,1,0:T(8,128)(2,1)}), bf16[16,64,512]{2,1,0:T(8,128)(2,1)S(1)}, u32[]{:S(2)}, u32[]{:S(2)}) async-start(bf16[16,64,512]{2,1,0:T(8,128)(2,1)} %get-tuple-element.33.after), calls=%async_computation.3 | async-start | bytes 2097152 | tf_op jit(solution)/shard_map/all_to_all | solution.py:231
  97.9 12.9 %collective-permute-start.7 = (bf16[4,64,512]{2,1,0:T(8,128)(2,1)S(1)}, bf16[4,64,512]{2,1,0:T(8,128)(2,1)S(1)}, u32[]{:S(2)}, u32[]{:S(2)}) collective-permute-start(bf16[4,64,512]{2,1,0:T(8,128)(2,1)S(1)} %get-tuple-element.35), channel_id=1, source_target_pairs={{0,8},{8,0},{16,24},{24,16},{32,40},{40,32},{48,56},{56,48},{1,9},... | collective-permute-start | bytes 786440 | tf_op jit(solution)/shard_map/ppermute | solution.py:297
  100.4 32.0 %collective-permute-start.4 = (bf16[256,576]{1,0:T(8,128)(2,1)}, bf16[256,576]{1,0:T(8,128)(2,1)S(1)}, u32[]{:S(2)}, u32[]{:S(2)}) collective-permute-start(bf16[256,576]{1,0:T(8,128)(2,1)} %get-tuple-element.28), channel_id=1, source_target_pairs={{0,2},{1,3},{2,0},{3,1},{4,6},{5,7},{6,4},{7,5},{8,10},{9,11},{10,... | collective-permute-start | bytes 884744 | tf_op jit(solution)/shard_map/ppermute | solution.py:227
  103.8 28.6 %collective-permute-start.5 = (bf16[256,576]{1,0:T(8,128)(2,1)}, bf16[256,576]{1,0:T(8,128)(2,1)S(1)}, u32[]{:S(2)}, u32[]{:S(2)}) collective-permute-start(bf16[256,576]{1,0:T(8,128)(2,1)} %get-tuple-element.29), channel_id=1, source_target_pairs={{0,3},{1,0},{2,1},{3,2},{4,7},{5,4},{6,5},{7,6},{8,11},{9,8},{10,9... | collective-permute-start | bytes 884744 | tf_op jit(solution)/shard_map/ppermute | solution.py:227
  105.7 26.7 %collective-permute-start.3 = (bf16[256,576]{1,0:T(8,128)(2,1)}, bf16[256,576]{1,0:T(8,128)(2,1)}, u32[]{:S(2)}, u32[]{:S(2)}) collective-permute-start(bf16[256,576]{1,0:T(8,128)(2,1)} %get-tuple-element.27.after2), channel_id=1, source_target_pairs={{0,1},{1,2},{2,3},{3,0},{4,5},{5,6},{6,7},{7,4},{8,9},{9,10},{10,1... | collective-permute-start | bytes 884744 | tf_op jit(solution)/shard_map/ppermute | solution.py:227
  111.5 12.7 %collective-permute-start.8 = (bf16[2,64,512]{2,1,0:T(8,128)(2,1)S(1)}, bf16[2,64,512]{2,1,0:T(8,128)(2,1)S(1)}, u32[]{:S(2)}, u32[]{:S(2)}) collective-permute-start(bf16[2,64,512]{2,1,0:T(8,128)(2,1)S(1)} %get-tuple-element.37), channel_id=1, source_target_pairs={{0,16},{8,24},{16,0},{24,8},{32,48},{40,56},{48,32},{56,40},{1,17}... | collective-permute-start | bytes 393224 | tf_op jit(solution)/shard_map/ppermute | solution.py:297
  115.3 21.6 %all-to-all-start.4 = ((f32[32,8,128]{2,1,0:T(8,128)}), f32[32,8,128]{2,1,0:T(8,128)S(1)}, u32[]{:S(2)}, u32[]{:S(2)}) async-start(f32[32,8,128]{2,1,0:T(8,128)} %shard_map.75.after), calls=%async_computation.4 | async-start | bytes 262144 | tf_op jit(solution)/shard_map/all_to_all | solution.py:231
  124.8 11.4 %collective-permute-start.9 = (bf16[1,64,512]{2,1,0:T(8,128)(2,1)S(1)}, bf16[1,64,512]{2,1,0:T(8,128)(2,1)S(1)}, u32[]{:S(2)}, u32[]{:S(2)}) collective-permute-start(bf16[1,64,512]{2,1,0:T(8,128)(2,1)S(1)} %get-tuple-element.39), channel_id=1, source_target_pairs={{0,32},{8,40},{16,48},{24,56},{32,0},{40,8},{48,16},{56,24},{1,33}... | collective-permute-start | bytes 196616 | tf_op jit(solution)/shard_map/ppermute | solution.py:297

commit v6 on v5

--- a/solution.py
+++ b/solution.py
@@ -10,6 +10,7 @@
 softmax_scale = 0.07216878364870323
 f32, bf16 = jnp.float32, jnp.bfloat16
 TILE = 256
+TOKEN = ((8, 128), jnp.float32)
 SLOT = 16
 
 
@@ -52,7 +53,8 @@
     out[:, lat + width :] = jnp.zeros((out.shape[0], out.shape[1] - lat - width), out.dtype)
 
 
-def columns_kernel(block, n_z, n_grp, n_core, hid, out):
+def columns_kernel(block, n_z, n_grp, n_core, hid, out, token):
+    token[...] = jnp.zeros(token.shape, token.dtype)
     k_dev, model = hid.shape
     n_data = model // (n_z * n_grp * block)
     span = n_z * n_grp * block
@@ -118,9 +120,10 @@
 
 
 def dscores_kernel(lat, pos, stats, st, e_ref, dp_ref, *refs):
-    blocks, (ds_ref, rope_ref, mine, other, p_ref) = refs[:-5], refs[-5:]
+    n_x = stats.shape[0]
+    blocks, (keys, rope_ref, mine, other) = refs[:n_x], refs[n_x : n_x + 4]
+    own, keep, send, p_ref, ds_ref = refs[n_x + 4 :]
     y, x = pos[1], pos[2]
-    n_x = len(blocks)
     rows = refs[0].shape[0]
     tiles = e_ref.shape[0] // TILE
     grp, half_keys, _ = rope_ref.shape
@@ -169,20 +172,25 @@
         first = i * per // 2
         for out, side in ((mine, y), (other, 1 - y)):
             out[first : first + per // 2] = jnp.where(side == 0, v[:, 0], v[:, 1])
-
-
-def query_kernel(ds_ref, keys, *outs):
-    rows = outs[0].shape[0]
-    per = TILE // keys.shape[1]
-    for b, out in enumerate(outs):
+    dq = []
+    for b in range(n_x):
         v = None
-        for i in range(ds_ref.shape[0] // TILE):
-            a = tn(
-                ds_ref[i * TILE : (i + 1) * TILE, b * rows : (b + 1) * rows],
-                key_tile(keys, i, per),
-            )
+        for i in range(tiles):
+            part = slice(i * TILE, (i + 1) * TILE)
+            a = tn(ds_ref[part, b * rows : (b + 1) * rows], key_tile(keys, i, per))
             v = a if v is None else v + a
-        out[...] = (v * softmax_scale).astype(out.dtype)
+        dq.append(v * softmax_scale)
+    own[...] = dq[0]
+    even = lax.rem(x, 2) == 0
+    keep[...] = jnp.where(even, dq[3], dq[1])
+    send[...] = jnp.concatenate([jnp.where(even, dq[1], dq[3]), dq[2]], axis=1).astype(bf16)
+
+
+def query_half_kernel(own, keep, came, own_out, send, token):
+    token[...] = jnp.zeros(token.shape, token.dtype)
+    width = own.shape[1]
+    own_out[...] = own[...] + came[:, :width].astype(f32)
+    send[...] = (keep[...] + came[:, width:].astype(f32)).astype(bf16)
 
 
 def weight_kernel(parts, cols, after, after2, rope_ref, out):
@@ -195,11 +203,22 @@
         out[i] = tn(low, cols[i]).astype(bf16)
 
 
-def weight_half_kernel(parts, after, out):
+def weight_half_kernel(parts, after, out, token):
+    token[...] = jnp.zeros(token.shape, token.dtype)
+    n_z = out.shape[0]
+    half = SLOT // 2
     v = jnp.sum(parts[...].astype(f32), axis=0)
     v = jnp.swapaxes(v, 0, 1)
     v = v.reshape(v.shape[0] // SLOT, SLOT, v.shape[1])
-    out[...] = jnp.concatenate([v[:, : SLOT // 2], v[:, SLOT // 2 :]], axis=2)
+    v = jnp.concatenate([v[:, :half], v[:, half:]], axis=2)
+    for i in range(v.shape[0]):
+        w = i // n_z
+        out[i % n_z, w * half : (w + 1) * half] = v[i]
+
+
+def weight_next_kernel(parts, out):
+    v = jnp.sum(parts[...], axis=0)
+    out[...] = v.reshape(out.shape)
 
 
 def weight_sum_kernel(parts, out):
@@ -209,7 +228,8 @@
 
 
 def halve_kernel(bit, pos, a, b, after, *refs):
-    keep, send = refs[-2:]
+    keep, send, token = refs
+    token[...] = jnp.zeros(token.shape, token.dtype)
     mine = (pos[0] >> bit) & 1
     for i in range(keep.shape[0]):
         at, away = 2 * i + mine, 2 * i + 1 - mine
@@ -251,8 +271,16 @@
     blocks = [own] + [fetch(own, k, nx) for k in range(1, nx)]
 
     wide = nw * nz * SLOT
-    (cols,) = call(
-        functools.partial(columns_kernel, block, nz, ny * nx, nc), [((nc * ny * nx, k_dev, wide), bf16)], 1,
+    def halve(bit, a, b, token):
+        n = nz >> (bit + 1)
+        kept, sent, token = call(
+            functools.partial(halve_kernel, bit), [((n, k_dev, lat), f32), ((n, k_dev, lat), bf16), TOKEN], 4,
+            smem=(0,), unused=(3,), flops=8 * n * k_dev * lat, moved=12 * n * k_dev * lat,
+        )(pos, a, b, token)
+        return kept, lax.ppermute(sent, "z", [(i, i ^ (1 << bit)) for i in range(nz)]), token
+
+    cols, token = call(
+        functools.partial(columns_kernel, block, nz, ny * nx, nc), [((nc * ny * nx, k_dev, wide), bf16), TOKEN], 1,
         flops=2 * k_dev * model * 1024, moved=4 * k_dev * model, limit=20,
     )(hidden[0])
     e, dp, st = call(
@@ -260,48 +288,41 @@
         [((n_keys, n_rows), f32)] * 2 + [((4 * nx, rows), f32)], 7, smem=(0,),
         unused=(2,),
         flops=2 * pairs * (width + lat), moved=8 * pairs, limit=20,
-    )(pos, keys, cols, *blocks)
+    )(pos, keys, token, *blocks)
     stats = trade(jnp.broadcast_to(st[None], (nx,) + st.shape), "x")
-    ds, rope_part, mine, other = call(
+    rope_part, mine, other, dq_own, dq_keep, dq_send = call(
         functools.partial(dscores_kernel, lat),
-        [((n_keys, n_rows), bf16), ((nz * ny, k_dev // 2, 2 * rope), bf16)] + [((nz, k_dev, lat), bf16)] * 2,
-        9, smem=(0,), scratch=[pltpu.VMEM((n_keys, n_rows), bf16)],
-        flops=2 * pairs * (rope + 2 * lat), moved=12 * pairs,
-    )(pos, stats, st, e, dp, *blocks)
+        [((nz * ny, k_dev // 2, 2 * rope), bf16)] + [((nz, k_dev, lat), bf16)] * 2
+        + [((rows, width), f32)] * 2 + [((rows, 2 * width), bf16)],
+        10, smem=(0,), scratch=[pltpu.VMEM((n_keys, n_rows), bf16)] * 2,
+        flops=2 * pairs * (2 * width + lat), moved=10 * pairs,
+    )(pos, stats, st, e, dp, *blocks, keys)
     rope_part = trade(rope_part, ("z", "y"))
+    dq_came = lax.ppermute(dq_send, "x", [(0, 1), (1, 0), (2, 3), (3, 2)])
+    dq_own, dq_send, dq_token = call(
+        query_half_kernel, [((rows, width), f32), ((rows, width), bf16), TOKEN], 3, moved=16 * rows * width
+    )(dq_own, dq_keep, dq_came)
+    dq_came = lax.ppermute(dq_send, "x", [(0, 3), (3, 0), (1, 2), (2, 1)])
     other = lax.ppermute(other, "y", swap)
-    dq = call(
-        query_kernel, [((rows, width), f32)] + [((rows, width), bf16)] * (nx - 1), 2,
-        flops=2 * pairs * width, moved=4 * pairs,
-    )(ds, keys)
+    kept, came, token = halve(0, mine, other, token)
     rope_sum, terms = call(
         weight_kernel, [((k_dev, rope), f32), ((nc * ny * nx, rope, wide), bf16)], 4, unused=(2, 3),
-        flops=2 * k_dev * nc * ny * nx * wide * rope, moved=4 * k_dev * model, limit=20,
-    )(rope_part, cols, other, dq[1])
-    after = terms
+        flops=2 * k_dev * nc * ny * nx * wide * rope, moved=4 * k_dev * model,
+    )(rope_part, cols, token, dq_token)
     terms = trade(terms, ("c", "y", "x"))
-    dq = [dq[0]] + [fetch(dq[k], nx - k, nx) for k in range(1, nx)]
-    kept, came = mine, other
-    for bit in range(3):
-        if bit == 2:
-            (terms,) = call(
-                weight_half_kernel, [((nw * nz, SLOT // 2, 2 * rope), f32)], 2, unused=(1,)
-            )(terms, kept)
-            after = terms
-            terms = trade(terms, ("w", "z"))
-        n = nz >> (bit + 1)
-        kept, sent = call(
-            functools.partial(halve_kernel, bit), [((n, k_dev, lat), f32), ((n, k_dev, lat), bf16)], 4,
-            smem=(0,), unused=(3,), flops=8 * n * k_dev * lat, moved=12 * n * k_dev * lat, limit=20,
-        )(pos, kept, came, after)
-        came = lax.ppermute(sent, "z", [(i, i ^ (1 << bit)) for i in range(nz)])
+    kept, came, token = halve(1, kept, came, token)
+    terms, token = call(
+        weight_half_kernel, [((nz, nw * SLOT // 2, 2 * rope), f32), TOKEN], 2, unused=(1,)
+    )(terms, token)
+    terms = trade(terms, "z")
+    kept, came, token = halve(2, kept, came, token)
+    (terms,) = call(weight_next_kernel, [((nw, SLOT // 2, 2 * rope), f32)], 1)(terms)
+    terms = trade(terms, "w")
+    dquery = (dq_own + dq_came.astype(f32)).astype(bf16)
     (dweight,) = call(weight_sum_kernel, [((block, rope), f32)], 1)(terms)
     (dlatent,) = call(latent_sum_kernel, [((k_dev, width), f32)], 3)(kept, came, rope_sum)
 
-    total = dq[0]
-    for part in dq[1:]:
-        total = total + part.astype(f32)
-    return total.astype(bf16).reshape(query.shape), dlatent[None], dweight
+    return dquery.reshape(query.shape), dlatent[None], dweight
 
 
 def solution(mesh):

time: 139 us -> 160 us (1.15); the launches traced: 138 us -> 157 us
  waiting for transfers between devices: 29 us -> 49.4 us
    ppermute x3 -> x5, waiting for transfers between devices: 1.9 us -> 12.6 us  [the longest x3 12.6 us: halve(): lax.ppermute(sent, 'z', [(i, i ^ 1 << bit) for i in range(nz)])]
    ppermute x6 -> x3, starting transfers between devices: 19.1 us -> 8.64 us  [fetch(): return lax.ppermute(value, 'x', [(s, (s - offset) % n) for s in range(n)])]
    ppermute x3 -> x5, starting transfers between devices: 12.9 us -> 17.8 us  [the longest x3 13.5 us: halve(): lax.ppermute(sent, 'z', [(i, i ^ 1 << bit) for i in range(nz)])]
    all_to_all x4 -> x5, waiting for transfers between devices: 6.24 us -> 10.7 us  [trade(): return lax.all_to_all(value, axes, 0, 0, tiled=True)]
    all_to_all x4 -> x5, starting transfers between devices: 32.9 us -> 37.2 us  [trade(): return lax.all_to_all(value, axes, 0, 0, tiled=True)]
    ppermute x1, waiting for transfers between devices: 0.01 us -> 4.22 us  [body(): other = lax.ppermute(other, 'y', swap)]
    unnamed x22 -> x26, local copies, waits for them, and re-layouts: 7.12 us -> 8.19 us
    ppermute x6 -> x3, waiting for transfers between devices: 20.9 us -> 21.8 us  [fetch(): return lax.ppermute(value, 'x', [(s, (s - offset) % n) for s in range(n)])]
  transfers between devices with their start and end apart: 14 -> 14, of which waited for: 6 -> 10; matrix products, arithmetic and copies ran while one was open for 1% -> 1% of each run, Pallas kernels for 5% -> 4%
where the time goes in v6:
time: 160 us; the launch traced here: 157 us
  starting transfers between devices  66.9 us (42%)
  waiting for transfers between devices  49.4 us (31%)
  Pallas kernels  20.2 us (13%)
  local copies, waits for them, and re-layouts  10.4 us (6%)
  blocking collectives  8.12 us (5%)
    all_to_all x5, starting transfers between devices, trade(): return lax.all_to_all(value, axes, 0, 0, tiled=True)  37.2 us
    ppermute x3, waiting for transfers between devices, fetch(): return lax.ppermute(value, 'x', [(s, (s - offset) % n) for s in range(n)])  21.8 us
    ppermute x3, starting transfers between devices, halve(): lax.ppermute(sent, 'z', [(i, i ^ 1 << bit) for i in range(nz)])  13.5 us
    ppermute x3, waiting for transfers between devices, halve(): lax.ppermute(sent, 'z', [(i, i ^ 1 << bit) for i in range(nz)])  12.6 us
    all_to_all x5, waiting for transfers between devices, trade(): return lax.all_to_all(value, axes, 0, 0, tiled=True)  10.7 us
    ppermute x3, starting transfers between devices, fetch(): return lax.ppermute(value, 'x', [(s, (s - offset) % n) for s in range(n)])  8.64 us
    unnamed x26, local copies, waits for them, and re-layouts  8.19 us
    all_to_all x1, blocking collectives, trade(): return lax.all_to_all(value, axes, 0, 0, tiled=True)  8.12 us
  transfers between devices with their start and end apart: 14, of which 10 were waited for; matrix products, arithmetic and copies ran while one was open for 1% of the time, Pallas kernels for 4%

profile of v6, /device:TPU:6, one launch (start us, length us, event | category | flops | bytes accessed | tf_op | source)
XLA Modules:
  0.0 156.8 jit_solution(14648205577808751679)
XLA Ops:
  0.7 2.2 %broadcast_in_dim.17 = bf16[16,64,576]{2,1,0:T(8,128)(2,1)} broadcast(bf16[64,576]{1,0:T(8,128)(2,1)} %bitcast.14), dimensions={1,2} | broadcast | bytes 1253376 | tf_op jit(solution)/shard_map/broadcast_in_dim | solution.py:267
  2.8 11.4 %all-to-all-start = ((bf16[16,64,576]{2,1,0:T(8,128)(2,1)}), bf16[16,64,576]{2,1,0:T(8,128)(2,1)S(1)}, u32[]{:S(2)}, u32[]{:S(2)}) async-start(bf16[16,64,576]{2,1,0:T(8,128)(2,1)} %broadcast_in_dim.17), calls=%async_computation | async-start | bytes 2621440 | tf_op jit(solution)/shard_map/all_to_all | solution.py:251
  14.3 2.4 %collective-permute-start.2 = (bf16[256,1152]{1,0:T(8,128)(2,1)S(1)}, bf16[256,1152]{1,0:T(8,128)(2,1)S(1)}, u32[]{:S(2)}, u32[]{:S(2)}) collective-permute-start(bf16[256,1152]{1,0:T(8,128)(2,1)S(1)} %shard_map.68.refs_0_), channel_id=1, source_target_pairs={{0,1},{1,2},{2,3},{3,0},{4,5},{5,6},{6,7},{7,4},{8,9},{9,10},{10,1... | collective-permute-start | bytes 1769480 | tf_op jit(solution)/shard_map/ppermute | solution.py:247
  16.7 4.3 %collective-permute-start.1 = (bf16[256,1152]{1,0:T(8,128)(2,1)S(1)}, bf16[256,1152]{1,0:T(8,128)(2,1)}, u32[]{:S(2)}, u32[]{:S(2)}) collective-permute-start(bf16[256,1152]{1,0:T(8,128)(2,1)S(1)} %shard_map.68.refs_0_), channel_id=1, source_target_pairs={{0,2},{1,3},{2,0},{3,1},{4,6},{5,7},{6,4},{7,5},{8,10},{9,11},{10,... | collective-permute-start | bytes 1769480 | tf_op jit(solution)/shard_map/ppermute | solution.py:247
  21.1 1.9 %collective-permute-start = (bf16[256,1152]{1,0:T(8,128)(2,1)S(1)}, bf16[256,1152]{1,0:T(8,128)(2,1)}, u32[]{:S(2)}, u32[]{:S(2)}) collective-permute-start(bf16[256,1152]{1,0:T(8,128)(2,1)S(1)} %shard_map.68.refs_0_), channel_id=1, source_target_pairs={{0,3},{1,0},{2,1},{3,2},{4,7},{5,4},{6,5},{7,6},{8,11},{9,8},{10,9... | collective-permute-start | bytes 1769480 | tf_op jit(solution)/shard_map/ppermute | solution.py:247
  23.0 1.2 copy-done.10
  24.2 1.3 shard_map.67
  25.5 6.9 %collective-permute-done.2.refs_3_ = bf16[256,1152]{1,0:T(8,128)(2,1)S(1)} collective-permute-done((bf16[256,1152]{1,0:T(8,128)(2,1)S(1)}, bf16[256,1152]{1,0:T(8,128)(2,1)S(1)}, u32[]{:S(2)}, u32[]{:S(2)}) %collective-permute-start.2) | collective-permute-done | bytes 589856 | tf_op jit(solution)/shard_map/ppermute | solution.py:247
  32.5 4.1 %collective-permute-done.1.refs_2_ = bf16[256,1152]{1,0:T(8,128)(2,1)} collective-permute-done((bf16[256,1152]{1,0:T(8,128)(2,1)S(1)}, bf16[256,1152]{1,0:T(8,128)(2,1)}, u32[]{:S(2)}, u32[]{:S(2)}) %collective-permute-start.1) | collective-permute-done | bytes 589856 | tf_op jit(solution)/shard_map/ppermute | solution.py:247
  36.6 10.8 %collective-permute-done.refs_1_ = bf16[256,1152]{1,0:T(8,128)(2,1)} collective-permute-done((bf16[256,1152]{1,0:T(8,128)(2,1)S(1)}, bf16[256,1152]{1,0:T(8,128)(2,1)}, u32[]{:S(2)}, u32[]{:S(2)}) %collective-permute-start) | collective-permute-done | bytes 589856 | tf_op jit(solution)/shard_map/ppermute | solution.py:247
  47.8 4.6 %shard_map.69 = (f32[1024,1024]{1,0:T(8,128)S(1)}, f32[1024,1024]{1,0:T(8,128)S(1)}, f32[16,256]{1,0:T(8,128)S(1)}) custom-call(s32[3]{0:T(128)S(1)} %pad_add_fusion.pos, bf16[16,64,576]{2,1,0:T(8,128)(2,1)S(1)} %all-to-all-done.keys.refs_4_, f32[8,128]{1,0:T(8,128)S(1)} %get-tuple-element.29.after, bf16[256,1152]{1,0:T(8,128)(2,1)S(1)} %shard_map.68.refs_0_, ...), custom_call_target="tpu_custom_call" | custom-call | flops 2281701376 | bytes 8388608 | tf_op jit(solution)/shard_map/pallas_call | solution.py:286
  52.4 8.1 %all_to_all.30.stats = f32[4,16,256]{2,1,0:T(8,128)S(1)} all-to-all(f32[4,16,256]{2,1,0:T(8,128)S(1)} %broadcast_in_dim.18), channel_id=1, replica_groups=mesh['w'=4,'c'=2,'z'=8,'y'=2,'x'=4] {'x'}, dimensions={0} | all-to-all | bytes 131072 | tf_op jit(solution)/shard_map/all_to_all | solution.py:251
  60.5 7.2 %shard_map.70 = (bf16[16,32,128]{2,1,0:T(8,128)(2,1)}, bf16[8,64,512]{2,1,0:T(8,128)(2,1)S(1)}, bf16[8,64,512]{2,1,0:T(8,128)(2,1)}, f32[256,576]{1,0:T(8,128)S(...) custom-call(s32[3]{0:T(128)S(1)} %pad_add_fusion.pos, f32[4,16,256]{2,1,0:T(8,128)S(1)} %all_to_all.30.stats, ...), custom_call_target="tpu_custom_call" | custom-call | flops 3489660928 | bytes 10485760 | tf_op jit(solution)/shard_map/pallas_call | solution.py:293
  70.2 2.3 %collective-permute-start.3 = (bf16[256,1152]{1,0:T(8,128)(2,1)}, bf16[256,1152]{1,0:T(8,128)(2,1)S(1)}, u32[]{:S(2)}, u32[]{:S(2)}) collective-permute-start(bf16[256,1152]{1,0:T(8,128)(2,1)} %get-tuple-element.35), channel_id=1, source_target_pairs={{0,1},{1,0},{2,3},{3,2},{4,5},{5,4},{6,7},{7,6},{8,9},{9,8},{10,11... | collective-permute-start | bytes 1769480 | tf_op jit(solution)/shard_map/ppermute | solution.py:301
  72.5 3.3 %collective-permute-start.5 = (bf16[8,64,512]{2,1,0:T(8,128)(2,1)}, bf16[8,64,512]{2,1,0:T(8,128)(2,1)S(1)}, u32[]{:S(2)}, u32[]{:S(2)}) collective-permute-start(bf16[8,64,512]{2,1,0:T(8,128)(2,1)} %get-tuple-element.39), channel_id=1, source_target_pairs={{0,4},{4,0},{1,5},{5,1},{2,6},{6,2},{3,7},{7,3},{8,12},{12,8},{9,1... | collective-permute-start | bytes 1572872 | tf_op jit(solution)/shard_map/ppermute | solution.py:306
  75.8 6.8 %all-to-all-start.2 = ((bf16[16,32,128]{2,1,0:T(8,128)(2,1)}), bf16[16,32,128]{2,1,0:T(8,128)(2,1)S(1)}, u32[]{:S(2)}, u32[]{:S(2)}) async-start(bf16[16,32,128]{2,1,0:T(8,128)(2,1)} %get-tuple-element.45), calls=%async_computation.2 | async-start | bytes 262144 | tf_op jit(solution)/shard_map/all_to_all | solution.py:251
  82.6 4.2 %collective-permute-done.5.b = bf16[8,64,512]{2,1,0:T(8,128)(2,1)S(1)} collective-permute-done((bf16[8,64,512]{2,1,0:T(8,128)(2,1)}, bf16[8,64,512]{2,1,0:T(8,128)(2,1)S(1)}, u32[]{:S(2)}, u32[]{:S(2)}) %collective-permute-start.5) | collective-permute-done | bytes 524320 | tf_op jit(solution)/shard_map/ppermute | solution.py:306
  89.2 1.1 copy-done.1
  90.3 1.1 copy-done.3
  92.4 1.5 shard_map.74
  94.6 6.8 %all-to-all-start.3 = ((bf16[16,64,512]{2,1,0:T(8,128)(2,1)}), bf16[16,64,512]{2,1,0:T(8,128)(2,1)S(1)}, u32[]{:S(2)}, u32[]{:S(2)}) async-start(bf16[16,64,512]{2,1,0:T(8,128)(2,1)} %get-tuple-element.48), calls=%async_computation.3 | async-start | bytes 2097152 | tf_op jit(solution)/shard_map/all_to_all | solution.py:251
  101.4 2.7 %collective-permute-start.6 = (bf16[4,64,512]{2,1,0:T(8,128)(2,1)}, bf16[4,64,512]{2,1,0:T(8,128)(2,1)S(1)}, u32[]{:S(2)}, u32[]{:S(2)}) collective-permute-start(bf16[4,64,512]{2,1,0:T(8,128)(2,1)} %copy-done.12), channel_id=1, source_target_pairs={{0,8},{8,0},{16,24},{24,16},{32,40},{40,32},{48,56},{56,48},{1,9},... | collective-permute-start | bytes 786440 | tf_op jit(solution)/shard_map/ppermute | solution.py:280
  104.1 2.0 %collective-permute-start.4 = (bf16[256,576]{1,0:T(8,128)(2,1)}, bf16[256,576]{1,0:T(8,128)(2,1)S(1)}, u32[]{:S(2)}, u32[]{:S(2)}) collective-permute-start(bf16[256,576]{1,0:T(8,128)(2,1)} %copy-done.11), channel_id=1, source_target_pairs={{0,3},{3,0},{1,2},{2,1},{4,7},{7,4},{5,6},{6,5},{8,11},{11,8},{9,1... | collective-permute-start | bytes 884744 | tf_op jit(solution)/shard_map/ppermute | solution.py:305
  106.1 5.7 %collective-permute-done.6.b = bf16[4,64,512]{2,1,0:T(8,128)(2,1)S(1)} collective-permute-done((bf16[4,64,512]{2,1,0:T(8,128)(2,1)}, bf16[4,64,512]{2,1,0:T(8,128)(2,1)S(1)}, u32[]{:S(2)}, u32[]{:S(2)}) %collective-permute-start.6) | collective-permute-done | bytes 262176 | tf_op jit(solution)/shard_map/ppermute | solution.py:280
  112.5 3.3 %all-to-all-done.3.parts = bf16[16,64,512]{2,1,0:T(8,128)(2,1)S(1)} async-done(((bf16[16,64,512]{2,1,0:T(8,128)(2,1)}), bf16[16,64,512]{2,1,0:T(8,128)(2,1)S(1)}, u32[]{:S(2)}, u32[]{:S(2)}) %all-to-all-start.3) | async-done | bytes 1048608 | tf_op jit(solution)/shard_map/all_to_all | solution.py:251
  116.7 6.0 %all-to-all-start.4 = ((f32[8,32,128]{2,1,0:T(8,128)}), f32[8,32,128]{2,1,0:T(8,128)S(1)}, u32[]{:S(2)}, u32[]{:S(2)}) async-start(f32[8,32,128]{2,1,0:T(8,128)} %get-tuple-element.54), calls=%async_computation.4 | async-start | bytes 262144 | tf_op jit(solution)/shard_map/all_to_all | solution.py:251
  122.7 4.8 %collective-permute-start.7 = (bf16[2,64,512]{2,1,0:T(8,128)(2,1)S(1)}, bf16[2,64,512]{2,1,0:T(8,128)(2,1)S(1)}, u32[]{:S(2)}, u32[]{:S(2)}) collective-permute-start(bf16[2,64,512]{2,1,0:T(8,128)(2,1)S(1)} %get-tuple-element.44), channel_id=1, source_target_pairs={{0,16},{8,24},{16,0},{24,8},{32,48},{40,56},{48,32},{56,40},{1,17}... | collective-permute-start | bytes 393224 | tf_op jit(solution)/shard_map/ppermute | solution.py:280
  127.5 6.9 %collective-permute-done.7.b = bf16[2,64,512]{2,1,0:T(8,128)(2,1)S(1)} collective-permute-done((bf16[2,64,512]{2,1,0:T(8,128)(2,1)S(1)}, bf16[2,64,512]{2,1,0:T(8,128)(2,1)S(1)}, u32[]{:S(2)}, u32[]{:S(2)}) %collective-permute-start.7) | collective-permute-done | bytes 131104 | tf_op jit(solution)/shard_map/ppermute | solution.py:280
  134.4 1.1 shard_map.76
  135.5 6.0 %collective-permute-start.8 = (bf16[1,64,512]{2,1,0:T(8,128)(2,1)S(1)}, bf16[1,64,512]{2,1,0:T(8,128)(2,1)S(1)}, u32[]{:S(2)}, u32[]{:S(2)}) collective-permute-start(bf16[1,64,512]{2,1,0:T(8,128)(2,1)S(1)} %get-tuple-element.52), channel_id=1, source_target_pairs={{0,32},{8,40},{16,48},{24,56},{32,0},{40,8},{48,16},{56,24},{1,33}... | collective-permute-start | bytes 196616 | tf_op jit(solution)/shard_map/ppermute | solution.py:280
  142.1 6.2 %all-to-all-start.5 = ((f32[4,8,128]{2,1,0:T(8,128)}), f32[4,8,128]{2,1,0:T(8,128)S(1)}, u32[]{:S(2)}, u32[]{:S(2)}) async-start(f32[4,8,128]{2,1,0:T(8,128)} %shard_map.78), calls=%async_computation.5 | async-start | bytes 32768 | tf_op jit(solution)/shard_map/all_to_all | solution.py:251
  149.8 6.3 %all-to-all-done.5.parts = f32[4,8,128]{2,1,0:T(8,128)S(1)} async-done(((f32[4,8,128]{2,1,0:T(8,128)}), f32[4,8,128]{2,1,0:T(8,128)S(1)}, u32[]{:S(2)}, u32[]{:S(2)}) %all-to-all-start.5) | async-done | bytes 16416 | tf_op jit(solution)/shard_map/all_to_all | solution.py:251
  (40 shorter events, 11.4 us)
Async XLA Ops:
  0.6 13.6 %copy-start.7 = (bf16[1,4,64,512]{3,2,1,0:T(8,128)(2,1)S(1)}, bf16[1,4,64,512]{3,2,1,0:T(8,128)(2,1)}, u32[]{:S(2)}) copy-start(bf16[1,4,64,512]{3,2,1,0:T(8,128)(2,1)} %param.6) | copy-start | bytes 786436
  0.6 13.6 %copy-start.6 = (bf16[1,4,64,576]{3,2,1,0:T(8,128)(2,1)S(1)}, bf16[1,4,64,576]{3,2,1,0:T(8,128)(2,1)}, u32[]{:S(2)}) copy-start(bf16[1,4,64,576]{3,2,1,0:T(8,128)(2,1)} %param.4) | copy-start | bytes 884740
  2.8 45.0 %all-to-all-start = ((bf16[16,64,576]{2,1,0:T(8,128)(2,1)}), bf16[16,64,576]{2,1,0:T(8,128)(2,1)S(1)}, u32[]{:S(2)}, u32[]{:S(2)}) async-start(bf16[16,64,576]{2,1,0:T(8,128)(2,1)} %broadcast_in_dim.17), calls=%async_computation | async-start | bytes 2621440 | tf_op jit(solution)/shard_map/all_to_all | solution.py:251
  14.3 18.1 %collective-permute-start.2 = (bf16[256,1152]{1,0:T(8,128)(2,1)S(1)}, bf16[256,1152]{1,0:T(8,128)(2,1)S(1)}, u32[]{:S(2)}, u32[]{:S(2)}) collective-permute-start(bf16[256,1152]{1,0:T(8,128)(2,1)S(1)} %shard_map.68.refs_0_), channel_id=1, source_target_pairs={{0,1},{1,2},{2,3},{3,0},{4,5},{5,6},{6,7},{7,4},{8,9},{9,10},{10,1... | collective-permute-start | bytes 1769480 | tf_op jit(solution)/shard_map/ppermute | solution.py:247
  16.7 19.8 %collective-permute-start.1 = (bf16[256,1152]{1,0:T(8,128)(2,1)S(1)}, bf16[256,1152]{1,0:T(8,128)(2,1)}, u32[]{:S(2)}, u32[]{:S(2)}) collective-permute-start(bf16[256,1152]{1,0:T(8,128)(2,1)S(1)} %shard_map.68.refs_0_), channel_id=1, source_target_pairs={{0,2},{1,3},{2,0},{3,1},{4,6},{5,7},{6,4},{7,5},{8,10},{9,11},{10,... | collective-permute-start | bytes 1769480 | tf_op jit(solution)/shard_map/ppermute | solution.py:247
  21.1 26.3 %collective-permute-start = (bf16[256,1152]{1,0:T(8,128)(2,1)S(1)}, bf16[256,1152]{1,0:T(8,128)(2,1)}, u32[]{:S(2)}, u32[]{:S(2)}) collective-permute-start(bf16[256,1152]{1,0:T(8,128)(2,1)S(1)} %shard_map.68.refs_0_), channel_id=1, source_target_pairs={{0,3},{1,0},{2,1},{3,2},{4,7},{5,4},{6,5},{7,6},{8,11},{9,8},{10,9... | collective-permute-start | bytes 1769480 | tf_op jit(solution)/shard_map/ppermute | solution.py:247
  23.0 1.2 copy-start.10
  67.7 0.9 copy-start
  68.6 0.8 copy-start.2
  69.4 0.8 copy-start.4
  70.2 18.3 %collective-permute-start.3 = (bf16[256,1152]{1,0:T(8,128)(2,1)}, bf16[256,1152]{1,0:T(8,128)(2,1)S(1)}, u32[]{:S(2)}, u32[]{:S(2)}) collective-permute-start(bf16[256,1152]{1,0:T(8,128)(2,1)} %get-tuple-element.35), channel_id=1, source_target_pairs={{0,1},{1,0},{2,3},{3,2},{4,5},{5,4},{6,7},{7,6},{8,9},{9,8},{10,11... | collective-permute-start | bytes 1769480 | tf_op jit(solution)/shard_map/ppermute | solution.py:301
  72.5 14.3 %collective-permute-start.5 = (bf16[8,64,512]{2,1,0:T(8,128)(2,1)}, bf16[8,64,512]{2,1,0:T(8,128)(2,1)S(1)}, u32[]{:S(2)}, u32[]{:S(2)}) collective-permute-start(bf16[8,64,512]{2,1,0:T(8,128)(2,1)} %get-tuple-element.39), channel_id=1, source_target_pairs={{0,4},{4,0},{1,5},{5,1},{2,6},{6,2},{3,7},{7,3},{8,12},{12,8},{9,1... | collective-permute-start | bytes 1572872 | tf_op jit(solution)/shard_map/ppermute | solution.py:306
  75.8 16.6 %all-to-all-start.2 = ((bf16[16,32,128]{2,1,0:T(8,128)(2,1)}), bf16[16,32,128]{2,1,0:T(8,128)(2,1)S(1)}, u32[]{:S(2)}, u32[]{:S(2)}) async-start(bf16[16,32,128]{2,1,0:T(8,128)(2,1)} %get-tuple-element.45), calls=%async_computation.2 | async-start | bytes 262144 | tf_op jit(solution)/shard_map/all_to_all | solution.py:251
  86.8 1.0 copy-start.5
  88.5 0.7 copy-start.12
  89.2 1.1 copy-start.1
  90.3 1.1 copy-start.3
  91.6 2.9 %copy-start.11 = (bf16[256,576]{1,0:T(8,128)(2,1)}, bf16[256,576]{1,0:T(8,128)(2,1)S(1)}, u32[]{:S(2)}) copy-start(bf16[256,576]{1,0:T(8,128)(2,1)S(1)} %get-tuple-element.37) | copy-start | bytes 884740
  93.9 0.6 copy-start.8
  94.6 54.6 %copy-start.9 = (f32[64,64]{1,0:T(8,128)S(1)}, f32[64,64]{1,0:T(8,128)}, u32[]{:S(2)}) copy-start(f32[64,64]{1,0:T(8,128)} %copy-done.8) | copy-start | bytes 49156
  94.6 21.2 %all-to-all-start.3 = ((bf16[16,64,512]{2,1,0:T(8,128)(2,1)}), bf16[16,64,512]{2,1,0:T(8,128)(2,1)S(1)}, u32[]{:S(2)}, u32[]{:S(2)}) async-start(bf16[16,64,512]{2,1,0:T(8,128)(2,1)} %get-tuple-element.48), calls=%async_computation.3 | async-start | bytes 2097152 | tf_op jit(solution)/shard_map/all_to_all | solution.py:251
  101.4 10.5 %collective-permute-start.6 = (bf16[4,64,512]{2,1,0:T(8,128)(2,1)}, bf16[4,64,512]{2,1,0:T(8,128)(2,1)S(1)}, u32[]{:S(2)}, u32[]{:S(2)}) collective-permute-start(bf16[4,64,512]{2,1,0:T(8,128)(2,1)} %copy-done.12), channel_id=1, source_target_pairs={{0,8},{8,0},{16,24},{24,16},{32,40},{40,32},{48,56},{56,48},{1,9},... | collective-permute-start | bytes 786440 | tf_op jit(solution)/shard_map/ppermute | solution.py:280
  104.1 44.2 %collective-permute-start.4 = (bf16[256,576]{1,0:T(8,128)(2,1)}, bf16[256,576]{1,0:T(8,128)(2,1)S(1)}, u32[]{:S(2)}, u32[]{:S(2)}) collective-permute-start(bf16[256,576]{1,0:T(8,128)(2,1)} %copy-done.11), channel_id=1, source_target_pairs={{0,3},{3,0},{1,2},{2,1},{4,7},{7,4},{5,6},{6,5},{8,11},{11,8},{9,1... | collective-permute-start | bytes 884744 | tf_op jit(solution)/shard_map/ppermute | solution.py:305
  116.7 24.8 %all-to-all-start.4 = ((f32[8,32,128]{2,1,0:T(8,128)}), f32[8,32,128]{2,1,0:T(8,128)S(1)}, u32[]{:S(2)}, u32[]{:S(2)}) async-start(f32[8,32,128]{2,1,0:T(8,128)} %get-tuple-element.54), calls=%async_computation.4 | async-start | bytes 262144 | tf_op jit(solution)/shard_map/all_to_all | solution.py:251
  122.7 11.7 %collective-permute-start.7 = (bf16[2,64,512]{2,1,0:T(8,128)(2,1)S(1)}, bf16[2,64,512]{2,1,0:T(8,128)(2,1)S(1)}, u32[]{:S(2)}, u32[]{:S(2)}) collective-permute-start(bf16[2,64,512]{2,1,0:T(8,128)(2,1)S(1)} %get-tuple-element.44), channel_id=1, source_target_pairs={{0,16},{8,24},{16,0},{24,8},{32,48},{40,56},{48,32},{56,40},{1,17}... | collective-permute-start | bytes 393224 | tf_op jit(solution)/shard_map/ppermute | solution.py:280
  135.5 13.6 %collective-permute-start.8 = (bf16[1,64,512]{2,1,0:T(8,128)(2,1)S(1)}, bf16[1,64,512]{2,1,0:T(8,128)(2,1)S(1)}, u32[]{:S(2)}, u32[]{:S(2)}) collective-permute-start(bf16[1,64,512]{2,1,0:T(8,128)(2,1)S(1)} %get-tuple-element.52), channel_id=1, source_target_pairs={{0,32},{8,40},{16,48},{24,56},{32,0},{40,8},{48,16},{56,24},{1,33}... | collective-permute-start | bytes 196616 | tf_op jit(solution)/shard_map/ppermute | solution.py:280
  142.1 14.0 %all-to-all-start.5 = ((f32[4,8,128]{2,1,0:T(8,128)}), f32[4,8,128]{2,1,0:T(8,128)S(1)}, u32[]{:S(2)}, u32[]{:S(2)}) async-start(f32[4,8,128]{2,1,0:T(8,128)} %shard_map.78), calls=%async_computation.5 | async-start | bytes 32768 | tf_op jit(solution)/shard_map/all_to_all | solution.py:251

commit v7 on v5

--- a/solution.py
+++ b/solution.py
@@ -10,6 +10,7 @@
 softmax_scale = 0.07216878364870323
 f32, bf16 = jnp.float32, jnp.bfloat16
 TILE = 256
+TOKEN = ((8, 128), jnp.float32)
 SLOT = 16
 
 
@@ -25,7 +26,7 @@
     return lax.dot_general(a, b, (((0,), (0,)), ((), ())), preferred_element_type=f32)
 
 
-def call(kernel, outs, n_in, smem=(), unused=(), scratch=(), flops=0, moved=0, limit=20):
+def call(kernel, outs, n_in, smem=(), unused=(), scratch=(), flops=0, moved=0, in_hbm=False, limit=20):
     vmem = pl.BlockSpec(memory_space=pltpu.VMEM)
     specs = [
         pl.BlockSpec(memory_space=pltpu.SMEM)
@@ -35,9 +36,9 @@
     ]
     return pl.pallas_call(
         kernel,
-        out_shape=[jax.ShapeDtypeStruct(s, d) for s, d in outs],
+        out_shape=[pltpu.HBM(s, d) if in_hbm else jax.ShapeDtypeStruct(s, d) for s, d in outs],
         in_specs=specs,
-        out_specs=[vmem] * len(outs),
+        out_specs=[pl.BlockSpec(memory_space=pltpu.HBM) if in_hbm else vmem] * len(outs),
         scratch_shapes=scratch,
         compiler_params=pltpu.CompilerParams(vmem_limit_bytes=limit * 2**20),
         cost_estimate=pl.CostEstimate(flops=flops, bytes_accessed=moved, transcendentals=0),
@@ -52,7 +53,8 @@
     out[:, lat + width :] = jnp.zeros((out.shape[0], out.shape[1] - lat - width), out.dtype)
 
 
-def columns_kernel(block, n_z, n_grp, n_core, hid, out):
+def columns_kernel(block, n_z, n_grp, n_core, hid, out, token):
+    token[...] = jnp.zeros(token.shape, token.dtype)
     k_dev, model = hid.shape
     n_data = model // (n_z * n_grp * block)
     span = n_z * n_grp * block
@@ -118,9 +120,11 @@
 
 
 def dscores_kernel(lat, pos, stats, st, e_ref, dp_ref, *refs):
-    blocks, (ds_ref, rope_ref, mine, other, p_ref) = refs[:-5], refs[-5:]
+    n_x = stats.shape[0]
+    blocks, outs, (sems, *held) = refs[:n_x], refs[n_x : n_x + 4], refs[n_x + 4 :]
+    ds_ref, rope_ref, mine, other, p_ref = held
+    copies = [pltpu.make_async_copy(held[i], outs[i], sems.at[i]) for i in range(4)]
     y, x = pos[1], pos[2]
-    n_x = len(blocks)
     rows = refs[0].shape[0]
     tiles = e_ref.shape[0] // TILE
     grp, half_keys, _ = rope_ref.shape
@@ -144,6 +148,7 @@
             p = e_ref[part, cols] * f
             p_ref[part, cols] = p.astype(bf16)
             ds_ref[part, cols] = (p * (dp_ref[part, cols] - delta)).astype(bf16)
+    copies[0].start()
     for i in range(tiles):
         part = slice(i * TILE, (i + 1) * TILE)
         r = None
@@ -155,6 +160,7 @@
         for j in range(TILE // k_dev):
             k = r[j * k_dev : (j + 1) * k_dev]
             rope_ref[i * (TILE // k_dev) + j] = jnp.concatenate([k[:half_keys], k[half_keys:]], axis=1)
+    copies[1].start()
     per = TILE // k_dev
     for i in range(tiles):
         part = slice(i * TILE, (i + 1) * TILE)
@@ -169,9 +175,14 @@
         first = i * per // 2
         for out, side in ((mine, y), (other, 1 - y)):
             out[first : first + per // 2] = jnp.where(side == 0, v[:, 0], v[:, 1])
-
-
-def query_kernel(ds_ref, keys, *outs):
+    copies[2].start()
+    copies[3].start()
+    for copy in copies:
+        copy.wait()
+
+
+def query_kernel(ds_ref, keys, token, *outs):
+    token[...] = jnp.zeros(token.shape, token.dtype)
     rows = outs[0].shape[0]
     per = TILE // keys.shape[1]
     for b, out in enumerate(outs):
@@ -195,7 +206,8 @@
         out[i] = tn(low, cols[i]).astype(bf16)
 
 
-def weight_half_kernel(parts, after, out):
+def weight_half_kernel(parts, after, out, token):
+    token[...] = jnp.zeros(token.shape, token.dtype)
     v = jnp.sum(parts[...].astype(f32), axis=0)
     v = jnp.swapaxes(v, 0, 1)
     v = v.reshape(v.shape[0] // SLOT, SLOT, v.shape[1])
@@ -209,7 +221,8 @@
 
 
 def halve_kernel(bit, pos, a, b, after, *refs):
-    keep, send = refs[-2:]
+    keep, send, token = refs
+    token[...] = jnp.zeros(token.shape, token.dtype)
     mine = (pos[0] >> bit) & 1
     for i in range(keep.shape[0]):
         at, away = 2 * i + mine, 2 * i + 1 - mine
@@ -251,8 +264,8 @@
     blocks = [own] + [fetch(own, k, nx) for k in range(1, nx)]
 
     wide = nw * nz * SLOT
-    (cols,) = call(
-        functools.partial(columns_kernel, block, nz, ny * nx, nc), [((nc * ny * nx, k_dev, wide), bf16)], 1,
+    cols, token = call(
+        functools.partial(columns_kernel, block, nz, ny * nx, nc), [((nc * ny * nx, k_dev, wide), bf16), TOKEN], 1,
         flops=2 * k_dev * model * 1024, moved=4 * k_dev * model, limit=20,
     )(hidden[0])
     e, dp, st = call(
@@ -260,40 +273,46 @@
         [((n_keys, n_rows), f32)] * 2 + [((4 * nx, rows), f32)], 7, smem=(0,),
         unused=(2,),
         flops=2 * pairs * (width + lat), moved=8 * pairs, limit=20,
-    )(pos, keys, cols, *blocks)
+    )(pos, keys, token, *blocks)
     stats = trade(jnp.broadcast_to(st[None], (nx,) + st.shape), "x")
     ds, rope_part, mine, other = call(
         functools.partial(dscores_kernel, lat),
         [((n_keys, n_rows), bf16), ((nz * ny, k_dev // 2, 2 * rope), bf16)] + [((nz, k_dev, lat), bf16)] * 2,
-        9, smem=(0,), scratch=[pltpu.VMEM((n_keys, n_rows), bf16)],
+        9, smem=(0,), in_hbm=True,
+        scratch=[
+            pltpu.SemaphoreType.DMA((4,)),
+            pltpu.VMEM((n_keys, n_rows), bf16),
+            pltpu.VMEM((nz * ny, k_dev // 2, 2 * rope), bf16),
+            pltpu.VMEM((nz, k_dev, lat), bf16),
+            pltpu.VMEM((nz, k_dev, lat), bf16),
+            pltpu.VMEM((n_keys, n_rows), bf16),
+        ],
         flops=2 * pairs * (rope + 2 * lat), moved=12 * pairs,
     )(pos, stats, st, e, dp, *blocks)
     rope_part = trade(rope_part, ("z", "y"))
     other = lax.ppermute(other, "y", swap)
-    dq = call(
-        query_kernel, [((rows, width), f32)] + [((rows, width), bf16)] * (nx - 1), 2,
+    dq_token, *dq = call(
+        query_kernel, [TOKEN, ((rows, width), f32)] + [((rows, width), bf16)] * (nx - 1), 2,
         flops=2 * pairs * width, moved=4 * pairs,
     )(ds, keys)
     rope_sum, terms = call(
         weight_kernel, [((k_dev, rope), f32), ((nc * ny * nx, rope, wide), bf16)], 4, unused=(2, 3),
         flops=2 * k_dev * nc * ny * nx * wide * rope, moved=4 * k_dev * model, limit=20,
-    )(rope_part, cols, other, dq[1])
-    after = terms
+    )(rope_part, cols, other, dq_token)
     terms = trade(terms, ("c", "y", "x"))
     dq = [dq[0]] + [fetch(dq[k], nx - k, nx) for k in range(1, nx)]
     kept, came = mine, other
     for bit in range(3):
         if bit == 2:
-            (terms,) = call(
-                weight_half_kernel, [((nw * nz, SLOT // 2, 2 * rope), f32)], 2, unused=(1,)
-            )(terms, kept)
-            after = terms
+            terms, token = call(
+                weight_half_kernel, [((nw * nz, SLOT // 2, 2 * rope), f32), TOKEN], 2, unused=(1,)
+            )(terms, token)
             terms = trade(terms, ("w", "z"))
         n = nz >> (bit + 1)
-        kept, sent = call(
-            functools.partial(halve_kernel, bit), [((n, k_dev, lat), f32), ((n, k_dev, lat), bf16)], 4,
+        kept, sent, token = call(
+            functools.partial(halve_kernel, bit), [((n, k_dev, lat), f32), ((n, k_dev, lat), bf16), TOKEN], 4,
             smem=(0,), unused=(3,), flops=8 * n * k_dev * lat, moved=12 * n * k_dev * lat, limit=20,
-        )(pos, kept, came, after)
+        )(pos, kept, came, token)
         came = lax.ppermute(sent, "z", [(i, i ^ (1 << bit)) for i in range(nz)])
     (dweight,) = call(weight_sum_kernel, [((block, rope), f32)], 1)(terms)
     (dlatent,) = call(latent_sum_kernel, [((k_dev, width), f32)], 3)(kept, came, rope_sum)

time: 139 us -> 137 us (0.986)
  the two profiles are of different devices: /device:TPU:6 before, /device:TPU:40 now
where the time goes in v7:
time: 137 us; the launch traced here: 136 us
  starting transfers between devices  71.4 us (52%)
  waiting for transfers between devices  23.7 us (17%)
  Pallas kernels  20.6 us (15%)
  blocking collectives  9.72 us (7%)
  local copies, waits for them, and re-layouts  8.08 us (6%)
  other arithmetic  2.02 us (1%)
    all_to_all x4, starting transfers between devices, trade(): return lax.all_to_all(value, axes, 0, 0, tiled=True)  33.6 us
    ppermute x6, starting transfers between devices, fetch(): return lax.ppermute(value, 'x', [(s, (s - offset) % n) for s in range(n)])  22.7 us
    ppermute x6, waiting for transfers between devices, fetch(): return lax.ppermute(value, 'x', [(s, (s - offset) % n) for s in range(n)])  18 us
    ppermute x3, starting transfers between devices, body(): came = lax.ppermute(sent, 'z', [(i, i ^ 1 << bit) for i in range(nz)])  12.5 us
    all_to_all x1, blocking collectives, trade(): return lax.all_to_all(value, axes, 0, 0, tiled=True)  9.72 us
    pallas_call x1, Pallas kernels, body(): call(functools.partial(dscores_kernel, lat), [((n_keys, n_rows), bf16), (...  5.91 us
    unnamed x20, local copies, waits for them, and re-layouts  5.9 us
    pallas_call x1, Pallas kernels, body(): call(functools.partial(scores_kernel, lat, heads), [((n_keys, n_rows), f3...  4.35 us
  transfers between devices with their start and end apart: 14, of which 5 were waited for; matrix products, arithmetic and copies ran while one was open for 1% of the time, Pallas kernels for 5%

profile of v7, /device:TPU:40, one launch (start us, length us, event | category | flops | bytes accessed | tf_op | source)
XLA Modules:
  0.0 136.4 jit_solution(17059792459394659378)
XLA Ops:
  0.7 2.2 %broadcast_in_dim.17 = bf16[16,64,576]{2,1,0:T(8,128)(2,1)} broadcast(bf16[64,576]{1,0:T(8,128)(2,1)} %bitcast.14), dimensions={1,2} | broadcast | bytes 1253376 | tf_op jit(solution)/shard_map/broadcast_in_dim | solution.py:260
  2.8 11.8 %all-to-all-start = ((bf16[16,64,576]{2,1,0:T(8,128)(2,1)}), bf16[16,64,576]{2,1,0:T(8,128)(2,1)S(1)}, u32[]{:S(2)}, u32[]{:S(2)}) async-start(bf16[16,64,576]{2,1,0:T(8,128)(2,1)} %broadcast_in_dim.17), calls=%async_computation | async-start | bytes 2621440 | tf_op jit(solution)/shard_map/all_to_all | solution.py:244
  14.7 3.4 %collective-permute-start.2 = (bf16[256,1152]{1,0:T(8,128)(2,1)S(1)}, bf16[256,1152]{1,0:T(8,128)(2,1)S(1)}, u32[]{:S(2)}, u32[]{:S(2)}) collective-permute-start(bf16[256,1152]{1,0:T(8,128)(2,1)S(1)} %shard_map.68.refs_0_), channel_id=1, source_target_pairs={{0,1},{1,2},{2,3},{3,0},{4,5},{5,6},{6,7},{7,4},{8,9},{9,10},{10,1... | collective-permute-start | bytes 1769480 | tf_op jit(solution)/shard_map/ppermute | solution.py:240
  18.1 4.6 %collective-permute-start.1 = (bf16[256,1152]{1,0:T(8,128)(2,1)S(1)}, bf16[256,1152]{1,0:T(8,128)(2,1)S(1)}, u32[]{:S(2)}, u32[]{:S(2)}) collective-permute-start(bf16[256,1152]{1,0:T(8,128)(2,1)S(1)} %shard_map.68.refs_0_), channel_id=1, source_target_pairs={{0,2},{1,3},{2,0},{3,1},{4,6},{5,7},{6,4},{7,5},{8,10},{9,11},{10,... | collective-permute-start | bytes 1769480 | tf_op jit(solution)/shard_map/ppermute | solution.py:240
  22.8 3.3 %collective-permute-start = (bf16[256,1152]{1,0:T(8,128)(2,1)S(1)}, bf16[256,1152]{1,0:T(8,128)(2,1)}, u32[]{:S(2)}, u32[]{:S(2)}) collective-permute-start(bf16[256,1152]{1,0:T(8,128)(2,1)S(1)} %shard_map.68.refs_0_), channel_id=1, source_target_pairs={{0,3},{1,0},{2,1},{3,2},{4,7},{5,4},{6,5},{7,6},{8,11},{9,8},{10,9... | collective-permute-start | bytes 1769480 | tf_op jit(solution)/shard_map/ppermute | solution.py:240
  26.1 1.2 copy-done.6
  27.3 1.3 shard_map.67
  28.6 1.0 copy-done
  29.6 3.5 %collective-permute-done.2.refs_3_ = bf16[256,1152]{1,0:T(8,128)(2,1)S(1)} collective-permute-done((bf16[256,1152]{1,0:T(8,128)(2,1)S(1)}, bf16[256,1152]{1,0:T(8,128)(2,1)S(1)}, u32[]{:S(2)}, u32[]{:S(2)}) %collective-permute-start.2) | collective-permute-done | bytes 589856 | tf_op jit(solution)/shard_map/ppermute | solution.py:240
  33.1 12.9 %collective-permute-done.1.refs_2_ = bf16[256,1152]{1,0:T(8,128)(2,1)S(1)} collective-permute-done((bf16[256,1152]{1,0:T(8,128)(2,1)S(1)}, bf16[256,1152]{1,0:T(8,128)(2,1)S(1)}, u32[]{:S(2)}, u32[]{:S(2)}) %collective-permute-start.1) | collective-permute-done | bytes 589856 | tf_op jit(solution)/shard_map/ppermute | solution.py:240
  45.9 1.7 %collective-permute-done.refs_1_ = bf16[256,1152]{1,0:T(8,128)(2,1)} collective-permute-done((bf16[256,1152]{1,0:T(8,128)(2,1)S(1)}, bf16[256,1152]{1,0:T(8,128)(2,1)}, u32[]{:S(2)}, u32[]{:S(2)}) %collective-permute-start) | collective-permute-done | bytes 589856 | tf_op jit(solution)/shard_map/ppermute | solution.py:240
  47.6 4.4 %shard_map.69 = (f32[1024,1024]{1,0:T(8,128)S(1)}, f32[1024,1024]{1,0:T(8,128)S(1)}, f32[16,256]{1,0:T(8,128)S(1)}) custom-call(s32[3]{0:T(128)S(1)} %pad_add_fusion.pos, bf16[16,64,576]{2,1,0:T(8,128)(2,1)S(1)} %all-to-all-done.keys, f32[8,128]{1,0:T(8,128)S(1)} %get-tuple-element.29.after, bf16[256,1152]{1,0:T(8,128)(2,1)S(1)} %shard_map.68.refs_0_, ...), custom_call_target="tpu_custom_call" | custom-call | flops 2281701376 | bytes 8388608 | tf_op jit(solution)/shard_map/pallas_call | solution.py:271
  52.0 9.7 %all_to_all.25.stats = f32[4,16,256]{2,1,0:T(8,128)S(1)} all-to-all(f32[4,16,256]{2,1,0:T(8,128)S(1)} %broadcast_in_dim.18), channel_id=1, replica_groups=mesh['w'=4,'c'=2,'z'=8,'y'=2,'x'=4] {'x'}, dimensions={0} | all-to-all | bytes 131072 | tf_op jit(solution)/shard_map/all_to_all | solution.py:244
  61.7 5.9 %shard_map.70 = (bf16[1024,1024]{1,0:T(8,128)(2,1)}, bf16[16,32,128]{2,1,0:T(8,128)(2,1)}, bf16[8,64,512]{2,1,0:T(8,128)(2,1)}, bf16[8,64,512]{2,1,0:T(8,128)(2,1)}) custom-call(s32[3]{0:T(128)S(1)} %pad_add_fusion.pos, f32[4,16,256]{2,1,0:T(8,128)S(1)} %all_to_all.25.stats, f32[16,256]{1,0:T(8,128)S(1)} %get-tuple-element.30.st, ...), custom_call_target="tpu_custom_call" | custom-call | flops 2281701376 | bytes 12582912 | tf_op jit(solution)/shard_map/pallas_call | solution.py:278
  67.6 2.5 %collective-permute-start.6 = (bf16[8,64,512]{2,1,0:T(8,128)(2,1)}, bf16[8,64,512]{2,1,0:T(8,128)(2,1)S(1)}, u32[]{:S(2)}, u32[]{:S(2)}) collective-permute-start(bf16[8,64,512]{2,1,0:T(8,128)(2,1)} %get-tuple-element.39), channel_id=1, source_target_pairs={{0,4},{4,0},{1,5},{5,1},{2,6},{6,2},{3,7},{7,3},{8,12},{12,8},{9,1... | collective-permute-start | bytes 1572872 | tf_op jit(solution)/shard_map/ppermute | solution.py:293
  70.2 8.1 %all-to-all-start.2 = ((bf16[16,32,128]{2,1,0:T(8,128)(2,1)}), bf16[16,32,128]{2,1,0:T(8,128)(2,1)}, u32[]{:S(2)}, u32[]{:S(2)}) async-start(bf16[16,32,128]{2,1,0:T(8,128)(2,1)} %get-tuple-element.45), calls=%async_computation.2 | async-start | bytes 262144 | tf_op jit(solution)/shard_map/all_to_all | solution.py:244
  78.2 1.6 %copy-done.5 = bf16[1024,1024]{1,0:T(8,128)(2,1)S(1)} copy-done((bf16[1024,1024]{1,0:T(8,128)(2,1)S(1)}, bf16[1024,1024]{1,0:T(8,128)(2,1)}, u32[]{:S(2)}) %copy-start.5) | copy-done | bytes 2097176
  79.8 1.8 %shard_map.71 = (f32[8,128]{1,0:T(8,128)S(1)}, f32[256,576]{1,0:T(8,128)S(1)}, bf16[256,576]{1,0:T(8,128)(2,1)S(1)}, bf16[256,576]{1,0:T(8,128)(2,1)S(1)}, bf16[256,576]{1,0:T(8,128)(2,1)S(1)}) custom-call(bf16[1024,1024]{1,0:T(8,128)(2,1)S(1)} %copy-done.5, bf16[16,64,576]{2,1,0:T(8,128)(2,1)S(1)} %all-to-all-done.keys), custom_call_target="tpu_custom_call" | custom-call | flops 1207959552 | bytes 4194304 | tf_op jit(solution)/shard_map/pallas_call | solution.py:294
  83.8 4.2 %all-to-all-done.2.parts = bf16[16,32,128]{2,1,0:T(8,128)(2,1)} async-done(((bf16[16,32,128]{2,1,0:T(8,128)(2,1)}), bf16[16,32,128]{2,1,0:T(8,128)(2,1)}, u32[]{:S(2)}, u32[]{:S(2)}) %all-to-all-start.2) | async-done | bytes 131104 | tf_op jit(solution)/shard_map/all_to_all | solution.py:244
  88.0 2.4 %shard_map.74 = (f32[64,64]{1,0:T(8,128)S(1)}, bf16[16,64,512]{2,1,0:T(8,128)(2,1)}) custom-call(bf16[16,32,128]{2,1,0:T(8,128)(2,1)} %all-to-all-done.2.parts, bf16[16,64,512]{2,1,0:T(8,128)(2,1)S(1)} %copy-done.1, bf16[8,64,512]{2,1,0:T(8,128)(2,1)S(1)} %collective-permute-done.6.b.after, f32[8,128]{1,0:T(8,128)S(1)} %get-tuple-element.47.after2), custom_call_target="tpu_custom_call" | custom-call | flops 67108864 | bytes 1835008 | tf_op jit(solution)/shard_map/pallas_call | solution.py:298
  90.5 4.0 %all-to-all-start.3 = ((bf16[16,64,512]{2,1,0:T(8,128)(2,1)}), bf16[16,64,512]{2,1,0:T(8,128)(2,1)S(1)}, u32[]{:S(2)}, u32[]{:S(2)}) async-start(bf16[16,64,512]{2,1,0:T(8,128)(2,1)} %get-tuple-element.48), calls=%async_computation.3 | async-start | bytes 2097152 | tf_op jit(solution)/shard_map/all_to_all | solution.py:244
  95.2 2.5 %collective-permute-start.7 = (bf16[4,64,512]{2,1,0:T(8,128)(2,1)S(1)}, bf16[4,64,512]{2,1,0:T(8,128)(2,1)S(1)}, u32[]{:S(2)}, u32[]{:S(2)}) collective-permute-start(bf16[4,64,512]{2,1,0:T(8,128)(2,1)S(1)} %get-tuple-element.41), channel_id=1, source_target_pairs={{0,8},{8,0},{16,24},{24,16},{32,40},{40,32},{48,56},{56,48},{1,9},... | collective-permute-start | bytes 786440 | tf_op jit(solution)/shard_map/ppermute | solution.py:316
  97.6 3.4 %collective-permute-start.3 = (bf16[256,576]{1,0:T(8,128)(2,1)}, bf16[256,576]{1,0:T(8,128)(2,1)S(1)}, u32[]{:S(2)}, u32[]{:S(2)}) collective-permute-start(bf16[256,576]{1,0:T(8,128)(2,1)} %copy-done.9), channel_id=1, source_target_pairs={{0,1},{1,2},{2,3},{3,0},{4,5},{5,6},{6,7},{7,4},{8,9},{9,10},{10,1... | collective-permute-start | bytes 884744 | tf_op jit(solution)/shard_map/ppermute | solution.py:240
  101.0 4.6 %collective-permute-start.4 = (bf16[256,576]{1,0:T(8,128)(2,1)}, bf16[256,576]{1,0:T(8,128)(2,1)}, u32[]{:S(2)}, u32[]{:S(2)}) collective-permute-start(bf16[256,576]{1,0:T(8,128)(2,1)} %copy-done.8), channel_id=1, source_target_pairs={{0,2},{1,3},{2,0},{3,1},{4,6},{5,7},{6,4},{7,5},{8,10},{9,11},{10,... | collective-permute-start | bytes 884744 | tf_op jit(solution)/shard_map/ppermute | solution.py:240
  105.6 3.4 %collective-permute-start.5 = (bf16[256,576]{1,0:T(8,128)(2,1)}, bf16[256,576]{1,0:T(8,128)(2,1)}, u32[]{:S(2)}, u32[]{:S(2)}) collective-permute-start(bf16[256,576]{1,0:T(8,128)(2,1)} %copy-done.7), channel_id=1, source_target_pairs={{0,3},{1,0},{2,1},{3,2},{4,7},{5,4},{6,5},{7,6},{8,11},{9,8},{10,9... | collective-permute-start | bytes 884744 | tf_op jit(solution)/shard_map/ppermute | solution.py:240
  109.6 2.8 %collective-permute-start.8 = (bf16[2,64,512]{2,1,0:T(8,128)(2,1)S(1)}, bf16[2,64,512]{2,1,0:T(8,128)(2,1)S(1)}, u32[]{:S(2)}, u32[]{:S(2)}) collective-permute-start(bf16[2,64,512]{2,1,0:T(8,128)(2,1)S(1)} %get-tuple-element.44), channel_id=1, source_target_pairs={{0,16},{8,24},{16,0},{24,8},{32,48},{40,56},{48,32},{56,40},{1,17}... | collective-permute-start | bytes 393224 | tf_op jit(solution)/shard_map/ppermute | solution.py:316
  112.4 1.0 shard_map.75
  113.4 9.8 %all-to-all-start.4 = ((f32[32,8,128]{2,1,0:T(8,128)}), f32[32,8,128]{2,1,0:T(8,128)S(1)}, u32[]{:S(2)}, u32[]{:S(2)}) async-start(f32[32,8,128]{2,1,0:T(8,128)} %get-tuple-element.54), calls=%async_computation.4 | async-start | bytes 262144 | tf_op jit(solution)/shard_map/all_to_all | solution.py:244
  123.1 1.1 shard_map.76
  124.3 7.3 %collective-permute-start.9 = (bf16[1,64,512]{2,1,0:T(8,128)(2,1)S(1)}, bf16[1,64,512]{2,1,0:T(8,128)(2,1)S(1)}, u32[]{:S(2)}, u32[]{:S(2)}) collective-permute-start(bf16[1,64,512]{2,1,0:T(8,128)(2,1)S(1)} %get-tuple-element.52), channel_id=1, source_target_pairs={{0,32},{8,40},{16,48},{24,56},{32,0},{40,8},{48,16},{56,24},{1,33}... | collective-permute-start | bytes 196616 | tf_op jit(solution)/shard_map/ppermute | solution.py:316
  131.6 1.9 %add_convert_fusion = bf16[256,576]{1,0:T(8,128)(2,1)} fusion(bf16[256,576]{1,0:T(8,128)(2,1)} %collective-permute-done.5, bf16[256,576]{1,0:T(8,128)(2,1)} %collective-permute-done.4, f32[256,576]{1,0:T(8,128)S(1)} %get-tuple-element.34, bf16[256,576]{1,0:T(8,128)(2,1)S(1)} %collective-permute-done.3), kind=kLoop, calls=%fused_computation | loop fusion | flops 1032192 | bytes 1769472 | tf_op jit(solution)/shard_map/convert_element_type | solution.py:323
  133.5 1.5 %collective-permute-done.9.b = bf16[1,64,512]{2,1,0:T(8,128)(2,1)S(1)} collective-permute-done((bf16[1,64,512]{2,1,0:T(8,128)(2,1)S(1)}, bf16[1,64,512]{2,1,0:T(8,128)(2,1)S(1)}, u32[]{:S(2)}, u32[]{:S(2)}) %collective-permute-start.9) | collective-permute-done | bytes 65568 | tf_op jit(solution)/shard_map/ppermute | solution.py:316
  (33 shorter events, 5.0 us)
Async XLA Ops:
  0.6 14.0 %copy-start.4 = (bf16[1,4,64,512]{3,2,1,0:T(8,128)(2,1)S(1)}, bf16[1,4,64,512]{3,2,1,0:T(8,128)(2,1)}, u32[]{:S(2)}) copy-start(bf16[1,4,64,512]{3,2,1,0:T(8,128)(2,1)} %param.6) | copy-start | bytes 786436
  0.6 14.0 %copy-start.3 = (bf16[1,4,64,576]{3,2,1,0:T(8,128)(2,1)S(1)}, bf16[1,4,64,576]{3,2,1,0:T(8,128)(2,1)}, u32[]{:S(2)}) copy-start(bf16[1,4,64,576]{3,2,1,0:T(8,128)(2,1)} %param.4) | copy-start | bytes 884740
  2.8 44.8 %all-to-all-start = ((bf16[16,64,576]{2,1,0:T(8,128)(2,1)}), bf16[16,64,576]{2,1,0:T(8,128)(2,1)S(1)}, u32[]{:S(2)}, u32[]{:S(2)}) async-start(bf16[16,64,576]{2,1,0:T(8,128)(2,1)} %broadcast_in_dim.17), calls=%async_computation | async-start | bytes 2621440 | tf_op jit(solution)/shard_map/all_to_all | solution.py:244
  14.7 18.4 %collective-permute-start.2 = (bf16[256,1152]{1,0:T(8,128)(2,1)S(1)}, bf16[256,1152]{1,0:T(8,128)(2,1)S(1)}, u32[]{:S(2)}, u32[]{:S(2)}) collective-permute-start(bf16[256,1152]{1,0:T(8,128)(2,1)S(1)} %shard_map.68.refs_0_), channel_id=1, source_target_pairs={{0,1},{1,2},{2,3},{3,0},{4,5},{5,6},{6,7},{7,4},{8,9},{9,10},{10,1... | collective-permute-start | bytes 1769480 | tf_op jit(solution)/shard_map/ppermute | solution.py:240
  18.1 27.8 %collective-permute-start.1 = (bf16[256,1152]{1,0:T(8,128)(2,1)S(1)}, bf16[256,1152]{1,0:T(8,128)(2,1)S(1)}, u32[]{:S(2)}, u32[]{:S(2)}) collective-permute-start(bf16[256,1152]{1,0:T(8,128)(2,1)S(1)} %shard_map.68.refs_0_), channel_id=1, source_target_pairs={{0,2},{1,3},{2,0},{3,1},{4,6},{5,7},{6,4},{7,5},{8,10},{9,11},{10,... | collective-permute-start | bytes 1769480 | tf_op jit(solution)/shard_map/ppermute | solution.py:240
  22.8 24.8 %collective-permute-start = (bf16[256,1152]{1,0:T(8,128)(2,1)S(1)}, bf16[256,1152]{1,0:T(8,128)(2,1)}, u32[]{:S(2)}, u32[]{:S(2)}) collective-permute-start(bf16[256,1152]{1,0:T(8,128)(2,1)S(1)} %shard_map.68.refs_0_), channel_id=1, source_target_pairs={{0,3},{1,0},{2,1},{3,2},{4,7},{5,4},{6,5},{7,6},{8,11},{9,8},{10,9... | collective-permute-start | bytes 1769480 | tf_op jit(solution)/shard_map/ppermute | solution.py:240
  26.1 1.2 copy-start.6
  28.6 1.0 copy-start
  67.6 20.4 %collective-permute-start.6 = (bf16[8,64,512]{2,1,0:T(8,128)(2,1)}, bf16[8,64,512]{2,1,0:T(8,128)(2,1)S(1)}, u32[]{:S(2)}, u32[]{:S(2)}) collective-permute-start(bf16[8,64,512]{2,1,0:T(8,128)(2,1)} %get-tuple-element.39), channel_id=1, source_target_pairs={{0,4},{4,0},{1,5},{5,1},{2,6},{6,2},{3,7},{7,3},{8,12},{12,8},{9,1... | collective-permute-start | bytes 1572872 | tf_op jit(solution)/shard_map/ppermute | solution.py:293
  70.2 17.9 %all-to-all-start.2 = ((bf16[16,32,128]{2,1,0:T(8,128)(2,1)}), bf16[16,32,128]{2,1,0:T(8,128)(2,1)}, u32[]{:S(2)}, u32[]{:S(2)}) async-start(bf16[16,32,128]{2,1,0:T(8,128)(2,1)} %get-tuple-element.45), calls=%async_computation.2 | async-start | bytes 262144 | tf_op jit(solution)/shard_map/all_to_all | solution.py:244
  78.2 1.6 %copy-start.5 = (bf16[1024,1024]{1,0:T(8,128)(2,1)S(1)}, bf16[1024,1024]{1,0:T(8,128)(2,1)}, u32[]{:S(2)}) copy-start(bf16[1024,1024]{1,0:T(8,128)(2,1)} %get-tuple-element.33.ds_ref) | copy-start | bytes 6291460
  79.8 8.2 %copy-start.1 = (bf16[16,64,512]{2,1,0:T(8,128)(2,1)S(1)}, bf16[16,64,512]{2,1,0:T(8,128)(2,1)}, u32[]{:S(2)}) copy-start(bf16[16,64,512]{2,1,0:T(8,128)(2,1)} %copy-done) | copy-start | bytes 3145732
  81.6 0.7 copy-start.7
  82.4 0.7 copy-start.8
  83.1 0.7 copy-start.9
  83.8 10.7 %copy-start.2 = (bf16[8,64,512]{2,1,0:T(8,128)(2,1)S(1)}, bf16[8,64,512]{2,1,0:T(8,128)(2,1)}, u32[]{:S(2)}) copy-start(bf16[8,64,512]{2,1,0:T(8,128)(2,1)} %get-tuple-element.38.a) | copy-start | bytes 1572868
  90.5 21.9 %all-to-all-start.3 = ((bf16[16,64,512]{2,1,0:T(8,128)(2,1)}), bf16[16,64,512]{2,1,0:T(8,128)(2,1)S(1)}, u32[]{:S(2)}, u32[]{:S(2)}) async-start(bf16[16,64,512]{2,1,0:T(8,128)(2,1)} %get-tuple-element.48), calls=%async_computation.3 | async-start | bytes 2097152 | tf_op jit(solution)/shard_map/all_to_all | solution.py:244
  95.2 13.8 %collective-permute-start.7 = (bf16[4,64,512]{2,1,0:T(8,128)(2,1)S(1)}, bf16[4,64,512]{2,1,0:T(8,128)(2,1)S(1)}, u32[]{:S(2)}, u32[]{:S(2)}) collective-permute-start(bf16[4,64,512]{2,1,0:T(8,128)(2,1)S(1)} %get-tuple-element.41), channel_id=1, source_target_pairs={{0,8},{8,0},{16,24},{24,16},{32,40},{40,32},{48,56},{56,48},{1,9},... | collective-permute-start | bytes 786440 | tf_op jit(solution)/shard_map/ppermute | solution.py:316
  97.6 33.9 %collective-permute-start.3 = (bf16[256,576]{1,0:T(8,128)(2,1)}, bf16[256,576]{1,0:T(8,128)(2,1)S(1)}, u32[]{:S(2)}, u32[]{:S(2)}) collective-permute-start(bf16[256,576]{1,0:T(8,128)(2,1)} %copy-done.9), channel_id=1, source_target_pairs={{0,1},{1,2},{2,3},{3,0},{4,5},{5,6},{6,7},{7,4},{8,9},{9,10},{10,1... | collective-permute-start | bytes 884744 | tf_op jit(solution)/shard_map/ppermute | solution.py:240
  101.0 30.6 %collective-permute-start.4 = (bf16[256,576]{1,0:T(8,128)(2,1)}, bf16[256,576]{1,0:T(8,128)(2,1)}, u32[]{:S(2)}, u32[]{:S(2)}) collective-permute-start(bf16[256,576]{1,0:T(8,128)(2,1)} %copy-done.8), channel_id=1, source_target_pairs={{0,2},{1,3},{2,0},{3,1},{4,6},{5,7},{6,4},{7,5},{8,10},{9,11},{10,... | collective-permute-start | bytes 884744 | tf_op jit(solution)/shard_map/ppermute | solution.py:240
  105.6 26.0 %collective-permute-start.5 = (bf16[256,576]{1,0:T(8,128)(2,1)}, bf16[256,576]{1,0:T(8,128)(2,1)}, u32[]{:S(2)}, u32[]{:S(2)}) collective-permute-start(bf16[256,576]{1,0:T(8,128)(2,1)} %copy-done.7), channel_id=1, source_target_pairs={{0,3},{1,0},{2,1},{3,2},{4,7},{5,4},{6,5},{7,6},{8,11},{9,8},{10,9... | collective-permute-start | bytes 884744 | tf_op jit(solution)/shard_map/ppermute | solution.py:240
  109.6 13.5 %collective-permute-start.8 = (bf16[2,64,512]{2,1,0:T(8,128)(2,1)S(1)}, bf16[2,64,512]{2,1,0:T(8,128)(2,1)S(1)}, u32[]{:S(2)}, u32[]{:S(2)}) collective-permute-start(bf16[2,64,512]{2,1,0:T(8,128)(2,1)S(1)} %get-tuple-element.44), channel_id=1, source_target_pairs={{0,16},{8,24},{16,0},{24,8},{32,48},{40,56},{48,32},{56,40},{1,17}... | collective-permute-start | bytes 393224 | tf_op jit(solution)/shard_map/ppermute | solution.py:316
  113.4 22.4 %all-to-all-start.4 = ((f32[32,8,128]{2,1,0:T(8,128)}), f32[32,8,128]{2,1,0:T(8,128)S(1)}, u32[]{:S(2)}, u32[]{:S(2)}) async-start(f32[32,8,128]{2,1,0:T(8,128)} %get-tuple-element.54), calls=%async_computation.4 | async-start | bytes 262144 | tf_op jit(solution)/shard_map/all_to_all | solution.py:244
  124.3 10.8 %collective-permute-start.9 = (bf16[1,64,512]{2,1,0:T(8,128)(2,1)S(1)}, bf16[1,64,512]{2,1,0:T(8,128)(2,1)S(1)}, u32[]{:S(2)}, u32[]{:S(2)}) collective-permute-start(bf16[1,64,512]{2,1,0:T(8,128)(2,1)S(1)} %get-tuple-element.52), channel_id=1, source_target_pairs={{0,32},{8,40},{16,48},{24,56},{32,0},{40,8},{48,16},{56,24},{1,33}... | collective-permute-start | bytes 196616 | tf_op jit(solution)/shard_map/ppermute | solution.py:316

commit v8 on v7

--- a/solution.py
+++ b/solution.py
@@ -196,6 +196,11 @@
         out[...] = (v * softmax_scale).astype(out.dtype)
 
 
+def query_hop_kernel(keep, came, send, token):
+    token[...] = jnp.zeros(token.shape, token.dtype)
+    send[...] = (keep[...].astype(f32) + came[...].astype(f32)).astype(send.dtype)
+
+
 def weight_kernel(parts, cols, after, after2, rope_ref, out):
     v = jnp.sum(parts[...].astype(f32), axis=0)
     e = v.shape[1] // 2
@@ -206,7 +211,7 @@
         out[i] = tn(low, cols[i]).astype(bf16)
 
 
-def weight_half_kernel(parts, after, out, token):
+def weight_half_kernel(parts, after, after2, out, token):
     token[...] = jnp.zeros(token.shape, token.dtype)
     v = jnp.sum(parts[...].astype(f32), axis=0)
     v = jnp.swapaxes(v, 0, 1)
@@ -300,13 +305,15 @@
         flops=2 * k_dev * nc * ny * nx * wide * rope, moved=4 * k_dev * model, limit=20,
     )(rope_part, cols, other, dq_token)
     terms = trade(terms, ("c", "y", "x"))
-    dq = [dq[0]] + [fetch(dq[k], nx - k, nx) for k in range(1, nx)]
+    came = fetch(dq[2], nx - 1, nx)
+    dq_send, dq_token = call(query_hop_kernel, [((rows, width), bf16), TOKEN], 2)(dq[1], came)
+    dq = [dq[0], fetch(dq_send, nx - 1, nx), fetch(dq[3], 1, nx)]
     kept, came = mine, other
     for bit in range(3):
         if bit == 2:
             terms, token = call(
-                weight_half_kernel, [((nw * nz, SLOT // 2, 2 * rope), f32), TOKEN], 2, unused=(1,)
-            )(terms, token)
+                weight_half_kernel, [((nw * nz, SLOT // 2, 2 * rope), f32), TOKEN], 3, unused=(1, 2)
+            )(terms, token, dq_token)
             terms = trade(terms, ("w", "z"))
         n = nz >> (bit + 1)
         kept, sent, token = call(

time: 137 us -> 148 us (1.080)
  the two profiles are of different devices: /device:TPU:40 before, /device:TPU:6 now
where the time goes in v8:
time: 148 us; the launch traced here: 147 us
  starting transfers between devices  66.8 us (45%)
  waiting for transfers between devices  39.6 us (27%)
  Pallas kernels  21.2 us (14%)
  local copies, waits for them, and re-layouts  8.35 us (6%)
  blocking collectives  8.13 us (5%)
  other arithmetic  1.9 us (1%)
    ppermute x6, waiting for transfers between devices, fetch(): return lax.ppermute(value, 'x', [(s, (s - offset) % n) for s in range(n)])  32.2 us
    all_to_all x4, starting transfers between devices, trade(): return lax.all_to_all(value, axes, 0, 0, tiled=True)  32 us
    ppermute x6, starting transfers between devices, fetch(): return lax.ppermute(value, 'x', [(s, (s - offset) % n) for s in range(n)])  18.8 us
    ppermute x3, starting transfers between devices, body(): came = lax.ppermute(sent, 'z', [(i, i ^ 1 << bit) for i in range(nz)])  12.8 us
    all_to_all x1, blocking collectives, trade(): return lax.all_to_all(value, axes, 0, 0, tiled=True)  8.13 us
    unnamed x20, local copies, waits for them, and re-layouts  6.17 us
    pallas_call x1, Pallas kernels, body(): call(functools.partial(dscores_kernel, lat), [((n_keys, n_rows), bf16), (...  6.04 us
    all_to_all x4, waiting for transfers between devices, trade(): return lax.all_to_all(value, axes, 0, 0, tiled=True)  5.42 us
  transfers between devices with their start and end apart: 14, of which 7 were waited for; matrix products, arithmetic and copies ran while one was open for 1% of the time, Pallas kernels for 5%

profile of v8, /device:TPU:6, one launch (start us, length us, event | category | flops | bytes accessed | tf_op | source)
XLA Modules:
  0.0 146.9 jit_solution(13595367407168497328)
XLA Ops:
  0.7 2.2 %broadcast_in_dim.17 = bf16[16,64,576]{2,1,0:T(8,128)(2,1)} broadcast(bf16[64,576]{1,0:T(8,128)(2,1)} %bitcast.14), dimensions={1,2} | broadcast | bytes 1253376 | tf_op jit(solution)/shard_map/broadcast_in_dim | solution.py:265
  2.8 11.4 %all-to-all-start = ((bf16[16,64,576]{2,1,0:T(8,128)(2,1)}), bf16[16,64,576]{2,1,0:T(8,128)(2,1)S(1)}, u32[]{:S(2)}, u32[]{:S(2)}) async-start(bf16[16,64,576]{2,1,0:T(8,128)(2,1)} %broadcast_in_dim.17), calls=%async_computation | async-start | bytes 2621440 | tf_op jit(solution)/shard_map/all_to_all | solution.py:249
  14.3 2.4 %collective-permute-start.2 = (bf16[256,1152]{1,0:T(8,128)(2,1)S(1)}, bf16[256,1152]{1,0:T(8,128)(2,1)S(1)}, u32[]{:S(2)}, u32[]{:S(2)}) collective-permute-start(bf16[256,1152]{1,0:T(8,128)(2,1)S(1)} %shard_map.68.refs_0_), channel_id=1, source_target_pairs={{0,1},{1,2},{2,3},{3,0},{4,5},{5,6},{6,7},{7,4},{8,9},{9,10},{10,1... | collective-permute-start | bytes 1769480 | tf_op jit(solution)/shard_map/ppermute | solution.py:245
  16.7 4.3 %collective-permute-start.1 = (bf16[256,1152]{1,0:T(8,128)(2,1)S(1)}, bf16[256,1152]{1,0:T(8,128)(2,1)S(1)}, u32[]{:S(2)}, u32[]{:S(2)}) collective-permute-start(bf16[256,1152]{1,0:T(8,128)(2,1)S(1)} %shard_map.68.refs_0_), channel_id=1, source_target_pairs={{0,2},{1,3},{2,0},{3,1},{4,6},{5,7},{6,4},{7,5},{8,10},{9,11},{10,... | collective-permute-start | bytes 1769480 | tf_op jit(solution)/shard_map/ppermute | solution.py:245
  21.1 1.9 %collective-permute-start = (bf16[256,1152]{1,0:T(8,128)(2,1)S(1)}, bf16[256,1152]{1,0:T(8,128)(2,1)}, u32[]{:S(2)}, u32[]{:S(2)}) collective-permute-start(bf16[256,1152]{1,0:T(8,128)(2,1)S(1)} %shard_map.68.refs_0_), channel_id=1, source_target_pairs={{0,3},{1,0},{2,1},{3,2},{4,7},{5,4},{6,5},{7,6},{8,11},{9,8},{10,9... | collective-permute-start | bytes 1769480 | tf_op jit(solution)/shard_map/ppermute | solution.py:245
  23.0 1.2 copy-done.8
  24.2 1.3 shard_map.67
  25.5 1.0 copy-done
  26.5 6.0 %collective-permute-done.2.refs_3_ = bf16[256,1152]{1,0:T(8,128)(2,1)S(1)} collective-permute-done((bf16[256,1152]{1,0:T(8,128)(2,1)S(1)}, bf16[256,1152]{1,0:T(8,128)(2,1)S(1)}, u32[]{:S(2)}, u32[]{:S(2)}) %collective-permute-start.2) | collective-permute-done | bytes 589856 | tf_op jit(solution)/shard_map/ppermute | solution.py:245
  32.5 4.0 %collective-permute-done.1.refs_2_ = bf16[256,1152]{1,0:T(8,128)(2,1)S(1)} collective-permute-done((bf16[256,1152]{1,0:T(8,128)(2,1)S(1)}, bf16[256,1152]{1,0:T(8,128)(2,1)S(1)}, u32[]{:S(2)}, u32[]{:S(2)}) %collective-permute-start.1) | collective-permute-done | bytes 589856 | tf_op jit(solution)/shard_map/ppermute | solution.py:245
  36.5 10.9 %collective-permute-done.refs_1_ = bf16[256,1152]{1,0:T(8,128)(2,1)} collective-permute-done((bf16[256,1152]{1,0:T(8,128)(2,1)S(1)}, bf16[256,1152]{1,0:T(8,128)(2,1)}, u32[]{:S(2)}, u32[]{:S(2)}) %collective-permute-start) | collective-permute-done | bytes 589856 | tf_op jit(solution)/shard_map/ppermute | solution.py:245
  47.8 4.4 %shard_map.69 = (f32[1024,1024]{1,0:T(8,128)S(1)}, f32[1024,1024]{1,0:T(8,128)S(1)}, f32[16,256]{1,0:T(8,128)S(1)}) custom-call(s32[3]{0:T(128)S(1)} %pad_add_fusion.pos, bf16[16,64,576]{2,1,0:T(8,128)(2,1)S(1)} %all-to-all-done.keys, f32[8,128]{1,0:T(8,128)S(1)} %get-tuple-element.31.after, bf16[256,1152]{1,0:T(8,128)(2,1)S(1)} %shard_map.68.refs_0_, ...), custom_call_target="tpu_custom_call" | custom-call | flops 2281701376 | bytes 8388608 | tf_op jit(solution)/shard_map/pallas_call | solution.py:276
  52.2 8.1 %all_to_all.25.stats = f32[4,16,256]{2,1,0:T(8,128)S(1)} all-to-all(f32[4,16,256]{2,1,0:T(8,128)S(1)} %broadcast_in_dim.18), channel_id=1, replica_groups=mesh['w'=4,'c'=2,'z'=8,'y'=2,'x'=4] {'x'}, dimensions={0} | all-to-all | bytes 131072 | tf_op jit(solution)/shard_map/all_to_all | solution.py:249
  60.3 6.0 %shard_map.70 = (bf16[1024,1024]{1,0:T(8,128)(2,1)}, bf16[16,32,128]{2,1,0:T(8,128)(2,1)}, bf16[8,64,512]{2,1,0:T(8,128)(2,1)}, bf16[8,64,512]{2,1,0:T(8,128)(2,1)}) custom-call(s32[3]{0:T(128)S(1)} %pad_add_fusion.pos, f32[4,16,256]{2,1,0:T(8,128)S(1)} %all_to_all.25.stats, f32[16,256]{1,0:T(8,128)S(1)} %get-tuple-element.32.st, ...), custom_call_target="tpu_custom_call" | custom-call | flops 2281701376 | bytes 12582912 | tf_op jit(solution)/shard_map/pallas_call | solution.py:283
  66.4 3.3 %collective-permute-start.6 = (bf16[8,64,512]{2,1,0:T(8,128)(2,1)}, bf16[8,64,512]{2,1,0:T(8,128)(2,1)S(1)}, u32[]{:S(2)}, u32[]{:S(2)}) collective-permute-start(bf16[8,64,512]{2,1,0:T(8,128)(2,1)} %get-tuple-element.42), channel_id=1, source_target_pairs={{0,4},{4,0},{1,5},{5,1},{2,6},{6,2},{3,7},{7,3},{8,12},{12,8},{9,1... | collective-permute-start | bytes 1572872 | tf_op jit(solution)/shard_map/ppermute | solution.py:298
  69.7 6.8 %all-to-all-start.2 = ((bf16[16,32,128]{2,1,0:T(8,128)(2,1)}), bf16[16,32,128]{2,1,0:T(8,128)(2,1)}, u32[]{:S(2)}, u32[]{:S(2)}) async-start(bf16[16,32,128]{2,1,0:T(8,128)(2,1)} %get-tuple-element.48), calls=%async_computation.2 | async-start | bytes 262144 | tf_op jit(solution)/shard_map/all_to_all | solution.py:249
  76.5 1.6 %copy-done.7 = bf16[1024,1024]{1,0:T(8,128)(2,1)S(1)} copy-done((bf16[1024,1024]{1,0:T(8,128)(2,1)S(1)}, bf16[1024,1024]{1,0:T(8,128)(2,1)}, u32[]{:S(2)}) %copy-start.7) | copy-done | bytes 2097176
  78.1 2.2 %shard_map.71 = (f32[8,128]{1,0:T(8,128)S(1)}, f32[256,576]{1,0:T(8,128)S(1)}, bf16[256,576]{1,0:T(8,128)(2,1)S(1)}, bf16[256,576]{1,0:T(8,128)(2,1)}, bf16[256,576]{1,0:T(8,128)(2,1)S(1)}) custom-call(bf16[1024,1024]{1,0:T(8,128)(2,1)S(1)} %copy-done.7, bf16[16,64,576]{2,1,0:T(8,128)(2,1)S(1)} %all-to-all-done.keys), custom_call_target="tpu_custom_call" | custom-call | flops 1207959552 | bytes 4194304 | tf_op jit(solution)/shard_map/pallas_call | solution.py:299
  81.7 5.0 %all-to-all-done.2.parts = bf16[16,32,128]{2,1,0:T(8,128)(2,1)} async-done(((bf16[16,32,128]{2,1,0:T(8,128)(2,1)}), bf16[16,32,128]{2,1,0:T(8,128)(2,1)}, u32[]{:S(2)}, u32[]{:S(2)}) %all-to-all-start.2) | async-done | bytes 131104 | tf_op jit(solution)/shard_map/all_to_all | solution.py:249
  86.8 2.4 %shard_map.75 = (f32[64,64]{1,0:T(8,128)S(1)}, bf16[16,64,512]{2,1,0:T(8,128)(2,1)}) custom-call(bf16[16,32,128]{2,1,0:T(8,128)(2,1)} %all-to-all-done.2.parts, bf16[16,64,512]{2,1,0:T(8,128)(2,1)S(1)} %copy-done.1, bf16[8,64,512]{2,1,0:T(8,128)(2,1)S(1)} %collective-permute-done.6.b.after, f32[8,128]{1,0:T(8,128)S(1)} %get-tuple-element.50.after2), custom_call_target="tpu_custom_call" | custom-call | flops 67108864 | bytes 1835008 | tf_op jit(solution)/shard_map/pallas_call | solution.py:303
  89.2 5.5 %all-to-all-start.3 = ((bf16[16,64,512]{2,1,0:T(8,128)(2,1)}), bf16[16,64,512]{2,1,0:T(8,128)(2,1)S(1)}, u32[]{:S(2)}, u32[]{:S(2)}) async-start(bf16[16,64,512]{2,1,0:T(8,128)(2,1)} %get-tuple-element.51), calls=%async_computation.3 | async-start | bytes 2097152 | tf_op jit(solution)/shard_map/all_to_all | solution.py:249
  94.6 2.1 %collective-permute-start.3 = (bf16[256,576]{1,0:T(8,128)(2,1)}, bf16[256,576]{1,0:T(8,128)(2,1)S(1)}, u32[]{:S(2)}, u32[]{:S(2)}) collective-permute-start(bf16[256,576]{1,0:T(8,128)(2,1)} %get-tuple-element.38), channel_id=1, source_target_pairs={{0,1},{1,2},{2,3},{3,0},{4,5},{5,6},{6,7},{7,4},{8,9},{9,10},{10,1... | collective-permute-start | bytes 884744 | tf_op jit(solution)/shard_map/ppermute | solution.py:245
  97.4 2.4 %collective-permute-start.7 = (bf16[4,64,512]{2,1,0:T(8,128)(2,1)S(1)}, bf16[4,64,512]{2,1,0:T(8,128)(2,1)S(1)}, u32[]{:S(2)}, u32[]{:S(2)}) collective-permute-start(bf16[4,64,512]{2,1,0:T(8,128)(2,1)S(1)} %get-tuple-element.44), channel_id=1, source_target_pairs={{0,8},{8,0},{16,24},{24,16},{32,40},{40,32},{48,56},{56,48},{1,9},... | collective-permute-start | bytes 786440 | tf_op jit(solution)/shard_map/ppermute | solution.py:323
  99.9 3.8 %collective-permute-start.5 = (bf16[256,576]{1,0:T(8,128)(2,1)}, bf16[256,576]{1,0:T(8,128)(2,1)S(1)}, u32[]{:S(2)}, u32[]{:S(2)}) collective-permute-start(bf16[256,576]{1,0:T(8,128)(2,1)} %copy-done.9), channel_id=1, source_target_pairs={{0,3},{1,0},{2,1},{3,2},{4,7},{5,4},{6,5},{7,6},{8,11},{9,8},{10,9... | collective-permute-start | bytes 884744 | tf_op jit(solution)/shard_map/ppermute | solution.py:245
  103.7 11.4 %collective-permute-done.3.came = bf16[256,576]{1,0:T(8,128)(2,1)S(1)} collective-permute-done((bf16[256,576]{1,0:T(8,128)(2,1)}, bf16[256,576]{1,0:T(8,128)(2,1)S(1)}, u32[]{:S(2)}, u32[]{:S(2)}) %collective-permute-start.3) | collective-permute-done | bytes 294944 | tf_op jit(solution)/shard_map/ppermute | solution.py:245
  116.1 4.3 %collective-permute-start.4 = (bf16[256,576]{1,0:T(8,128)(2,1)S(1)}, bf16[256,576]{1,0:T(8,128)(2,1)}, u32[]{:S(2)}, u32[]{:S(2)}) collective-permute-start(bf16[256,576]{1,0:T(8,128)(2,1)S(1)} %get-tuple-element.39), channel_id=1, source_target_pairs={{0,1},{1,2},{2,3},{3,0},{4,5},{5,6},{6,7},{7,4},{8,9},{9,10},{10,1... | collective-permute-start | bytes 884744 | tf_op jit(solution)/shard_map/ppermute | solution.py:245
  120.9 2.7 %collective-permute-start.8 = (bf16[2,64,512]{2,1,0:T(8,128)(2,1)S(1)}, bf16[2,64,512]{2,1,0:T(8,128)(2,1)S(1)}, u32[]{:S(2)}, u32[]{:S(2)}) collective-permute-start(bf16[2,64,512]{2,1,0:T(8,128)(2,1)S(1)} %get-tuple-element.47), channel_id=1, source_target_pairs={{0,16},{8,24},{16,0},{24,8},{32,48},{40,56},{48,32},{56,40},{1,17}... | collective-permute-start | bytes 393224 | tf_op jit(solution)/shard_map/ppermute | solution.py:323
  124.6 8.3 %all-to-all-start.4 = ((f32[32,8,128]{2,1,0:T(8,128)}), f32[32,8,128]{2,1,0:T(8,128)S(1)}, u32[]{:S(2)}, u32[]{:S(2)}) async-start(f32[32,8,128]{2,1,0:T(8,128)} %get-tuple-element.58), calls=%async_computation.4 | async-start | bytes 262144 | tf_op jit(solution)/shard_map/all_to_all | solution.py:249
  132.9 1.1 shard_map.77
  134.1 7.6 %collective-permute-start.9 = (bf16[1,64,512]{2,1,0:T(8,128)(2,1)S(1)}, bf16[1,64,512]{2,1,0:T(8,128)(2,1)S(1)}, u32[]{:S(2)}, u32[]{:S(2)}) collective-permute-start(bf16[1,64,512]{2,1,0:T(8,128)(2,1)S(1)} %get-tuple-element.56), channel_id=1, source_target_pairs={{0,32},{8,40},{16,48},{24,56},{32,0},{40,8},{48,16},{56,24},{1,33}... | collective-permute-start | bytes 196616 | tf_op jit(solution)/shard_map/ppermute | solution.py:323
  141.7 1.8 %add_convert_fusion = bf16[256,576]{1,0:T(8,128)(2,1)} fusion(bf16[256,576]{1,0:T(8,128)(2,1)S(1)} %collective-permute-done.5, f32[256,576]{1,0:T(8,128)S(1)} %get-tuple-element.36, bf16[256,576]{1,0:T(8,128)(2,1)} %collective-permute-done.4), kind=kLoop, calls=%fused_computation | loop fusion | flops 737280 | bytes 1474560 | tf_op jit(solution)/shard_map/convert_element_type | solution.py:330
  143.5 2.0 %collective-permute-done.9.b = bf16[1,64,512]{2,1,0:T(8,128)(2,1)S(1)} collective-permute-done((bf16[1,64,512]{2,1,0:T(8,128)(2,1)S(1)}, bf16[1,64,512]{2,1,0:T(8,128)(2,1)S(1)}, u32[]{:S(2)}, u32[]{:S(2)}) %collective-permute-start.9) | collective-permute-done | bytes 65568 | tf_op jit(solution)/shard_map/ppermute | solution.py:323
  (34 shorter events, 6.6 us)
Async XLA Ops:
  0.6 13.6 %copy-start.6 = (bf16[1,4,64,512]{3,2,1,0:T(8,128)(2,1)S(1)}, bf16[1,4,64,512]{3,2,1,0:T(8,128)(2,1)}, u32[]{:S(2)}) copy-start(bf16[1,4,64,512]{3,2,1,0:T(8,128)(2,1)} %param.6) | copy-start | bytes 786436
  0.6 13.6 %copy-start.3 = (bf16[1,4,64,576]{3,2,1,0:T(8,128)(2,1)S(1)}, bf16[1,4,64,576]{3,2,1,0:T(8,128)(2,1)}, u32[]{:S(2)}) copy-start(bf16[1,4,64,576]{3,2,1,0:T(8,128)(2,1)} %param.4) | copy-start | bytes 884740
  2.8 45.0 %all-to-all-start = ((bf16[16,64,576]{2,1,0:T(8,128)(2,1)}), bf16[16,64,576]{2,1,0:T(8,128)(2,1)S(1)}, u32[]{:S(2)}, u32[]{:S(2)}) async-start(bf16[16,64,576]{2,1,0:T(8,128)(2,1)} %broadcast_in_dim.17), calls=%async_computation | async-start | bytes 2621440 | tf_op jit(solution)/shard_map/all_to_all | solution.py:249
  14.3 18.1 %collective-permute-start.2 = (bf16[256,1152]{1,0:T(8,128)(2,1)S(1)}, bf16[256,1152]{1,0:T(8,128)(2,1)S(1)}, u32[]{:S(2)}, u32[]{:S(2)}) collective-permute-start(bf16[256,1152]{1,0:T(8,128)(2,1)S(1)} %shard_map.68.refs_0_), channel_id=1, source_target_pairs={{0,1},{1,2},{2,3},{3,0},{4,5},{5,6},{6,7},{7,4},{8,9},{9,10},{10,1... | collective-permute-start | bytes 1769480 | tf_op jit(solution)/shard_map/ppermute | solution.py:245
  16.7 19.7 %collective-permute-start.1 = (bf16[256,1152]{1,0:T(8,128)(2,1)S(1)}, bf16[256,1152]{1,0:T(8,128)(2,1)S(1)}, u32[]{:S(2)}, u32[]{:S(2)}) collective-permute-start(bf16[256,1152]{1,0:T(8,128)(2,1)S(1)} %shard_map.68.refs_0_), channel_id=1, source_target_pairs={{0,2},{1,3},{2,0},{3,1},{4,6},{5,7},{6,4},{7,5},{8,10},{9,11},{10,... | collective-permute-start | bytes 1769480 | tf_op jit(solution)/shard_map/ppermute | solution.py:245
  21.1 26.3 %collective-permute-start = (bf16[256,1152]{1,0:T(8,128)(2,1)S(1)}, bf16[256,1152]{1,0:T(8,128)(2,1)}, u32[]{:S(2)}, u32[]{:S(2)}) collective-permute-start(bf16[256,1152]{1,0:T(8,128)(2,1)S(1)} %shard_map.68.refs_0_), channel_id=1, source_target_pairs={{0,3},{1,0},{2,1},{3,2},{4,7},{5,4},{6,5},{7,6},{8,11},{9,8},{10,9... | collective-permute-start | bytes 1769480 | tf_op jit(solution)/shard_map/ppermute | solution.py:245
  23.0 1.2 copy-start.8
  25.5 1.0 copy-start
  66.4 20.4 %collective-permute-start.6 = (bf16[8,64,512]{2,1,0:T(8,128)(2,1)}, bf16[8,64,512]{2,1,0:T(8,128)(2,1)S(1)}, u32[]{:S(2)}, u32[]{:S(2)}) collective-permute-start(bf16[8,64,512]{2,1,0:T(8,128)(2,1)} %get-tuple-element.42), channel_id=1, source_target_pairs={{0,4},{4,0},{1,5},{5,1},{2,6},{6,2},{3,7},{7,3},{8,12},{12,8},{9,1... | collective-permute-start | bytes 1572872 | tf_op jit(solution)/shard_map/ppermute | solution.py:298
  69.7 17.1 %all-to-all-start.2 = ((bf16[16,32,128]{2,1,0:T(8,128)(2,1)}), bf16[16,32,128]{2,1,0:T(8,128)(2,1)}, u32[]{:S(2)}, u32[]{:S(2)}) async-start(bf16[16,32,128]{2,1,0:T(8,128)(2,1)} %get-tuple-element.48), calls=%async_computation.2 | async-start | bytes 262144 | tf_op jit(solution)/shard_map/all_to_all | solution.py:249
  76.5 1.6 %copy-start.7 = (bf16[1024,1024]{1,0:T(8,128)(2,1)S(1)}, bf16[1024,1024]{1,0:T(8,128)(2,1)}, u32[]{:S(2)}) copy-start(bf16[1024,1024]{1,0:T(8,128)(2,1)} %get-tuple-element.35.ds_ref) | copy-start | bytes 6291460
  78.1 8.6 %copy-start.1 = (bf16[16,64,512]{2,1,0:T(8,128)(2,1)S(1)}, bf16[16,64,512]{2,1,0:T(8,128)(2,1)}, u32[]{:S(2)}) copy-start(bf16[16,64,512]{2,1,0:T(8,128)(2,1)} %copy-done) | copy-start | bytes 3145732
  80.3 0.7 copy-start.4
  81.0 0.7 copy-start.9
  81.7 15.0 %copy-start.2 = (bf16[8,64,512]{2,1,0:T(8,128)(2,1)S(1)}, bf16[8,64,512]{2,1,0:T(8,128)(2,1)}, u32[]{:S(2)}) copy-start(bf16[8,64,512]{2,1,0:T(8,128)(2,1)} %get-tuple-element.41.a) | copy-start | bytes 1572868
  89.2 34.5 %all-to-all-start.3 = ((bf16[16,64,512]{2,1,0:T(8,128)(2,1)}), bf16[16,64,512]{2,1,0:T(8,128)(2,1)S(1)}, u32[]{:S(2)}, u32[]{:S(2)}) async-start(bf16[16,64,512]{2,1,0:T(8,128)(2,1)} %get-tuple-element.51), calls=%async_computation.3 | async-start | bytes 2097152 | tf_op jit(solution)/shard_map/all_to_all | solution.py:249
  94.6 20.4 %collective-permute-start.3 = (bf16[256,576]{1,0:T(8,128)(2,1)}, bf16[256,576]{1,0:T(8,128)(2,1)S(1)}, u32[]{:S(2)}, u32[]{:S(2)}) collective-permute-start(bf16[256,576]{1,0:T(8,128)(2,1)} %get-tuple-element.38), channel_id=1, source_target_pairs={{0,1},{1,2},{2,3},{3,0},{4,5},{5,6},{6,7},{7,4},{8,9},{9,10},{10,1... | collective-permute-start | bytes 884744 | tf_op jit(solution)/shard_map/ppermute | solution.py:245
  97.4 22.9 %collective-permute-start.7 = (bf16[4,64,512]{2,1,0:T(8,128)(2,1)S(1)}, bf16[4,64,512]{2,1,0:T(8,128)(2,1)S(1)}, u32[]{:S(2)}, u32[]{:S(2)}) collective-permute-start(bf16[4,64,512]{2,1,0:T(8,128)(2,1)S(1)} %get-tuple-element.44), channel_id=1, source_target_pairs={{0,8},{8,0},{16,24},{24,16},{32,40},{40,32},{48,56},{56,48},{1,9},... | collective-permute-start | bytes 786440 | tf_op jit(solution)/shard_map/ppermute | solution.py:323
  99.9 41.8 %collective-permute-start.5 = (bf16[256,576]{1,0:T(8,128)(2,1)}, bf16[256,576]{1,0:T(8,128)(2,1)S(1)}, u32[]{:S(2)}, u32[]{:S(2)}) collective-permute-start(bf16[256,576]{1,0:T(8,128)(2,1)} %copy-done.9), channel_id=1, source_target_pairs={{0,3},{1,0},{2,1},{3,2},{4,7},{5,4},{6,5},{7,6},{8,11},{9,8},{10,9... | collective-permute-start | bytes 884744 | tf_op jit(solution)/shard_map/ppermute | solution.py:245
  115.0 1.0 copy-start.5
  116.1 25.6 %collective-permute-start.4 = (bf16[256,576]{1,0:T(8,128)(2,1)S(1)}, bf16[256,576]{1,0:T(8,128)(2,1)}, u32[]{:S(2)}, u32[]{:S(2)}) collective-permute-start(bf16[256,576]{1,0:T(8,128)(2,1)S(1)} %get-tuple-element.39), channel_id=1, source_target_pairs={{0,1},{1,2},{2,3},{3,0},{4,5},{5,6},{6,7},{7,4},{8,9},{9,10},{10,1... | collective-permute-start | bytes 884744 | tf_op jit(solution)/shard_map/ppermute | solution.py:245
  120.9 12.0 %collective-permute-start.8 = (bf16[2,64,512]{2,1,0:T(8,128)(2,1)S(1)}, bf16[2,64,512]{2,1,0:T(8,128)(2,1)S(1)}, u32[]{:S(2)}, u32[]{:S(2)}) collective-permute-start(bf16[2,64,512]{2,1,0:T(8,128)(2,1)S(1)} %get-tuple-element.47), channel_id=1, source_target_pairs={{0,16},{8,24},{16,0},{24,8},{32,48},{40,56},{48,32},{56,40},{1,17}... | collective-permute-start | bytes 393224 | tf_op jit(solution)/shard_map/ppermute | solution.py:323
  124.6 21.5 %all-to-all-start.4 = ((f32[32,8,128]{2,1,0:T(8,128)}), f32[32,8,128]{2,1,0:T(8,128)S(1)}, u32[]{:S(2)}, u32[]{:S(2)}) async-start(f32[32,8,128]{2,1,0:T(8,128)} %get-tuple-element.58), calls=%async_computation.4 | async-start | bytes 262144 | tf_op jit(solution)/shard_map/all_to_all | solution.py:249
  134.1 11.4 %collective-permute-start.9 = (bf16[1,64,512]{2,1,0:T(8,128)(2,1)S(1)}, bf16[1,64,512]{2,1,0:T(8,128)(2,1)S(1)}, u32[]{:S(2)}, u32[]{:S(2)}) collective-permute-start(bf16[1,64,512]{2,1,0:T(8,128)(2,1)S(1)} %get-tuple-element.56), channel_id=1, source_target_pairs={{0,32},{8,40},{16,48},{24,56},{32,0},{40,8},{48,16},{56,24},{1,33}... | collective-permute-start | bytes 196616 | tf_op jit(solution)/shard_map/ppermute | solution.py:323

commit v9 on v7

--- a/solution.py
+++ b/solution.py
@@ -10,6 +10,7 @@
 softmax_scale = 0.07216878364870323
 f32, bf16 = jnp.float32, jnp.bfloat16
 TILE = 256
+Z = ("zh", "zl")
 TOKEN = ((8, 128), jnp.float32)
 SLOT = 16
 
@@ -53,7 +54,7 @@
     out[:, lat + width :] = jnp.zeros((out.shape[0], out.shape[1] - lat - width), out.dtype)
 
 
-def columns_kernel(block, n_z, n_grp, n_core, hid, out, token):
+def columns_kernel(block, n_z, n_low, n_grp, n_core, hid, out, token):
     token[...] = jnp.zeros(token.shape, token.dtype)
     k_dev, model = hid.shape
     n_data = model // (n_z * n_grp * block)
@@ -61,16 +62,22 @@
     wide = n_z * SLOT
     c = lax.broadcasted_iota(jnp.int32, (span, n_grp * wide), 0)
     o = lax.broadcasted_iota(jnp.int32, (span, n_grp * wide), 1)
-    g, zz, k = o // wide, (o % wide) // SLOT, o % SLOT
+    g, k = o // wide, o % SLOT
+    n_high = n_z // n_low
+    zz = (o % wide) // SLOT
+    zz = zz % n_high * n_low + zz // n_high
     pick = jnp.where((c == (zz * n_grp + g) * block + k) & (k < block), 1.0, 0.0).astype(bf16)
     stacked = jnp.concatenate([hid[:, d * span : (d + 1) * span] for d in range(n_data)])
     moved = nn(stacked, pick).astype(bf16)
     for d in range(n_data):
-        first = d // n_core * wide
-        for g in range(n_grp):
-            out[d % n_core * n_grp + g, :, first : first + wide] = moved[
-                d * k_dev : (d + 1) * k_dev, g * wide : (g + 1) * wide
-            ]
+        part = wide // n_low
+        first = d // n_core * part
+        for low in range(n_low):
+            for g in range(n_grp):
+                at = g * wide + low * part
+                out[(d % n_core * n_low + low) * n_grp + g, :, first : first + part] = moved[
+                    d * k_dev : (d + 1) * k_dev, at : at + part
+                ]
 
 
 def key_tile(keys, i, per):
@@ -245,7 +252,8 @@
 
 
 def body(query, latent, dout, hidden):
-    nw, nc, nz, ny, nx = (lax.axis_size(a) for a in ("w", "c", "z", "y", "x"))
+    nw, nc, nh, nl, ny, nx = (lax.axis_size(a) for a in ("w", "c", "zh", "zl", "y", "x"))
+    nz = nh * nl
     tok, heads, width = query.shape[1:]
     lat = dout.shape[3]
     rope = width - lat
@@ -255,17 +263,18 @@
     pairs = n_rows * n_keys
     block = model // (nw * nc * nz * ny * nx)
     swap = [(0, 1), (1, 0)]
-    pos = jnp.stack([lax.axis_index(a) for a in ("z", "y", "x")]).astype(jnp.int32)
-
-    keys = trade(jnp.broadcast_to(latent, (nz * ny, k_dev, width)), ("z", "y"))
+    pos = jnp.stack([lax.axis_index(a) for a in (Z, "y", "x")]).astype(jnp.int32)
+
+    keys = trade(jnp.broadcast_to(latent, (nz * ny, k_dev, width)), Z + ("y",))
     (own,) = call(pack_kernel, [((rows, -(-(lat + width) // 128) * 128), bf16)], 2, moved=4 * rows * width)(
         dout.reshape(rows, lat), query.reshape(rows, width)
     )
     blocks = [own] + [fetch(own, k, nx) for k in range(1, nx)]
 
-    wide = nw * nz * SLOT
+    wide = nw * nh * SLOT
     cols, token = call(
-        functools.partial(columns_kernel, block, nz, ny * nx, nc), [((nc * ny * nx, k_dev, wide), bf16), TOKEN], 1,
+        functools.partial(columns_kernel, block, nz, nl, ny * nx, nc),
+        [((nc * nl * ny * nx, k_dev, wide), bf16), TOKEN], 1,
         flops=2 * k_dev * model * 1024, moved=4 * k_dev * model, limit=20,
     )(hidden[0])
     e, dp, st = call(
@@ -289,31 +298,31 @@
         ],
         flops=2 * pairs * (rope + 2 * lat), moved=12 * pairs,
     )(pos, stats, st, e, dp, *blocks)
-    rope_part = trade(rope_part, ("z", "y"))
+    rope_part = trade(rope_part, Z + ("y",))
     other = lax.ppermute(other, "y", swap)
     dq_token, *dq = call(
         query_kernel, [TOKEN, ((rows, width), f32)] + [((rows, width), bf16)] * (nx - 1), 2,
         flops=2 * pairs * width, moved=4 * pairs,
     )(ds, keys)
     rope_sum, terms = call(
-        weight_kernel, [((k_dev, rope), f32), ((nc * ny * nx, rope, wide), bf16)], 4, unused=(2, 3),
-        flops=2 * k_dev * nc * ny * nx * wide * rope, moved=4 * k_dev * model, limit=20,
+        weight_kernel, [((k_dev, rope), f32), ((nc * nl * ny * nx, rope, wide), bf16)], 4, unused=(2, 3),
+        flops=2 * k_dev * model * rope, moved=4 * k_dev * model, limit=20,
     )(rope_part, cols, other, dq_token)
-    terms = trade(terms, ("c", "y", "x"))
+    terms = trade(terms, ("c", "zl", "y", "x"))
     dq = [dq[0]] + [fetch(dq[k], nx - k, nx) for k in range(1, nx)]
     kept, came = mine, other
     for bit in range(3):
         if bit == 2:
             terms, token = call(
-                weight_half_kernel, [((nw * nz, SLOT // 2, 2 * rope), f32), TOKEN], 2, unused=(1,)
+                weight_half_kernel, [((nw * nh, SLOT // 2, 2 * rope), f32), TOKEN], 2, unused=(1,)
             )(terms, token)
-            terms = trade(terms, ("w", "z"))
+            terms = trade(terms, ("w", "zh"))
         n = nz >> (bit + 1)
         kept, sent, token = call(
             functools.partial(halve_kernel, bit), [((n, k_dev, lat), f32), ((n, k_dev, lat), bf16), TOKEN], 4,
             smem=(0,), unused=(3,), flops=8 * n * k_dev * lat, moved=12 * n * k_dev * lat, limit=20,
         )(pos, kept, came, token)
-        came = lax.ppermute(sent, "z", [(i, i ^ (1 << bit)) for i in range(nz)])
+        came = lax.ppermute(sent, Z, [(i, i ^ (1 << bit)) for i in range(nz)])
     (dweight,) = call(weight_sum_kernel, [((block, rope), f32)], 1)(terms)
     (dlatent,) = call(latent_sum_kernel, [((k_dev, width), f32)], 3)(kept, came, rope_sum)
 
@@ -324,8 +333,8 @@
 
 
 def solution(mesh):
-    fine = Mesh(mesh.devices.reshape(4, 2, 8, 2, 4), ("w", "c", "z", "y", "x"))
-    dp, sp = ("w", "c"), ("z", "y", "x")
+    fine = Mesh(mesh.devices.reshape(4, 2, 4, 2, 2, 4), ("w", "c", "zh", "zl", "y", "x"))
+    dp, sp = ("w", "c"), ("zh", "zl", "y", "x")
     tokens = P(dp, sp, None, None)
     keys = P(dp, sp, None)
     return jax.shard_map(

time: 137 us -> 142 us (1.036)
  the two profiles are of different devices: /device:TPU:40 before, /device:TPU:6 now
where the time goes in v9:
time: 142 us; the launch traced here: 140 us
  starting transfers between devices  67.1 us (47%)
  waiting for transfers between devices  33.1 us (23%)
  Pallas kernels  20.8 us (15%)
  blocking collectives  8.13 us (6%)
  local copies, waits for them, and re-layouts  8.08 us (6%)
  other arithmetic  2.02 us (1%)
    all_to_all x4, starting transfers between devices, trade(): return lax.all_to_all(value, axes, 0, 0, tiled=True)  32.6 us
    ppermute x6, waiting for transfers between devices, fetch(): return lax.ppermute(value, 'x', [(s, (s - offset) % n) for s in range(n)])  20.6 us
    ppermute x6, starting transfers between devices, fetch(): return lax.ppermute(value, 'x', [(s, (s - offset) % n) for s in range(n)])  17.3 us
    ppermute x3, starting transfers between devices, body(): came = lax.ppermute(sent, Z, [(i, i ^ 1 << bit) for i in range(nz)])  13.9 us
    all_to_all x1, blocking collectives, trade(): return lax.all_to_all(value, axes, 0, 0, tiled=True)  8.13 us
    ppermute x3, waiting for transfers between devices, body(): came = lax.ppermute(sent, Z, [(i, i ^ 1 << bit) for i in range(nz)])  7.31 us
    pallas_call x1, Pallas kernels, body(): call(functools.partial(dscores_kernel, lat), [((n_keys, n_rows), bf16), (...  5.91 us
    unnamed x20, local copies, waits for them, and re-layouts  5.89 us
  transfers between devices with their start and end apart: 14, of which 8 were waited for; matrix products, arithmetic and copies ran while one was open for 1% of the time, Pallas kernels for 5%

profile of v9, /device:TPU:6, one launch (start us, length us, event | category | flops | bytes accessed | tf_op | source)
XLA Modules:
  0.0 140.2 jit_solution(12953471935251258977)
XLA Ops:
  0.7 2.2 %broadcast_in_dim.17 = bf16[16,64,576]{2,1,0:T(8,128)(2,1)} broadcast(bf16[64,576]{1,0:T(8,128)(2,1)} %bitcast.14), dimensions={1,2} | broadcast | bytes 1253376 | tf_op jit(solution)/shard_map/broadcast_in_dim | solution.py:268
  2.8 11.4 %all-to-all-start = ((bf16[16,64,576]{2,1,0:T(8,128)(2,1)}), bf16[16,64,576]{2,1,0:T(8,128)(2,1)S(1)}, u32[]{:S(2)}, u32[]{:S(2)}) async-start(bf16[16,64,576]{2,1,0:T(8,128)(2,1)} %broadcast_in_dim.17), calls=%async_computation | async-start | bytes 2621440 | tf_op jit(solution)/shard_map/all_to_all | solution.py:251
  14.4 2.4 %collective-permute-start.2 = (bf16[256,1152]{1,0:T(8,128)(2,1)S(1)}, bf16[256,1152]{1,0:T(8,128)(2,1)S(1)}, u32[]{:S(2)}, u32[]{:S(2)}) collective-permute-start(bf16[256,1152]{1,0:T(8,128)(2,1)S(1)} %shard_map.68.refs_0_), channel_id=1, source_target_pairs={{0,1},{1,2},{2,3},{3,0},{4,5},{5,6},{6,7},{7,4},{8,9},{9,10},{10,1... | collective-permute-start | bytes 1769480 | tf_op jit(solution)/shard_map/ppermute | solution.py:247
  16.7 4.3 %collective-permute-start.1 = (bf16[256,1152]{1,0:T(8,128)(2,1)S(1)}, bf16[256,1152]{1,0:T(8,128)(2,1)S(1)}, u32[]{:S(2)}, u32[]{:S(2)}) collective-permute-start(bf16[256,1152]{1,0:T(8,128)(2,1)S(1)} %shard_map.68.refs_0_), channel_id=1, source_target_pairs={{0,2},{1,3},{2,0},{3,1},{4,6},{5,7},{6,4},{7,5},{8,10},{9,11},{10,... | collective-permute-start | bytes 1769480 | tf_op jit(solution)/shard_map/ppermute | solution.py:247
  21.1 1.9 %collective-permute-start = (bf16[256,1152]{1,0:T(8,128)(2,1)S(1)}, bf16[256,1152]{1,0:T(8,128)(2,1)}, u32[]{:S(2)}, u32[]{:S(2)}) collective-permute-start(bf16[256,1152]{1,0:T(8,128)(2,1)S(1)} %shard_map.68.refs_0_), channel_id=1, source_target_pairs={{0,3},{1,0},{2,1},{3,2},{4,7},{5,4},{6,5},{7,6},{8,11},{9,8},{10,9... | collective-permute-start | bytes 1769480 | tf_op jit(solution)/shard_map/ppermute | solution.py:247
  23.0 1.2 copy-done.6
  24.2 1.6 %shard_map.67 = (bf16[32,64,256]{2,1,0:T(8,128)(2,1)S(1)}, f32[8,128]{1,0:T(8,128)S(1)}) custom-call(bf16[64,7168]{1,0:T(8,128)(2,1)S(1)} %bitcast.11), custom_call_target="tpu_custom_call" | custom-call | flops 939524096 | bytes 1835008 | tf_op jit(solution)/shard_map/pallas_call | solution.py:275
  25.8 1.0 copy-done
  26.8 5.7 %collective-permute-done.2.refs_3_ = bf16[256,1152]{1,0:T(8,128)(2,1)S(1)} collective-permute-done((bf16[256,1152]{1,0:T(8,128)(2,1)S(1)}, bf16[256,1152]{1,0:T(8,128)(2,1)S(1)}, u32[]{:S(2)}, u32[]{:S(2)}) %collective-permute-start.2) | collective-permute-done | bytes 589856 | tf_op jit(solution)/shard_map/ppermute | solution.py:247
  32.5 4.0 %collective-permute-done.1.refs_2_ = bf16[256,1152]{1,0:T(8,128)(2,1)S(1)} collective-permute-done((bf16[256,1152]{1,0:T(8,128)(2,1)S(1)}, bf16[256,1152]{1,0:T(8,128)(2,1)S(1)}, u32[]{:S(2)}, u32[]{:S(2)}) %collective-permute-start.1) | collective-permute-done | bytes 589856 | tf_op jit(solution)/shard_map/ppermute | solution.py:247
  36.5 10.9 %collective-permute-done.refs_1_ = bf16[256,1152]{1,0:T(8,128)(2,1)} collective-permute-done((bf16[256,1152]{1,0:T(8,128)(2,1)S(1)}, bf16[256,1152]{1,0:T(8,128)(2,1)}, u32[]{:S(2)}, u32[]{:S(2)}) %collective-permute-start) | collective-permute-done | bytes 589856 | tf_op jit(solution)/shard_map/ppermute | solution.py:247
  47.8 4.3 %shard_map.69 = (f32[1024,1024]{1,0:T(8,128)S(1)}, f32[1024,1024]{1,0:T(8,128)S(1)}, f32[16,256]{1,0:T(8,128)S(1)}) custom-call(s32[3]{0:T(128)S(1)} %pad_add_fusion.pos, bf16[16,64,576]{2,1,0:T(8,128)(2,1)S(1)} %all-to-all-done.keys, f32[8,128]{1,0:T(8,128)S(1)} %get-tuple-element.29.after, bf16[256,1152]{1,0:T(8,128)(2,1)S(1)} %shard_map.68.refs_0_, ...), custom_call_target="tpu_custom_call" | custom-call | flops 2281701376 | bytes 8388608 | tf_op jit(solution)/shard_map/pallas_call | solution.py:280
  52.2 8.1 %all_to_all.25.stats = f32[4,16,256]{2,1,0:T(8,128)S(1)} all-to-all(f32[4,16,256]{2,1,0:T(8,128)S(1)} %broadcast_in_dim.18), channel_id=1, replica_groups=mesh['w'=4,'c'=2,'zh'=4,'zl'=2,'y'=2,'x'=4] {'x'}, dimensions={0} | all-to-all | bytes 131072 | tf_op jit(solution)/shard_map/all_to_all | solution.py:251
  60.3 5.9 %shard_map.70 = (bf16[1024,1024]{1,0:T(8,128)(2,1)}, bf16[16,32,128]{2,1,0:T(8,128)(2,1)}, bf16[8,64,512]{2,1,0:T(8,128)(2,1)}, bf16[8,64,512]{2,1,0:T(8,128)(2,1)}) custom-call(s32[3]{0:T(128)S(1)} %pad_add_fusion.pos, f32[4,16,256]{2,1,0:T(8,128)S(1)} %all_to_all.25.stats, f32[16,256]{1,0:T(8,128)S(1)} %get-tuple-element.30.st, ...), custom_call_target="tpu_custom_call" | custom-call | flops 2281701376 | bytes 12582912 | tf_op jit(solution)/shard_map/pallas_call | solution.py:287
  66.2 3.3 %collective-permute-start.6 = (bf16[8,64,512]{2,1,0:T(8,128)(2,1)}, bf16[8,64,512]{2,1,0:T(8,128)(2,1)S(1)}, u32[]{:S(2)}, u32[]{:S(2)}) collective-permute-start(bf16[8,64,512]{2,1,0:T(8,128)(2,1)} %get-tuple-element.39), channel_id=1, source_target_pairs={{0,4},{4,0},{1,5},{5,1},{2,6},{6,2},{3,7},{7,3},{8,12},{12,8},{9,1... | collective-permute-start | bytes 1572872 | tf_op jit(solution)/shard_map/ppermute | solution.py:302
  69.5 6.8 %all-to-all-start.2 = ((bf16[16,32,128]{2,1,0:T(8,128)(2,1)}), bf16[16,32,128]{2,1,0:T(8,128)(2,1)}, u32[]{:S(2)}, u32[]{:S(2)}) async-start(bf16[16,32,128]{2,1,0:T(8,128)(2,1)} %get-tuple-element.45), calls=%async_computation.2 | async-start | bytes 262144 | tf_op jit(solution)/shard_map/all_to_all | solution.py:251
  76.3 1.6 %copy-done.5 = bf16[1024,1024]{1,0:T(8,128)(2,1)S(1)} copy-done((bf16[1024,1024]{1,0:T(8,128)(2,1)S(1)}, bf16[1024,1024]{1,0:T(8,128)(2,1)}, u32[]{:S(2)}) %copy-start.5) | copy-done | bytes 2097176
  77.9 1.8 %shard_map.71 = (f32[8,128]{1,0:T(8,128)S(1)}, f32[256,576]{1,0:T(8,128)S(1)}, bf16[256,576]{1,0:T(8,128)(2,1)S(1)}, bf16[256,576]{1,0:T(8,128)(2,1)S(1)}, bf16[256,576]{1,0:T(8,128)(2,1)S(1)}) custom-call(bf16[1024,1024]{1,0:T(8,128)(2,1)S(1)} %copy-done.5, bf16[16,64,576]{2,1,0:T(8,128)(2,1)S(1)} %all-to-all-done.keys), custom_call_target="tpu_custom_call" | custom-call | flops 1207959552 | bytes 4194304 | tf_op jit(solution)/shard_map/pallas_call | solution.py:303
  81.9 4.4 %all-to-all-done.2.parts = bf16[16,32,128]{2,1,0:T(8,128)(2,1)} async-done(((bf16[16,32,128]{2,1,0:T(8,128)(2,1)}), bf16[16,32,128]{2,1,0:T(8,128)(2,1)}, u32[]{:S(2)}, u32[]{:S(2)}) %all-to-all-start.2) | async-done | bytes 131104 | tf_op jit(solution)/shard_map/all_to_all | solution.py:251
  86.3 2.4 %shard_map.74 = (f32[64,64]{1,0:T(8,128)S(1)}, bf16[32,64,256]{2,1,0:T(8,128)(2,1)}) custom-call(bf16[16,32,128]{2,1,0:T(8,128)(2,1)} %all-to-all-done.2.parts, bf16[32,64,256]{2,1,0:T(8,128)(2,1)S(1)} %copy-done.1, bf16[8,64,512]{2,1,0:T(8,128)(2,1)S(1)} %collective-permute-done.6.b.after, f32[8,128]{1,0:T(8,128)S(1)} %get-tuple-element.47.after2), custom_call_target="tpu_custom_call" | custom-call | flops 58720256 | bytes 1835008 | tf_op jit(solution)/shard_map/pallas_call | solution.py:307
  88.8 5.9 %all-to-all-start.3 = ((bf16[32,64,256]{2,1,0:T(8,128)(2,1)}), bf16[32,64,256]{2,1,0:T(8,128)(2,1)S(1)}, u32[]{:S(2)}, u32[]{:S(2)}) async-start(bf16[32,64,256]{2,1,0:T(8,128)(2,1)} %get-tuple-element.48), calls=%async_computation.3 | async-start | bytes 2097152 | tf_op jit(solution)/shard_map/all_to_all | solution.py:251
  95.4 3.4 %collective-permute-start.7 = (bf16[4,64,512]{2,1,0:T(8,128)(2,1)S(1)}, bf16[4,64,512]{2,1,0:T(8,128)(2,1)S(1)}, u32[]{:S(2)}, u32[]{:S(2)}) collective-permute-start(bf16[4,64,512]{2,1,0:T(8,128)(2,1)S(1)} %get-tuple-element.41), channel_id=1, source_target_pairs={{0,8},{8,0},{16,24},{24,16},{32,40},{40,32},{48,56},{56,48},{1,9},... | collective-permute-start | bytes 786440 | tf_op jit(solution)/shard_map/ppermute | solution.py:325
  98.7 2.5 %collective-permute-start.3 = (bf16[256,576]{1,0:T(8,128)(2,1)}, bf16[256,576]{1,0:T(8,128)(2,1)S(1)}, u32[]{:S(2)}, u32[]{:S(2)}) collective-permute-start(bf16[256,576]{1,0:T(8,128)(2,1)} %copy-done.9), channel_id=1, source_target_pairs={{0,1},{1,2},{2,3},{3,0},{4,5},{5,6},{6,7},{7,4},{8,9},{9,10},{10,1... | collective-permute-start | bytes 884744 | tf_op jit(solution)/shard_map/ppermute | solution.py:247
  101.2 4.3 %collective-permute-start.4 = (bf16[256,576]{1,0:T(8,128)(2,1)}, bf16[256,576]{1,0:T(8,128)(2,1)}, u32[]{:S(2)}, u32[]{:S(2)}) collective-permute-start(bf16[256,576]{1,0:T(8,128)(2,1)} %copy-done.8), channel_id=1, source_target_pairs={{0,2},{1,3},{2,0},{3,1},{4,6},{5,7},{6,4},{7,5},{8,10},{9,11},{10,... | collective-permute-start | bytes 884744 | tf_op jit(solution)/shard_map/ppermute | solution.py:247
  105.5 1.9 %collective-permute-start.5 = (bf16[256,576]{1,0:T(8,128)(2,1)}, bf16[256,576]{1,0:T(8,128)(2,1)}, u32[]{:S(2)}, u32[]{:S(2)}) collective-permute-start(bf16[256,576]{1,0:T(8,128)(2,1)} %copy-done.7), channel_id=1, source_target_pairs={{0,3},{1,0},{2,1},{3,2},{4,7},{5,4},{6,5},{7,6},{8,11},{9,8},{10,9... | collective-permute-start | bytes 884744 | tf_op jit(solution)/shard_map/ppermute | solution.py:247
  107.4 6.7 %collective-permute-done.7.b = bf16[4,64,512]{2,1,0:T(8,128)(2,1)S(1)} collective-permute-done((bf16[4,64,512]{2,1,0:T(8,128)(2,1)S(1)}, bf16[4,64,512]{2,1,0:T(8,128)(2,1)S(1)}, u32[]{:S(2)}, u32[]{:S(2)}) %collective-permute-start.7) | collective-permute-done | bytes 262176 | tf_op jit(solution)/shard_map/ppermute | solution.py:325
  114.7 2.8 %collective-permute-start.8 = (bf16[2,64,512]{2,1,0:T(8,128)(2,1)S(1)}, bf16[2,64,512]{2,1,0:T(8,128)(2,1)S(1)}, u32[]{:S(2)}, u32[]{:S(2)}) collective-permute-start(bf16[2,64,512]{2,1,0:T(8,128)(2,1)S(1)} %get-tuple-element.44), channel_id=1, source_target_pairs={{0,16},{8,24},{16,0},{24,8},{32,48},{40,56},{48,32},{56,40},{1,17}... | collective-permute-start | bytes 393224 | tf_op jit(solution)/shard_map/ppermute | solution.py:325
  117.6 0.9 shard_map.75
  118.5 8.4 %all-to-all-start.4 = ((f32[16,8,128]{2,1,0:T(8,128)}), f32[16,8,128]{2,1,0:T(8,128)S(1)}, u32[]{:S(2)}, u32[]{:S(2)}) async-start(f32[16,8,128]{2,1,0:T(8,128)} %get-tuple-element.54), calls=%async_computation.4 | async-start | bytes 131072 | tf_op jit(solution)/shard_map/all_to_all | solution.py:251
  127.0 1.1 shard_map.76
  128.1 7.7 %collective-permute-start.9 = (bf16[1,64,512]{2,1,0:T(8,128)(2,1)S(1)}, bf16[1,64,512]{2,1,0:T(8,128)(2,1)S(1)}, u32[]{:S(2)}, u32[]{:S(2)}) collective-permute-start(bf16[1,64,512]{2,1,0:T(8,128)(2,1)S(1)} %get-tuple-element.52), channel_id=1, source_target_pairs={{0,32},{8,40},{16,48},{24,56},{32,0},{40,8},{48,16},{56,24},{1,33}... | collective-permute-start | bytes 196616 | tf_op jit(solution)/shard_map/ppermute | solution.py:325
  135.9 1.9 %add_convert_fusion = bf16[256,576]{1,0:T(8,128)(2,1)} fusion(bf16[256,576]{1,0:T(8,128)(2,1)} %collective-permute-done.5, bf16[256,576]{1,0:T(8,128)(2,1)} %collective-permute-done.4, f32[256,576]{1,0:T(8,128)S(1)} %get-tuple-element.34, bf16[256,576]{1,0:T(8,128)(2,1)S(1)} %collective-permute-done.3), kind=kLoop, calls=%fused_computation | loop fusion | flops 1032192 | bytes 1769472 | tf_op jit(solution)/shard_map/convert_element_type | solution.py:332
  (33 shorter events, 6.4 us)
Async XLA Ops:
  0.6 13.6 %copy-start.4 = (bf16[1,4,64,512]{3,2,1,0:T(8,128)(2,1)S(1)}, bf16[1,4,64,512]{3,2,1,0:T(8,128)(2,1)}, u32[]{:S(2)}) copy-start(bf16[1,4,64,512]{3,2,1,0:T(8,128)(2,1)} %param.6) | copy-start | bytes 786436
  0.6 13.6 %copy-start.3 = (bf16[1,4,64,576]{3,2,1,0:T(8,128)(2,1)S(1)}, bf16[1,4,64,576]{3,2,1,0:T(8,128)(2,1)}, u32[]{:S(2)}) copy-start(bf16[1,4,64,576]{3,2,1,0:T(8,128)(2,1)} %param.4) | copy-start | bytes 884740
  2.8 45.0 %all-to-all-start = ((bf16[16,64,576]{2,1,0:T(8,128)(2,1)}), bf16[16,64,576]{2,1,0:T(8,128)(2,1)S(1)}, u32[]{:S(2)}, u32[]{:S(2)}) async-start(bf16[16,64,576]{2,1,0:T(8,128)(2,1)} %broadcast_in_dim.17), calls=%async_computation | async-start | bytes 2621440 | tf_op jit(solution)/shard_map/all_to_all | solution.py:251
  14.4 18.1 %collective-permute-start.2 = (bf16[256,1152]{1,0:T(8,128)(2,1)S(1)}, bf16[256,1152]{1,0:T(8,128)(2,1)S(1)}, u32[]{:S(2)}, u32[]{:S(2)}) collective-permute-start(bf16[256,1152]{1,0:T(8,128)(2,1)S(1)} %shard_map.68.refs_0_), channel_id=1, source_target_pairs={{0,1},{1,2},{2,3},{3,0},{4,5},{5,6},{6,7},{7,4},{8,9},{9,10},{10,1... | collective-permute-start | bytes 1769480 | tf_op jit(solution)/shard_map/ppermute | solution.py:247
  16.7 19.7 %collective-permute-start.1 = (bf16[256,1152]{1,0:T(8,128)(2,1)S(1)}, bf16[256,1152]{1,0:T(8,128)(2,1)S(1)}, u32[]{:S(2)}, u32[]{:S(2)}) collective-permute-start(bf16[256,1152]{1,0:T(8,128)(2,1)S(1)} %shard_map.68.refs_0_), channel_id=1, source_target_pairs={{0,2},{1,3},{2,0},{3,1},{4,6},{5,7},{6,4},{7,5},{8,10},{9,11},{10,... | collective-permute-start | bytes 1769480 | tf_op jit(solution)/shard_map/ppermute | solution.py:247
  21.1 26.3 %collective-permute-start = (bf16[256,1152]{1,0:T(8,128)(2,1)S(1)}, bf16[256,1152]{1,0:T(8,128)(2,1)}, u32[]{:S(2)}, u32[]{:S(2)}) collective-permute-start(bf16[256,1152]{1,0:T(8,128)(2,1)S(1)} %shard_map.68.refs_0_), channel_id=1, source_target_pairs={{0,3},{1,0},{2,1},{3,2},{4,7},{5,4},{6,5},{7,6},{8,11},{9,8},{10,9... | collective-permute-start | bytes 1769480 | tf_op jit(solution)/shard_map/ppermute | solution.py:247
  23.0 1.2 copy-start.6
  25.8 1.0 copy-start
  66.2 20.1 %collective-permute-start.6 = (bf16[8,64,512]{2,1,0:T(8,128)(2,1)}, bf16[8,64,512]{2,1,0:T(8,128)(2,1)S(1)}, u32[]{:S(2)}, u32[]{:S(2)}) collective-permute-start(bf16[8,64,512]{2,1,0:T(8,128)(2,1)} %get-tuple-element.39), channel_id=1, source_target_pairs={{0,4},{4,0},{1,5},{5,1},{2,6},{6,2},{3,7},{7,3},{8,12},{12,8},{9,1... | collective-permute-start | bytes 1572872 | tf_op jit(solution)/shard_map/ppermute | solution.py:302
  69.5 16.8 %all-to-all-start.2 = ((bf16[16,32,128]{2,1,0:T(8,128)(2,1)}), bf16[16,32,128]{2,1,0:T(8,128)(2,1)}, u32[]{:S(2)}, u32[]{:S(2)}) async-start(bf16[16,32,128]{2,1,0:T(8,128)(2,1)} %get-tuple-element.45), calls=%async_computation.2 | async-start | bytes 262144 | tf_op jit(solution)/shard_map/all_to_all | solution.py:251
  76.3 1.6 %copy-start.5 = (bf16[1024,1024]{1,0:T(8,128)(2,1)S(1)}, bf16[1024,1024]{1,0:T(8,128)(2,1)}, u32[]{:S(2)}) copy-start(bf16[1024,1024]{1,0:T(8,128)(2,1)} %get-tuple-element.33.ds_ref) | copy-start | bytes 6291460
  77.9 8.4 %copy-start.1 = (bf16[32,64,256]{2,1,0:T(8,128)(2,1)S(1)}, bf16[32,64,256]{2,1,0:T(8,128)(2,1)}, u32[]{:S(2)}) copy-start(bf16[32,64,256]{2,1,0:T(8,128)(2,1)} %copy-done) | copy-start | bytes 3145732
  79.8 0.7 copy-start.7
  80.5 0.7 copy-start.8
  81.2 0.7 copy-start.9
  81.9 12.8 %copy-start.2 = (bf16[8,64,512]{2,1,0:T(8,128)(2,1)S(1)}, bf16[8,64,512]{2,1,0:T(8,128)(2,1)}, u32[]{:S(2)}) copy-start(bf16[8,64,512]{2,1,0:T(8,128)(2,1)} %get-tuple-element.38.a) | copy-start | bytes 1572868
  88.8 28.8 %all-to-all-start.3 = ((bf16[32,64,256]{2,1,0:T(8,128)(2,1)}), bf16[32,64,256]{2,1,0:T(8,128)(2,1)S(1)}, u32[]{:S(2)}, u32[]{:S(2)}) async-start(bf16[32,64,256]{2,1,0:T(8,128)(2,1)} %get-tuple-element.48), calls=%async_computation.3 | async-start | bytes 2097152 | tf_op jit(solution)/shard_map/all_to_all | solution.py:251
  95.4 18.8 %collective-permute-start.7 = (bf16[4,64,512]{2,1,0:T(8,128)(2,1)S(1)}, bf16[4,64,512]{2,1,0:T(8,128)(2,1)S(1)}, u32[]{:S(2)}, u32[]{:S(2)}) collective-permute-start(bf16[4,64,512]{2,1,0:T(8,128)(2,1)S(1)} %get-tuple-element.41), channel_id=1, source_target_pairs={{0,8},{8,0},{16,24},{24,16},{32,40},{40,32},{48,56},{56,48},{1,9},... | collective-permute-start | bytes 786440 | tf_op jit(solution)/shard_map/ppermute | solution.py:325
  98.7 37.1 %collective-permute-start.3 = (bf16[256,576]{1,0:T(8,128)(2,1)}, bf16[256,576]{1,0:T(8,128)(2,1)S(1)}, u32[]{:S(2)}, u32[]{:S(2)}) collective-permute-start(bf16[256,576]{1,0:T(8,128)(2,1)} %copy-done.9), channel_id=1, source_target_pairs={{0,1},{1,2},{2,3},{3,0},{4,5},{5,6},{6,7},{7,4},{8,9},{9,10},{10,1... | collective-permute-start | bytes 884744 | tf_op jit(solution)/shard_map/ppermute | solution.py:247
  101.2 34.6 %collective-permute-start.4 = (bf16[256,576]{1,0:T(8,128)(2,1)}, bf16[256,576]{1,0:T(8,128)(2,1)}, u32[]{:S(2)}, u32[]{:S(2)}) collective-permute-start(bf16[256,576]{1,0:T(8,128)(2,1)} %copy-done.8), channel_id=1, source_target_pairs={{0,2},{1,3},{2,0},{3,1},{4,6},{5,7},{6,4},{7,5},{8,10},{9,11},{10,... | collective-permute-start | bytes 884744 | tf_op jit(solution)/shard_map/ppermute | solution.py:247
  105.5 30.4 %collective-permute-start.5 = (bf16[256,576]{1,0:T(8,128)(2,1)}, bf16[256,576]{1,0:T(8,128)(2,1)}, u32[]{:S(2)}, u32[]{:S(2)}) collective-permute-start(bf16[256,576]{1,0:T(8,128)(2,1)} %copy-done.7), channel_id=1, source_target_pairs={{0,3},{1,0},{2,1},{3,2},{4,7},{5,4},{6,5},{7,6},{8,11},{9,8},{10,9... | collective-permute-start | bytes 884744 | tf_op jit(solution)/shard_map/ppermute | solution.py:247
  114.7 12.2 %collective-permute-start.8 = (bf16[2,64,512]{2,1,0:T(8,128)(2,1)S(1)}, bf16[2,64,512]{2,1,0:T(8,128)(2,1)S(1)}, u32[]{:S(2)}, u32[]{:S(2)}) collective-permute-start(bf16[2,64,512]{2,1,0:T(8,128)(2,1)S(1)} %get-tuple-element.44), channel_id=1, source_target_pairs={{0,16},{8,24},{16,0},{24,8},{32,48},{40,56},{48,32},{56,40},{1,17}... | collective-permute-start | bytes 393224 | tf_op jit(solution)/shard_map/ppermute | solution.py:325
  118.5 21.0 %all-to-all-start.4 = ((f32[16,8,128]{2,1,0:T(8,128)}), f32[16,8,128]{2,1,0:T(8,128)S(1)}, u32[]{:S(2)}, u32[]{:S(2)}) async-start(f32[16,8,128]{2,1,0:T(8,128)} %get-tuple-element.54), calls=%async_computation.4 | async-start | bytes 131072 | tf_op jit(solution)/shard_map/all_to_all | solution.py:251
  128.1 10.3 %collective-permute-start.9 = (bf16[1,64,512]{2,1,0:T(8,128)(2,1)S(1)}, bf16[1,64,512]{2,1,0:T(8,128)(2,1)S(1)}, u32[]{:S(2)}, u32[]{:S(2)}) collective-permute-start(bf16[1,64,512]{2,1,0:T(8,128)(2,1)S(1)} %get-tuple-element.52), channel_id=1, source_target_pairs={{0,32},{8,40},{16,48},{24,56},{32,0},{40,8},{48,16},{56,24},{1,33}... | collective-permute-start | bytes 196616 | tf_op jit(solution)/shard_map/ppermute | solution.py:325

commit v10 on v7

--- a/solution.py
+++ b/solution.py
@@ -51,6 +51,13 @@
     out[:, :lat] = dout[...]
     out[:, lat : lat + width] = query[...]
     out[:, lat + width :] = jnp.zeros((out.shape[0], out.shape[1] - lat - width), out.dtype)
+
+
+def latent_copies_kernel(latent, out):
+    half = latent.shape[0] // 2
+    packed = jnp.concatenate([latent[:half], latent[half:]], axis=1)
+    for i in range(out.shape[0]):
+        out[i] = packed
 
 
 def columns_kernel(block, n_z, n_grp, n_core, hid, out, token):
@@ -78,8 +85,11 @@
     return k.reshape(k.shape[0] * k.shape[1], k.shape[2])
 
 
-def scores_kernel(lat, heads, pos, keys, after, *refs):
-    blocks, (e_ref, dp_ref, st_ref) = refs[:-3], refs[-3:]
+def scores_kernel(lat, heads, pos, packed, after, *refs):
+    blocks, (e_ref, dp_ref, st_ref, keys) = refs[:-4], refs[-4:]
+    wide = keys.shape[2]
+    for i in range(keys.shape[0]):
+        keys[i] = jnp.concatenate([packed[i, :, :wide], packed[i, :, wide:]])
     z, y, x = pos[0], pos[1], pos[2]
     grp, k_dev, width = keys.shape
     n_x = len(blocks)
@@ -93,7 +103,7 @@
         q, o = t[:, lat : lat + width], t[:, :lat]
         cols = slice(b * rows, (b + 1) * rows)
         lane = lax.broadcasted_iota(jnp.int32, (k_dev, rows), 1)
-        q_pos = ((z * 2 + y) * n_x + lax.rem(x + b, n_x)) * tok + lane // heads + first_query
+        q_pos = ((z * 2 + y) * n_x + lax.rem(x + n_x - b, n_x)) * tok + lane // heads + first_query
         top = None
         for i in range(tiles):
             s = nt(key_tile(keys, i, per), q) * softmax_scale
@@ -133,7 +143,7 @@
         cols = slice(b * rows, (b + 1) * rows)
         theirs = []
         for s in range(n_x):
-            at = lax.rem(x + b + n_x - s, n_x)
+            at = lax.rem(s + b + n_x - x, n_x)
             v = stats[s, 0:4]
             for j in range(1, n_x):
                 v = jnp.where(at == j, stats[s, 4 * j : 4 * j + 4], v)
@@ -257,23 +267,27 @@
     swap = [(0, 1), (1, 0)]
     pos = jnp.stack([lax.axis_index(a) for a in ("z", "y", "x")]).astype(jnp.int32)
 
-    keys = trade(jnp.broadcast_to(latent, (nz * ny, k_dev, width)), ("z", "y"))
+    (packed,) = call(
+        latent_copies_kernel, [((nz * ny, k_dev // 2, 2 * width), bf16)], 1, moved=2 * nz * ny * k_dev * width
+    )(latent[0])
+    packed = trade(packed, ("z", "y"))
     (own,) = call(pack_kernel, [((rows, -(-(lat + width) // 128) * 128), bf16)], 2, moved=4 * rows * width)(
         dout.reshape(rows, lat), query.reshape(rows, width)
     )
-    blocks = [own] + [fetch(own, k, nx) for k in range(1, nx)]
+    blocks = [own] + [fetch(own, nx - k, nx) for k in range(1, nx)]
 
     wide = nw * nz * SLOT
     cols, token = call(
         functools.partial(columns_kernel, block, nz, ny * nx, nc), [((nc * ny * nx, k_dev, wide), bf16), TOKEN], 1,
         flops=2 * k_dev * model * 1024, moved=4 * k_dev * model, limit=20,
     )(hidden[0])
-    e, dp, st = call(
+    e, dp, st, keys = call(
         functools.partial(scores_kernel, lat, heads),
-        [((n_keys, n_rows), f32)] * 2 + [((4 * nx, rows), f32)], 7, smem=(0,),
+        [((n_keys, n_rows), f32)] * 2 + [((4 * nx, rows), f32), ((nz * ny, k_dev, width), bf16)],
+        7, smem=(0,),
         unused=(2,),
         flops=2 * pairs * (width + lat), moved=8 * pairs, limit=20,
-    )(pos, keys, token, *blocks)
+    )(pos, packed, token, *blocks)
     stats = trade(jnp.broadcast_to(st[None], (nx,) + st.shape), "x")
     ds, rope_part, mine, other = call(
         functools.partial(dscores_kernel, lat),
@@ -300,7 +314,7 @@
         flops=2 * k_dev * nc * ny * nx * wide * rope, moved=4 * k_dev * model, limit=20,
     )(rope_part, cols, other, dq_token)
     terms = trade(terms, ("c", "y", "x"))
-    dq = [dq[0]] + [fetch(dq[k], nx - k, nx) for k in range(1, nx)]
+    dq = [dq[0]] + [fetch(dq[k], k, nx) for k in range(1, nx)]
     kept, came = mine, other
     for bit in range(3):
         if bit == 2:

time: 137 us -> 139 us (1.015)
  the two profiles are of different devices: /device:TPU:40 before, /device:TPU:6 now
where the time goes in v10:
time: 139 us; the launch traced here: 137 us
  starting transfers between devices  68.8 us (49%)
  waiting for transfers between devices  28.4 us (20%)
  Pallas kernels  21.1 us (15%)
  blocking collectives  8.54 us (6%)
  local copies, waits for them, and re-layouts  7.13 us (5%)
  other arithmetic  2.15 us (2%)
    all_to_all x4, starting transfers between devices, trade(): return lax.all_to_all(value, axes, 0, 0, tiled=True)  32.8 us
    ppermute x6, waiting for transfers between devices, fetch(): return lax.ppermute(value, 'x', [(s, (s - offset) % n) for s in range(n)])  20.8 us
    ppermute x6, starting transfers between devices, fetch(): return lax.ppermute(value, 'x', [(s, (s - offset) % n) for s in range(n)])  19.6 us
    ppermute x3, starting transfers between devices, body(): came = lax.ppermute(sent, 'z', [(i, i ^ 1 << bit) for i in range(nz)])  12.9 us
    all_to_all x1, blocking collectives, trade(): return lax.all_to_all(value, axes, 0, 0, tiled=True)  8.54 us
    unnamed x16, local copies, waits for them, and re-layouts  7.13 us
    pallas_call x1, Pallas kernels, body(): call(functools.partial(dscores_kernel, lat), [((n_keys, n_rows), bf16), (...  6.06 us
    all_to_all x4, waiting for transfers between devices, trade(): return lax.all_to_all(value, axes, 0, 0, tiled=True)  6 us
  transfers between devices with their start and end apart: 14, of which 4 were waited for; matrix products, arithmetic and copies ran while one was open for 2% of the time, Pallas kernels for 5%

profile of v10, /device:TPU:6, one launch (start us, length us, event | category | flops | bytes accessed | tf_op | source)
XLA Modules:
  0.0 137.1 jit_solution(9520924348152608270)
XLA Ops:
  1.6 1.2 shard_map.67
  2.8 11.4 %all-to-all-start = ((bf16[16,32,1152]{2,1,0:T(8,128)(2,1)}), bf16[16,32,1152]{2,1,0:T(8,128)(2,1)S(1)}, u32[]{:S(2)}, u32[]{:S(2)}) async-start(bf16[16,32,1152]{2,1,0:T(8,128)(2,1)} %shard_map.67), calls=%async_computation | async-start | bytes 2359296 | tf_op jit(solution)/shard_map/all_to_all | solution.py:254
  14.3 2.7 %collective-permute-start.2 = (bf16[256,1152]{1,0:T(8,128)(2,1)S(1)}, bf16[256,1152]{1,0:T(8,128)(2,1)S(1)}, u32[]{:S(2)}, u32[]{:S(2)}) collective-permute-start(bf16[256,1152]{1,0:T(8,128)(2,1)S(1)} %shard_map.69.refs_0_), channel_id=1, source_target_pairs={{0,3},{1,0},{2,1},{3,2},{4,7},{5,4},{6,5},{7,6},{8,11},{9,8},{10,9... | collective-permute-start | bytes 1769480 | tf_op jit(solution)/shard_map/ppermute | solution.py:250
  17.0 3.0 %collective-permute-start.1 = (bf16[256,1152]{1,0:T(8,128)(2,1)S(1)}, bf16[256,1152]{1,0:T(8,128)(2,1)}, u32[]{:S(2)}, u32[]{:S(2)}) collective-permute-start(bf16[256,1152]{1,0:T(8,128)(2,1)S(1)} %shard_map.69.refs_0_), channel_id=1, source_target_pairs={{0,2},{1,3},{2,0},{3,1},{4,6},{5,7},{6,4},{7,5},{8,10},{9,11},{10,... | collective-permute-start | bytes 1769480 | tf_op jit(solution)/shard_map/ppermute | solution.py:250
  20.1 4.0 %collective-permute-start = (bf16[256,1152]{1,0:T(8,128)(2,1)S(1)}, bf16[256,1152]{1,0:T(8,128)(2,1)}, u32[]{:S(2)}, u32[]{:S(2)}) collective-permute-start(bf16[256,1152]{1,0:T(8,128)(2,1)S(1)} %shard_map.69.refs_0_), channel_id=1, source_target_pairs={{0,1},{1,2},{2,3},{3,0},{4,5},{5,6},{6,7},{7,4},{8,9},{9,10},{10,1... | collective-permute-start | bytes 1769480 | tf_op jit(solution)/shard_map/ppermute | solution.py:250
  24.1 1.2 copy-done.5
  25.3 1.3 shard_map.68
  26.6 18.2 %collective-permute-done.2.refs_3_ = bf16[256,1152]{1,0:T(8,128)(2,1)S(1)} collective-permute-done((bf16[256,1152]{1,0:T(8,128)(2,1)S(1)}, bf16[256,1152]{1,0:T(8,128)(2,1)S(1)}, u32[]{:S(2)}, u32[]{:S(2)}) %collective-permute-start.2) | collective-permute-done | bytes 589856 | tf_op jit(solution)/shard_map/ppermute | solution.py:250
  44.8 2.6 %collective-permute-done.refs_1_ = bf16[256,1152]{1,0:T(8,128)(2,1)} collective-permute-done((bf16[256,1152]{1,0:T(8,128)(2,1)S(1)}, bf16[256,1152]{1,0:T(8,128)(2,1)}, u32[]{:S(2)}, u32[]{:S(2)}) %collective-permute-start) | collective-permute-done | bytes 589856 | tf_op jit(solution)/shard_map/ppermute | solution.py:250
  47.5 4.5 %shard_map.70 = (f32[1024,1024]{1,0:T(8,128)S(1)}, f32[1024,1024]{1,0:T(8,128)S(1)}, f32[16,256]{1,0:T(8,128)S(1)}, bf16[16,64,576]{2,1,0:T(8,128)(2,1)S(1)}) custom-call(s32[3]{0:T(128)S(1)} %pad_add_fusion.pos, bf16[16,32,1152]{2,1,0:T(8,128)(2,1)S(1)} %all-to-all-done.packed, f32[8,128]{1,0:T(8,128)S(1)} %get-tuple-element.30.after, ...), custom_call_target="tpu_custom_call" | custom-call | flops 2281701376 | bytes 8388608 | tf_op jit(solution)/shard_map/pallas_call | solution.py:284
  52.0 1.1 copy-done.6
  53.0 8.5 %all_to_all.25.stats = f32[4,16,256]{2,1,0:T(8,128)S(1)} all-to-all(f32[4,16,256]{2,1,0:T(8,128)S(1)} %broadcast_in_dim.4), channel_id=1, replica_groups=mesh['w'=4,'c'=2,'z'=8,'y'=2,'x'=4] {'x'}, dimensions={0} | all-to-all | bytes 131072 | tf_op jit(solution)/shard_map/all_to_all | solution.py:254
  61.6 6.1 %shard_map.71 = (bf16[1024,1024]{1,0:T(8,128)(2,1)}, bf16[16,32,128]{2,1,0:T(8,128)(2,1)}, bf16[8,64,512]{2,1,0:T(8,128)(2,1)}, bf16[8,64,512]{2,1,0:T(8,128)(2,1)}) custom-call(s32[3]{0:T(128)S(1)} %pad_add_fusion.pos, f32[4,16,256]{2,1,0:T(8,128)S(1)} %all_to_all.25.stats, f32[16,256]{1,0:T(8,128)S(1)} %get-tuple-element.31.st, ...), custom_call_target="tpu_custom_call" | custom-call | flops 2281701376 | bytes 12582912 | tf_op jit(solution)/shard_map/pallas_call | solution.py:292
  67.6 3.5 %collective-permute-start.6 = (bf16[8,64,512]{2,1,0:T(8,128)(2,1)}, bf16[8,64,512]{2,1,0:T(8,128)(2,1)S(1)}, u32[]{:S(2)}, u32[]{:S(2)}) collective-permute-start(bf16[8,64,512]{2,1,0:T(8,128)(2,1)} %get-tuple-element.41), channel_id=1, source_target_pairs={{0,4},{4,0},{1,5},{5,1},{2,6},{6,2},{3,7},{7,3},{8,12},{12,8},{9,1... | collective-permute-start | bytes 1572872 | tf_op jit(solution)/shard_map/ppermute | solution.py:307
  71.2 6.8 %all-to-all-start.2 = ((bf16[16,32,128]{2,1,0:T(8,128)(2,1)}), bf16[16,32,128]{2,1,0:T(8,128)(2,1)S(1)}, u32[]{:S(2)}, u32[]{:S(2)}) async-start(bf16[16,32,128]{2,1,0:T(8,128)(2,1)} %get-tuple-element.47), calls=%async_computation.2 | async-start | bytes 262144 | tf_op jit(solution)/shard_map/all_to_all | solution.py:254
  78.0 1.6 %copy-done.4 = bf16[1024,1024]{1,0:T(8,128)(2,1)S(1)} copy-done((bf16[1024,1024]{1,0:T(8,128)(2,1)S(1)}, bf16[1024,1024]{1,0:T(8,128)(2,1)}, u32[]{:S(2)}) %copy-start.4) | copy-done | bytes 2097176
  79.6 1.3 copy-done.7
  80.9 1.8 %shard_map.72 = (f32[8,128]{1,0:T(8,128)S(1)}, f32[256,576]{1,0:T(8,128)S(1)}, bf16[256,576]{1,0:T(8,128)(2,1)S(1)}, bf16[256,576]{1,0:T(8,128)(2,1)S(1)}, bf16[256,576]{1,0:T(8,128)(2,1)S(1)}) custom-call(bf16[1024,1024]{1,0:T(8,128)(2,1)S(1)} %copy-done.4, bf16[16,64,576]{2,1,0:T(8,128)(2,1)S(1)} %copy-done.7), custom_call_target="tpu_custom_call" | custom-call | flops 1207959552 | bytes 4194304 | tf_op jit(solution)/shard_map/pallas_call | solution.py:308
  82.7 6.0 %all-to-all-done.2.parts = bf16[16,32,128]{2,1,0:T(8,128)(2,1)S(1)} async-done(((bf16[16,32,128]{2,1,0:T(8,128)(2,1)}), bf16[16,32,128]{2,1,0:T(8,128)(2,1)S(1)}, u32[]{:S(2)}, u32[]{:S(2)}) %all-to-all-start.2) | async-done | bytes 131104 | tf_op jit(solution)/shard_map/all_to_all | solution.py:254
  88.7 1.5 %shard_map.75 = (f32[64,64]{1,0:T(8,128)S(1)}, bf16[16,64,512]{2,1,0:T(8,128)(2,1)}) custom-call(bf16[16,32,128]{2,1,0:T(8,128)(2,1)S(1)} %all-to-all-done.2.parts, bf16[16,64,512]{2,1,0:T(8,128)(2,1)S(1)} %get-tuple-element.48.cols, bf16[8,64,512]{2,1,0:T(8,128)(2,1)S(1)} %collective-permute-done.6.b.after, f32[8,128]{1,0:T(8,128)S(1)} %get-tuple-element.49.after2), custom_call_target="tpu_custom_call" | custom-call | flops 67108864 | bytes 1835008 | tf_op jit(solution)/shard_map/pallas_call | solution.py:312
  90.3 5.6 %all-to-all-start.3 = ((bf16[16,64,512]{2,1,0:T(8,128)(2,1)}), bf16[16,64,512]{2,1,0:T(8,128)(2,1)S(1)}, u32[]{:S(2)}, u32[]{:S(2)}) async-start(bf16[16,64,512]{2,1,0:T(8,128)(2,1)} %get-tuple-element.50), calls=%async_computation.3 | async-start | bytes 2097152 | tf_op jit(solution)/shard_map/all_to_all | solution.py:254
  95.9 1.0 copy-done
  97.6 2.4 %collective-permute-start.7 = (bf16[4,64,512]{2,1,0:T(8,128)(2,1)S(1)}, bf16[4,64,512]{2,1,0:T(8,128)(2,1)S(1)}, u32[]{:S(2)}, u32[]{:S(2)}) collective-permute-start(bf16[4,64,512]{2,1,0:T(8,128)(2,1)S(1)} %get-tuple-element.43), channel_id=1, source_target_pairs={{0,8},{8,0},{16,24},{24,16},{32,40},{40,32},{48,56},{56,48},{1,9},... | collective-permute-start | bytes 786440 | tf_op jit(solution)/shard_map/ppermute | solution.py:330
  100.1 2.8 %collective-permute-start.3 = (bf16[256,576]{1,0:T(8,128)(2,1)S(1)}, bf16[256,576]{1,0:T(8,128)(2,1)}, u32[]{:S(2)}, u32[]{:S(2)}) collective-permute-start(bf16[256,576]{1,0:T(8,128)(2,1)S(1)} %get-tuple-element.37), channel_id=1, source_target_pairs={{0,3},{1,0},{2,1},{3,2},{4,7},{5,4},{6,5},{7,6},{8,11},{9,8},{10,9... | collective-permute-start | bytes 884744 | tf_op jit(solution)/shard_map/ppermute | solution.py:250
  102.8 2.7 %collective-permute-start.4 = (bf16[256,576]{1,0:T(8,128)(2,1)S(1)}, bf16[256,576]{1,0:T(8,128)(2,1)}, u32[]{:S(2)}, u32[]{:S(2)}) collective-permute-start(bf16[256,576]{1,0:T(8,128)(2,1)S(1)} %get-tuple-element.38), channel_id=1, source_target_pairs={{0,2},{1,3},{2,0},{3,1},{4,6},{5,7},{6,4},{7,5},{8,10},{9,11},{10,... | collective-permute-start | bytes 884744 | tf_op jit(solution)/shard_map/ppermute | solution.py:250
  105.5 4.4 %collective-permute-start.5 = (bf16[256,576]{1,0:T(8,128)(2,1)S(1)}, bf16[256,576]{1,0:T(8,128)(2,1)}, u32[]{:S(2)}, u32[]{:S(2)}) collective-permute-start(bf16[256,576]{1,0:T(8,128)(2,1)S(1)} %get-tuple-element.39), channel_id=1, source_target_pairs={{0,1},{1,2},{2,3},{3,0},{4,5},{5,6},{6,7},{7,4},{8,9},{9,10},{10,1... | collective-permute-start | bytes 884744 | tf_op jit(solution)/shard_map/ppermute | solution.py:250
  110.5 2.9 %collective-permute-start.8 = (bf16[2,64,512]{2,1,0:T(8,128)(2,1)S(1)}, bf16[2,64,512]{2,1,0:T(8,128)(2,1)S(1)}, u32[]{:S(2)}, u32[]{:S(2)}) collective-permute-start(bf16[2,64,512]{2,1,0:T(8,128)(2,1)S(1)} %get-tuple-element.46), channel_id=1, source_target_pairs={{0,16},{8,24},{16,0},{24,8},{32,48},{40,56},{48,32},{56,40},{1,17}... | collective-permute-start | bytes 393224 | tf_op jit(solution)/shard_map/ppermute | solution.py:330
  114.3 8.9 %all-to-all-start.4 = ((f32[32,8,128]{2,1,0:T(8,128)}), f32[32,8,128]{2,1,0:T(8,128)S(1)}, u32[]{:S(2)}, u32[]{:S(2)}) async-start(f32[32,8,128]{2,1,0:T(8,128)} %get-tuple-element.56), calls=%async_computation.4 | async-start | bytes 262144 | tf_op jit(solution)/shard_map/all_to_all | solution.py:254
  123.3 1.1 shard_map.77
  124.4 7.6 %collective-permute-start.9 = (bf16[1,64,512]{2,1,0:T(8,128)(2,1)S(1)}, bf16[1,64,512]{2,1,0:T(8,128)(2,1)S(1)}, u32[]{:S(2)}, u32[]{:S(2)}) collective-permute-start(bf16[1,64,512]{2,1,0:T(8,128)(2,1)S(1)} %get-tuple-element.54), channel_id=1, source_target_pairs={{0,32},{8,40},{16,48},{24,56},{32,0},{40,8},{48,16},{56,24},{1,33}... | collective-permute-start | bytes 196616 | tf_op jit(solution)/shard_map/ppermute | solution.py:330
  132.1 2.1 %add_convert_fusion = bf16[256,576]{1,0:T(8,128)(2,1)} fusion(bf16[256,576]{1,0:T(8,128)(2,1)} %collective-permute-done.5, bf16[256,576]{1,0:T(8,128)(2,1)} %collective-permute-done.4, f32[256,576]{1,0:T(8,128)S(1)} %get-tuple-element.36, bf16[256,576]{1,0:T(8,128)(2,1)} %collective-permute-done.3), kind=kLoop, calls=%fused_computation | loop fusion | flops 1032192 | bytes 1769472 | tf_op jit(solution)/shard_map/convert_element_type | solution.py:337
  134.1 1.6 %collective-permute-done.9.b = bf16[1,64,512]{2,1,0:T(8,128)(2,1)S(1)} collective-permute-done((bf16[1,64,512]{2,1,0:T(8,128)(2,1)S(1)}, bf16[1,64,512]{2,1,0:T(8,128)(2,1)S(1)}, u32[]{:S(2)}, u32[]{:S(2)}) %collective-permute-start.9) | collective-permute-done | bytes 65568 | tf_op jit(solution)/shard_map/ppermute | solution.py:330
  (29 shorter events, 4.7 us)
Async XLA Ops:
  0.6 13.6 %copy-start.2 = (bf16[1,4,64,512]{3,2,1,0:T(8,128)(2,1)S(1)}, bf16[1,4,64,512]{3,2,1,0:T(8,128)(2,1)}, u32[]{:S(2)}) copy-start(bf16[1,4,64,512]{3,2,1,0:T(8,128)(2,1)} %param.6) | copy-start | bytes 786436
  0.6 13.6 %copy-start.1 = (bf16[1,4,64,576]{3,2,1,0:T(8,128)(2,1)S(1)}, bf16[1,4,64,576]{3,2,1,0:T(8,128)(2,1)}, u32[]{:S(2)}) copy-start(bf16[1,4,64,576]{3,2,1,0:T(8,128)(2,1)} %param.4) | copy-start | bytes 884740
  0.7 0.9 copy-start.3
  2.8 44.7 %all-to-all-start = ((bf16[16,32,1152]{2,1,0:T(8,128)(2,1)}), bf16[16,32,1152]{2,1,0:T(8,128)(2,1)S(1)}, u32[]{:S(2)}, u32[]{:S(2)}) async-start(bf16[16,32,1152]{2,1,0:T(8,128)(2,1)} %shard_map.67), calls=%async_computation | async-start | bytes 2359296 | tf_op jit(solution)/shard_map/all_to_all | solution.py:254
  14.3 30.5 %collective-permute-start.2 = (bf16[256,1152]{1,0:T(8,128)(2,1)S(1)}, bf16[256,1152]{1,0:T(8,128)(2,1)S(1)}, u32[]{:S(2)}, u32[]{:S(2)}) collective-permute-start(bf16[256,1152]{1,0:T(8,128)(2,1)S(1)} %shard_map.69.refs_0_), channel_id=1, source_target_pairs={{0,3},{1,0},{2,1},{3,2},{4,7},{5,4},{6,5},{7,6},{8,11},{9,8},{10,9... | collective-permute-start | bytes 1769480 | tf_op jit(solution)/shard_map/ppermute | solution.py:250
  17.0 27.8 %collective-permute-start.1 = (bf16[256,1152]{1,0:T(8,128)(2,1)S(1)}, bf16[256,1152]{1,0:T(8,128)(2,1)}, u32[]{:S(2)}, u32[]{:S(2)}) collective-permute-start(bf16[256,1152]{1,0:T(8,128)(2,1)S(1)} %shard_map.69.refs_0_), channel_id=1, source_target_pairs={{0,2},{1,3},{2,0},{3,1},{4,6},{5,7},{6,4},{7,5},{8,10},{9,11},{10,... | collective-permute-start | bytes 1769480 | tf_op jit(solution)/shard_map/ppermute | solution.py:250
  20.1 27.4 %collective-permute-start = (bf16[256,1152]{1,0:T(8,128)(2,1)S(1)}, bf16[256,1152]{1,0:T(8,128)(2,1)}, u32[]{:S(2)}, u32[]{:S(2)}) collective-permute-start(bf16[256,1152]{1,0:T(8,128)(2,1)S(1)} %shard_map.69.refs_0_), channel_id=1, source_target_pairs={{0,1},{1,2},{2,3},{3,0},{4,5},{5,6},{6,7},{7,4},{8,9},{9,10},{10,1... | collective-permute-start | bytes 1769480 | tf_op jit(solution)/shard_map/ppermute | solution.py:250
  24.1 1.2 copy-start.5
  52.0 1.1 copy-start.6
  67.6 21.1 %collective-permute-start.6 = (bf16[8,64,512]{2,1,0:T(8,128)(2,1)}, bf16[8,64,512]{2,1,0:T(8,128)(2,1)S(1)}, u32[]{:S(2)}, u32[]{:S(2)}) collective-permute-start(bf16[8,64,512]{2,1,0:T(8,128)(2,1)} %get-tuple-element.41), channel_id=1, source_target_pairs={{0,4},{4,0},{1,5},{5,1},{2,6},{6,2},{3,7},{7,3},{8,12},{12,8},{9,1... | collective-permute-start | bytes 1572872 | tf_op jit(solution)/shard_map/ppermute | solution.py:307
  71.2 17.5 %all-to-all-start.2 = ((bf16[16,32,128]{2,1,0:T(8,128)(2,1)}), bf16[16,32,128]{2,1,0:T(8,128)(2,1)S(1)}, u32[]{:S(2)}, u32[]{:S(2)}) async-start(bf16[16,32,128]{2,1,0:T(8,128)(2,1)} %get-tuple-element.47), calls=%async_computation.2 | async-start | bytes 262144 | tf_op jit(solution)/shard_map/all_to_all | solution.py:254
  78.0 1.6 %copy-start.4 = (bf16[1024,1024]{1,0:T(8,128)(2,1)S(1)}, bf16[1024,1024]{1,0:T(8,128)(2,1)}, u32[]{:S(2)}) copy-start(bf16[1024,1024]{1,0:T(8,128)(2,1)} %get-tuple-element.34.ds_ref) | copy-start | bytes 6291460
  79.6 1.3 copy-start.7
  90.3 23.1 %all-to-all-start.3 = ((bf16[16,64,512]{2,1,0:T(8,128)(2,1)}), bf16[16,64,512]{2,1,0:T(8,128)(2,1)S(1)}, u32[]{:S(2)}, u32[]{:S(2)}) async-start(bf16[16,64,512]{2,1,0:T(8,128)(2,1)} %get-tuple-element.50), calls=%async_computation.3 | async-start | bytes 2097152 | tf_op jit(solution)/shard_map/all_to_all | solution.py:254
  95.9 1.0 copy-start
  97.6 12.3 %collective-permute-start.7 = (bf16[4,64,512]{2,1,0:T(8,128)(2,1)S(1)}, bf16[4,64,512]{2,1,0:T(8,128)(2,1)S(1)}, u32[]{:S(2)}, u32[]{:S(2)}) collective-permute-start(bf16[4,64,512]{2,1,0:T(8,128)(2,1)S(1)} %get-tuple-element.43), channel_id=1, source_target_pairs={{0,8},{8,0},{16,24},{24,16},{32,40},{40,32},{48,56},{56,48},{1,9},... | collective-permute-start | bytes 786440 | tf_op jit(solution)/shard_map/ppermute | solution.py:330
  100.1 32.0 %collective-permute-start.3 = (bf16[256,576]{1,0:T(8,128)(2,1)S(1)}, bf16[256,576]{1,0:T(8,128)(2,1)}, u32[]{:S(2)}, u32[]{:S(2)}) collective-permute-start(bf16[256,576]{1,0:T(8,128)(2,1)S(1)} %get-tuple-element.37), channel_id=1, source_target_pairs={{0,3},{1,0},{2,1},{3,2},{4,7},{5,4},{6,5},{7,6},{8,11},{9,8},{10,9... | collective-permute-start | bytes 884744 | tf_op jit(solution)/shard_map/ppermute | solution.py:250
  102.8 29.2 %collective-permute-start.4 = (bf16[256,576]{1,0:T(8,128)(2,1)S(1)}, bf16[256,576]{1,0:T(8,128)(2,1)}, u32[]{:S(2)}, u32[]{:S(2)}) collective-permute-start(bf16[256,576]{1,0:T(8,128)(2,1)S(1)} %get-tuple-element.38), channel_id=1, source_target_pairs={{0,2},{1,3},{2,0},{3,1},{4,6},{5,7},{6,4},{7,5},{8,10},{9,11},{10,... | collective-permute-start | bytes 884744 | tf_op jit(solution)/shard_map/ppermute | solution.py:250
  105.5 26.6 %collective-permute-start.5 = (bf16[256,576]{1,0:T(8,128)(2,1)S(1)}, bf16[256,576]{1,0:T(8,128)(2,1)}, u32[]{:S(2)}, u32[]{:S(2)}) collective-permute-start(bf16[256,576]{1,0:T(8,128)(2,1)S(1)} %get-tuple-element.39), channel_id=1, source_target_pairs={{0,1},{1,2},{2,3},{3,0},{4,5},{5,6},{6,7},{7,4},{8,9},{9,10},{10,1... | collective-permute-start | bytes 884744 | tf_op jit(solution)/shard_map/ppermute | solution.py:250
  110.5 12.8 %collective-permute-start.8 = (bf16[2,64,512]{2,1,0:T(8,128)(2,1)S(1)}, bf16[2,64,512]{2,1,0:T(8,128)(2,1)S(1)}, u32[]{:S(2)}, u32[]{:S(2)}) collective-permute-start(bf16[2,64,512]{2,1,0:T(8,128)(2,1)S(1)} %get-tuple-element.46), channel_id=1, source_target_pairs={{0,16},{8,24},{16,0},{24,8},{32,48},{40,56},{48,32},{56,40},{1,17}... | collective-permute-start | bytes 393224 | tf_op jit(solution)/shard_map/ppermute | solution.py:330
  114.3 22.1 %all-to-all-start.4 = ((f32[32,8,128]{2,1,0:T(8,128)}), f32[32,8,128]{2,1,0:T(8,128)S(1)}, u32[]{:S(2)}, u32[]{:S(2)}) async-start(f32[32,8,128]{2,1,0:T(8,128)} %get-tuple-element.56), calls=%async_computation.4 | async-start | bytes 262144 | tf_op jit(solution)/shard_map/all_to_all | solution.py:254
  124.4 11.3 %collective-permute-start.9 = (bf16[1,64,512]{2,1,0:T(8,128)(2,1)S(1)}, bf16[1,64,512]{2,1,0:T(8,128)(2,1)S(1)}, u32[]{:S(2)}, u32[]{:S(2)}) collective-permute-start(bf16[1,64,512]{2,1,0:T(8,128)(2,1)S(1)} %get-tuple-element.54), channel_id=1, source_target_pairs={{0,32},{8,40},{16,48},{24,56},{32,0},{40,8},{48,16},{56,24},{1,33}... | collective-permute-start | bytes 196616 | tf_op jit(solution)/shard_map/ppermute | solution.py:330

commit v11 on v7

--- a/solution.py
+++ b/solution.py
@@ -122,15 +122,14 @@
 def dscores_kernel(lat, pos, stats, st, e_ref, dp_ref, *refs):
     n_x = stats.shape[0]
     blocks, outs, (sems, *held) = refs[:n_x], refs[n_x : n_x + 4], refs[n_x + 4 :]
-    ds_ref, rope_ref, mine, other, p_ref = held
-    copies = [pltpu.make_async_copy(held[i], outs[i], sems.at[i]) for i in range(4)]
+    ds_ref, rope_ref, _, _, p_ref = held
     y, x = pos[1], pos[2]
     rows = refs[0].shape[0]
     tiles = e_ref.shape[0] // TILE
     grp, half_keys, _ = rope_ref.shape
     k_dev = 2 * half_keys
+    factors = []
     for b in range(n_x):
-        cols = slice(b * rows, (b + 1) * rows)
         theirs = []
         for s in range(n_x):
             at = lax.rem(x + b + n_x - s, n_x)
@@ -143,40 +142,51 @@
         total = sum(v[1:2] * u for v, u in zip(theirs, w))
         delta = sum(v[2:3] * u for v, u in zip(theirs, w)) / total
         f = jnp.exp(st[4 * b : 4 * b + 1] - top) / total
-        for i in range(tiles):
-            part = slice(i * TILE, (i + 1) * TILE)
+        factors.append((f, delta))
+    per = TILE // k_dev
+    rope = rope_ref.shape[2] // 2
+    copies = []
+
+    def send(which, rows_of):
+        copies.append(
+            pltpu.make_async_copy(held[which].at[rows_of], outs[which].at[rows_of], sems.at[len(copies)])
+        )
+        copies[-1].start()
+
+    def weigh(i):
+        part = slice(i * TILE, (i + 1) * TILE)
+        for b, (f, delta) in enumerate(factors):
+            cols = slice(b * rows, (b + 1) * rows)
             p = e_ref[part, cols] * f
             p_ref[part, cols] = p.astype(bf16)
             ds_ref[part, cols] = (p * (dp_ref[part, cols] - delta)).astype(bf16)
-    copies[0].start()
-    for i in range(tiles):
-        part = slice(i * TILE, (i + 1) * TILE)
-        r = None
-        for b, t in enumerate(blocks):
-            q = t[:, 2 * lat : 2 * lat + rope_ref.shape[2] // 2]
-            v = nn(ds_ref[part, b * rows : (b + 1) * rows], q)
-            r = v if r is None else r + v
-        r = (r * softmax_scale).astype(bf16)
-        for j in range(TILE // k_dev):
-            k = r[j * k_dev : (j + 1) * k_dev]
-            rope_ref[i * (TILE // k_dev) + j] = jnp.concatenate([k[:half_keys], k[half_keys:]], axis=1)
-    copies[1].start()
-    per = TILE // k_dev
-    for i in range(tiles):
+        send(0, pl.ds(i * TILE, TILE))
+
+    def multiply(i):
         part = slice(i * TILE, (i + 1) * TILE)
         v = None
         for b, t in enumerate(blocks):
-            a = nn(ds_ref[part, b * rows : (b + 1) * rows], t[:, lat : 2 * lat])
+            a = nn(ds_ref[part, b * rows : (b + 1) * rows], t[:, lat : 2 * lat + rope])
             v = a if v is None else v + a
         v = v * softmax_scale
+        r, v = v[:, lat:].astype(bf16), v[:, :lat]
+        for j in range(per):
+            k = r[j * k_dev : (j + 1) * k_dev]
+            rope_ref[i * per + j] = jnp.concatenate([k[:half_keys], k[half_keys:]], axis=1)
         for b, t in enumerate(blocks):
             v += nn(p_ref[part, b * rows : (b + 1) * rows], t[:, :lat])
         v = v.astype(bf16).reshape(per // 2, 2, k_dev, lat)
         first = i * per // 2
-        for out, side in ((mine, y), (other, 1 - y)):
-            out[first : first + per // 2] = jnp.where(side == 0, v[:, 0], v[:, 1])
-    copies[2].start()
-    copies[3].start()
+        for which, side in ((2, y), (3, 1 - y)):
+            held[which][first : first + per // 2] = jnp.where(side == 0, v[:, 0], v[:, 1])
+            send(which, pl.ds(first, per // 2))
+
+    weigh(0)
+    for i in range(tiles):
+        if i + 1 < tiles:
+            weigh(i + 1)
+        multiply(i)
+    send(1, pl.ds(0, grp))
     for copy in copies:
         copy.wait()
 
@@ -230,7 +240,7 @@
         send[i] = (a[away].astype(f32) + b[away].astype(f32)).astype(send.dtype)
 
 
-def latent_sum_kernel(a, b, rope, out):
+def latent_sum_kernel(a, b, rope, after, out):
     lat = a.shape[2]
     out[:, :lat] = a[0] + b[0].astype(f32)
     out[:, lat:] = rope[...]
@@ -280,7 +290,7 @@
         [((n_keys, n_rows), bf16), ((nz * ny, k_dev // 2, 2 * rope), bf16)] + [((nz, k_dev, lat), bf16)] * 2,
         9, smem=(0,), in_hbm=True,
         scratch=[
-            pltpu.SemaphoreType.DMA((4,)),
+            pltpu.SemaphoreType.DMA((3 * n_keys // TILE + 1,)),
             pltpu.VMEM((n_keys, n_rows), bf16),
             pltpu.VMEM((nz * ny, k_dev // 2, 2 * rope), bf16),
             pltpu.VMEM((nz, k_dev, lat), bf16),
@@ -315,7 +325,7 @@
         )(pos, kept, came, token)
         came = lax.ppermute(sent, "z", [(i, i ^ (1 << bit)) for i in range(nz)])
     (dweight,) = call(weight_sum_kernel, [((block, rope), f32)], 1)(terms)
-    (dlatent,) = call(latent_sum_kernel, [((k_dev, width), f32)], 3)(kept, came, rope_sum)
+    (dlatent,) = call(latent_sum_kernel, [((k_dev, width), f32)], 4, unused=(3,))(kept, came, rope_sum, dweight)
 
     total = dq[0]
     for part in dq[1:]:

time: 137 us -> 137 us (level)
  the two profiles are of different devices: /device:TPU:40 before, /device:TPU:8 now
where the time goes in v11:
time: 137 us; the launch traced here: 136 us
  starting transfers between devices  71 us (52%)
  waiting for transfers between devices  24 us (18%)
  Pallas kernels  19.7 us (14%)
  blocking collectives  9.73 us (7%)
  local copies, waits for them, and re-layouts  8.8 us (6%)
  other arithmetic  2.02 us (1%)
    all_to_all x4, starting transfers between devices, trade(): return lax.all_to_all(value, axes, 0, 0, tiled=True)  32.8 us
    ppermute x6, starting transfers between devices, fetch(): return lax.ppermute(value, 'x', [(s, (s - offset) % n) for s in range(n)])  22.7 us
    ppermute x6, waiting for transfers between devices, fetch(): return lax.ppermute(value, 'x', [(s, (s - offset) % n) for s in range(n)])  18 us
    ppermute x3, starting transfers between devices, body(): came = lax.ppermute(sent, 'z', [(i, i ^ 1 << bit) for i in range(nz)])  12.9 us
    all_to_all x1, blocking collectives, trade(): return lax.all_to_all(value, axes, 0, 0, tiled=True)  9.73 us
    unnamed x22, local copies, waits for them, and re-layouts  6.62 us
    all_to_all x4, waiting for transfers between devices, trade(): return lax.all_to_all(value, axes, 0, 0, tiled=True)  6.04 us
    pallas_call x1, Pallas kernels, body(): call(functools.partial(dscores_kernel, lat), [((n_keys, n_rows), bf16), (...  5.08 us
  transfers between devices with their start and end apart: 14, of which 5 were waited for; matrix products, arithmetic and copies ran while one was open for 1% of the time, Pallas kernels for 5%

profile of v11, /device:TPU:8, one launch (start us, length us, event | category | flops | bytes accessed | tf_op | source)
XLA Modules:
  0.0 136.2 jit_solution(8022449035120334678)
XLA Ops:
  0.7 2.2 %broadcast_in_dim.17 = bf16[16,64,576]{2,1,0:T(8,128)(2,1)} broadcast(bf16[64,576]{1,0:T(8,128)(2,1)} %bitcast.14), dimensions={1,2} | broadcast | bytes 1253376 | tf_op jit(solution)/shard_map/broadcast_in_dim | solution.py:270
  2.8 11.8 %all-to-all-start = ((bf16[16,64,576]{2,1,0:T(8,128)(2,1)}), bf16[16,64,576]{2,1,0:T(8,128)(2,1)S(1)}, u32[]{:S(2)}, u32[]{:S(2)}) async-start(bf16[16,64,576]{2,1,0:T(8,128)(2,1)} %broadcast_in_dim.17), calls=%async_computation | async-start | bytes 2621440 | tf_op jit(solution)/shard_map/all_to_all | solution.py:254
  14.7 3.4 %collective-permute-start.2 = (bf16[256,1152]{1,0:T(8,128)(2,1)S(1)}, bf16[256,1152]{1,0:T(8,128)(2,1)S(1)}, u32[]{:S(2)}, u32[]{:S(2)}) collective-permute-start(bf16[256,1152]{1,0:T(8,128)(2,1)S(1)} %shard_map.68.refs_0_), channel_id=1, source_target_pairs={{0,1},{1,2},{2,3},{3,0},{4,5},{5,6},{6,7},{7,4},{8,9},{9,10},{10,1... | collective-permute-start | bytes 1769480 | tf_op jit(solution)/shard_map/ppermute | solution.py:250
  18.1 4.6 %collective-permute-start.1 = (bf16[256,1152]{1,0:T(8,128)(2,1)S(1)}, bf16[256,1152]{1,0:T(8,128)(2,1)S(1)}, u32[]{:S(2)}, u32[]{:S(2)}) collective-permute-start(bf16[256,1152]{1,0:T(8,128)(2,1)S(1)} %shard_map.68.refs_0_), channel_id=1, source_target_pairs={{0,2},{1,3},{2,0},{3,1},{4,6},{5,7},{6,4},{7,5},{8,10},{9,11},{10,... | collective-permute-start | bytes 1769480 | tf_op jit(solution)/shard_map/ppermute | solution.py:250
  22.7 3.3 %collective-permute-start = (bf16[256,1152]{1,0:T(8,128)(2,1)S(1)}, bf16[256,1152]{1,0:T(8,128)(2,1)}, u32[]{:S(2)}, u32[]{:S(2)}) collective-permute-start(bf16[256,1152]{1,0:T(8,128)(2,1)S(1)} %shard_map.68.refs_0_), channel_id=1, source_target_pairs={{0,3},{1,0},{2,1},{3,2},{4,7},{5,4},{6,5},{7,6},{8,11},{9,8},{10,9... | collective-permute-start | bytes 1769480 | tf_op jit(solution)/shard_map/ppermute | solution.py:250
  26.1 1.2 copy-done.7
  27.3 1.3 shard_map.67
  28.6 1.0 copy-done
  29.6 3.4 %collective-permute-done.2.refs_3_ = bf16[256,1152]{1,0:T(8,128)(2,1)S(1)} collective-permute-done((bf16[256,1152]{1,0:T(8,128)(2,1)S(1)}, bf16[256,1152]{1,0:T(8,128)(2,1)S(1)}, u32[]{:S(2)}, u32[]{:S(2)}) %collective-permute-start.2) | collective-permute-done | bytes 589856 | tf_op jit(solution)/shard_map/ppermute | solution.py:250
  33.1 12.9 %collective-permute-done.1.refs_2_ = bf16[256,1152]{1,0:T(8,128)(2,1)S(1)} collective-permute-done((bf16[256,1152]{1,0:T(8,128)(2,1)S(1)}, bf16[256,1152]{1,0:T(8,128)(2,1)S(1)}, u32[]{:S(2)}, u32[]{:S(2)}) %collective-permute-start.1) | collective-permute-done | bytes 589856 | tf_op jit(solution)/shard_map/ppermute | solution.py:250
  45.9 1.7 %collective-permute-done.refs_1_ = bf16[256,1152]{1,0:T(8,128)(2,1)} collective-permute-done((bf16[256,1152]{1,0:T(8,128)(2,1)S(1)}, bf16[256,1152]{1,0:T(8,128)(2,1)}, u32[]{:S(2)}, u32[]{:S(2)}) %collective-permute-start) | collective-permute-done | bytes 589856 | tf_op jit(solution)/shard_map/ppermute | solution.py:250
  47.6 4.3 %shard_map.69 = (f32[1024,1024]{1,0:T(8,128)S(1)}, f32[1024,1024]{1,0:T(8,128)S(1)}, f32[16,256]{1,0:T(8,128)S(1)}) custom-call(s32[3]{0:T(128)S(1)} %pad_add_fusion.pos, bf16[16,64,576]{2,1,0:T(8,128)(2,1)S(1)} %all-to-all-done.keys, f32[8,128]{1,0:T(8,128)S(1)} %get-tuple-element.29.after, bf16[256,1152]{1,0:T(8,128)(2,1)S(1)} %shard_map.68.refs_0_, ...), custom_call_target="tpu_custom_call" | custom-call | flops 2281701376 | bytes 8388608 | tf_op jit(solution)/shard_map/pallas_call | solution.py:281
  52.0 9.7 %all_to_all.25.stats = f32[4,16,256]{2,1,0:T(8,128)S(1)} all-to-all(f32[4,16,256]{2,1,0:T(8,128)S(1)} %broadcast_in_dim.18), channel_id=1, replica_groups=mesh['w'=4,'c'=2,'z'=8,'y'=2,'x'=4] {'x'}, dimensions={0} | all-to-all | bytes 131072 | tf_op jit(solution)/shard_map/all_to_all | solution.py:254
  61.7 5.1 %shard_map.70 = (bf16[1024,1024]{1,0:T(8,128)(2,1)}, bf16[16,32,128]{2,1,0:T(8,128)(2,1)}, bf16[8,64,512]{2,1,0:T(8,128)(2,1)}, bf16[8,64,512]{2,1,0:T(8,128)(2,1)}) custom-call(s32[3]{0:T(128)S(1)} %pad_add_fusion.pos, f32[4,16,256]{2,1,0:T(8,128)S(1)} %all_to_all.25.stats, f32[16,256]{1,0:T(8,128)S(1)} %get-tuple-element.30.st, ...), custom_call_target="tpu_custom_call" | custom-call | flops 2281701376 | bytes 12582912 | tf_op jit(solution)/shard_map/pallas_call | solution.py:288
  66.8 2.6 %collective-permute-start.6 = (bf16[8,64,512]{2,1,0:T(8,128)(2,1)}, bf16[8,64,512]{2,1,0:T(8,128)(2,1)S(1)}, u32[]{:S(2)}, u32[]{:S(2)}) collective-permute-start(bf16[8,64,512]{2,1,0:T(8,128)(2,1)} %get-tuple-element.39), channel_id=1, source_target_pairs={{0,4},{4,0},{1,5},{5,1},{2,6},{6,2},{3,7},{7,3},{8,12},{12,8},{9,1... | collective-permute-start | bytes 1572872 | tf_op jit(solution)/shard_map/ppermute | solution.py:303
  69.3 8.1 %all-to-all-start.2 = ((bf16[16,32,128]{2,1,0:T(8,128)(2,1)}), bf16[16,32,128]{2,1,0:T(8,128)(2,1)}, u32[]{:S(2)}, u32[]{:S(2)}) async-start(bf16[16,32,128]{2,1,0:T(8,128)(2,1)} %get-tuple-element.45), calls=%async_computation.2 | async-start | bytes 262144 | tf_op jit(solution)/shard_map/all_to_all | solution.py:254
  77.4 1.6 %copy-done.6 = bf16[1024,1024]{1,0:T(8,128)(2,1)S(1)} copy-done((bf16[1024,1024]{1,0:T(8,128)(2,1)S(1)}, bf16[1024,1024]{1,0:T(8,128)(2,1)}, u32[]{:S(2)}) %copy-start.6) | copy-done | bytes 2097176
  79.0 1.8 %shard_map.71 = (f32[8,128]{1,0:T(8,128)S(1)}, f32[256,576]{1,0:T(8,128)S(1)}, bf16[256,576]{1,0:T(8,128)(2,1)S(1)}, bf16[256,576]{1,0:T(8,128)(2,1)S(1)}, bf16[256,576]{1,0:T(8,128)(2,1)S(1)}) custom-call(bf16[1024,1024]{1,0:T(8,128)(2,1)S(1)} %copy-done.6, bf16[16,64,576]{2,1,0:T(8,128)(2,1)S(1)} %all-to-all-done.keys), custom_call_target="tpu_custom_call" | custom-call | flops 1207959552 | bytes 4194304 | tf_op jit(solution)/shard_map/pallas_call | solution.py:304
  83.0 4.2 %all-to-all-done.2.parts = bf16[16,32,128]{2,1,0:T(8,128)(2,1)} async-done(((bf16[16,32,128]{2,1,0:T(8,128)(2,1)}), bf16[16,32,128]{2,1,0:T(8,128)(2,1)}, u32[]{:S(2)}, u32[]{:S(2)}) %all-to-all-start.2) | async-done | bytes 131104 | tf_op jit(solution)/shard_map/all_to_all | solution.py:254
  87.2 2.4 %shard_map.74 = (f32[64,64]{1,0:T(8,128)S(1)}, bf16[16,64,512]{2,1,0:T(8,128)(2,1)}) custom-call(bf16[16,32,128]{2,1,0:T(8,128)(2,1)} %all-to-all-done.2.parts, bf16[16,64,512]{2,1,0:T(8,128)(2,1)S(1)} %copy-done.1, bf16[8,64,512]{2,1,0:T(8,128)(2,1)S(1)} %collective-permute-done.6.b.after, f32[8,128]{1,0:T(8,128)S(1)} %get-tuple-element.47.after2), custom_call_target="tpu_custom_call" | custom-call | flops 67108864 | bytes 1835008 | tf_op jit(solution)/shard_map/pallas_call | solution.py:308
  89.6 4.0 %all-to-all-start.3 = ((bf16[16,64,512]{2,1,0:T(8,128)(2,1)}), bf16[16,64,512]{2,1,0:T(8,128)(2,1)S(1)}, u32[]{:S(2)}, u32[]{:S(2)}) async-start(bf16[16,64,512]{2,1,0:T(8,128)(2,1)} %get-tuple-element.48), calls=%async_computation.3 | async-start | bytes 2097152 | tf_op jit(solution)/shard_map/all_to_all | solution.py:254
  94.3 2.4 %collective-permute-start.7 = (bf16[4,64,512]{2,1,0:T(8,128)(2,1)S(1)}, bf16[4,64,512]{2,1,0:T(8,128)(2,1)S(1)}, u32[]{:S(2)}, u32[]{:S(2)}) collective-permute-start(bf16[4,64,512]{2,1,0:T(8,128)(2,1)S(1)} %get-tuple-element.41), channel_id=1, source_target_pairs={{0,8},{8,0},{16,24},{24,16},{32,40},{40,32},{48,56},{56,48},{1,9},... | collective-permute-start | bytes 786440 | tf_op jit(solution)/shard_map/ppermute | solution.py:326
  96.7 3.4 %collective-permute-start.3 = (bf16[256,576]{1,0:T(8,128)(2,1)}, bf16[256,576]{1,0:T(8,128)(2,1)S(1)}, u32[]{:S(2)}, u32[]{:S(2)}) collective-permute-start(bf16[256,576]{1,0:T(8,128)(2,1)} %copy-done.10), channel_id=1, source_target_pairs={{0,1},{1,2},{2,3},{3,0},{4,5},{5,6},{6,7},{7,4},{8,9},{9,10},{10,1... | collective-permute-start | bytes 884744 | tf_op jit(solution)/shard_map/ppermute | solution.py:250
  100.1 4.6 %collective-permute-start.4 = (bf16[256,576]{1,0:T(8,128)(2,1)}, bf16[256,576]{1,0:T(8,128)(2,1)}, u32[]{:S(2)}, u32[]{:S(2)}) collective-permute-start(bf16[256,576]{1,0:T(8,128)(2,1)} %copy-done.9), channel_id=1, source_target_pairs={{0,2},{1,3},{2,0},{3,1},{4,6},{5,7},{6,4},{7,5},{8,10},{9,11},{10,... | collective-permute-start | bytes 884744 | tf_op jit(solution)/shard_map/ppermute | solution.py:250
  104.7 3.4 %collective-permute-start.5 = (bf16[256,576]{1,0:T(8,128)(2,1)}, bf16[256,576]{1,0:T(8,128)(2,1)}, u32[]{:S(2)}, u32[]{:S(2)}) collective-permute-start(bf16[256,576]{1,0:T(8,128)(2,1)} %copy-done.8), channel_id=1, source_target_pairs={{0,3},{1,0},{2,1},{3,2},{4,7},{5,4},{6,5},{7,6},{8,11},{9,8},{10,9... | collective-permute-start | bytes 884744 | tf_op jit(solution)/shard_map/ppermute | solution.py:250
  108.7 2.9 %collective-permute-start.8 = (bf16[2,64,512]{2,1,0:T(8,128)(2,1)S(1)}, bf16[2,64,512]{2,1,0:T(8,128)(2,1)S(1)}, u32[]{:S(2)}, u32[]{:S(2)}) collective-permute-start(bf16[2,64,512]{2,1,0:T(8,128)(2,1)S(1)} %get-tuple-element.44), channel_id=1, source_target_pairs={{0,16},{8,24},{16,0},{24,8},{32,48},{40,56},{48,32},{56,40},{1,17}... | collective-permute-start | bytes 393224 | tf_op jit(solution)/shard_map/ppermute | solution.py:326
  111.6 1.0 shard_map.75
  112.6 8.9 %all-to-all-start.4 = ((f32[32,8,128]{2,1,0:T(8,128)}), f32[32,8,128]{2,1,0:T(8,128)S(1)}, u32[]{:S(2)}, u32[]{:S(2)}) async-start(f32[32,8,128]{2,1,0:T(8,128)} %get-tuple-element.54), calls=%async_computation.4 | async-start | bytes 262144 | tf_op jit(solution)/shard_map/all_to_all | solution.py:254
  121.6 1.1 shard_map.76
  122.7 7.6 %collective-permute-start.9 = (bf16[1,64,512]{2,1,0:T(8,128)(2,1)S(1)}, bf16[1,64,512]{2,1,0:T(8,128)(2,1)S(1)}, u32[]{:S(2)}, u32[]{:S(2)}) collective-permute-start(bf16[1,64,512]{2,1,0:T(8,128)(2,1)S(1)} %get-tuple-element.52), channel_id=1, source_target_pairs={{0,32},{8,40},{16,48},{24,56},{32,0},{40,8},{48,16},{56,24},{1,33}... | collective-permute-start | bytes 196616 | tf_op jit(solution)/shard_map/ppermute | solution.py:326
  130.3 1.9 %add_convert_fusion = bf16[256,576]{1,0:T(8,128)(2,1)} fusion(bf16[256,576]{1,0:T(8,128)(2,1)} %collective-permute-done.5, bf16[256,576]{1,0:T(8,128)(2,1)} %collective-permute-done.4, f32[256,576]{1,0:T(8,128)S(1)} %get-tuple-element.34, bf16[256,576]{1,0:T(8,128)(2,1)S(1)} %collective-permute-done.3), kind=kLoop, calls=%fused_computation | loop fusion | flops 1032192 | bytes 1769472 | tf_op jit(solution)/shard_map/convert_element_type | solution.py:333
  132.3 1.8 %all-to-all-done.4.parts = f32[32,8,128]{2,1,0:T(8,128)S(1)} async-done(((f32[32,8,128]{2,1,0:T(8,128)}), f32[32,8,128]{2,1,0:T(8,128)S(1)}, u32[]{:S(2)}, u32[]{:S(2)}) %all-to-all-start.4) | async-done | bytes 131104 | tf_op jit(solution)/shard_map/all_to_all | solution.py:254
  (35 shorter events, 5.7 us)
Async XLA Ops:
  0.6 14.0 %copy-start.4 = (bf16[1,4,64,512]{3,2,1,0:T(8,128)(2,1)S(1)}, bf16[1,4,64,512]{3,2,1,0:T(8,128)(2,1)}, u32[]{:S(2)}) copy-start(bf16[1,4,64,512]{3,2,1,0:T(8,128)(2,1)} %param.6) | copy-start | bytes 786436
  0.6 14.0 %copy-start.3 = (bf16[1,4,64,576]{3,2,1,0:T(8,128)(2,1)S(1)}, bf16[1,4,64,576]{3,2,1,0:T(8,128)(2,1)}, u32[]{:S(2)}) copy-start(bf16[1,4,64,576]{3,2,1,0:T(8,128)(2,1)} %param.4) | copy-start | bytes 884740
  2.8 44.8 %all-to-all-start = ((bf16[16,64,576]{2,1,0:T(8,128)(2,1)}), bf16[16,64,576]{2,1,0:T(8,128)(2,1)S(1)}, u32[]{:S(2)}, u32[]{:S(2)}) async-start(bf16[16,64,576]{2,1,0:T(8,128)(2,1)} %broadcast_in_dim.17), calls=%async_computation | async-start | bytes 2621440 | tf_op jit(solution)/shard_map/all_to_all | solution.py:254
  14.7 18.4 %collective-permute-start.2 = (bf16[256,1152]{1,0:T(8,128)(2,1)S(1)}, bf16[256,1152]{1,0:T(8,128)(2,1)S(1)}, u32[]{:S(2)}, u32[]{:S(2)}) collective-permute-start(bf16[256,1152]{1,0:T(8,128)(2,1)S(1)} %shard_map.68.refs_0_), channel_id=1, source_target_pairs={{0,1},{1,2},{2,3},{3,0},{4,5},{5,6},{6,7},{7,4},{8,9},{9,10},{10,1... | collective-permute-start | bytes 1769480 | tf_op jit(solution)/shard_map/ppermute | solution.py:250
  18.1 27.8 %collective-permute-start.1 = (bf16[256,1152]{1,0:T(8,128)(2,1)S(1)}, bf16[256,1152]{1,0:T(8,128)(2,1)S(1)}, u32[]{:S(2)}, u32[]{:S(2)}) collective-permute-start(bf16[256,1152]{1,0:T(8,128)(2,1)S(1)} %shard_map.68.refs_0_), channel_id=1, source_target_pairs={{0,2},{1,3},{2,0},{3,1},{4,6},{5,7},{6,4},{7,5},{8,10},{9,11},{10,... | collective-permute-start | bytes 1769480 | tf_op jit(solution)/shard_map/ppermute | solution.py:250
  22.7 24.8 %collective-permute-start = (bf16[256,1152]{1,0:T(8,128)(2,1)S(1)}, bf16[256,1152]{1,0:T(8,128)(2,1)}, u32[]{:S(2)}, u32[]{:S(2)}) collective-permute-start(bf16[256,1152]{1,0:T(8,128)(2,1)S(1)} %shard_map.68.refs_0_), channel_id=1, source_target_pairs={{0,3},{1,0},{2,1},{3,2},{4,7},{5,4},{6,5},{7,6},{8,11},{9,8},{10,9... | collective-permute-start | bytes 1769480 | tf_op jit(solution)/shard_map/ppermute | solution.py:250
  26.1 1.2 copy-start.7
  28.6 1.0 copy-start
  66.8 20.4 %collective-permute-start.6 = (bf16[8,64,512]{2,1,0:T(8,128)(2,1)}, bf16[8,64,512]{2,1,0:T(8,128)(2,1)S(1)}, u32[]{:S(2)}, u32[]{:S(2)}) collective-permute-start(bf16[8,64,512]{2,1,0:T(8,128)(2,1)} %get-tuple-element.39), channel_id=1, source_target_pairs={{0,4},{4,0},{1,5},{5,1},{2,6},{6,2},{3,7},{7,3},{8,12},{12,8},{9,1... | collective-permute-start | bytes 1572872 | tf_op jit(solution)/shard_map/ppermute | solution.py:303
  69.3 17.9 %all-to-all-start.2 = ((bf16[16,32,128]{2,1,0:T(8,128)(2,1)}), bf16[16,32,128]{2,1,0:T(8,128)(2,1)}, u32[]{:S(2)}, u32[]{:S(2)}) async-start(bf16[16,32,128]{2,1,0:T(8,128)(2,1)} %get-tuple-element.45), calls=%async_computation.2 | async-start | bytes 262144 | tf_op jit(solution)/shard_map/all_to_all | solution.py:254
  77.4 1.6 %copy-start.6 = (bf16[1024,1024]{1,0:T(8,128)(2,1)S(1)}, bf16[1024,1024]{1,0:T(8,128)(2,1)}, u32[]{:S(2)}) copy-start(bf16[1024,1024]{1,0:T(8,128)(2,1)} %get-tuple-element.33.ds_ref) | copy-start | bytes 6291460
  79.0 8.2 %copy-start.1 = (bf16[16,64,512]{2,1,0:T(8,128)(2,1)S(1)}, bf16[16,64,512]{2,1,0:T(8,128)(2,1)}, u32[]{:S(2)}) copy-start(bf16[16,64,512]{2,1,0:T(8,128)(2,1)} %copy-done) | copy-start | bytes 3145732
  80.8 0.7 copy-start.8
  81.6 0.7 copy-start.9
  82.3 0.7 copy-start.10
  83.0 10.6 %copy-start.2 = (bf16[8,64,512]{2,1,0:T(8,128)(2,1)S(1)}, bf16[8,64,512]{2,1,0:T(8,128)(2,1)}, u32[]{:S(2)}) copy-start(bf16[8,64,512]{2,1,0:T(8,128)(2,1)} %get-tuple-element.38.a) | copy-start | bytes 1572868
  89.6 22.0 %all-to-all-start.3 = ((bf16[16,64,512]{2,1,0:T(8,128)(2,1)}), bf16[16,64,512]{2,1,0:T(8,128)(2,1)S(1)}, u32[]{:S(2)}, u32[]{:S(2)}) async-start(bf16[16,64,512]{2,1,0:T(8,128)(2,1)} %get-tuple-element.48), calls=%async_computation.3 | async-start | bytes 2097152 | tf_op jit(solution)/shard_map/all_to_all | solution.py:254
  94.3 13.8 %collective-permute-start.7 = (bf16[4,64,512]{2,1,0:T(8,128)(2,1)S(1)}, bf16[4,64,512]{2,1,0:T(8,128)(2,1)S(1)}, u32[]{:S(2)}, u32[]{:S(2)}) collective-permute-start(bf16[4,64,512]{2,1,0:T(8,128)(2,1)S(1)} %get-tuple-element.41), channel_id=1, source_target_pairs={{0,8},{8,0},{16,24},{24,16},{32,40},{40,32},{48,56},{56,48},{1,9},... | collective-permute-start | bytes 786440 | tf_op jit(solution)/shard_map/ppermute | solution.py:326
  96.7 33.6 %collective-permute-start.3 = (bf16[256,576]{1,0:T(8,128)(2,1)}, bf16[256,576]{1,0:T(8,128)(2,1)S(1)}, u32[]{:S(2)}, u32[]{:S(2)}) collective-permute-start(bf16[256,576]{1,0:T(8,128)(2,1)} %copy-done.10), channel_id=1, source_target_pairs={{0,1},{1,2},{2,3},{3,0},{4,5},{5,6},{6,7},{7,4},{8,9},{9,10},{10,1... | collective-permute-start | bytes 884744 | tf_op jit(solution)/shard_map/ppermute | solution.py:250
  100.1 30.2 %collective-permute-start.4 = (bf16[256,576]{1,0:T(8,128)(2,1)}, bf16[256,576]{1,0:T(8,128)(2,1)}, u32[]{:S(2)}, u32[]{:S(2)}) collective-permute-start(bf16[256,576]{1,0:T(8,128)(2,1)} %copy-done.9), channel_id=1, source_target_pairs={{0,2},{1,3},{2,0},{3,1},{4,6},{5,7},{6,4},{7,5},{8,10},{9,11},{10,... | collective-permute-start | bytes 884744 | tf_op jit(solution)/shard_map/ppermute | solution.py:250
  104.7 25.6 %collective-permute-start.5 = (bf16[256,576]{1,0:T(8,128)(2,1)}, bf16[256,576]{1,0:T(8,128)(2,1)}, u32[]{:S(2)}, u32[]{:S(2)}) collective-permute-start(bf16[256,576]{1,0:T(8,128)(2,1)} %copy-done.8), channel_id=1, source_target_pairs={{0,3},{1,0},{2,1},{3,2},{4,7},{5,4},{6,5},{7,6},{8,11},{9,8},{10,9... | collective-permute-start | bytes 884744 | tf_op jit(solution)/shard_map/ppermute | solution.py:250
  108.7 12.8 %collective-permute-start.8 = (bf16[2,64,512]{2,1,0:T(8,128)(2,1)S(1)}, bf16[2,64,512]{2,1,0:T(8,128)(2,1)S(1)}, u32[]{:S(2)}, u32[]{:S(2)}) collective-permute-start(bf16[2,64,512]{2,1,0:T(8,128)(2,1)S(1)} %get-tuple-element.44), channel_id=1, source_target_pairs={{0,16},{8,24},{16,0},{24,8},{32,48},{40,56},{48,32},{56,40},{1,17}... | collective-permute-start | bytes 393224 | tf_op jit(solution)/shard_map/ppermute | solution.py:326
  112.6 21.5 %all-to-all-start.4 = ((f32[32,8,128]{2,1,0:T(8,128)}), f32[32,8,128]{2,1,0:T(8,128)S(1)}, u32[]{:S(2)}, u32[]{:S(2)}) async-start(f32[32,8,128]{2,1,0:T(8,128)} %get-tuple-element.54), calls=%async_computation.4 | async-start | bytes 262144 | tf_op jit(solution)/shard_map/all_to_all | solution.py:254
  122.7 12.1 %collective-permute-start.9 = (bf16[1,64,512]{2,1,0:T(8,128)(2,1)S(1)}, bf16[1,64,512]{2,1,0:T(8,128)(2,1)S(1)}, u32[]{:S(2)}, u32[]{:S(2)}) collective-permute-start(bf16[1,64,512]{2,1,0:T(8,128)(2,1)S(1)} %get-tuple-element.52), channel_id=1, source_target_pairs={{0,32},{8,40},{16,48},{24,56},{32,0},{40,8},{48,16},{56,24},{1,33}... | collective-permute-start | bytes 196616 | tf_op jit(solution)/shard_map/ppermute | solution.py:326
  134.8 0.7 copy-start.5

commit v12 on v11

--- a/solution.py
+++ b/solution.py
@@ -240,7 +240,7 @@
         send[i] = (a[away].astype(f32) + b[away].astype(f32)).astype(send.dtype)
 
 
-def latent_sum_kernel(a, b, rope, after, out):
+def latent_sum_kernel(a, b, rope, out):
     lat = a.shape[2]
     out[:, :lat] = a[0] + b[0].astype(f32)
     out[:, lat:] = rope[...]
@@ -325,7 +325,7 @@
         )(pos, kept, came, token)
         came = lax.ppermute(sent, "z", [(i, i ^ (1 << bit)) for i in range(nz)])
     (dweight,) = call(weight_sum_kernel, [((block, rope), f32)], 1)(terms)
-    (dlatent,) = call(latent_sum_kernel, [((k_dev, width), f32)], 4, unused=(3,))(kept, came, rope_sum, dweight)
+    (dlatent,) = call(latent_sum_kernel, [((k_dev, width), f32)], 3)(kept, came, rope_sum)
 
     total = dq[0]
     for part in dq[1:]:

time: 137 us -> 137 us (level)
  the two profiles are of different devices: /device:TPU:8 before, /device:TPU:40 now
where the time goes in v12:
time: 137 us; the launch traced here: 136 us
  starting transfers between devices  71.4 us (52%)
  waiting for transfers between devices  23.7 us (17%)
  Pallas kernels  19.8 us (14%)
  blocking collectives  9.72 us (7%)
  local copies, waits for them, and re-layouts  8.08 us (6%)
  other arithmetic  2.02 us (1%)
    all_to_all x4, starting transfers between devices, trade(): return lax.all_to_all(value, axes, 0, 0, tiled=True)  33.6 us
    ppermute x6, starting transfers between devices, fetch(): return lax.ppermute(value, 'x', [(s, (s - offset) % n) for s in range(n)])  22.7 us
    ppermute x6, waiting for transfers between devices, fetch(): return lax.ppermute(value, 'x', [(s, (s - offset) % n) for s in range(n)])  18 us
    ppermute x3, starting transfers between devices, body(): came = lax.ppermute(sent, 'z', [(i, i ^ 1 << bit) for i in range(nz)])  12.5 us
    all_to_all x1, blocking collectives, trade(): return lax.all_to_all(value, axes, 0, 0, tiled=True)  9.72 us
    unnamed x20, local copies, waits for them, and re-layouts  5.9 us
    pallas_call x1, Pallas kernels, body(): call(functools.partial(dscores_kernel, lat), [((n_keys, n_rows), bf16), (...  5.08 us
    pallas_call x1, Pallas kernels, body(): call(functools.partial(scores_kernel, lat, heads), [((n_keys, n_rows), f3...  4.35 us
  transfers between devices with their start and end apart: 14, of which 5 were waited for; matrix products, arithmetic and copies ran while one was open for 1% of the time, Pallas kernels for 5%

profile of v12, /device:TPU:40, one launch (start us, length us, event | category | flops | bytes accessed | tf_op | source)
XLA Modules:
  0.0 135.6 jit_solution(610183016070639576)
XLA Ops:
  0.7 2.2 %broadcast_in_dim.17 = bf16[16,64,576]{2,1,0:T(8,128)(2,1)} broadcast(bf16[64,576]{1,0:T(8,128)(2,1)} %bitcast.14), dimensions={1,2} | broadcast | bytes 1253376 | tf_op jit(solution)/shard_map/broadcast_in_dim | solution.py:270
  2.8 11.8 %all-to-all-start = ((bf16[16,64,576]{2,1,0:T(8,128)(2,1)}), bf16[16,64,576]{2,1,0:T(8,128)(2,1)S(1)}, u32[]{:S(2)}, u32[]{:S(2)}) async-start(bf16[16,64,576]{2,1,0:T(8,128)(2,1)} %broadcast_in_dim.17), calls=%async_computation | async-start | bytes 2621440 | tf_op jit(solution)/shard_map/all_to_all | solution.py:254
  14.7 3.4 %collective-permute-start.2 = (bf16[256,1152]{1,0:T(8,128)(2,1)S(1)}, bf16[256,1152]{1,0:T(8,128)(2,1)S(1)}, u32[]{:S(2)}, u32[]{:S(2)}) collective-permute-start(bf16[256,1152]{1,0:T(8,128)(2,1)S(1)} %shard_map.68.refs_0_), channel_id=1, source_target_pairs={{0,1},{1,2},{2,3},{3,0},{4,5},{5,6},{6,7},{7,4},{8,9},{9,10},{10,1... | collective-permute-start | bytes 1769480 | tf_op jit(solution)/shard_map/ppermute | solution.py:250
  18.1 4.6 %collective-permute-start.1 = (bf16[256,1152]{1,0:T(8,128)(2,1)S(1)}, bf16[256,1152]{1,0:T(8,128)(2,1)S(1)}, u32[]{:S(2)}, u32[]{:S(2)}) collective-permute-start(bf16[256,1152]{1,0:T(8,128)(2,1)S(1)} %shard_map.68.refs_0_), channel_id=1, source_target_pairs={{0,2},{1,3},{2,0},{3,1},{4,6},{5,7},{6,4},{7,5},{8,10},{9,11},{10,... | collective-permute-start | bytes 1769480 | tf_op jit(solution)/shard_map/ppermute | solution.py:250
  22.8 3.3 %collective-permute-start = (bf16[256,1152]{1,0:T(8,128)(2,1)S(1)}, bf16[256,1152]{1,0:T(8,128)(2,1)}, u32[]{:S(2)}, u32[]{:S(2)}) collective-permute-start(bf16[256,1152]{1,0:T(8,128)(2,1)S(1)} %shard_map.68.refs_0_), channel_id=1, source_target_pairs={{0,3},{1,0},{2,1},{3,2},{4,7},{5,4},{6,5},{7,6},{8,11},{9,8},{10,9... | collective-permute-start | bytes 1769480 | tf_op jit(solution)/shard_map/ppermute | solution.py:250
  26.1 1.2 copy-done.6
  27.3 1.3 shard_map.67
  28.6 1.0 copy-done
  29.6 3.5 %collective-permute-done.2.refs_3_ = bf16[256,1152]{1,0:T(8,128)(2,1)S(1)} collective-permute-done((bf16[256,1152]{1,0:T(8,128)(2,1)S(1)}, bf16[256,1152]{1,0:T(8,128)(2,1)S(1)}, u32[]{:S(2)}, u32[]{:S(2)}) %collective-permute-start.2) | collective-permute-done | bytes 589856 | tf_op jit(solution)/shard_map/ppermute | solution.py:250
  33.1 12.9 %collective-permute-done.1.refs_2_ = bf16[256,1152]{1,0:T(8,128)(2,1)S(1)} collective-permute-done((bf16[256,1152]{1,0:T(8,128)(2,1)S(1)}, bf16[256,1152]{1,0:T(8,128)(2,1)S(1)}, u32[]{:S(2)}, u32[]{:S(2)}) %collective-permute-start.1) | collective-permute-done | bytes 589856 | tf_op jit(solution)/shard_map/ppermute | solution.py:250
  45.9 1.7 %collective-permute-done.refs_1_ = bf16[256,1152]{1,0:T(8,128)(2,1)} collective-permute-done((bf16[256,1152]{1,0:T(8,128)(2,1)S(1)}, bf16[256,1152]{1,0:T(8,128)(2,1)}, u32[]{:S(2)}, u32[]{:S(2)}) %collective-permute-start) | collective-permute-done | bytes 589856 | tf_op jit(solution)/shard_map/ppermute | solution.py:250
  47.6 4.4 %shard_map.69 = (f32[1024,1024]{1,0:T(8,128)S(1)}, f32[1024,1024]{1,0:T(8,128)S(1)}, f32[16,256]{1,0:T(8,128)S(1)}) custom-call(s32[3]{0:T(128)S(1)} %pad_add_fusion.pos, bf16[16,64,576]{2,1,0:T(8,128)(2,1)S(1)} %all-to-all-done.keys, f32[8,128]{1,0:T(8,128)S(1)} %get-tuple-element.29.after, bf16[256,1152]{1,0:T(8,128)(2,1)S(1)} %shard_map.68.refs_0_, ...), custom_call_target="tpu_custom_call" | custom-call | flops 2281701376 | bytes 8388608 | tf_op jit(solution)/shard_map/pallas_call | solution.py:281
  52.0 9.7 %all_to_all.25.stats = f32[4,16,256]{2,1,0:T(8,128)S(1)} all-to-all(f32[4,16,256]{2,1,0:T(8,128)S(1)} %broadcast_in_dim.18), channel_id=1, replica_groups=mesh['w'=4,'c'=2,'z'=8,'y'=2,'x'=4] {'x'}, dimensions={0} | all-to-all | bytes 131072 | tf_op jit(solution)/shard_map/all_to_all | solution.py:254
  61.7 5.1 %shard_map.70 = (bf16[1024,1024]{1,0:T(8,128)(2,1)}, bf16[16,32,128]{2,1,0:T(8,128)(2,1)}, bf16[8,64,512]{2,1,0:T(8,128)(2,1)}, bf16[8,64,512]{2,1,0:T(8,128)(2,1)}) custom-call(s32[3]{0:T(128)S(1)} %pad_add_fusion.pos, f32[4,16,256]{2,1,0:T(8,128)S(1)} %all_to_all.25.stats, f32[16,256]{1,0:T(8,128)S(1)} %get-tuple-element.30.st, ...), custom_call_target="tpu_custom_call" | custom-call | flops 2281701376 | bytes 12582912 | tf_op jit(solution)/shard_map/pallas_call | solution.py:288
  66.8 2.5 %collective-permute-start.6 = (bf16[8,64,512]{2,1,0:T(8,128)(2,1)}, bf16[8,64,512]{2,1,0:T(8,128)(2,1)S(1)}, u32[]{:S(2)}, u32[]{:S(2)}) collective-permute-start(bf16[8,64,512]{2,1,0:T(8,128)(2,1)} %get-tuple-element.39), channel_id=1, source_target_pairs={{0,4},{4,0},{1,5},{5,1},{2,6},{6,2},{3,7},{7,3},{8,12},{12,8},{9,1... | collective-permute-start | bytes 1572872 | tf_op jit(solution)/shard_map/ppermute | solution.py:303
  69.3 8.1 %all-to-all-start.2 = ((bf16[16,32,128]{2,1,0:T(8,128)(2,1)}), bf16[16,32,128]{2,1,0:T(8,128)(2,1)}, u32[]{:S(2)}, u32[]{:S(2)}) async-start(bf16[16,32,128]{2,1,0:T(8,128)(2,1)} %get-tuple-element.45), calls=%async_computation.2 | async-start | bytes 262144 | tf_op jit(solution)/shard_map/all_to_all | solution.py:254
  77.4 1.6 %copy-done.5 = bf16[1024,1024]{1,0:T(8,128)(2,1)S(1)} copy-done((bf16[1024,1024]{1,0:T(8,128)(2,1)S(1)}, bf16[1024,1024]{1,0:T(8,128)(2,1)}, u32[]{:S(2)}) %copy-start.5) | copy-done | bytes 2097176
  79.0 1.8 %shard_map.71 = (f32[8,128]{1,0:T(8,128)S(1)}, f32[256,576]{1,0:T(8,128)S(1)}, bf16[256,576]{1,0:T(8,128)(2,1)S(1)}, bf16[256,576]{1,0:T(8,128)(2,1)S(1)}, bf16[256,576]{1,0:T(8,128)(2,1)S(1)}) custom-call(bf16[1024,1024]{1,0:T(8,128)(2,1)S(1)} %copy-done.5, bf16[16,64,576]{2,1,0:T(8,128)(2,1)S(1)} %all-to-all-done.keys), custom_call_target="tpu_custom_call" | custom-call | flops 1207959552 | bytes 4194304 | tf_op jit(solution)/shard_map/pallas_call | solution.py:304
  83.0 4.2 %all-to-all-done.2.parts = bf16[16,32,128]{2,1,0:T(8,128)(2,1)} async-done(((bf16[16,32,128]{2,1,0:T(8,128)(2,1)}), bf16[16,32,128]{2,1,0:T(8,128)(2,1)}, u32[]{:S(2)}, u32[]{:S(2)}) %all-to-all-start.2) | async-done | bytes 131104 | tf_op jit(solution)/shard_map/all_to_all | solution.py:254
  87.2 2.4 %shard_map.74 = (f32[64,64]{1,0:T(8,128)S(1)}, bf16[16,64,512]{2,1,0:T(8,128)(2,1)}) custom-call(bf16[16,32,128]{2,1,0:T(8,128)(2,1)} %all-to-all-done.2.parts, bf16[16,64,512]{2,1,0:T(8,128)(2,1)S(1)} %copy-done.1, bf16[8,64,512]{2,1,0:T(8,128)(2,1)S(1)} %collective-permute-done.6.b.after, f32[8,128]{1,0:T(8,128)S(1)} %get-tuple-element.47.after2), custom_call_target="tpu_custom_call" | custom-call | flops 67108864 | bytes 1835008 | tf_op jit(solution)/shard_map/pallas_call | solution.py:308
  89.6 4.0 %all-to-all-start.3 = ((bf16[16,64,512]{2,1,0:T(8,128)(2,1)}), bf16[16,64,512]{2,1,0:T(8,128)(2,1)S(1)}, u32[]{:S(2)}, u32[]{:S(2)}) async-start(bf16[16,64,512]{2,1,0:T(8,128)(2,1)} %get-tuple-element.48), calls=%async_computation.3 | async-start | bytes 2097152 | tf_op jit(solution)/shard_map/all_to_all | solution.py:254
  94.3 2.5 %collective-permute-start.7 = (bf16[4,64,512]{2,1,0:T(8,128)(2,1)S(1)}, bf16[4,64,512]{2,1,0:T(8,128)(2,1)S(1)}, u32[]{:S(2)}, u32[]{:S(2)}) collective-permute-start(bf16[4,64,512]{2,1,0:T(8,128)(2,1)S(1)} %get-tuple-element.41), channel_id=1, source_target_pairs={{0,8},{8,0},{16,24},{24,16},{32,40},{40,32},{48,56},{56,48},{1,9},... | collective-permute-start | bytes 786440 | tf_op jit(solution)/shard_map/ppermute | solution.py:326
  96.8 3.4 %collective-permute-start.3 = (bf16[256,576]{1,0:T(8,128)(2,1)}, bf16[256,576]{1,0:T(8,128)(2,1)S(1)}, u32[]{:S(2)}, u32[]{:S(2)}) collective-permute-start(bf16[256,576]{1,0:T(8,128)(2,1)} %copy-done.9), channel_id=1, source_target_pairs={{0,1},{1,2},{2,3},{3,0},{4,5},{5,6},{6,7},{7,4},{8,9},{9,10},{10,1... | collective-permute-start | bytes 884744 | tf_op jit(solution)/shard_map/ppermute | solution.py:250
  100.2 4.6 %collective-permute-start.4 = (bf16[256,576]{1,0:T(8,128)(2,1)}, bf16[256,576]{1,0:T(8,128)(2,1)}, u32[]{:S(2)}, u32[]{:S(2)}) collective-permute-start(bf16[256,576]{1,0:T(8,128)(2,1)} %copy-done.8), channel_id=1, source_target_pairs={{0,2},{1,3},{2,0},{3,1},{4,6},{5,7},{6,4},{7,5},{8,10},{9,11},{10,... | collective-permute-start | bytes 884744 | tf_op jit(solution)/shard_map/ppermute | solution.py:250
  104.8 3.4 %collective-permute-start.5 = (bf16[256,576]{1,0:T(8,128)(2,1)}, bf16[256,576]{1,0:T(8,128)(2,1)}, u32[]{:S(2)}, u32[]{:S(2)}) collective-permute-start(bf16[256,576]{1,0:T(8,128)(2,1)} %copy-done.7), channel_id=1, source_target_pairs={{0,3},{1,0},{2,1},{3,2},{4,7},{5,4},{6,5},{7,6},{8,11},{9,8},{10,9... | collective-permute-start | bytes 884744 | tf_op jit(solution)/shard_map/ppermute | solution.py:250
  108.8 2.8 %collective-permute-start.8 = (bf16[2,64,512]{2,1,0:T(8,128)(2,1)S(1)}, bf16[2,64,512]{2,1,0:T(8,128)(2,1)S(1)}, u32[]{:S(2)}, u32[]{:S(2)}) collective-permute-start(bf16[2,64,512]{2,1,0:T(8,128)(2,1)S(1)} %get-tuple-element.44), channel_id=1, source_target_pairs={{0,16},{8,24},{16,0},{24,8},{32,48},{40,56},{48,32},{56,40},{1,17}... | collective-permute-start | bytes 393224 | tf_op jit(solution)/shard_map/ppermute | solution.py:326
  111.6 1.0 shard_map.75
  112.5 9.8 %all-to-all-start.4 = ((f32[32,8,128]{2,1,0:T(8,128)}), f32[32,8,128]{2,1,0:T(8,128)S(1)}, u32[]{:S(2)}, u32[]{:S(2)}) async-start(f32[32,8,128]{2,1,0:T(8,128)} %get-tuple-element.54), calls=%async_computation.4 | async-start | bytes 262144 | tf_op jit(solution)/shard_map/all_to_all | solution.py:254
  122.3 1.1 shard_map.76
  123.5 7.3 %collective-permute-start.9 = (bf16[1,64,512]{2,1,0:T(8,128)(2,1)S(1)}, bf16[1,64,512]{2,1,0:T(8,128)(2,1)S(1)}, u32[]{:S(2)}, u32[]{:S(2)}) collective-permute-start(bf16[1,64,512]{2,1,0:T(8,128)(2,1)S(1)} %get-tuple-element.52), channel_id=1, source_target_pairs={{0,32},{8,40},{16,48},{24,56},{32,0},{40,8},{48,16},{56,24},{1,33}... | collective-permute-start | bytes 196616 | tf_op jit(solution)/shard_map/ppermute | solution.py:326
  130.8 1.9 %add_convert_fusion = bf16[256,576]{1,0:T(8,128)(2,1)} fusion(bf16[256,576]{1,0:T(8,128)(2,1)} %collective-permute-done.5, bf16[256,576]{1,0:T(8,128)(2,1)} %collective-permute-done.4, f32[256,576]{1,0:T(8,128)S(1)} %get-tuple-element.34, bf16[256,576]{1,0:T(8,128)(2,1)S(1)} %collective-permute-done.3), kind=kLoop, calls=%fused_computation | loop fusion | flops 1032192 | bytes 1769472 | tf_op jit(solution)/shard_map/convert_element_type | solution.py:333
  132.7 1.5 %collective-permute-done.9.b = bf16[1,64,512]{2,1,0:T(8,128)(2,1)S(1)} collective-permute-done((bf16[1,64,512]{2,1,0:T(8,128)(2,1)S(1)}, bf16[1,64,512]{2,1,0:T(8,128)(2,1)S(1)}, u32[]{:S(2)}, u32[]{:S(2)}) %collective-permute-start.9) | collective-permute-done | bytes 65568 | tf_op jit(solution)/shard_map/ppermute | solution.py:326
  (33 shorter events, 5.0 us)
Async XLA Ops:
  0.6 14.0 %copy-start.4 = (bf16[1,4,64,512]{3,2,1,0:T(8,128)(2,1)S(1)}, bf16[1,4,64,512]{3,2,1,0:T(8,128)(2,1)}, u32[]{:S(2)}) copy-start(bf16[1,4,64,512]{3,2,1,0:T(8,128)(2,1)} %param.6) | copy-start | bytes 786436
  0.6 14.0 %copy-start.3 = (bf16[1,4,64,576]{3,2,1,0:T(8,128)(2,1)S(1)}, bf16[1,4,64,576]{3,2,1,0:T(8,128)(2,1)}, u32[]{:S(2)}) copy-start(bf16[1,4,64,576]{3,2,1,0:T(8,128)(2,1)} %param.4) | copy-start | bytes 884740
  2.8 44.8 %all-to-all-start = ((bf16[16,64,576]{2,1,0:T(8,128)(2,1)}), bf16[16,64,576]{2,1,0:T(8,128)(2,1)S(1)}, u32[]{:S(2)}, u32[]{:S(2)}) async-start(bf16[16,64,576]{2,1,0:T(8,128)(2,1)} %broadcast_in_dim.17), calls=%async_computation | async-start | bytes 2621440 | tf_op jit(solution)/shard_map/all_to_all | solution.py:254
  14.7 18.4 %collective-permute-start.2 = (bf16[256,1152]{1,0:T(8,128)(2,1)S(1)}, bf16[256,1152]{1,0:T(8,128)(2,1)S(1)}, u32[]{:S(2)}, u32[]{:S(2)}) collective-permute-start(bf16[256,1152]{1,0:T(8,128)(2,1)S(1)} %shard_map.68.refs_0_), channel_id=1, source_target_pairs={{0,1},{1,2},{2,3},{3,0},{4,5},{5,6},{6,7},{7,4},{8,9},{9,10},{10,1... | collective-permute-start | bytes 1769480 | tf_op jit(solution)/shard_map/ppermute | solution.py:250
  18.1 27.8 %collective-permute-start.1 = (bf16[256,1152]{1,0:T(8,128)(2,1)S(1)}, bf16[256,1152]{1,0:T(8,128)(2,1)S(1)}, u32[]{:S(2)}, u32[]{:S(2)}) collective-permute-start(bf16[256,1152]{1,0:T(8,128)(2,1)S(1)} %shard_map.68.refs_0_), channel_id=1, source_target_pairs={{0,2},{1,3},{2,0},{3,1},{4,6},{5,7},{6,4},{7,5},{8,10},{9,11},{10,... | collective-permute-start | bytes 1769480 | tf_op jit(solution)/shard_map/ppermute | solution.py:250
  22.8 24.8 %collective-permute-start = (bf16[256,1152]{1,0:T(8,128)(2,1)S(1)}, bf16[256,1152]{1,0:T(8,128)(2,1)}, u32[]{:S(2)}, u32[]{:S(2)}) collective-permute-start(bf16[256,1152]{1,0:T(8,128)(2,1)S(1)} %shard_map.68.refs_0_), channel_id=1, source_target_pairs={{0,3},{1,0},{2,1},{3,2},{4,7},{5,4},{6,5},{7,6},{8,11},{9,8},{10,9... | collective-permute-start | bytes 1769480 | tf_op jit(solution)/shard_map/ppermute | solution.py:250
  26.1 1.2 copy-start.6
  28.6 1.0 copy-start
  66.8 20.4 %collective-permute-start.6 = (bf16[8,64,512]{2,1,0:T(8,128)(2,1)}, bf16[8,64,512]{2,1,0:T(8,128)(2,1)S(1)}, u32[]{:S(2)}, u32[]{:S(2)}) collective-permute-start(bf16[8,64,512]{2,1,0:T(8,128)(2,1)} %get-tuple-element.39), channel_id=1, source_target_pairs={{0,4},{4,0},{1,5},{5,1},{2,6},{6,2},{3,7},{7,3},{8,12},{12,8},{9,1... | collective-permute-start | bytes 1572872 | tf_op jit(solution)/shard_map/ppermute | solution.py:303
  69.3 17.9 %all-to-all-start.2 = ((bf16[16,32,128]{2,1,0:T(8,128)(2,1)}), bf16[16,32,128]{2,1,0:T(8,128)(2,1)}, u32[]{:S(2)}, u32[]{:S(2)}) async-start(bf16[16,32,128]{2,1,0:T(8,128)(2,1)} %get-tuple-element.45), calls=%async_computation.2 | async-start | bytes 262144 | tf_op jit(solution)/shard_map/all_to_all | solution.py:254
  77.4 1.6 %copy-start.5 = (bf16[1024,1024]{1,0:T(8,128)(2,1)S(1)}, bf16[1024,1024]{1,0:T(8,128)(2,1)}, u32[]{:S(2)}) copy-start(bf16[1024,1024]{1,0:T(8,128)(2,1)} %get-tuple-element.33.ds_ref) | copy-start | bytes 6291460
  79.0 8.2 %copy-start.1 = (bf16[16,64,512]{2,1,0:T(8,128)(2,1)S(1)}, bf16[16,64,512]{2,1,0:T(8,128)(2,1)}, u32[]{:S(2)}) copy-start(bf16[16,64,512]{2,1,0:T(8,128)(2,1)} %copy-done) | copy-start | bytes 3145732
  80.8 0.7 copy-start.7
  81.6 0.7 copy-start.8
  82.3 0.7 copy-start.9
  83.0 10.7 %copy-start.2 = (bf16[8,64,512]{2,1,0:T(8,128)(2,1)S(1)}, bf16[8,64,512]{2,1,0:T(8,128)(2,1)}, u32[]{:S(2)}) copy-start(bf16[8,64,512]{2,1,0:T(8,128)(2,1)} %get-tuple-element.38.a) | copy-start | bytes 1572868
  89.6 21.9 %all-to-all-start.3 = ((bf16[16,64,512]{2,1,0:T(8,128)(2,1)}), bf16[16,64,512]{2,1,0:T(8,128)(2,1)S(1)}, u32[]{:S(2)}, u32[]{:S(2)}) async-start(bf16[16,64,512]{2,1,0:T(8,128)(2,1)} %get-tuple-element.48), calls=%async_computation.3 | async-start | bytes 2097152 | tf_op jit(solution)/shard_map/all_to_all | solution.py:254
  94.3 13.8 %collective-permute-start.7 = (bf16[4,64,512]{2,1,0:T(8,128)(2,1)S(1)}, bf16[4,64,512]{2,1,0:T(8,128)(2,1)S(1)}, u32[]{:S(2)}, u32[]{:S(2)}) collective-permute-start(bf16[4,64,512]{2,1,0:T(8,128)(2,1)S(1)} %get-tuple-element.41), channel_id=1, source_target_pairs={{0,8},{8,0},{16,24},{24,16},{32,40},{40,32},{48,56},{56,48},{1,9},... | collective-permute-start | bytes 786440 | tf_op jit(solution)/shard_map/ppermute | solution.py:326
  96.8 33.9 %collective-permute-start.3 = (bf16[256,576]{1,0:T(8,128)(2,1)}, bf16[256,576]{1,0:T(8,128)(2,1)S(1)}, u32[]{:S(2)}, u32[]{:S(2)}) collective-permute-start(bf16[256,576]{1,0:T(8,128)(2,1)} %copy-done.9), channel_id=1, source_target_pairs={{0,1},{1,2},{2,3},{3,0},{4,5},{5,6},{6,7},{7,4},{8,9},{9,10},{10,1... | collective-permute-start | bytes 884744 | tf_op jit(solution)/shard_map/ppermute | solution.py:250
  100.2 30.6 %collective-permute-start.4 = (bf16[256,576]{1,0:T(8,128)(2,1)}, bf16[256,576]{1,0:T(8,128)(2,1)}, u32[]{:S(2)}, u32[]{:S(2)}) collective-permute-start(bf16[256,576]{1,0:T(8,128)(2,1)} %copy-done.8), channel_id=1, source_target_pairs={{0,2},{1,3},{2,0},{3,1},{4,6},{5,7},{6,4},{7,5},{8,10},{9,11},{10,... | collective-permute-start | bytes 884744 | tf_op jit(solution)/shard_map/ppermute | solution.py:250
  104.8 26.0 %collective-permute-start.5 = (bf16[256,576]{1,0:T(8,128)(2,1)}, bf16[256,576]{1,0:T(8,128)(2,1)}, u32[]{:S(2)}, u32[]{:S(2)}) collective-permute-start(bf16[256,576]{1,0:T(8,128)(2,1)} %copy-done.7), channel_id=1, source_target_pairs={{0,3},{1,0},{2,1},{3,2},{4,7},{5,4},{6,5},{7,6},{8,11},{9,8},{10,9... | collective-permute-start | bytes 884744 | tf_op jit(solution)/shard_map/ppermute | solution.py:250
  108.8 13.5 %collective-permute-start.8 = (bf16[2,64,512]{2,1,0:T(8,128)(2,1)S(1)}, bf16[2,64,512]{2,1,0:T(8,128)(2,1)S(1)}, u32[]{:S(2)}, u32[]{:S(2)}) collective-permute-start(bf16[2,64,512]{2,1,0:T(8,128)(2,1)S(1)} %get-tuple-element.44), channel_id=1, source_target_pairs={{0,16},{8,24},{16,0},{24,8},{32,48},{40,56},{48,32},{56,40},{1,17}... | collective-permute-start | bytes 393224 | tf_op jit(solution)/shard_map/ppermute | solution.py:326
  112.5 22.4 %all-to-all-start.4 = ((f32[32,8,128]{2,1,0:T(8,128)}), f32[32,8,128]{2,1,0:T(8,128)S(1)}, u32[]{:S(2)}, u32[]{:S(2)}) async-start(f32[32,8,128]{2,1,0:T(8,128)} %get-tuple-element.54), calls=%async_computation.4 | async-start | bytes 262144 | tf_op jit(solution)/shard_map/all_to_all | solution.py:254
  123.5 10.8 %collective-permute-start.9 = (bf16[1,64,512]{2,1,0:T(8,128)(2,1)S(1)}, bf16[1,64,512]{2,1,0:T(8,128)(2,1)S(1)}, u32[]{:S(2)}, u32[]{:S(2)}) collective-permute-start(bf16[1,64,512]{2,1,0:T(8,128)(2,1)S(1)} %get-tuple-element.52), channel_id=1, source_target_pairs={{0,32},{8,40},{16,48},{24,56},{32,0},{40,8},{48,16},{56,24},{1,33}... | collective-permute-start | bytes 196616 | tf_op jit(solution)/shard_map/ppermute | solution.py:326
